TPU v7x, 32 devices: a whole 2x2x4 slice. The times are simulated.
32 devices in a mesh: val: 16 (over z, y, core), qry: 2 (over x).
Axes of the slice: x: 2, y: 2, z: 4, core: 2. Of those that a mesh axis runs over, the one named last changes fastest.
Arguments:
- queries: bfloat16 [3072, 512], P('qry'), may hold values from -20 to 20
- pool_keys: bfloat16 [8192, 512], P('val'), may hold values from -20 to 20
- pool_values: bfloat16 [8192, 512], P('val'), may hold values from -6 to 6
- out_grad: bfloat16 [3072, 512], P('qry'), may hold values from -6 to 6
- lse: float32 [2, 3072], P(None, 'qry'), as said below
- compat: int32 [2, 16, 12], P(None, 'val', 'qry'), may hold values from 0 to 1, as said below
- targets: int32 [3072, 2], P('qry'), may hold values from 0 to 8191
Outputs:
- query_grad: bfloat16 [3072, 512], P('qry')
- key_grad: bfloat16 [8192, 512], P(('val', 'qry'))
- value_grad: bfloat16 [8192, 512], P(('val', 'qry'))
Inputs may be any that keep to these rules, and one draw needn't show every extreme that they name: `lse`: the forward pass's value: the log of the sum over allowed j of exp(scores[h, i, j]). `compat`: 1 where a block of 512 pool values and a block of 256 queries are type-compatible for that head.
All inputs are finite; a program needn't handle non-finite values.
Results may differ from a plain program's by a relative error of at most 0.0053.
Values may be sent and summed in bfloat16 or wider, within the bound.
No kernel may reach another device: no remote copies, remote signals or barrier semaphores. Data moves between devices by JAX's collectives and lax.ppermute only.
A program may use at most 128 MiB of HBM per device.

v0:
```python
from functools import partial

import jax
import jax.numpy as jnp
from jax import lax
from jax.sharding import PartitionSpec as P


def on_device(queries, pool_keys, pool_values, out_grad, lse, compat, targets):
    num_heads = compat.shape[0]
    head_width = queries.shape[1] // num_heads
    query_count = queries.shape[0]
    value_count = pool_keys.shape[0]
    value_blocks = compat.shape[1]
    query_block = query_count // compat.shape[2]
    value_block = value_count // value_blocks
    score_scale = head_width ** (-0.5)
    value_index = lax.axis_index("val")
    offset = value_index * value_count
    block_ids = value_index * value_blocks + jnp.arange(value_blocks, dtype=jnp.int32)
    positions = jnp.arange(value_count, dtype=jnp.int32)

    def head_slices(head_index, first_row):
        col_low = head_index * head_width
        query_tile = queries[first_row : first_row + query_count, col_low : col_low + head_width]
        grad_tile = out_grad[first_row : first_row + query_count, col_low : col_low + head_width]
        return (
            query_tile,
            grad_tile,
            pool_keys[:, col_low : col_low + head_width],
            pool_values[:, col_low : col_low + head_width],
        )

    def first_pass(head_index, first_row, allowed):
        query_tile, grad_tile, key_head, value_head = head_slices(head_index, first_row)
        scores = score_scale * jnp.einsum(
            "qd,kd->qk", query_tile, key_head, preferred_element_type=jnp.float32
        )
        dprobs = jnp.einsum("qd,kd->qk", grad_tile, value_head, preferred_element_type=jnp.float32)
        lse_rows = lse[head_index, first_row : first_row + query_count]
        soft_probs = jnp.where(allowed, jnp.exp(scores - lse_rows[:, None]), 0.0)
        return (soft_probs, dprobs)

    records = []
    for head_index in range(num_heads):
        first_row = 0
        target_ids = targets[first_row : first_row + query_count, head_index]
        block_marks = compat[
            head_index, :, first_row // query_block : (first_row + query_count) // query_block
        ]
        per_query = jnp.broadcast_to(
            jnp.transpose(block_marks)[:, None, :],
            (query_count // query_block, query_block, value_blocks),
        ).reshape(query_count, value_blocks)
        target_hits = (target_ids // value_block)[:, None] == block_ids[None, :]
        usable = (per_query == 1) | target_hits
        layout_allowed = jnp.broadcast_to(
            usable[:, :, None], (query_count, value_blocks, value_block)
        ).reshape(query_count, value_count)
        onehot = ((target_ids - offset)[:, None] == positions[None, :]).astype(jnp.float32)
        allowed, onehot, is_live = (layout_allowed, onehot, jnp.any(usable))
        compute = partial(first_pass, head_index, first_row, allowed)
        outcome = compute()
        records.append((head_index, first_row, allowed, onehot, is_live, outcome))
    local_delta = jnp.stack(
        [
            jnp.concatenate(
                [
                    jnp.sum(record[5][0] * record[5][1], axis=1)
                    for record in records
                    if record[0] == head_index
                ]
            )
            for head_index in range(num_heads)
        ]
    )
    row_delta = lax.psum(local_delta, "val")

    def second_pass(head_index, first_row, soft_probs, dprobs, onehot):
        query_tile, grad_tile, key_head, value_head = head_slices(head_index, first_row)
        delta_rows = row_delta[head_index, first_row : first_row + query_count]
        dscores = soft_probs * (dprobs - delta_rows[:, None] + 1.0) - onehot
        probs_low = soft_probs.astype(jnp.bfloat16)
        dscores_low = dscores.astype(jnp.bfloat16)
        query_term = score_scale * jnp.einsum(
            "qk,kd->qd", dscores_low, key_head, preferred_element_type=jnp.float32
        )
        key_term = score_scale * jnp.einsum(
            "qk,qd->kd", dscores_low, query_tile, preferred_element_type=jnp.float32
        )
        value_term = jnp.einsum(
            "qk,qd->kd", probs_low, grad_tile, preferred_element_type=jnp.float32
        )
        return (query_term, key_term, value_term)

    query_lists = [[] for head_index in range(num_heads)]
    key_sums = [
        jnp.zeros((value_count, head_width), jnp.float32) for head_index in range(num_heads)
    ]
    value_sums = [
        jnp.zeros((value_count, head_width), jnp.float32) for head_index in range(num_heads)
    ]
    for record in records:
        compute = partial(second_pass, record[0], record[1], record[5][0], record[5][1], record[3])
        outcome = compute()
        query_lists[record[0]].append(outcome[0])
        key_sums[record[0]] = outcome[1]
        value_sums[record[0]] = outcome[2]
    query_part = jnp.concatenate([pieces[0] for pieces in query_lists], axis=1)
    pool_part = jnp.concatenate(key_sums + value_sums, axis=1)
    query_grad = lax.psum(query_part, "val").astype(jnp.bfloat16)
    split_width = num_heads * head_width
    pool_whole = lax.psum(pool_part, "qry")
    share_rows = value_count // lax.axis_size("qry")
    pool_grad = lax.dynamic_slice_in_dim(
        pool_whole, lax.axis_index("qry") * share_rows, share_rows, 0
    )
    return (
        query_grad,
        pool_grad[:, :split_width].astype(jnp.bfloat16),
        pool_grad[:, split_width:].astype(jnp.bfloat16),
    )


def solution(mesh):
    placed = (
        P("qry", None),
        P("val", None),
        P("val", None),
        P("qry", None),
        P(None, "qry"),
        P(None, "val", "qry"),
        P("qry", None),
    )
    return jax.shard_map(
        on_device,
        mesh=mesh,
        in_specs=placed,
        out_specs=(P("qry", None), P(("val", "qry"), None), P(("val", "qry"), None)),
        check_vma=False,
    )
```

profile of v0, /device:TPU:0, one launch (start us, length us, event | category | flops | bytes accessed | tf_op | source)
XLA Modules:
  0.0 215.7 jit_solution(4878931245627023506)
XLA Ops:
  0.6 0.7 compare_bitcast_fusion
  1.3 0.1 broadcast_bitcast_fusion
  1.4 0.9 or_reduce_fusion.1
  2.3 0.0 copy-start.16
  2.3 0.0 copy-start.10
  2.3 0.0 copy-start.12
  2.4 1.9 fusion.16
  4.3 0.0 copy-done.16
  4.3 0.0 copy-start
  4.4 0.0 copy-done.10
  4.4 0.0 copy-done.12
  4.4 0.0 copy-start.8
  4.4 0.0 copy-start.14
  4.4 1.0 multiply_reduce_fusion.1
  5.4 0.6 copy-done
  6.0 0.9 copy-done.8
  6.9 0.1 copy-done.14
  7.0 0.6 fusion.11
  7.6 0.0 copy-start.2
  7.6 0.0 copy-start.15
  7.6 2.7 %multiply_reduce_fusion = (f32[1536]{0:T(1024)S(1)}, f32[1536,512]{0,1:T(8,128)}) fusion(f32[1536,512]{0,1:T(8,128)S(1)} %fusion.11, f32[1536]{0:T(1024)S(1)} %get-tuple-element.13, bf16[512,512]{1,0:T(8,128)(2,1)S(1)} %copy-done.10, bf16[1536,512]{1,0:T(8,128)(2,1)S(1)} %copy-done.12, pred[1536]{0:T(1024)(128)(4,1)S(1)} %get-tuple-element.11), kind=kOutput, calls=%fused_computation.13 | convolution fusion | flops 406583808 | bytes 7356416 | tf_op jit(solution)/shard_map/qd,kd->qk/dot_general | solution.py:36
  10.3 0.0 copy-done.2
  10.4 63.0 %psum.21 = f32[2,1536]{1,0:T(2,128)S(1)} all-reduce(f32[2,1536]{1,0:T(2,128)S(1)} %pad_maximum_fusion.2), channel_id=1, replica_groups=mesh['val'=16,'qry'=2] {'val'}, use_global_device_ids=true, to_apply=%region_2.3 | all-reduce | flops 3072 | bytes 24576 | tf_op jit(solution)/shard_map/psum | solution.py:77
  73.3 0.0 copy-done.15
  73.4 0.0 copy-start.13
  73.4 0.0 copy-start.1
  73.4 0.0 copy-start.3
  73.4 2.9 %subtract_convert_fusion.1 = bf16[1536,512]{0,1:T(8,128)(2,1)S(1)} fusion(f32[1536,512]{0,1:T(8,128)S(1)} %get-tuple-element.21, f32[1536,512]{0,1:T(8,128)} %copy-done, s32[1536]{0:T(1024)S(1)} %get-tuple-element.8, f32[1536]{0:T(1024)S(1)} %get-tuple-element.6), kind=kLoop, calls=%fused_computation.11 | loop fusion | flops 5505024 | bytes 7876608 | tf_op jit(solution)/shard_map/convert_element_type | solution.py:84
  76.3 0.0 copy-done.13
  76.3 0.0 copy-start.4
  76.4 0.6 convolution_multiply_fusion.5
  77.0 0.0 copy-done.1
  77.0 1.3 copy-done.3
  78.2 0.8 subtract_convert_fusion
  79.1 0.0 copy-done.4
  79.1 0.0 copy-start.6
  79.1 0.0 copy-start.9
  79.1 0.6 convolution_multiply_fusion.4
  79.8 1.3 copy-done.9
  81.1 0.6 fusion.8
  81.7 0.0 copy-done.6
  81.7 0.6 fusion.6
  82.4 0.2 pad_maximum_fusion.1
  82.5 47.0 %all-reduce.2 = bf16[512,1024]{0,1:T(8,128)(2,1)S(1)} all-reduce(f32[512,1024]{0,1:T(8,128)S(1)} %pad_maximum_fusion.1), channel_id=1, replica_groups=mesh['val'=16,'qry'=2] {'qry'}, use_global_device_ids=true, to_apply=%region_4.5 | all-reduce | flops 524288 | bytes 3145728 | tf_op jit(solution)/shard_map/psum | solution.py:113
  129.6 0.0 copy-start.5
  129.7 0.8 copy.11
  130.5 0.8 copy.12
  131.4 0.0 copy-done.5
  131.4 0.0 copy-start.7
  131.4 0.0 copy-start.11
  131.4 1.7 convolution_multiply_fusion.3
  133.1 0.0 copy-done.7
  133.1 0.0 copy-done.11
  133.1 0.6 convolution_multiply_fusion.2
  133.7 1.9 pad_maximum_fusion
  135.6 78.5 %all-reduce.3 = bf16[1536,512]{0,1:T(8,128)(2,1)S(1)} all-reduce(f32[1536,512]{0,1:T(8,128)} %pad_maximum_fusion), channel_id=1, replica_groups=mesh['val'=16,'qry'=2] {'val'}, use_global_device_ids=true, to_apply=%region_3.4 | all-reduce | flops 786432 | bytes 4718592 | tf_op jit(solution)/shard_map/psum | solution.py:111
  214.1 1.6 copy.10
  (10 shorter events, 0.2 us)
Async XLA Ops:
  2.3 2.0 copy-start.16
  2.3 2.0 copy-start.10
  2.3 2.0 copy-start.12
  4.3 1.7 copy-start
  4.4 2.5 %copy-start.8 = (bf16[1536,512]{1,0:T(8,128)(2,1)S(1)}, bf16[1536,512]{1,0:T(8,128)(2,1)}, u32[]{:S(2)}) copy-start(bf16[1536,512]{1,0:T(8,128)(2,1)} %param.10) | copy-start | bytes 4718596
  4.4 2.6 %copy-start.14 = (bf16[512,512]{1,0:T(8,128)(2,1)S(1)}, bf16[512,512]{1,0:T(8,128)(2,1)}, u32[]{:S(2)}) copy-start(bf16[512,512]{1,0:T(8,128)(2,1)} %param.9) | copy-start | bytes 1572868
  7.6 2.7 %copy-start.2 = (f32[1536,512]{0,1:T(8,128)}, f32[1536,512]{0,1:T(8,128)S(1)}, u32[]{:S(2)}) copy-start(f32[1536,512]{0,1:T(8,128)S(1)} %fusion.11) | copy-start | bytes 9437188
  7.6 65.8 %copy-start.15 = (s32[1536,2]{0,1:T(2,128)S(1)}, s32[1536,2]{0,1:T(2,128)}, u32[]{:S(2)}) copy-start(s32[1536,2]{0,1:T(2,128)} %param.13) | copy-start | bytes 36868
  73.4 2.9 %copy-start.13 = (bf16[1536,512]{1,0:T(8,128)(2,1)S(1)}, bf16[1536,512]{1,0:T(8,128)(2,1)}, u32[]{:S(2)}) copy-start(bf16[1536,512]{1,0:T(8,128)(2,1)} %param.7) | copy-start | bytes 4718596
  73.4 3.6 %copy-start.1 = (f32[1536,512]{0,1:T(8,128)S(1)}, f32[1536,512]{0,1:T(8,128)}, u32[]{:S(2)}) copy-start(f32[1536,512]{0,1:T(8,128)} %get-tuple-element.19) | copy-start | bytes 9437188
  73.4 4.8 %copy-start.3 = (f32[1536,512]{0,1:T(8,128)S(1)}, f32[1536,512]{0,1:T(8,128)}, u32[]{:S(2)}) copy-start(f32[1536,512]{0,1:T(8,128)} %copy-done.2) | copy-start | bytes 9437188
  76.3 2.7 %copy-start.4 = (bf16[1536,512]{0,1:T(8,128)(2,1)}, bf16[1536,512]{0,1:T(8,128)(2,1)S(1)}, u32[]{:S(2)}) copy-start(bf16[1536,512]{0,1:T(8,128)(2,1)S(1)} %subtract_convert_fusion.1) | copy-start | bytes 4718596
  79.1 2.6 %copy-start.6 = (bf16[1536,512]{0,1:T(8,128)(2,1)}, bf16[1536,512]{0,1:T(8,128)(2,1)S(1)}, u32[]{:S(2)}) copy-start(bf16[1536,512]{0,1:T(8,128)(2,1)S(1)} %subtract_convert_fusion) | copy-start | bytes 4718596
  79.1 2.0 copy-start.9
  129.6 1.8 copy-start.5
  131.4 1.7 copy-start.7
  131.4 1.7 copy-start.11
where the time goes:
time: 216 us
  blocking collectives  188 us (87%)
  matrix products  11.1 us (5%)
  local copies, waits for them, and re-layouts  7.74 us (4%)
  other arithmetic  7.41 us (3%)
    psum x1, blocking collectives, on_device(): query_grad = lax.psum(query_part, 'val').astype(jnp.bfloat16)  78.5 us
    psum x1, blocking collectives, on_device(): row_delta = lax.psum(local_delta, 'val')  63 us
    psum x1, blocking collectives, on_device(): pool_whole = lax.psum(pool_part, 'qry')  47 us
    unnamed x40, local copies, waits for them, and re-layouts  7.58 us

commit v1 on v0

v1 whole, which is shorter than its diff:
```python
import math
from functools import partial

import jax
import jax.numpy as jnp
from jax import lax
from jax.experimental import pallas as pl
from jax.experimental.pallas import tpu as pltpu
from jax.sharding import PartitionSpec as P

LOG2E = math.log2(math.e)
MASKED = 1e30
NT = (((1,), (1,)), ((), ()))
NN = (((1,), (0,)), ((), ()))
TN = (((0,), (0,)), ((), ()))
VMEM_LIMIT = 40 * 1024 * 1024


def dot(a, b, dims):
    return lax.dot_general(a, b, dims, preferred_element_type=jnp.float32)


def row_terms(place, compat, lse_ref, targets_ref, head, block, value_count):
    target = targets_ref[pl.ds(head, 1), :]
    local = target - place[0] * value_count
    hit = (local >= 0) & (local < value_count)
    usable = hit | (compat[head, 0, block] == 1)
    lse_rows = jnp.where(usable, lse_ref[pl.ds(head, 1), :], MASKED) * LOG2E
    return lse_rows, local


def scatter_rows(place, total, own_ref, send_ref, columns):
    parts = send_ref.shape[0] + 1
    share = total.shape[0] // parts
    start = pl.multiple_of(place[1] * share, share)
    own_ref[:, columns] = total[pl.ds(start, share), :]
    for step in range(1, parts):
        other = lax.rem(place[1] + step, parts)
        start = pl.multiple_of(other * share, share)
        send_ref[step - 1, :, columns] = total[pl.ds(start, share), :].astype(jnp.bfloat16)


def forward_kernel(
    place, compat, q_ref, g_ref, k_ref, v_ref, lse_ref, targets_ref,
    delta_ref, own_ref, send_ref, total, *, heads, scale,
):
    block = pl.program_id(0)
    value_count, width = k_ref.shape[0], k_ref.shape[1] // heads
    for head in range(heads):
        columns = slice(head * width, (head + 1) * width)
        lse_rows, _ = row_terms(place, compat, lse_ref, targets_ref, head, block, value_count)
        scores = dot(k_ref[:, columns], q_ref[:, columns], NT)
        probs = jnp.exp2(scores * (scale * LOG2E) - lse_rows)
        dprobs = dot(v_ref[:, columns], g_ref[:, columns], NT)
        delta_ref[head : head + 1, :] = jnp.sum(probs * dprobs, axis=0, keepdims=True)
        term = dot(probs.astype(jnp.bfloat16), g_ref[:, columns], NN)

        @pl.when(block == 0)
        def _():
            total[head] = term

        @pl.when(block > 0)
        def _():
            total[head] += term

    @pl.when(block == pl.num_programs(0) - 1)
    def _():
        for head in range(heads):
            columns = slice(head * width, (head + 1) * width)
            scatter_rows(place, total.at[head], own_ref, send_ref, columns)


def backward_kernel(
    place, compat, q_ref, g_ref, k_ref, v_ref, lse_ref, targets_ref, delta_ref,
    query_ref, own_ref, send_ref, total, *, scale,
):
    block = pl.program_id(0)
    head = place[2]
    value_count = k_ref.shape[0]
    lse_rows, local = row_terms(place, compat, lse_ref, targets_ref, head, block, value_count)
    delta_rows = delta_ref[pl.ds(head, 1), :] - 1.0
    scores = dot(k_ref[...], q_ref[...], NT)
    probs = jnp.exp2(scores * (scale * LOG2E) - lse_rows)
    dprobs = dot(v_ref[...], g_ref[...], NT)
    dscores = probs * (dprobs - delta_rows)
    slots = lax.broadcasted_iota(jnp.int32, dscores.shape, 0)
    low = jnp.where(slots == local, dscores - 1.0, dscores).astype(jnp.bfloat16)
    query_ref[...] = (scale * dot(low, k_ref[...], TN)).astype(query_ref.dtype)
    term = scale * dot(low, q_ref[...], NN)

    @pl.when(block == 0)
    def _():
        total[...] = term

    @pl.when(block > 0)
    def _():
        total[...] += term

    @pl.when(block == pl.num_programs(0) - 1)
    def _():
        scatter_rows(place, total, own_ref, send_ref, slice(None))


def cost(queries, values, width, dots):
    return pl.CostEstimate(
        flops=2 * dots * queries * values * width,
        bytes_accessed=4 * (queries + values) * width,
        transcendentals=queries * values,
    )


def forward(place, compat, queries, keys, values, grads, lse, targets, parts):
    heads, _, blocks = compat.shape
    query_count, wide = queries.shape
    value_count = keys.shape[0]
    block = query_count // blocks
    share = value_count // parts
    rows = pl.BlockSpec((block, wide), lambda i, *_: (i, 0))
    pool = pl.BlockSpec((value_count, wide), lambda i, *_: (0, 0))
    flat = pl.BlockSpec((heads, block), lambda i, *_: (0, i))
    return pl.pallas_call(
        partial(forward_kernel, heads=heads, scale=(wide // heads) ** -0.5),
        grid_spec=pltpu.PrefetchScalarGridSpec(
            num_scalar_prefetch=2,
            grid=(blocks,),
            in_specs=[rows, rows, pool, pool, flat, flat],
            out_specs=[
                flat,
                pl.BlockSpec((share, wide), lambda i, *_: (0, 0)),
                pl.BlockSpec((parts - 1, share, wide), lambda i, *_: (0, 0, 0)),
            ],
            scratch_shapes=[pltpu.VMEM((heads, value_count, wide // heads), jnp.float32)],
        ),
        out_shape=[
            jax.ShapeDtypeStruct((heads, query_count), jnp.float32),
            jax.ShapeDtypeStruct((share, wide), jnp.float32),
            jax.ShapeDtypeStruct((parts - 1, share, wide), jnp.bfloat16),
        ],
        cost_estimate=cost(query_count, value_count, wide, 3),
        compiler_params=pltpu.CompilerParams(vmem_limit_bytes=VMEM_LIMIT),
        name="forward_pass",
    )(place, compat, queries, grads, keys, values, lse, targets)


def backward(place, compat, queries, keys, values, grads, lse, targets, delta, parts, out_dtype):
    heads, _, blocks = compat.shape
    query_count, wide = queries.shape
    width = wide // heads
    value_count = keys.shape[0]
    block = query_count // blocks
    share = value_count // parts
    rows = pl.BlockSpec((block, width), lambda i, place, _: (i, place[2]))
    pool = pl.BlockSpec((value_count, width), lambda i, place, _: (0, place[2]))
    flat = pl.BlockSpec((heads, block), lambda i, *_: (0, i))
    return pl.pallas_call(
        partial(backward_kernel, scale=width ** -0.5),
        grid_spec=pltpu.PrefetchScalarGridSpec(
            num_scalar_prefetch=2,
            grid=(blocks,),
            in_specs=[rows, rows, pool, pool, flat, flat, flat],
            out_specs=[
                pl.BlockSpec((block, width), lambda i, *_: (i, 0)),
                pl.BlockSpec((share, width), lambda i, *_: (0, 0)),
                pl.BlockSpec((parts - 1, share, width), lambda i, *_: (0, 0, 0)),
            ],
            scratch_shapes=[pltpu.VMEM((value_count, width), jnp.float32)],
        ),
        out_shape=[
            jax.ShapeDtypeStruct((query_count, width), out_dtype),
            jax.ShapeDtypeStruct((share, width), jnp.float32),
            jax.ShapeDtypeStruct((parts - 1, share, width), jnp.bfloat16),
        ],
        cost_estimate=cost(query_count, value_count, width, 4),
        compiler_params=pltpu.CompilerParams(vmem_limit_bytes=VMEM_LIMIT),
        name="backward_pass",
    )(place, compat, queries, grads, keys, values, lse, targets, delta)


def assemble_kernel(place, mine_ref, theirs_ref, out_ref, sems, *, chains, radix_y, radix_z):
    core, y, z = place[0], place[1], place[2]
    piece, width = mine_ref.shape[-2:]
    pieces = radix_y * radix_z
    copies = []
    for side, ref in enumerate((mine_ref, theirs_ref)):
        columns = pl.ds(pl.multiple_of((core ^ side) * width, width), width)
        for chain in range(chains):
            for step_y in range(radix_y):
                for step_z in range(radix_z):
                    index = chain * pieces + (y ^ step_y) * radix_z + (z ^ step_z)
                    rows = pl.ds(pl.multiple_of(index * piece, piece), piece)
                    copy = pltpu.make_async_copy(
                        ref.at[chain, step_y * radix_z + step_z],
                        out_ref.at[rows, columns],
                        sems.at[len(copies)],
                    )
                    copy.start()
                    copies.append(copy)
    for copy in copies:
        copy.wait()


def assemble(place, mine, theirs, radix_y, radix_z):
    chains, pieces, piece, width = mine.shape
    return pl.pallas_call(
        partial(assemble_kernel, chains=chains, radix_y=radix_y, radix_z=radix_z),
        grid_spec=pltpu.PrefetchScalarGridSpec(
            num_scalar_prefetch=1,
            grid=(),
            in_specs=[pl.BlockSpec(memory_space=pl.ANY)] * 2,
            out_specs=pl.BlockSpec(memory_space=pl.ANY),
            scratch_shapes=[pltpu.SemaphoreType.DMA((2 * chains * pieces,))],
        ),
        out_shape=jax.ShapeDtypeStruct((chains * pieces * piece, 2 * width), mine.dtype),
        name="assemble",
    )(place, mine, theirs)


def on_device(queries, pool_keys, pool_values, out_grad, lse, compat, targets):
    heads, value_blocks, _ = compat.shape
    query_count = queries.shape[0]
    width = queries.shape[1] // heads
    value_devices, parts = lax.axis_size("val"), lax.axis_size("qry")
    assert heads == 2 and value_blocks == 1 and value_devices % 8 == 0
    val, qry = lax.axis_index("val"), lax.axis_index("qry")
    radix_z = 4
    radix_y = value_devices // (2 * radix_z)
    core, y, z = lax.rem(val, 2), lax.rem(val // 2, radix_y), val // (2 * radix_y)

    def flip(array, mask):
        return lax.ppermute(array, "val", [(i, i ^ mask) for i in range(value_devices)])

    def turn(array, step):
        return lax.ppermute(array, "qry", [(i, (i + step) % parts) for i in range(parts)])

    def swap_shares(send):
        return [turn(send[step - 1], step) for step in range(1, parts)]

    def add(own, received):
        for array in received:
            own = own + array.astype(jnp.float32)
        return own

    operands = (compat, queries, pool_keys, pool_values, out_grad, lse, jnp.transpose(targets))

    def place(head):
        return jnp.stack([val, qry, head]).astype(jnp.int32)

    delta, value_own, value_send = forward(place(core), *operands, parts)
    stride = 1
    while stride < value_devices:
        delta = add(delta, [flip(delta, stride * step) for step in range(1, 4)])
        stride *= 4
    value_received = swap_shares(value_send)

    query_send, other_own, other_send = backward(
        place(1 - core), *operands, delta, parts, jnp.bfloat16
    )
    query_received = flip(query_send, 1)
    other_received = swap_shares(other_send)
    query_own, key_own, key_send = backward(place(core), *operands, delta, parts, jnp.float32)
    key_received = swap_shares(key_send)
    query_sum = add(query_own, [query_received])

    pieces = radix_y * radix_z
    chains = 2 if query_count % (2 * pieces * 16) == 0 else 1
    mine = []
    for chain in range(chains):
        rows = query_count // chains
        part = query_sum[chain * rows : (chain + 1) * rows]
        for radix, digit, stride in ((radix_y, y, 2), (radix_z, z, 2 * radix_y)):
            split = part.reshape(radix, part.shape[0] // radix, width)

            def pick(index):
                return lax.dynamic_index_in_dim(split, index, 0, keepdims=False)

            received = [
                flip(pick(digit ^ step).astype(jnp.bfloat16), stride * step)
                for step in range(1, radix)
            ]
            part = add(pick(digit), received)
        part = part.astype(jnp.bfloat16)[None]
        for radix, stride in ((radix_z, 2 * radix_y), (radix_y, 2)):
            part = jnp.concatenate(
                [part] + [flip(part, stride * step) for step in range(1, radix)], axis=0
            )
        mine.append(part)
    mine = jnp.stack(mine)
    theirs = flip(mine, 1)
    query_grad = assemble(
        jnp.stack([core, y, z]).astype(jnp.int32), mine, theirs, radix_y, radix_z
    )

    value_grad = add(value_own, value_received).astype(jnp.bfloat16)
    key_mine = add(key_own, key_received).astype(jnp.bfloat16)
    key_other = add(other_own, other_received).astype(jnp.bfloat16)
    key_grad = jnp.where(
        core == 0,
        jnp.concatenate([key_mine, key_other], axis=1),
        jnp.concatenate([key_other, key_mine], axis=1),
    )
    return query_grad, key_grad, value_grad


def solution(mesh):
    placed = (
        P("qry", None),
        P("val", None),
        P("val", None),
        P("qry", None),
        P(None, "qry"),
        P(None, "val", "qry"),
        P("qry", None),
    )
    return jax.shard_map(
        on_device,
        mesh=mesh,
        in_specs=placed,
        out_specs=(P("qry", None), P(("val", "qry"), None), P(("val", "qry"), None)),
        check_vma=False,
    )
```

time: 216 us -> 147 us (0.68)
  blocking collectives: 188 us -> 0 us
  Pallas kernels: 0 us -> 66 us
  starting transfers between devices: 0 us -> 32.7 us
  waiting for transfers between devices: 0 us -> 21.7 us
  local copies, waits for them, and re-layouts: 7.74 us -> 19.3 us
  matrix products: 11.1 us -> 0 us
  other arithmetic: 7.41 us -> 5.06 us
    psum x3 -> x0, blocking collectives: 188 us -> none  [the longest x1 78.5 us: on_device(): query_grad = lax.psum(query_part, 'val').astype(jnp.bfloat16)]
    pallas_call x0 -> x4, Pallas kernels: none -> 66 us  [the longest x1 49.7 us: assemble(): pl.pallas_call(partial(assemble_kernel, chains=chains, radix_y=radix_y, r...]
    ppermute x0 -> x27, starting transfers between devices: none -> 32.7 us  [the longest x24 30.1 us: flip(): lax.ppermute(array, 'val', [(i, i ^ mask) for i in range(value_devices)])]
    ppermute x0 -> x27, waiting for transfers between devices: none -> 21.7 us  [the longest x24 21.7 us: flip(): lax.ppermute(array, 'val', [(i, i ^ mask) for i in range(value_devices)])]
    unnamed x40 -> x50, local copies, waits for them, and re-layouts: 7.58 us -> 19.1 us
    dot_general x10 -> x0, matrix products: 11.1 us -> none  [the longest x2 3.73 us: first_pass(): jnp.einsum('qd,kd->qk', query_tile, key_head, preferred_element_type=jnp....]
  transfers between devices with their start and end apart: 0 -> 27, of which waited for: 0 -> 15; matrix products, arithmetic and copies ran while one was open for 0% -> 4% of each run, Pallas kernels for 0% -> 3%
where the time goes in v1:
time: 147 us; the launch traced here: 146 us
  Pallas kernels  66 us (45%)
  starting transfers between devices  32.7 us (22%)
  waiting for transfers between devices  21.7 us (15%)
  local copies, waits for them, and re-layouts  19.3 us (13%)
  other arithmetic  5.06 us (3%)
    pallas_call x1, Pallas kernels, assemble(): pl.pallas_call(partial(assemble_kernel, chains=chains, radix_y=radix_y, r...  49.7 us
    ppermute x24, starting transfers between devices, flip(): lax.ppermute(array, 'val', [(i, i ^ mask) for i in range(value_devices)])  30.1 us
    ppermute x24, waiting for transfers between devices, flip(): lax.ppermute(array, 'val', [(i, i ^ mask) for i in range(value_devices)])  21.7 us
    unnamed x50, local copies, waits for them, and re-layouts  19.1 us
    pallas_call x2, Pallas kernels, backward(): pl.pallas_call(partial(backward_kernel, scale=width ** (-0.5)), grid_spec...  9.5 us
    pallas_call x1, Pallas kernels, forward(): pl.pallas_call(partial(forward_kernel, heads=heads, scale=(wide // heads)...  6.81 us
  transfers between devices with their start and end apart: 27, of which 15 were waited for; matrix products, arithmetic and copies ran while one was open for 4% of the time, Pallas kernels for 3%

profile of v1, /device:TPU:0, one launch (start us, length us, event | category | flops | bytes accessed | tf_op | source)
XLA Modules:
  0.0 145.7 jit_solution(10976520952270021445)
XLA Ops:
  0.7 1.4 copy-done
  2.1 1.4 copy-done.2
  3.5 1.0 copy-done.5
  4.6 1.0 copy-done.8
  5.6 0.7 copy-done.11
  6.3 0.7 copy-done.14
  7.0 0.7 copy-done.17
  7.7 6.8 %forward_pass.1 = (f32[2,1536]{1,0:T(2,128)S(1)}, f32[256,512]{1,0:T(8,128)S(1)}, bf16[1,256,512]{2,1,0:T(8,128)(2,1)S(1)}) custom-call(s32[3]{0:T(128)S(1)} %pad_add_fusion.1.place, s32[2,1,6]{2,1,0:T(1,128)S(1)} %copy-done.17, bf16[1536,512]{1,0:T(8,128)(2,1)S(1)} %copy-done, bf16[1536,512]{1,0:T(8,128)(2,1)S(1)} %copy-done.2, ...), custom_call_target="tpu_custom_call" | custom-call | flops 2415919104 | bytes 4194304 | tf_op jit(solution)/shard_map/forward_pass/pallas_call | solution.py:121
  14.5 2.5 %collective-permute-start.2 = (f32[2,1536]{1,0:T(2,128)S(1)}, f32[2,1536]{1,0:T(2,128)S(1)}, u32[]{:S(2)}, u32[]{:S(2)}) collective-permute-start(f32[2,1536]{1,0:T(2,128)S(1)} %get-tuple-element.12), channel_id=1, source_target_pairs={{0,6},{2,4},{4,2},{6,0},{8,14},{10,12},{12,10},{14,8},{16,22},{18,... | collective-permute-start | bytes 36872 | tf_op jit(solution)/shard_map/ppermute | solution.py:230
  17.0 0.6 collective-permute-start.1
  17.7 0.7 collective-permute-done.2
  18.4 2.3 %collective-permute-done.1 = f32[2,1536]{1,0:T(2,128)S(1)} collective-permute-done((f32[2,1536]{1,0:T(2,128)S(1)}, f32[2,1536]{1,0:T(2,128)S(1)}, u32[]{:S(2)}, u32[]{:S(2)}) %collective-permute-start.1) | collective-permute-done | bytes 12320 | tf_op jit(solution)/shard_map/ppermute | solution.py:230
  20.7 3.7 %collective-permute-start.5 = (f32[2,1536]{1,0:T(2,128)S(1)}, f32[2,1536]{1,0:T(2,128)S(1)}, u32[]{:S(2)}, u32[]{:S(2)}) collective-permute-start(f32[2,1536]{1,0:T(2,128)S(1)} %add_add_fusion.1), channel_id=1, source_target_pairs={{0,24},{2,26},{4,28},{6,30},{8,16},{10,18},{12,20},{14,22},{16,8},... | collective-permute-start | bytes 36872 | tf_op jit(solution)/shard_map/ppermute | solution.py:230
  24.4 0.8 collective-permute-start.3
  25.3 1.2 collective-permute-done.5
  26.4 2.5 %collective-permute-done.4 = f32[2,1536]{1,0:T(2,128)S(1)} collective-permute-done((f32[2,1536]{1,0:T(2,128)S(1)}, f32[2,1536]{1,0:T(2,128)S(1)}, u32[]{:S(2)}, u32[]{:S(2)}) %collective-permute-start.4) | collective-permute-done | bytes 12320 | tf_op jit(solution)/shard_map/ppermute | solution.py:230
  29.0 1.4 copy-done.3
  30.4 1.0 copy-done.6
  31.5 1.0 copy-done.9
  32.5 0.7 copy-done.12
  33.2 0.7 copy-done.15
  33.9 0.7 copy-done.18
  34.6 4.8 %backward_pass.3 = (bf16[1536,256]{1,0:T(8,128)(2,1)S(1)}, f32[256,256]{1,0:T(8,128)S(1)}, bf16[1,256,256]{2,1,0:T(8,128)(2,1)S(1)}) custom-call(s32[3]{0:T(128)S(1)} %pad_add_fusion.3.place, s32[2,1,6]{2,1,0:T(1,128)S(1)} %copy-done.18, bf16[1536,512]{1,0:T(8,128)(2,1)S(1)} %copy-done.1, bf16[1536,512]{1,0:T(8,128)(2,1)S(1)} %copy-done.3, ...), custom_call_target="tpu_custom_call" | custom-call | flops 1610612736 | bytes 2097152 | tf_op jit(solution)/shard_map/backward_pass/pallas_call | solution.py:155
  39.4 1.6 %collective-permute-start.26 = (bf16[256,512]{1,0:T(8,128)(2,1)S(1)}, bf16[256,512]{1,0:T(8,128)(2,1)}, u32[]{:S(2)}, u32[]{:S(2)}) collective-permute-start(bf16[256,512]{1,0:T(8,128)(2,1)S(1)} %bitcast.64), channel_id=1, source_target_pairs={{0,1},{1,0},{2,3},{3,2},{4,5},{5,4},{6,7},{7,6},{8,9},{9,8},{10,11... | collective-permute-start | bytes 786440 | tf_op jit(solution)/shard_map/ppermute | solution.py:233
  41.0 1.4 copy-done.4
  42.4 1.0 copy-done.7
  43.4 1.0 copy-done.10
  44.5 0.7 copy-done.13
  45.2 0.7 copy-done.16
  45.9 0.7 copy-done.19
  46.6 4.7 %backward_pass.2 = (f32[1536,256]{1,0:T(8,128)S(1)}, f32[256,256]{1,0:T(8,128)S(1)}, bf16[1,256,256]{2,1,0:T(8,128)(2,1)S(1)}) custom-call(s32[3]{0:T(128)S(1)} %pad_add_fusion.1.place, s32[2,1,6]{2,1,0:T(1,128)S(1)} %copy-done.19, bf16[1536,512]{1,0:T(8,128)(2,1)S(1)} %copy-done.1, bf16[1536,512]{1,0:T(8,128)(2,1)S(1)} %copy-done.4, ...), custom_call_target="tpu_custom_call" | custom-call | flops 1610612736 | bytes 2097152 | tf_op jit(solution)/shard_map/backward_pass/pallas_call | solution.py:155
  51.3 1.3 convert_add_fusion
  52.8 0.7 collective-permute-start.7
  53.6 0.7 pad_add_fusion.place
  54.2 0.5 collective-permute-start.25
  54.8 1.4 collective-permute-start.15
  56.2 4.4 %collective-permute-done.7 = bf16[384,256]{1,0:T(8,128)(2,1)S(1)} collective-permute-done((bf16[384,256]{1,0:T(8,128)(2,1)S(1)}, bf16[384,256]{1,0:T(8,128)(2,1)S(1)}, u32[]{:S(2)}, u32[]{:S(2)}) %collective-permute-start.7) | collective-permute-done | bytes 196640 | tf_op jit(solution)/shard_map/ppermute | solution.py:230
  60.8 3.5 %collective-permute-start.10 = (bf16[96,256]{1,0:T(8,128)(2,1)S(1)}, bf16[96,256]{1,0:T(8,128)(2,1)S(1)}, u32[]{:S(2)}, u32[]{:S(2)}) collective-permute-start(bf16[96,256]{1,0:T(8,128)(2,1)S(1)} %get-tuple-element.28), channel_id=1, source_target_pairs={{0,24},{2,26},{4,28},{6,30},{8,16},{10,18},{12,20},{14,22},{16,8},... | collective-permute-start | bytes 147464 | tf_op jit(solution)/shard_map/ppermute | solution.py:230
  64.3 1.8 %collective-permute-start.9 = (bf16[96,256]{1,0:T(8,128)(2,1)S(1)}, bf16[96,256]{1,0:T(8,128)(2,1)S(1)}, u32[]{:S(2)}, u32[]{:S(2)}) collective-permute-start(bf16[96,256]{1,0:T(8,128)(2,1)S(1)} %get-tuple-element.29), channel_id=1, source_target_pairs={{0,16},{2,18},{4,20},{6,22},{8,24},{10,26},{12,28},{14,30},{16,0},... | collective-permute-start | bytes 147464 | tf_op jit(solution)/shard_map/ppermute | solution.py:230
  66.3 1.1 collective-permute-done.10
  67.4 3.2 %collective-permute-start.18 = (bf16[96,256]{1,0:T(8,128)(2,1)S(1)}, bf16[96,256]{1,0:T(8,128)(2,1)S(1)}, u32[]{:S(2)}, u32[]{:S(2)}) collective-permute-start(bf16[96,256]{1,0:T(8,128)(2,1)S(1)} %get-tuple-element.31), channel_id=1, source_target_pairs={{0,24},{2,26},{4,28},{6,30},{8,16},{10,18},{12,20},{14,22},{16,8},... | collective-permute-start | bytes 147464 | tf_op jit(solution)/shard_map/ppermute | solution.py:230
  70.6 0.8 collective-permute-start.17
  71.4 1.4 collective-permute-start.13
  72.8 0.6 collective-permute-done.18
  73.4 1.4 collective-permute-start.12
  74.8 1.6 %collective-permute-done.17 = bf16[96,256]{1,0:T(8,128)(2,1)S(1)} collective-permute-done((bf16[96,256]{1,0:T(8,128)(2,1)S(1)}, bf16[96,256]{1,0:T(8,128)(2,1)S(1)}, u32[]{:S(2)}, u32[]{:S(2)}) %collective-permute-start.17) | collective-permute-done | bytes 49184 | tf_op jit(solution)/shard_map/ppermute | solution.py:230
  76.5 0.8 collective-permute-start.11
  77.3 0.2 collective-permute-done.13
  77.5 1.8 %collective-permute-start.21 = (bf16[1,96,256]{2,1,0:T(8,128)(2,1)S(1)}, bf16[1,96,256]{2,1,0:T(8,128)(2,1)S(1)}, u32[]{:S(2)}, u32[]{:S(2)}) collective-permute-start(bf16[1,96,256]{2,1,0:T(8,128)(2,1)S(1)} %get-tuple-element.24), channel_id=1, source_target_pairs={{0,24},{2,26},{4,28},{6,30},{8,16},{10,18},{12,20},{14,22},{16,8},... | collective-permute-start | bytes 147464 | tf_op jit(solution)/shard_map/ppermute | solution.py:230
  79.3 0.2 collective-permute-done.12
  79.5 1.4 collective-permute-start.20
  80.9 0.1 collective-permute-done.11
  81.0 1.9 %collective-permute-start.19 = (bf16[1,96,256]{2,1,0:T(8,128)(2,1)S(1)}, bf16[1,96,256]{2,1,0:T(8,128)(2,1)S(1)}, u32[]{:S(2)}, u32[]{:S(2)}) collective-permute-start(bf16[1,96,256]{2,1,0:T(8,128)(2,1)S(1)} %get-tuple-element.24), channel_id=1, source_target_pairs={{0,8},{2,10},{4,12},{6,14},{8,0},{10,2},{12,4},{14,6},{16,24},{18,... | collective-permute-start | bytes 147464 | tf_op jit(solution)/shard_map/ppermute | solution.py:230
  82.9 0.5 collective-permute-done.21
  83.5 0.5 collective-permute-start.24
  84.0 0.5 collective-permute-done.20
  84.5 0.6 collective-permute-start.14
  85.2 1.4 collective-permute-start.22
  86.7 3.5 %collective-permute-done.14 = bf16[4,96,256]{2,1,0:T(8,128)(2,1)S(1)} collective-permute-done((bf16[4,96,256]{2,1,0:T(8,128)(2,1)S(1)}, bf16[4,96,256]{2,1,0:T(8,128)(2,1)S(1)}, u32[]{:S(2)}, u32[]{:S(2)}) %collective-permute-start.14) | collective-permute-done | bytes 196640 | tf_op jit(solution)/shard_map/ppermute | solution.py:230
  90.2 2.1 %collective-permute-done.22 = bf16[4,96,256]{2,1,0:T(8,128)(2,1)S(1)} collective-permute-done((bf16[4,96,256]{2,1,0:T(8,128)(2,1)S(1)}, bf16[4,96,256]{2,1,0:T(8,128)(2,1)S(1)}, u32[]{:S(2)}, u32[]{:S(2)}) %collective-permute-start.22) | collective-permute-done | bytes 196640 | tf_op jit(solution)/shard_map/ppermute | solution.py:230
  92.5 0.8 maximum_select_fusion
  93.4 1.7 %add_convert_fusion = bf16[256,512]{1,0:T(8,128)(2,1)} fusion(f32[256,512]{1,0:T(8,128)S(1)} %get-tuple-element.19, bf16[256,512]{1,0:T(8,128)(2,1)} %collective-permute-done.26), kind=kLoop, calls=%fused_computation.2 | loop fusion | flops 393216 | bytes 1048576 | tf_op jit(solution)/shard_map/convert_element_type | solution.py:293
  95.1 0.9 copy-done.21
  96.0 49.7 %assemble.1 = bf16[1536,512]{1,0:T(8,128)(2,1)} custom-call(s32[3]{0:T(128)} %pad_add_fusion.place, bf16[2,8,96,256]{3,2,1,0:T(8,128)(2,1)} %copy-done.20, bf16[2,8,96,256]{3,2,1,0:T(8,128)(2,1)} %copy-done.21), custom_call_target="tpu_custom_call" | custom-call | tf_op jit(solution)/shard_map/assemble/pallas_call | solution.py:204
  (68 shorter events, 1.2 us)
Async XLA Ops:
  0.7 1.4 copy-start
  2.1 1.4 copy-start.2
  3.5 1.0 copy-start.5
  4.6 1.0 copy-start.8
  5.6 0.7 copy-start.11
  6.3 0.7 copy-start.14
  7.0 0.7 copy-start.17
  7.7 21.3 %copy-start.1 = (bf16[1536,512]{1,0:T(8,128)(2,1)S(1)}, bf16[1536,512]{1,0:T(8,128)(2,1)}, u32[]{:S(2)}) copy-start(bf16[1536,512]{1,0:T(8,128)(2,1)} %q_ref.5) | copy-start | bytes 4718596
  14.5 3.9 %collective-permute-start.2 = (f32[2,1536]{1,0:T(2,128)S(1)}, f32[2,1536]{1,0:T(2,128)S(1)}, u32[]{:S(2)}, u32[]{:S(2)}) collective-permute-start(f32[2,1536]{1,0:T(2,128)S(1)} %get-tuple-element.12), channel_id=1, source_target_pairs={{0,6},{2,4},{4,2},{6,0},{8,14},{10,12},{12,10},{14,8},{16,22},{18,... | collective-permute-start | bytes 36872 | tf_op jit(solution)/shard_map/ppermute | solution.py:230
  17.0 3.7 %collective-permute-start.1 = (f32[2,1536]{1,0:T(2,128)S(1)}, f32[2,1536]{1,0:T(2,128)S(1)}, u32[]{:S(2)}, u32[]{:S(2)}) collective-permute-start(f32[2,1536]{1,0:T(2,128)S(1)} %get-tuple-element.12), channel_id=1, source_target_pairs={{0,4},{2,6},{4,0},{6,2},{8,12},{10,14},{12,8},{14,10},{16,20},{18,... | collective-permute-start | bytes 36872 | tf_op jit(solution)/shard_map/ppermute | solution.py:230
  17.6 3.1 %collective-permute-start = (f32[2,1536]{1,0:T(2,128)S(1)}, f32[2,1536]{1,0:T(2,128)S(1)}, u32[]{:S(2)}, u32[]{:S(2)}) collective-permute-start(f32[2,1536]{1,0:T(2,128)S(1)} %get-tuple-element.12), channel_id=1, source_target_pairs={{0,2},{2,0},{4,6},{6,4},{8,10},{10,8},{12,14},{14,12},{16,18},{18,... | collective-permute-start | bytes 36872 | tf_op jit(solution)/shard_map/ppermute | solution.py:230
  20.7 5.7 %collective-permute-start.5 = (f32[2,1536]{1,0:T(2,128)S(1)}, f32[2,1536]{1,0:T(2,128)S(1)}, u32[]{:S(2)}, u32[]{:S(2)}) collective-permute-start(f32[2,1536]{1,0:T(2,128)S(1)} %add_add_fusion.1), channel_id=1, source_target_pairs={{0,24},{2,26},{4,28},{6,30},{8,16},{10,18},{12,20},{14,22},{16,8},... | collective-permute-start | bytes 36872 | tf_op jit(solution)/shard_map/ppermute | solution.py:230
  24.4 4.6 %collective-permute-start.4 = (f32[2,1536]{1,0:T(2,128)S(1)}, f32[2,1536]{1,0:T(2,128)S(1)}, u32[]{:S(2)}, u32[]{:S(2)}) collective-permute-start(f32[2,1536]{1,0:T(2,128)S(1)} %add_add_fusion.1), channel_id=1, source_target_pairs={{0,16},{2,18},{4,20},{6,22},{8,24},{10,26},{12,28},{14,30},{16,0},... | collective-permute-start | bytes 36872 | tf_op jit(solution)/shard_map/ppermute | solution.py:230
  24.4 4.6 %collective-permute-start.3 = (f32[2,1536]{1,0:T(2,128)S(1)}, f32[2,1536]{1,0:T(2,128)S(1)}, u32[]{:S(2)}, u32[]{:S(2)}) collective-permute-start(f32[2,1536]{1,0:T(2,128)S(1)} %add_add_fusion.1), channel_id=1, source_target_pairs={{0,8},{2,10},{4,12},{6,14},{8,0},{10,2},{12,4},{14,6},{16,24},{18,... | collective-permute-start | bytes 36872 | tf_op jit(solution)/shard_map/ppermute | solution.py:230
  29.0 1.4 copy-start.3
  30.4 1.0 copy-start.6
  31.5 1.0 copy-start.9
  32.5 0.7 copy-start.12
  33.2 0.7 copy-start.15
  33.9 0.7 copy-start.18
  39.4 12.0 %collective-permute-start.6 = (bf16[1536,256]{1,0:T(8,128)(2,1)S(1)}, bf16[1536,256]{1,0:T(8,128)(2,1)}, u32[]{:S(2)}, u32[]{:S(2)}) collective-permute-start(bf16[1536,256]{1,0:T(8,128)(2,1)S(1)} %get-tuple-element.14), channel_id=1, source_target_pairs={{0,2},{2,0},{4,6},{6,4},{8,10},{10,8},{12,14},{14,12},{16,18},{18,... | collective-permute-start | bytes 2359304 | tf_op jit(solution)/shard_map/ppermute | solution.py:230
  39.4 53.9 %collective-permute-start.26 = (bf16[256,512]{1,0:T(8,128)(2,1)S(1)}, bf16[256,512]{1,0:T(8,128)(2,1)}, u32[]{:S(2)}, u32[]{:S(2)}) collective-permute-start(bf16[256,512]{1,0:T(8,128)(2,1)S(1)} %bitcast.64), channel_id=1, source_target_pairs={{0,1},{1,0},{2,3},{3,2},{4,5},{5,4},{6,7},{7,6},{8,9},{9,8},{10,11... | collective-permute-start | bytes 786440 | tf_op jit(solution)/shard_map/ppermute | solution.py:233
  41.0 1.4 copy-start.4
  42.4 1.0 copy-start.7
  43.4 1.0 copy-start.10
  44.5 0.7 copy-start.13
  45.2 0.7 copy-start.16
  45.9 0.7 copy-start.19
  52.8 7.8 %collective-permute-start.7 = (bf16[384,256]{1,0:T(8,128)(2,1)S(1)}, bf16[384,256]{1,0:T(8,128)(2,1)S(1)}, u32[]{:S(2)}, u32[]{:S(2)}) collective-permute-start(bf16[384,256]{1,0:T(8,128)(2,1)S(1)} %fusion), channel_id=1, source_target_pairs={{0,4},{2,6},{4,0},{6,2},{8,12},{10,14},{12,8},{14,10},{16,20},{18,... | collective-permute-start | bytes 589832 | tf_op jit(solution)/shard_map/ppermute | solution.py:230
  54.2 38.2 %collective-permute-start.25 = (bf16[256,256]{1,0:T(8,128)(2,1)S(1)}, bf16[256,256]{1,0:T(8,128)(2,1)S(1)}, u32[]{:S(2)}, u32[]{:S(2)}) collective-permute-start(bf16[256,256]{1,0:T(8,128)(2,1)S(1)} %bitcast.65), channel_id=1, source_target_pairs={{0,1},{1,0},{2,3},{3,2},{4,5},{5,4},{6,7},{7,6},{8,9},{9,8},{10,11... | collective-permute-start | bytes 393224 | tf_op jit(solution)/shard_map/ppermute | solution.py:233
  54.8 9.5 %collective-permute-start.15 = (bf16[384,256]{1,0:T(8,128)(2,1)S(1)}, bf16[384,256]{1,0:T(8,128)(2,1)S(1)}, u32[]{:S(2)}, u32[]{:S(2)}) collective-permute-start(bf16[384,256]{1,0:T(8,128)(2,1)S(1)} %fusion.1), channel_id=1, source_target_pairs={{0,4},{2,6},{4,0},{6,2},{8,12},{10,14},{12,8},{14,10},{16,20},{18,... | collective-permute-start | bytes 589832 | tf_op jit(solution)/shard_map/ppermute | solution.py:230
  60.7 5.5 %collective-permute-start.8 = (bf16[96,256]{1,0:T(8,128)(2,1)S(1)}, bf16[96,256]{1,0:T(8,128)(2,1)S(1)}, u32[]{:S(2)}, u32[]{:S(2)}) collective-permute-start(bf16[96,256]{1,0:T(8,128)(2,1)S(1)} %get-tuple-element.27), channel_id=1, source_target_pairs={{0,8},{2,10},{4,12},{6,14},{8,0},{10,2},{12,4},{14,6},{16,24},{18,... | collective-permute-start | bytes 147464 | tf_op jit(solution)/shard_map/ppermute | solution.py:230
  60.8 6.6 %collective-permute-start.10 = (bf16[96,256]{1,0:T(8,128)(2,1)S(1)}, bf16[96,256]{1,0:T(8,128)(2,1)S(1)}, u32[]{:S(2)}, u32[]{:S(2)}) collective-permute-start(bf16[96,256]{1,0:T(8,128)(2,1)S(1)} %get-tuple-element.28), channel_id=1, source_target_pairs={{0,24},{2,26},{4,28},{6,30},{8,16},{10,18},{12,20},{14,22},{16,8},... | collective-permute-start | bytes 147464 | tf_op jit(solution)/shard_map/ppermute | solution.py:230
  64.3 6.3 %collective-permute-start.9 = (bf16[96,256]{1,0:T(8,128)(2,1)S(1)}, bf16[96,256]{1,0:T(8,128)(2,1)S(1)}, u32[]{:S(2)}, u32[]{:S(2)}) collective-permute-start(bf16[96,256]{1,0:T(8,128)(2,1)S(1)} %get-tuple-element.29), channel_id=1, source_target_pairs={{0,16},{2,18},{4,20},{6,22},{8,24},{10,26},{12,28},{14,30},{16,0},... | collective-permute-start | bytes 147464 | tf_op jit(solution)/shard_map/ppermute | solution.py:230
  66.2 5.2 %collective-permute-start.16 = (bf16[96,256]{1,0:T(8,128)(2,1)S(1)}, bf16[96,256]{1,0:T(8,128)(2,1)S(1)}, u32[]{:S(2)}, u32[]{:S(2)}) collective-permute-start(bf16[96,256]{1,0:T(8,128)(2,1)S(1)} %get-tuple-element.30), channel_id=1, source_target_pairs={{0,8},{2,10},{4,12},{6,14},{8,0},{10,2},{12,4},{14,6},{16,24},{18,... | collective-permute-start | bytes 147464 | tf_op jit(solution)/shard_map/ppermute | solution.py:230
  67.4 6.0 %collective-permute-start.18 = (bf16[96,256]{1,0:T(8,128)(2,1)S(1)}, bf16[96,256]{1,0:T(8,128)(2,1)S(1)}, u32[]{:S(2)}, u32[]{:S(2)}) collective-permute-start(bf16[96,256]{1,0:T(8,128)(2,1)S(1)} %get-tuple-element.31), channel_id=1, source_target_pairs={{0,24},{2,26},{4,28},{6,30},{8,16},{10,18},{12,20},{14,22},{16,8},... | collective-permute-start | bytes 147464 | tf_op jit(solution)/shard_map/ppermute | solution.py:230
  70.6 5.9 %collective-permute-start.17 = (bf16[96,256]{1,0:T(8,128)(2,1)S(1)}, bf16[96,256]{1,0:T(8,128)(2,1)S(1)}, u32[]{:S(2)}, u32[]{:S(2)}) collective-permute-start(bf16[96,256]{1,0:T(8,128)(2,1)S(1)} %get-tuple-element.32), channel_id=1, source_target_pairs={{0,16},{2,18},{4,20},{6,22},{8,24},{10,26},{12,28},{14,30},{16,0},... | collective-permute-start | bytes 147464 | tf_op jit(solution)/shard_map/ppermute | solution.py:230
  71.4 6.1 %collective-permute-start.13 = (bf16[1,96,256]{2,1,0:T(8,128)(2,1)S(1)}, bf16[1,96,256]{2,1,0:T(8,128)(2,1)S(1)}, u32[]{:S(2)}, u32[]{:S(2)}) collective-permute-start(bf16[1,96,256]{2,1,0:T(8,128)(2,1)S(1)} %get-tuple-element.22), channel_id=1, source_target_pairs={{0,24},{2,26},{4,28},{6,30},{8,16},{10,18},{12,20},{14,22},{16,8},... | collective-permute-start | bytes 147464 | tf_op jit(solution)/shard_map/ppermute | solution.py:230
  73.4 6.1 %collective-permute-start.12 = (bf16[1,96,256]{2,1,0:T(8,128)(2,1)S(1)}, bf16[1,96,256]{2,1,0:T(8,128)(2,1)S(1)}, u32[]{:S(2)}, u32[]{:S(2)}) collective-permute-start(bf16[1,96,256]{2,1,0:T(8,128)(2,1)S(1)} %get-tuple-element.22), channel_id=1, source_target_pairs={{0,16},{2,18},{4,20},{6,22},{8,24},{10,26},{12,28},{14,30},{16,0},... | collective-permute-start | bytes 147464 | tf_op jit(solution)/shard_map/ppermute | solution.py:230
  76.5 4.5 %collective-permute-start.11 = (bf16[1,96,256]{2,1,0:T(8,128)(2,1)S(1)}, bf16[1,96,256]{2,1,0:T(8,128)(2,1)S(1)}, u32[]{:S(2)}, u32[]{:S(2)}) collective-permute-start(bf16[1,96,256]{2,1,0:T(8,128)(2,1)S(1)} %get-tuple-element.22), channel_id=1, source_target_pairs={{0,8},{2,10},{4,12},{6,14},{8,0},{10,2},{12,4},{14,6},{16,24},{18,... | collective-permute-start | bytes 147464 | tf_op jit(solution)/shard_map/ppermute | solution.py:230
  77.5 5.9 %collective-permute-start.21 = (bf16[1,96,256]{2,1,0:T(8,128)(2,1)S(1)}, bf16[1,96,256]{2,1,0:T(8,128)(2,1)S(1)}, u32[]{:S(2)}, u32[]{:S(2)}) collective-permute-start(bf16[1,96,256]{2,1,0:T(8,128)(2,1)S(1)} %get-tuple-element.24), channel_id=1, source_target_pairs={{0,24},{2,26},{4,28},{6,30},{8,16},{10,18},{12,20},{14,22},{16,8},... | collective-permute-start | bytes 147464 | tf_op jit(solution)/shard_map/ppermute | solution.py:230
  79.5 5.0 %collective-permute-start.20 = (bf16[1,96,256]{2,1,0:T(8,128)(2,1)S(1)}, bf16[1,96,256]{2,1,0:T(8,128)(2,1)S(1)}, u32[]{:S(2)}, u32[]{:S(2)}) collective-permute-start(bf16[1,96,256]{2,1,0:T(8,128)(2,1)S(1)} %get-tuple-element.24), channel_id=1, source_target_pairs={{0,16},{2,18},{4,20},{6,22},{8,24},{10,26},{12,28},{14,30},{16,0},... | collective-permute-start | bytes 147464 | tf_op jit(solution)/shard_map/ppermute | solution.py:230
  81.0 4.1 %collective-permute-start.19 = (bf16[1,96,256]{2,1,0:T(8,128)(2,1)S(1)}, bf16[1,96,256]{2,1,0:T(8,128)(2,1)S(1)}, u32[]{:S(2)}, u32[]{:S(2)}) collective-permute-start(bf16[1,96,256]{2,1,0:T(8,128)(2,1)S(1)} %get-tuple-element.24), channel_id=1, source_target_pairs={{0,8},{2,10},{4,12},{6,14},{8,0},{10,2},{12,4},{14,6},{16,24},{18,... | collective-permute-start | bytes 147464 | tf_op jit(solution)/shard_map/ppermute | solution.py:230
  83.5 9.0 %collective-permute-start.24 = (bf16[256,256]{1,0:T(8,128)(2,1)S(1)}, bf16[256,256]{1,0:T(8,128)(2,1)S(1)}, u32[]{:S(2)}, u32[]{:S(2)}) collective-permute-start(bf16[256,256]{1,0:T(8,128)(2,1)S(1)} %bitcast.66), channel_id=1, source_target_pairs={{0,1},{1,0},{2,3},{3,2},{4,5},{5,4},{6,7},{7,6},{8,9},{9,8},{10,11... | collective-permute-start | bytes 393224 | tf_op jit(solution)/shard_map/ppermute | solution.py:233
  84.5 5.7 %collective-permute-start.14 = (bf16[4,96,256]{2,1,0:T(8,128)(2,1)S(1)}, bf16[4,96,256]{2,1,0:T(8,128)(2,1)S(1)}, u32[]{:S(2)}, u32[]{:S(2)}) collective-permute-start(bf16[4,96,256]{2,1,0:T(8,128)(2,1)S(1)} %pad_maximum_fusion.1), channel_id=1, source_target_pairs={{0,4},{2,6},{4,0},{6,2},{8,12},{10,14},{12,8},{14,10},{16,20},{18,... | collective-permute-start | bytes 589832 | tf_op jit(solution)/shard_map/ppermute | solution.py:230
  85.2 7.1 %collective-permute-start.22 = (bf16[4,96,256]{2,1,0:T(8,128)(2,1)S(1)}, bf16[4,96,256]{2,1,0:T(8,128)(2,1)S(1)}, u32[]{:S(2)}, u32[]{:S(2)}) collective-permute-start(bf16[4,96,256]{2,1,0:T(8,128)(2,1)S(1)} %pad_maximum_fusion.2), channel_id=1, source_target_pairs={{0,4},{2,6},{4,0},{6,2},{8,12},{10,14},{12,8},{14,10},{16,20},{18,... | collective-permute-start | bytes 589832 | tf_op jit(solution)/shard_map/ppermute | solution.py:230
  92.4 2.7 %copy-start.20 = (bf16[2,8,96,256]{3,2,1,0:T(8,128)(2,1)}, bf16[2,8,96,256]{3,2,1,0:T(8,128)(2,1)S(1)}, u32[]{:S(2)}) copy-start(bf16[2,8,96,256]{3,2,1,0:T(8,128)(2,1)S(1)} %pad_maximum_fusion.mine_ref) | copy-start | bytes 2359300
  92.4 2.7 %collective-permute-start.23 = (bf16[2,8,96,256]{3,2,1,0:T(8,128)(2,1)S(1)}, bf16[2,8,96,256]{3,2,1,0:T(8,128)(2,1)S(1)}, u32[]{:S(2)}, u32[]{:S(2)}) collective-permute-start(bf16[2,8,96,256]{3,2,1,0:T(8,128)(2,1)S(1)} %pad_maximum_fusion.mine_ref), channel_id=1, source_target_pairs={{0,2},{2,0},{4,6},{6,4},{8,10},{10,8},{12,14},{14,12},{16,18},{18,... | collective-permute-start | bytes 2359304 | tf_op jit(solution)/shard_map/ppermute | solution.py:230
  95.1 0.9 copy-start.21

commit v2 on v1

--- a/solution.py
+++ b/solution.py
@@ -13,7 +13,7 @@
 NT = (((1,), (1,)), ((), ()))
 NN = (((1,), (0,)), ((), ()))
 TN = (((0,), (0,)), ((), ()))
-VMEM_LIMIT = 40 * 1024 * 1024
+VMEM_LIMIT = 60 * 1024 * 1024
 
 
 def dot(a, b, dims):
@@ -71,9 +71,9 @@
 
 
 def backward_kernel(
-    place, compat, q_ref, g_ref, k_ref, v_ref, lse_ref, targets_ref, delta_ref,
-    query_ref, own_ref, send_ref, total, *, scale,
+    place, compat, q_ref, g_ref, k_ref, v_ref, lse_ref, targets_ref, delta_ref, *rest, scale,
 ):
+    *earlier, query_ref, own_ref, send_ref, total = rest
     block = pl.program_id(0)
     head = place[2]
     value_count = k_ref.shape[0]
@@ -98,7 +98,16 @@
 
     @pl.when(block == pl.num_programs(0) - 1)
     def _():
-        scatter_rows(place, total, own_ref, send_ref, slice(None))
+        width = total.shape[1]
+        if earlier:
+            earlier_own, earlier_send = earlier
+            columns = pl.ds(pl.multiple_of((1 - head) * width, width), width)
+            own_ref[:, columns] = earlier_own[...]
+            send_ref[:, :, columns] = earlier_send[...]
+            columns = pl.ds(pl.multiple_of(head * width, width), width)
+        else:
+            columns = slice(None)
+        scatter_rows(place, total, own_ref, send_ref, columns)
 
 
 def cost(queries, values, width, dots):
@@ -142,7 +151,9 @@
     )(place, compat, queries, grads, keys, values, lse, targets)
 
 
-def backward(place, compat, queries, keys, values, grads, lse, targets, delta, parts, out_dtype):
+def backward(
+    place, compat, queries, keys, values, grads, lse, targets, delta, parts, out_dtype, earlier=()
+):
     heads, _, blocks = compat.shape
     query_count, wide = queries.shape
     width = wide // heads
@@ -152,67 +163,32 @@
     rows = pl.BlockSpec((block, width), lambda i, place, _: (i, place[2]))
     pool = pl.BlockSpec((value_count, width), lambda i, place, _: (0, place[2]))
     flat = pl.BlockSpec((heads, block), lambda i, *_: (0, i))
+    out_width = wide if earlier else width
+
+    def shares(columns):
+        return [
+            pl.BlockSpec((share, columns), lambda i, *_: (0, 0)),
+            pl.BlockSpec((parts - 1, share, columns), lambda i, *_: (0, 0, 0)),
+        ]
+
     return pl.pallas_call(
         partial(backward_kernel, scale=width ** -0.5),
         grid_spec=pltpu.PrefetchScalarGridSpec(
             num_scalar_prefetch=2,
             grid=(blocks,),
-            in_specs=[rows, rows, pool, pool, flat, flat, flat],
-            out_specs=[
-                pl.BlockSpec((block, width), lambda i, *_: (i, 0)),
-                pl.BlockSpec((share, width), lambda i, *_: (0, 0)),
-                pl.BlockSpec((parts - 1, share, width), lambda i, *_: (0, 0, 0)),
-            ],
+            in_specs=[rows, rows, pool, pool, flat, flat, flat] + (shares(width) if earlier else []),
+            out_specs=[pl.BlockSpec((block, width), lambda i, *_: (i, 0))] + shares(out_width),
             scratch_shapes=[pltpu.VMEM((value_count, width), jnp.float32)],
         ),
         out_shape=[
             jax.ShapeDtypeStruct((query_count, width), out_dtype),
-            jax.ShapeDtypeStruct((share, width), jnp.float32),
-            jax.ShapeDtypeStruct((parts - 1, share, width), jnp.bfloat16),
+            jax.ShapeDtypeStruct((share, out_width), jnp.float32),
+            jax.ShapeDtypeStruct((parts - 1, share, out_width), jnp.bfloat16),
         ],
         cost_estimate=cost(query_count, value_count, width, 4),
         compiler_params=pltpu.CompilerParams(vmem_limit_bytes=VMEM_LIMIT),
         name="backward_pass",
-    )(place, compat, queries, grads, keys, values, lse, targets, delta)
-
-
-def assemble_kernel(place, mine_ref, theirs_ref, out_ref, sems, *, chains, radix_y, radix_z):
-    core, y, z = place[0], place[1], place[2]
-    piece, width = mine_ref.shape[-2:]
-    pieces = radix_y * radix_z
-    copies = []
-    for side, ref in enumerate((mine_ref, theirs_ref)):
-        columns = pl.ds(pl.multiple_of((core ^ side) * width, width), width)
-        for chain in range(chains):
-            for step_y in range(radix_y):
-                for step_z in range(radix_z):
-                    index = chain * pieces + (y ^ step_y) * radix_z + (z ^ step_z)
-                    rows = pl.ds(pl.multiple_of(index * piece, piece), piece)
-                    copy = pltpu.make_async_copy(
-                        ref.at[chain, step_y * radix_z + step_z],
-                        out_ref.at[rows, columns],
-                        sems.at[len(copies)],
-                    )
-                    copy.start()
-                    copies.append(copy)
-    for copy in copies:
-        copy.wait()
-
-
-def assemble(place, mine, theirs, radix_y, radix_z):
-    chains, pieces, piece, width = mine.shape
-    return pl.pallas_call(
-        partial(assemble_kernel, chains=chains, radix_y=radix_y, radix_z=radix_z),
-        grid_spec=pltpu.PrefetchScalarGridSpec(
-            num_scalar_prefetch=1,
-            grid=(),
-            in_specs=[pl.BlockSpec(memory_space=pl.ANY)] * 2,
-            out_specs=pl.BlockSpec(memory_space=pl.ANY),
-            scratch_shapes=[pltpu.SemaphoreType.DMA((2 * chains * pieces,))],
-        ),
-        out_shape=jax.ShapeDtypeStruct((chains * pieces * piece, 2 * width), mine.dtype),
-        name="assemble",
-    )(place, mine, theirs)
+    )(place, compat, queries, grads, keys, values, lse, targets, delta, *earlier)
 
 
 def on_device(queries, pool_keys, pool_values, out_grad, lse, compat, targets):
@@ -246,58 +222,41 @@
         return jnp.stack([val, qry, head]).astype(jnp.int32)
 
     delta, value_own, value_send = forward(place(core), *operands, parts)
-    stride = 1
-    while stride < value_devices:
-        delta = add(delta, [flip(delta, stride * step) for step in range(1, 4)])
-        stride *= 4
+    delta = jnp.sum(lax.all_gather(delta, "val"), axis=0)
     value_received = swap_shares(value_send)
 
-    query_send, other_own, other_send = backward(
-        place(1 - core), *operands, delta, parts, jnp.bfloat16
-    )
+    query_send, *earlier = backward(place(1 - core), *operands, delta, parts, jnp.bfloat16)
     query_received = flip(query_send, 1)
-    other_received = swap_shares(other_send)
-    query_own, key_own, key_send = backward(place(core), *operands, delta, parts, jnp.float32)
+    query_own, key_own, key_send = backward(
+        place(core), *operands, delta, parts, jnp.float32, tuple(earlier)
+    )
     key_received = swap_shares(key_send)
     query_sum = add(query_own, [query_received])
 
     pieces = radix_y * radix_z
     chains = 2 if query_count % (2 * pieces * 16) == 0 else 1
+    piece = query_count // (pieces * chains)
+    query_sum = query_sum.reshape(radix_z, radix_y, chains, piece, width)
     mine = []
     for chain in range(chains):
-        rows = query_count // chains
-        part = query_sum[chain * rows : (chain + 1) * rows]
-        for radix, digit, stride in ((radix_y, y, 2), (radix_z, z, 2 * radix_y)):
-            split = part.reshape(radix, part.shape[0] // radix, width)
+        part = query_sum[:, :, chain]
+        for axis, radix, digit, stride in ((1, radix_y, y, 2), (0, radix_z, z, 2 * radix_y)):
 
             def pick(index):
-                return lax.dynamic_index_in_dim(split, index, 0, keepdims=False)
+                return lax.dynamic_index_in_dim(part, index, axis, keepdims=False)
 
             received = [
                 flip(pick(digit ^ step).astype(jnp.bfloat16), stride * step)
                 for step in range(1, radix)
             ]
             part = add(pick(digit), received)
-        part = part.astype(jnp.bfloat16)[None]
-        for radix, stride in ((radix_z, 2 * radix_y), (radix_y, 2)):
-            part = jnp.concatenate(
-                [part] + [flip(part, stride * step) for step in range(1, radix)], axis=0
-            )
-        mine.append(part)
-    mine = jnp.stack(mine)
-    theirs = flip(mine, 1)
-    query_grad = assemble(
-        jnp.stack([core, y, z]).astype(jnp.int32), mine, theirs, radix_y, radix_z
-    )
+        mine.append(part.astype(jnp.bfloat16))
+    gathered = lax.all_gather(jnp.concatenate(mine, axis=0), "val")
+    gathered = gathered.reshape(pieces, 2, chains * piece, width)
+    query_grad = jnp.transpose(gathered, (0, 2, 1, 3)).reshape(query_count, 2 * width)
 
     value_grad = add(value_own, value_received).astype(jnp.bfloat16)
-    key_mine = add(key_own, key_received).astype(jnp.bfloat16)
-    key_other = add(other_own, other_received).astype(jnp.bfloat16)
-    key_grad = jnp.where(
-        core == 0,
-        jnp.concatenate([key_mine, key_other], axis=1),
-        jnp.concatenate([key_other, key_mine], axis=1),
-    )
+    key_grad = add(key_own, key_received).astype(jnp.bfloat16)
     return query_grad, key_grad, value_grad
 
 

time: 147 us -> 131 us (0.89)
  Pallas kernels: 66 us -> 25.1 us
  blocking collectives: 0 us -> 23.9 us
  waiting for transfers between devices: 21.7 us -> 44.9 us
  starting transfers between devices: 32.7 us -> 11.7 us
  local copies, waits for them, and re-layouts: 19.3 us -> 4.74 us
  between operations: 0.93 us -> 14.2 us
    pallas_call x1 -> x0, Pallas kernels: 49.7 us -> none  [assemble(): pl.pallas_call(partial(assemble_kernel, chains=chains, radix_y=radix_y, r...]
    all_gather x0 -> x1, waiting for transfers between devices: none -> 25.8 us  [on_device(): gathered = lax.all_gather(jnp.concatenate(mine, axis=0), 'val')]
    all_gather x0 -> x1, blocking collectives: none -> 23.9 us  [on_device(): delta = jnp.sum(lax.all_gather(delta, 'val'), axis=0)]
    ppermute x24 -> x9, starting transfers between devices: 30.1 us -> 9.58 us  [flip(): lax.ppermute(array, 'val', [(i, i ^ mask) for i in range(value_devices)])]
    unnamed x50 -> x9, local copies, waits for them, and re-layouts: 19.1 us -> 1.5 us
    ppermute x24 -> x9, waiting for transfers between devices: 21.7 us -> 9.78 us  [flip(): lax.ppermute(array, 'val', [(i, i ^ mask) for i in range(value_devices)])]
    ppermute x3 -> x2, waiting for transfers between devices: 0.01 us -> 9.23 us  [turn(): lax.ppermute(array, 'qry', [(i, (i + step) % parts) for i in range(parts)])]
    pallas_call x2, Pallas kernels: 9.5 us -> 15.5 us  [backward(): pl.pallas_call(partial(backward_kernel, scale=width ** (-0.5)), grid_spec...]
  transfers between devices with their start and end apart: 27 -> 12, of which waited for: 15 -> 7; matrix products, arithmetic and copies ran while one was open for 4% -> 1% of each run, Pallas kernels for 3% -> 6%
where the time goes in v2:
time: 131 us; the launch traced here: 130 us
  waiting for transfers between devices  44.9 us (34%)
  Pallas kernels  25.1 us (19%)
  blocking collectives  23.9 us (18%)
  between operations  14.2 us (11%)
  starting transfers between devices  11.7 us (9%)
  other arithmetic  5.83 us (4%)
  local copies, waits for them, and re-layouts  4.74 us (4%)
    all_gather x1, waiting for transfers between devices, on_device(): gathered = lax.all_gather(jnp.concatenate(mine, axis=0), 'val')  25.8 us
    all_gather x1, blocking collectives, on_device(): delta = jnp.sum(lax.all_gather(delta, 'val'), axis=0)  23.9 us
    pallas_call x2, Pallas kernels, backward(): pl.pallas_call(partial(backward_kernel, scale=width ** (-0.5)), grid_spec...  15.5 us
    ppermute x9, waiting for transfers between devices, flip(): lax.ppermute(array, 'val', [(i, i ^ mask) for i in range(value_devices)])  9.78 us
    pallas_call x1, Pallas kernels, forward(): pl.pallas_call(partial(forward_kernel, heads=heads, scale=(wide // heads)...  9.58 us
    ppermute x9, starting transfers between devices, flip(): lax.ppermute(array, 'val', [(i, i ^ mask) for i in range(value_devices)])  9.58 us
    ppermute x2, waiting for transfers between devices, turn(): lax.ppermute(array, 'qry', [(i, (i + step) % parts) for i in range(parts)])  9.23 us
    reshape x1, local copies, waits for them, and re-layouts, on_device(): gathered = gathered.reshape(pieces, 2, chains * piece, width)  3.03 us
  transfers between devices with their start and end apart: 12, of which 7 were waited for; matrix products, arithmetic and copies ran while one was open for 1% of the time, Pallas kernels for 6%

profile of v2, /device:TPU:0, one launch (start us, length us, event | category | flops | bytes accessed | tf_op | source)
XLA Modules:
  0.0 130.4 jit_solution(2226928753353882327)
XLA Ops:
  7.2 0.0 all-gather.5.cloned.1.call-start
  7.2 0.7 pad_add_fusion.place
  7.9 0.6 pad_add_fusion.2.place
  8.5 9.6 %forward_pass.1 = (f32[2,1536]{1,0:T(2,128)}, f32[256,512]{1,0:T(8,128)}, bf16[1,256,512]{2,1,0:T(8,128)(2,1)}) custom-call(s32[3]{0:T(128)} %pad_add_fusion.place, s32[2,1,6]{2,1,0:T(1,128)} %compat.5, bf16[1536,512]{1,0:T(8,128)(2,1)} %q_ref.5, bf16[1536,512]{1,0:T(8,128)(2,1)} %g_ref.5, bf16[512,512]{1,0:T(8,128)(2,1)} %k_ref.5, bf16[512,512]{1,0:T(8,128)(2,1)} %v_ref.5, ...), custom_call_target="tpu_custom_call" | custom-call | flops 2415919104 | bytes 4194304 | tf_op jit(solution)/shard_map/forward_pass/pallas_call | solution.py:130
  18.1 23.9 %all-gather.2 = f32[16,2,1536]{2,1,0:T(2,128)S(1)} all-gather(f32[1,2,1536]{2,1,0:T(2,128)} %bitcast.60), channel_id=2, replica_groups=mesh['val'=16,'qry'=2] {'val'}, dimensions={0}, use_global_device_ids=true | all-gather | bytes 208896 | tf_op jit(solution)/shard_map/all_gather | solution.py:225
  41.9 0.7 reduce_sum.9.delta_ref
  42.6 7.6 %backward_pass.2 = (bf16[1536,256]{1,0:T(8,128)(2,1)}, f32[256,256]{1,0:T(8,128)}, bf16[1,256,256]{2,1,0:T(8,128)(2,1)}) custom-call(s32[3]{0:T(128)} %pad_add_fusion.2.place, s32[2,1,6]{2,1,0:T(1,128)} %compat.5, bf16[1536,512]{1,0:T(8,128)(2,1)} %q_ref.5, bf16[1536,512]{1,0:T(8,128)(2,1)} %g_ref.5, bf16[512,512]{1,0:T(8,128)(2,1)} %k_ref.5, ...), custom_call_target="tpu_custom_call" | custom-call | flops 1610612736 | bytes 2097152 | tf_op jit(solution)/shard_map/backward_pass/pallas_call | solution.py:174
  50.2 0.4 collective-permute-start
  50.6 8.0 %backward_pass.3 = (f32[1536,256]{1,0:T(8,128)}, f32[256,512]{1,0:T(8,128)}, bf16[1,256,512]{2,1,0:T(8,128)(2,1)}) custom-call(s32[3]{0:T(128)} %pad_add_fusion.place, s32[2,1,6]{2,1,0:T(1,128)} %compat.5, bf16[1536,512]{1,0:T(8,128)(2,1)} %q_ref.5, bf16[1536,512]{1,0:T(8,128)(2,1)} %g_ref.5, bf16[512,512]{1,0:T(8,128)(2,1)} %k_ref.5, ...), custom_call_target="tpu_custom_call" | custom-call | flops 1610612736 | bytes 2097152 | tf_op jit(solution)/shard_map/backward_pass/pallas_call | solution.py:174
  58.6 0.0 collective-permute-done
  58.6 1.6 %convert_add_fusion = f32[1536,256]{1,0:T(8,128)S(1)} fusion(f32[1536,256]{1,0:T(8,128)} %get-tuple-element.15, bf16[1536,256]{1,0:T(8,128)(2,1)S(1)} %collective-permute-done), kind=kLoop, calls=%fused_computation | loop fusion | flops 786432 | bytes 3932160 | tf_op jit(solution)/shard_map/add | solution.py:216
  60.1 0.1 fusion.14
  60.3 0.1 collective-permute-start.5
  60.4 0.0 copy-start.2
  60.5 0.0 copy-start.3
  60.5 0.0 copy-start
  60.5 2.0 %collective-permute-start.1 = (bf16[4,96,256]{2,1,0:T(8,128)(2,1)S(1)}, bf16[4,96,256]{2,1,0:T(8,128)(2,1)S(1)}, u32[]{:S(2)}, u32[]{:S(2)}) collective-permute-start(bf16[4,96,256]{2,1,0:T(8,128)(2,1)S(1)} %fusion.1), channel_id=1, source_target_pairs={{0,4},{2,6},{4,0},{6,2},{8,12},{10,14},{12,8},{14,10},{16,20},{18,... | collective-permute-start | bytes 589832 | tf_op jit(solution)/shard_map/ppermute | solution.py:206
  62.5 5.6 %collective-permute-done.5 = bf16[4,96,256]{2,1,0:T(8,128)(2,1)S(1)} collective-permute-done((bf16[4,96,256]{2,1,0:T(8,128)(2,1)S(1)}, bf16[4,96,256]{2,1,0:T(8,128)(2,1)S(1)}, u32[]{:S(2)}, u32[]{:S(2)}) %collective-permute-start.5) | collective-permute-done | bytes 196640 | tf_op jit(solution)/shard_map/ppermute | solution.py:206
  68.2 0.1 collective-permute-start.6
  68.3 0.1 collective-permute-start.8
  68.3 0.0 copy-start.1
  68.3 3.4 %collective-permute-start.7 = (bf16[96,256]{1,0:T(8,128)(2,1)S(1)}, bf16[96,256]{1,0:T(8,128)(2,1)S(1)}, u32[]{:S(2)}, u32[]{:S(2)}) collective-permute-start(bf16[96,256]{1,0:T(8,128)(2,1)S(1)} %get-tuple-element.28), channel_id=1, source_target_pairs={{0,16},{2,18},{4,20},{6,22},{8,24},{10,26},{12,28},{14,30},{16,0},... | collective-permute-start | bytes 147464 | tf_op jit(solution)/shard_map/ppermute | solution.py:206
  71.7 0.0 collective-permute-done.1
  71.8 1.0 collective-permute-start.2
  72.9 0.5 collective-permute-start.4
  73.3 0.0 collective-permute-done.6
  73.4 2.0 %collective-permute-start.3 = (bf16[96,256]{1,0:T(8,128)(2,1)S(1)}, bf16[96,256]{1,0:T(8,128)(2,1)S(1)}, u32[]{:S(2)}, u32[]{:S(2)}) collective-permute-start(bf16[96,256]{1,0:T(8,128)(2,1)S(1)} %get-tuple-element.25), channel_id=1, source_target_pairs={{0,16},{2,18},{4,20},{6,22},{8,24},{10,26},{12,28},{14,30},{16,0},... | collective-permute-start | bytes 147464 | tf_op jit(solution)/shard_map/ppermute | solution.py:206
  75.4 0.0 collective-permute-done.8
  75.4 1.5 %collective-permute-done.7 = bf16[96,256]{1,0:T(8,128)(2,1)S(1)} collective-permute-done((bf16[96,256]{1,0:T(8,128)(2,1)S(1)}, bf16[96,256]{1,0:T(8,128)(2,1)S(1)}, u32[]{:S(2)}, u32[]{:S(2)}) %collective-permute-start.7) | collective-permute-done | bytes 49184 | tf_op jit(solution)/shard_map/ppermute | solution.py:206
  76.9 0.0 collective-permute-done.2
  76.9 1.9 %collective-permute-done.4 = bf16[96,256]{1,0:T(8,128)(2,1)S(1)} collective-permute-done((bf16[96,256]{1,0:T(8,128)(2,1)S(1)}, bf16[96,256]{1,0:T(8,128)(2,1)S(1)}, u32[]{:S(2)}, u32[]{:S(2)}) %collective-permute-start.4) | collective-permute-done | bytes 49184 | tf_op jit(solution)/shard_map/ppermute | solution.py:206
  78.8 0.7 collective-permute-done.3
  79.6 0.6 pad_maximum_fusion
  80.3 0.0 all-gather.5.cloned.1.call-update
  80.3 0.0 copy-done.2
  80.3 1.6 %collective-permute-start.10 = (bf16[256,512]{1,0:T(8,128)(2,1)S(1)}, bf16[256,512]{1,0:T(8,128)(2,1)S(1)}, u32[]{:S(2)}, u32[]{:S(2)}) collective-permute-start(bf16[256,512]{1,0:T(8,128)(2,1)S(1)} %bitcast.61), channel_id=1, source_target_pairs={{0,1},{1,0},{2,3},{3,2},{4,5},{5,4},{6,7},{7,6},{8,9},{9,8},{10,11... | collective-permute-start | bytes 786440 | tf_op jit(solution)/shard_map/ppermute | solution.py:209
  81.9 0.0 copy-done.3
  81.9 0.5 collective-permute-start.9
  82.4 7.2 %collective-permute-done.10 = bf16[256,512]{1,0:T(8,128)(2,1)S(1)} collective-permute-done((bf16[256,512]{1,0:T(8,128)(2,1)S(1)}, bf16[256,512]{1,0:T(8,128)(2,1)S(1)}, u32[]{:S(2)}, u32[]{:S(2)}) %collective-permute-start.10) | collective-permute-done | bytes 262176 | tf_op jit(solution)/shard_map/ppermute | solution.py:209
  89.6 0.0 copy-done
  89.6 0.8 add_convert_fusion
  90.4 2.0 %collective-permute-done.9 = bf16[256,512]{1,0:T(8,128)(2,1)S(1)} collective-permute-done((bf16[256,512]{1,0:T(8,128)(2,1)S(1)}, bf16[256,512]{1,0:T(8,128)(2,1)S(1)}, u32[]{:S(2)}, u32[]{:S(2)}) %collective-permute-start.9) | collective-permute-done | bytes 262176 | tf_op jit(solution)/shard_map/ppermute | solution.py:209
  92.4 0.0 copy-done.1
  92.4 0.8 add_convert_fusion.1
  93.2 25.8 %all-gather.5.cloned.1.call-done = bf16[3072,256]{1,0:T(8,128)(2,1)} async-done(((bf16[192,256]{1,0:T(8,128)(2,1)}), bf16[3072,256]{1,0:T(8,128)(2,1)}) %all-gather.5.cloned.1.call-update) | async-done | bytes 1572880 | tf_op jit(solution)/shard_map/all_gather | solution.py:254
  119.0 3.0 %copy.13 = bf16[8,2,192,256]{3,1,2,0:T(2,128)(2,1)S(1)} copy(bf16[8,2,192,256]{3,2,1,0:T(8,128)(2,1)} %bitcast.58) | data formatting | bytes 3145728 | tf_op jit(solution)/shard_map/reshape | solution.py:255
  122.0 1.5 %copy.17 = bf16[192,8,2,256]{3,1,2,0:T(8,128)(2,1)} copy(bf16[192,8,2,256]{3,2,1,0:T(2,128)(2,1)S(1)} %bitcast.56) | data formatting | bytes 3145728
  (8 shorter events, 0.2 us)
Async XLA Ops:
  7.2 111.8 %all-gather.5.cloned.1.call-start = ((), (), s32[]{:S(2)}) async-start(), calls=%async_computation | async-start | bytes 1671168 | tf_op jit(solution)/shard_map/all_gather | solution.py:254
  50.2 8.4 %collective-permute-start = (bf16[1536,256]{1,0:T(8,128)(2,1)}, bf16[1536,256]{1,0:T(8,128)(2,1)S(1)}, u32[]{:S(2)}, u32[]{:S(2)}) collective-permute-start(bf16[1536,256]{1,0:T(8,128)(2,1)} %get-tuple-element.16), channel_id=1, source_target_pairs={{0,2},{2,0},{4,6},{6,4},{8,10},{10,8},{12,14},{14,12},{16,18},{18,... | collective-permute-start | bytes 2359304 | tf_op jit(solution)/shard_map/ppermute | solution.py:206
  60.3 7.8 %collective-permute-start.5 = (bf16[4,96,256]{2,1,0:T(8,128)(2,1)S(1)}, bf16[4,96,256]{2,1,0:T(8,128)(2,1)S(1)}, u32[]{:S(2)}, u32[]{:S(2)}) collective-permute-start(bf16[4,96,256]{2,1,0:T(8,128)(2,1)S(1)} %fusion), channel_id=1, source_target_pairs={{0,4},{2,6},{4,0},{6,2},{8,12},{10,14},{12,8},{14,10},{16,20},{18,... | collective-permute-start | bytes 589832 | tf_op jit(solution)/shard_map/ppermute | solution.py:206
  60.4 19.8 %copy-start.2 = (bf16[1,256,512]{2,1,0:T(8,128)(2,1)S(1)}, bf16[1,256,512]{2,1,0:T(8,128)(2,1)}, u32[]{:S(2)}) copy-start(bf16[1,256,512]{2,1,0:T(8,128)(2,1)} %get-tuple-element.20) | copy-start | bytes 786436
  60.5 21.4 %copy-start.3 = (bf16[1,256,512]{2,1,0:T(8,128)(2,1)S(1)}, bf16[1,256,512]{2,1,0:T(8,128)(2,1)}, u32[]{:S(2)}) copy-start(bf16[1,256,512]{2,1,0:T(8,128)(2,1)} %get-tuple-element.18) | copy-start | bytes 786436
  60.5 29.1 %copy-start = (f32[256,512]{1,0:T(8,128)S(1)}, f32[256,512]{1,0:T(8,128)}, u32[]{:S(2)}) copy-start(f32[256,512]{1,0:T(8,128)} %get-tuple-element.19) | copy-start | bytes 1572868
  60.5 11.3 %collective-permute-start.1 = (bf16[4,96,256]{2,1,0:T(8,128)(2,1)S(1)}, bf16[4,96,256]{2,1,0:T(8,128)(2,1)S(1)}, u32[]{:S(2)}, u32[]{:S(2)}) collective-permute-start(bf16[4,96,256]{2,1,0:T(8,128)(2,1)S(1)} %fusion.1), channel_id=1, source_target_pairs={{0,4},{2,6},{4,0},{6,2},{8,12},{10,14},{12,8},{14,10},{16,20},{18,... | collective-permute-start | bytes 589832 | tf_op jit(solution)/shard_map/ppermute | solution.py:206
  68.2 5.2 %collective-permute-start.6 = (bf16[96,256]{1,0:T(8,128)(2,1)S(1)}, bf16[96,256]{1,0:T(8,128)(2,1)S(1)}, u32[]{:S(2)}, u32[]{:S(2)}) collective-permute-start(bf16[96,256]{1,0:T(8,128)(2,1)S(1)} %get-tuple-element.26), channel_id=1, source_target_pairs={{0,8},{2,10},{4,12},{6,14},{8,0},{10,2},{12,4},{14,6},{16,24},{18,... | collective-permute-start | bytes 147464 | tf_op jit(solution)/shard_map/ppermute | solution.py:206
  68.3 7.1 %collective-permute-start.8 = (bf16[96,256]{1,0:T(8,128)(2,1)S(1)}, bf16[96,256]{1,0:T(8,128)(2,1)S(1)}, u32[]{:S(2)}, u32[]{:S(2)}) collective-permute-start(bf16[96,256]{1,0:T(8,128)(2,1)S(1)} %get-tuple-element.27), channel_id=1, source_target_pairs={{0,24},{2,26},{4,28},{6,30},{8,16},{10,18},{12,20},{14,22},{16,8},... | collective-permute-start | bytes 147464 | tf_op jit(solution)/shard_map/ppermute | solution.py:206
  68.3 24.1 %copy-start.1 = (f32[256,512]{1,0:T(8,128)S(1)}, f32[256,512]{1,0:T(8,128)}, u32[]{:S(2)}) copy-start(f32[256,512]{1,0:T(8,128)} %get-tuple-element.17) | copy-start | bytes 1572868
  68.3 8.6 %collective-permute-start.7 = (bf16[96,256]{1,0:T(8,128)(2,1)S(1)}, bf16[96,256]{1,0:T(8,128)(2,1)S(1)}, u32[]{:S(2)}, u32[]{:S(2)}) collective-permute-start(bf16[96,256]{1,0:T(8,128)(2,1)S(1)} %get-tuple-element.28), channel_id=1, source_target_pairs={{0,16},{2,18},{4,20},{6,22},{8,24},{10,26},{12,28},{14,30},{16,0},... | collective-permute-start | bytes 147464 | tf_op jit(solution)/shard_map/ppermute | solution.py:206
  71.8 5.1 %collective-permute-start.2 = (bf16[96,256]{1,0:T(8,128)(2,1)S(1)}, bf16[96,256]{1,0:T(8,128)(2,1)S(1)}, u32[]{:S(2)}, u32[]{:S(2)}) collective-permute-start(bf16[96,256]{1,0:T(8,128)(2,1)S(1)} %get-tuple-element.23), channel_id=1, source_target_pairs={{0,8},{2,10},{4,12},{6,14},{8,0},{10,2},{12,4},{14,6},{16,24},{18,... | collective-permute-start | bytes 147464 | tf_op jit(solution)/shard_map/ppermute | solution.py:206
  72.9 6.0 %collective-permute-start.4 = (bf16[96,256]{1,0:T(8,128)(2,1)S(1)}, bf16[96,256]{1,0:T(8,128)(2,1)S(1)}, u32[]{:S(2)}, u32[]{:S(2)}) collective-permute-start(bf16[96,256]{1,0:T(8,128)(2,1)S(1)} %get-tuple-element.24), channel_id=1, source_target_pairs={{0,24},{2,26},{4,28},{6,30},{8,16},{10,18},{12,20},{14,22},{16,8},... | collective-permute-start | bytes 147464 | tf_op jit(solution)/shard_map/ppermute | solution.py:206
  73.4 6.2 %collective-permute-start.3 = (bf16[96,256]{1,0:T(8,128)(2,1)S(1)}, bf16[96,256]{1,0:T(8,128)(2,1)S(1)}, u32[]{:S(2)}, u32[]{:S(2)}) collective-permute-start(bf16[96,256]{1,0:T(8,128)(2,1)S(1)} %get-tuple-element.25), channel_id=1, source_target_pairs={{0,16},{2,18},{4,20},{6,22},{8,24},{10,26},{12,28},{14,30},{16,0},... | collective-permute-start | bytes 147464 | tf_op jit(solution)/shard_map/ppermute | solution.py:206
  80.3 9.3 %collective-permute-start.10 = (bf16[256,512]{1,0:T(8,128)(2,1)S(1)}, bf16[256,512]{1,0:T(8,128)(2,1)S(1)}, u32[]{:S(2)}, u32[]{:S(2)}) collective-permute-start(bf16[256,512]{1,0:T(8,128)(2,1)S(1)} %bitcast.61), channel_id=1, source_target_pairs={{0,1},{1,0},{2,3},{3,2},{4,5},{5,4},{6,7},{7,6},{8,9},{9,8},{10,11... | collective-permute-start | bytes 786440 | tf_op jit(solution)/shard_map/ppermute | solution.py:209
  81.9 10.6 %collective-permute-start.9 = (bf16[256,512]{1,0:T(8,128)(2,1)S(1)}, bf16[256,512]{1,0:T(8,128)(2,1)S(1)}, u32[]{:S(2)}, u32[]{:S(2)}) collective-permute-start(bf16[256,512]{1,0:T(8,128)(2,1)S(1)} %bitcast.62), channel_id=1, source_target_pairs={{0,1},{1,0},{2,3},{3,2},{4,5},{5,4},{6,7},{7,6},{8,9},{9,8},{10,11... | collective-permute-start | bytes 786440 | tf_op jit(solution)/shard_map/ppermute | solution.py:209
Sparse Core Ops, SparseCore 0:
  80.4 38.5 all-gather.4

commit v3 on v0

v3 whole, which is shorter than its diff:
```python
import math
from functools import partial

import jax
import jax.numpy as jnp
from jax import lax
from jax.experimental import pallas as pl
from jax.experimental.pallas import tpu as pltpu
from jax.sharding import PartitionSpec as P

LOG2E = math.log2(math.e)
MASKED = 1e30
NT = (((1,), (1,)), ((), ()))
NN = (((1,), (0,)), ((), ()))
TN = (((0,), (0,)), ((), ()))
PARAMS = pltpu.CompilerParams(vmem_limit_bytes=24 * 1024 * 1024)
IN_VMEM = pl.BlockSpec(memory_space=pltpu.VMEM)
IN_SMEM = pl.BlockSpec(memory_space=pltpu.SMEM)
IN_HBM = pl.BlockSpec(memory_space=pl.ANY)


def dot(a, b, dims):
    return lax.dot_general(a, b, dims, preferred_element_type=jnp.float32)


def ways(start, size):
    return pl.ds(pl.multiple_of(start, size), size)


def forward_kernel(
    place, compat, q_hbm, g_hbm, k_hbm, v_hbm, lse_ref, targets_ref,
    delta_ref, probs_ref, score_ref, q_ref, g_ref, k_ref, v_ref, sems, *, heads, blocks, scale,
):
    value_count, width = k_ref.shape[0], k_ref.shape[1] // heads
    block = q_ref.shape[0] // blocks
    copies = [
        pltpu.make_async_copy(k_hbm, k_ref, sems.at[0]),
        pltpu.make_async_copy(v_hbm, v_ref, sems.at[1]),
    ]
    for index in range(blocks):
        rows = pl.ds(index * block, block)
        for half, (source, target) in enumerate(((q_hbm, q_ref), (g_hbm, g_ref))):
            copies.append(
                pltpu.make_async_copy(source.at[rows], target.at[rows], sems.at[2 + 2 * index + half])
            )
    for copy in copies:
        copy.start()
    copies[0].wait()
    copies[1].wait()
    for index in range(blocks):
        rows = slice(index * block, (index + 1) * block)
        copies[2 + 2 * index].wait()
        copies[3 + 2 * index].wait()
        for head in range(heads):
            columns = slice(head * width, (head + 1) * width)
            local = targets_ref[head : head + 1, rows] - place[0] * value_count
            hit = (local >= 0) & (local < value_count)
            compatible = compat[head, 0, index] == 1
            live = compatible | (jnp.max(jnp.where(hit, 1.0, 0.0)) > 0.0)

            @pl.when(live)
            def _():
                lse_rows = jnp.where(hit | compatible, lse_ref[head : head + 1, rows], MASKED) * LOG2E
                scores = dot(k_ref[:, columns], q_ref[rows, columns], NT)
                dprobs = dot(v_ref[:, columns], g_ref[rows, columns], NT)
                probs = jnp.exp2(scores * (scale * LOG2E) - lse_rows)
                delta_ref[head : head + 1, rows] = jnp.sum(probs * dprobs, axis=0, keepdims=True)
                terms = probs * (dprobs + 1.0)
                slots = lax.broadcasted_iota(jnp.int32, terms.shape, 0)
                probs_ref[head, :, rows] = probs
                score_ref[head, :, rows] = jnp.where(slots == local, terms - 1.0, terms)

            @pl.when(jnp.logical_not(live))
            def _():
                delta_ref[head : head + 1, rows] = jnp.zeros((1, block), jnp.float32)
                probs_ref[head, :, rows] = jnp.zeros((value_count, block), jnp.float32)
                score_ref[head, :, rows] = jnp.zeros((value_count, block), jnp.float32)


def value_kernel(place, probs_ref, g_ref, own_ref, send_ref):
    heads, _, _ = probs_ref.shape
    width = g_ref.shape[1] // heads
    share = own_ref.shape[0]
    parts = send_ref.shape[0] + 1
    for step in range(parts):
        rows = ways(lax.rem(place[1] + step, parts) * share, share)
        for head in range(heads):
            columns = slice(head * width, (head + 1) * width)
            term = dot(probs_ref[head, rows, :].astype(jnp.bfloat16), g_ref[:, columns], NN)
            if step == 0:
                own_ref[:, columns] = term
            else:
                send_ref[step - 1, :, columns] = term.astype(jnp.bfloat16)


def low_scores(delta_ref, probs_ref, score_ref, head, rows):
    gap = probs_ref[head, :, rows] * delta_ref[pl.ds(head, 1), rows]
    return (score_ref[head, :, rows] - gap).astype(jnp.bfloat16)


def other_kernel(
    place, delta_ref, probs_ref, score_ref, k_ref, low_ref, query_ref, *, chunk, scale
):
    head = 1 - place[2]
    width = query_ref.shape[1]
    keys = k_ref[:, ways(head * width, width)]
    for start in range(0, query_ref.shape[0], chunk):
        rows = slice(start, start + chunk)
        low = low_scores(delta_ref, probs_ref, score_ref, head, rows)
        low_ref[:, rows] = low
        query_ref[rows, :] = (scale * dot(low, keys, TN)).astype(jnp.bfloat16)


def key_kernel(
    place, delta_ref, probs_ref, score_ref, other_ref, q_ref, low_ref, own_ref, send_ref,
    *, chunk, scale,
):
    head = place[2]
    width = own_ref.shape[1] // 2
    share = own_ref.shape[0]
    parts = send_ref.shape[0] + 1
    for start in range(0, q_ref.shape[0], chunk):
        rows = slice(start, start + chunk)
        low_ref[:, rows] = low_scores(delta_ref, probs_ref, score_ref, head, rows)
    for step in range(parts - 1, -1, -1):
        rows = ways(lax.rem(place[1] + step, parts) * share, share)
        for source, index in ((other_ref, 1 - head), (low_ref, head)):
            columns = ways(index * width, width)
            term = scale * dot(source[rows, :], q_ref[:, columns], NN)
            if step == 0:
                own_ref[:, columns] = term
            else:
                send_ref[step - 1, :, columns] = term.astype(jnp.bfloat16)


def query_kernel(place, low_ref, k_ref, received_ref, keep_ref, send_ref, *, scale):
    chains, rows, width = keep_ref.shape
    keys = k_ref[:, ways(place[2] * width, width)]
    for target, other in ((send_ref, 1), (keep_ref, 0)):
        for chain in range(chains):
            start = (2 * chain + (place[3 + chain] ^ other)) * rows
            columns = ways(start, rows)
            term = scale * dot(low_ref[:, columns], keys, TN)
            total = term + received_ref[columns, :].astype(jnp.float32)
            target[chain] = total.astype(target.dtype)


def assemble_kernel(place, mine_ref, theirs_ref, out_ref, sems):
    chains, pieces, piece, width = mine_ref.shape
    copies = []
    for side, ref in enumerate((mine_ref, theirs_ref)):
        columns = ways((place[0] ^ side) * width, width)
        for chain in range(chains):
            for index in range(pieces):
                rows = ways((chain * pieces + (index ^ place[1 + chain])) * piece, piece)
                copies.append(
                    pltpu.make_async_copy(
                        ref.at[chain, index], out_ref.at[rows, columns], sems.at[len(copies)]
                    )
                )
                copies[-1].start()
    for copy in copies:
        copy.wait()


def call(kernel, name, inputs, in_specs, outputs, flops, scratch=(), out_specs=None):
    return pl.pallas_call(
        kernel,
        in_specs=in_specs,
        out_specs=[IN_VMEM] * len(outputs) if out_specs is None else out_specs,
        out_shape=outputs,
        scratch_shapes=list(scratch),
        cost_estimate=pl.CostEstimate(flops=flops, bytes_accessed=flops // 1000, transcendentals=0),
        compiler_params=PARAMS,
        name=name,
    )(*inputs)


def on_device(queries, pool_keys, pool_values, out_grad, lse, compat, targets):
    heads, value_blocks, blocks = compat.shape
    query_count, wide = queries.shape
    value_count = pool_keys.shape[0]
    width = wide // heads
    scale = width ** -0.5
    value_devices, parts = lax.axis_size("val"), lax.axis_size("qry")
    bits = value_devices.bit_length() - 1
    assert heads == 2 and value_blocks == 1 and value_devices == 1 << bits and bits >= 3
    val, qry = lax.axis_index("val"), lax.axis_index("qry")
    core = lax.rem(val, 2)
    share = value_count // parts
    f32, bf16 = jnp.float32, jnp.bfloat16

    def flip(array, mask):
        return lax.ppermute(array, "val", [(i, i ^ mask) for i in range(value_devices)])

    def swap_shares(send):
        return [
            lax.ppermute(send[step - 1], "qry", [(i, (i + step) % parts) for i in range(parts)])
            for step in range(1, parts)
        ]

    def add(own, received):
        for array in received:
            own = own + array.astype(f32)
        return own

    def bit_of(bit):
        return lax.rem(val // (1 << bit), 2)

    chains = 2 if query_count % (2 * value_devices // 2 * 16) == 0 else 1
    orders = [[1, 2], [2, 1]][:chains]
    orders = [order + list(range(3, bits)) for order in orders]
    place = jnp.stack([val, qry, core] + [bit_of(order[0]) for order in orders]).astype(jnp.int32)
    work = 2 * query_count * value_count * width

    delta, probs, terms, q_near, g_near, k_near = call(
        partial(forward_kernel, heads=heads, blocks=blocks, scale=scale),
        "forward_pass",
        (place,)
        + tuple(
            pltpu.with_memory_space_constraint(array, pltpu.HBM)
            for array in (
                compat, queries, out_grad, pool_keys, pool_values, lse, jnp.transpose(targets)
            )
        ),
        [IN_SMEM, IN_SMEM] + [IN_HBM] * 4 + [IN_VMEM] * 2,
        [
            pltpu.VMEM((heads, query_count), f32),
            pltpu.VMEM((heads, value_count, query_count), f32),
            pltpu.VMEM((heads, value_count, query_count), f32),
            pltpu.VMEM(queries.shape, bf16),
            pltpu.VMEM(queries.shape, bf16),
            pltpu.VMEM(pool_keys.shape, bf16),
        ],
        4 * work,
        [
            pltpu.VMEM(pool_values.shape, bf16),
            pltpu.SemaphoreType.DMA((2 + 2 * blocks,)),
        ],
    )
    shares = [
        pltpu.VMEM((share, wide), f32),
        pltpu.VMEM((parts - 1, share, wide), bf16),
    ]
    value_own, value_send = call(
        value_kernel, "value_terms", (place, probs, g_near), [IN_SMEM] + [IN_VMEM] * 2, shares, 2 * work
    )
    value_received = swap_shares(value_send)
    stride = 1
    while stride < value_devices:
        steps = min(4, value_devices // stride)
        delta = add(delta, [flip(delta, stride * step) for step in range(1, steps)])
        stride *= steps

    chunk = query_count // 3 if query_count % 384 == 0 else query_count
    low = pltpu.VMEM((value_count, query_count), bf16)
    low_other, query_send = call(
        partial(other_kernel, chunk=chunk, scale=scale),
        "other_head",
        (place, delta, probs, terms, k_near),
        [IN_SMEM] + [IN_VMEM] * 4,
        [low, pltpu.VMEM((query_count, width), bf16)],
        work,
    )
    query_received = flip(query_send, 1)
    low_mine, key_own, key_send = call(
        partial(key_kernel, chunk=chunk, scale=scale),
        "key_terms",
        (place, delta, probs, terms, low_other, q_near),
        [IN_SMEM] + [IN_VMEM] * 5,
        [low] + shares,
        2 * work,
    )
    key_received = swap_shares(key_send)
    half = query_count // (2 * chains)
    keep, send = call(
        partial(query_kernel, scale=scale),
        "own_head",
        (place, low_mine, k_near, query_received),
        [IN_SMEM] + [IN_VMEM] * 3,
        [pltpu.VMEM((chains, half, width), f32), pltpu.VMEM((chains, half, width), bf16)],
        work,
    )

    kept = [keep[chain] for chain in range(chains)]
    sent = [send[chain] for chain in range(chains)]
    own_piece = []
    for stage in range(bits - 1):
        received = [flip(sent[chain], 1 << orders[chain][stage]) for chain in range(chains)]
        for chain in range(chains):
            total = add(kept[chain], [received[chain]])
            if stage == bits - 2:
                kept[chain] = total.astype(bf16)
            else:
                bit = bit_of(orders[chain][stage + 1])
                split = total.reshape(2, total.shape[0] // 2, width)
                sent[chain] = lax.dynamic_index_in_dim(split, 1 - bit, 0, keepdims=False).astype(bf16)
                kept[chain] = lax.dynamic_index_in_dim(split, bit, 0, keepdims=False)
    for chain in range(chains):
        index = 0
        for bit in orders[chain]:
            index = 2 * index + bit_of(bit)
        own_piece.append(index)
    for stage in range(bits - 2, -1, -1):
        received = [flip(kept[chain], 1 << orders[chain][stage]) for chain in range(chains)]
        kept = [jnp.concatenate([kept[chain], received[chain]], axis=0) for chain in range(chains)]
    pieces = value_devices // 2
    mine = jnp.stack(kept).reshape(chains, pieces, query_count // (chains * pieces), width)
    theirs = flip(mine, 1)
    (query_grad,) = call(
        assemble_kernel,
        "assemble",
        (
            jnp.stack([core] + own_piece).astype(jnp.int32),
            pltpu.with_memory_space_constraint(mine, pltpu.VMEM),
            pltpu.with_memory_space_constraint(theirs, pltpu.VMEM),
        ),
        [IN_SMEM] + [IN_VMEM] * 2,
        [jax.ShapeDtypeStruct((query_count, wide), bf16)],
        1000 * query_count * wide,
        [pltpu.SemaphoreType.DMA((2 * chains * pieces,))],
        [IN_HBM],
    )
    value_grad = add(value_own, value_received).astype(bf16)
    key_grad = add(key_own, key_received).astype(bf16)
    return query_grad, key_grad, value_grad


def solution(mesh):
    placed = (
        P("qry", None),
        P("val", None),
        P("val", None),
        P("qry", None),
        P(None, "qry"),
        P(None, "val", "qry"),
        P("qry", None),
    )
    return jax.shard_map(
        on_device,
        mesh=mesh,
        in_specs=placed,
        out_specs=(P("qry", None), P(("val", "qry"), None), P(("val", "qry"), None)),
        check_vma=False,
    )
```

time: 216 us -> 87.7 us (0.41)
  blocking collectives: 188 us -> 0 us
  waiting for transfers between devices: 0 us -> 46 us
  starting transfers between devices: 0 us -> 18.8 us
  Pallas kernels: 0 us -> 16.1 us
  matrix products: 11.1 us -> 0 us
  local copies, waits for them, and re-layouts: 7.74 us -> 1 us
  other arithmetic: 7.41 us -> 4.03 us
    psum x3 -> x0, blocking collectives: 188 us -> none  [the longest x1 78.5 us: on_device(): query_grad = lax.psum(query_part, 'val').astype(jnp.bfloat16)]
    ppermute x0 -> x22, waiting for transfers between devices: none -> 46 us  [the longest x20 35.4 us: flip(): lax.ppermute(array, 'val', [(i, i ^ mask) for i in range(value_devices)])]
    ppermute x0 -> x22, starting transfers between devices: none -> 18.8 us  [the longest x20 16.7 us: flip(): lax.ppermute(array, 'val', [(i, i ^ mask) for i in range(value_devices)])]
    pallas_call x0 -> x6, Pallas kernels: none -> 16.1 us  [call(): pl.pallas_call(kernel, in_specs=in_specs, out_specs=[IN_VMEM] * len(outpu...]
    dot_general x10 -> x0, matrix products: 11.1 us -> none  [the longest x2 3.73 us: first_pass(): jnp.einsum('qd,kd->qk', query_tile, key_head, preferred_element_type=jnp....]
    unnamed x40 -> x8, local copies, waits for them, and re-layouts: 7.58 us -> 0.82 us
  transfers between devices with their start and end apart: 0 -> 22, of which waited for: 0 -> 19; matrix products, arithmetic and copies ran while one was open for 0% -> 4% of each run, Pallas kernels for 0% -> 5%
where the time goes in v3:
time: 87.7 us; the launch traced here: 86.8 us
  waiting for transfers between devices  46 us (52%)
  starting transfers between devices  18.8 us (21%)
  Pallas kernels  16.1 us (18%)
  other arithmetic  4.03 us (5%)
  local copies, waits for them, and re-layouts  1 us (1%)
  between operations  0.91 us (1%)
    ppermute x20, waiting for transfers between devices, flip(): lax.ppermute(array, 'val', [(i, i ^ mask) for i in range(value_devices)])  35.4 us
    ppermute x20, starting transfers between devices, flip(): lax.ppermute(array, 'val', [(i, i ^ mask) for i in range(value_devices)])  16.7 us
    pallas_call x6, Pallas kernels, call(): pl.pallas_call(kernel, in_specs=in_specs, out_specs=[IN_VMEM] * len(outpu...  16.1 us
    ppermute x2, waiting for transfers between devices, swap_shares(): lax.ppermute(send[step - 1], 'qry', [(i, (i + step) % parts) for i in ran...  10.6 us
    ppermute x2, starting transfers between devices, swap_shares(): lax.ppermute(send[step - 1], 'qry', [(i, (i + step) % parts) for i in ran...  2.03 us
    convert_element_type x1, other arithmetic, on_device(): key_grad = add(key_own, key_received).astype(bf16)  1.81 us
    convert_element_type x1, other arithmetic, on_device(): value_grad = add(value_own, value_received).astype(bf16)  1.81 us
  transfers between devices with their start and end apart: 22, of which 19 were waited for; matrix products, arithmetic and copies ran while one was open for 4% of the time, Pallas kernels for 5%

profile of v3, /device:TPU:0, one launch (start us, length us, event | category | flops | bytes accessed | tf_op | source)
XLA Modules:
  0.0 86.8 jit_solution(11599502407589543311)
XLA Ops:
  0.7 0.1 stack.45.place
  0.8 7.1 %forward_pass.1 = (f32[2,1536]{1,0:T(2,128)S(1)}, f32[2,512,1536]{2,1,0:T(8,128)S(1)}, f32[2,512,1536]{2,1,0:T(8,128)S(1)}, bf16[1536,512]{1,0:T(8,128)(2,1)S(1)...) custom-call(s32[5]{0:T(128)S(1)} %stack.45.place, s32[2,1,6]{2,1,0:T(1,128)} %compat.1, ...), custom_call_target="tpu_custom_call" | custom-call | flops 1610612736 | bytes 1610612 | tf_op jit(solution)/shard_map/forward_pass/pallas_call | solution.py:167
  7.9 0.0 copy-start
  7.9 0.1 collective-permute-start
  8.0 2.1 %collective-permute-start.1 = (f32[2,1536]{1,0:T(2,128)S(1)}, f32[2,1536]{1,0:T(2,128)S(1)}, u32[]{:S(2)}, u32[]{:S(2)}) collective-permute-start(f32[2,1536]{1,0:T(2,128)S(1)} %get-tuple-element.18), channel_id=1, source_target_pairs={{0,4},{2,6},{4,0},{6,2},{8,12},{10,14},{12,8},{14,10},{16,20},{18,... | collective-permute-start | bytes 36872 | tf_op jit(solution)/shard_map/ppermute | solution.py:194
  10.1 0.1 collective-permute-start.2
  10.1 0.0 collective-permute-done
  10.1 1.6 %collective-permute-done.1 = f32[2,1536]{1,0:T(2,128)S(1)} collective-permute-done((f32[2,1536]{1,0:T(2,128)S(1)}, f32[2,1536]{1,0:T(2,128)S(1)}, u32[]{:S(2)}, u32[]{:S(2)}) %collective-permute-start.1) | collective-permute-done | bytes 12320 | tf_op jit(solution)/shard_map/ppermute | solution.py:194
  11.7 1.4 %collective-permute-done.2 = f32[2,1536]{1,0:T(2,128)S(1)} collective-permute-done((f32[2,1536]{1,0:T(2,128)S(1)}, f32[2,1536]{1,0:T(2,128)S(1)}, u32[]{:S(2)}, u32[]{:S(2)}) %collective-permute-start.2) | collective-permute-done | bytes 12320 | tf_op jit(solution)/shard_map/ppermute | solution.py:194
  13.2 1.0 %collective-permute-start.3 = (f32[2,1536]{1,0:T(2,128)S(1)}, f32[2,1536]{1,0:T(2,128)S(1)}, u32[]{:S(2)}, u32[]{:S(2)}) collective-permute-start(f32[2,1536]{1,0:T(2,128)S(1)} %add_add_fusion.1), channel_id=1, source_target_pairs={{0,8},{2,10},{4,12},{6,14},{8,0},{10,2},{12,4},{14,6},{16,24},{18,... | collective-permute-start | bytes 36872 | tf_op jit(solution)/shard_map/ppermute | solution.py:194
  14.2 3.4 %collective-permute-start.4 = (f32[2,1536]{1,0:T(2,128)S(1)}, f32[2,1536]{1,0:T(2,128)S(1)}, u32[]{:S(2)}, u32[]{:S(2)}) collective-permute-start(f32[2,1536]{1,0:T(2,128)S(1)} %add_add_fusion.1), channel_id=1, source_target_pairs={{0,16},{2,18},{4,20},{6,22},{8,24},{10,26},{12,28},{14,30},{16,0},... | collective-permute-start | bytes 36872 | tf_op jit(solution)/shard_map/ppermute | solution.py:194
  17.6 0.0 collective-permute-start.5
  17.6 0.0 collective-permute-done.3
  17.6 1.6 %collective-permute-done.4 = f32[2,1536]{1,0:T(2,128)S(1)} collective-permute-done((f32[2,1536]{1,0:T(2,128)S(1)}, f32[2,1536]{1,0:T(2,128)S(1)}, u32[]{:S(2)}, u32[]{:S(2)}) %collective-permute-start.4) | collective-permute-done | bytes 12320 | tf_op jit(solution)/shard_map/ppermute | solution.py:194
  19.3 3.8 %collective-permute-done.5 = f32[2,1536]{1,0:T(2,128)S(1)} collective-permute-done((f32[2,1536]{1,0:T(2,128)S(1)}, f32[2,1536]{1,0:T(2,128)S(1)}, u32[]{:S(2)}, u32[]{:S(2)}) %collective-permute-start.5) | collective-permute-done | bytes 12320 | tf_op jit(solution)/shard_map/ppermute | solution.py:194
  23.1 1.7 %other_head.1 = (bf16[512,1536]{1,0:T(8,128)(2,1)S(1)}, bf16[1536,256]{1,0:T(8,128)(2,1)S(1)}) custom-call(s32[5]{0:T(128)S(1)} %stack.45.place, f32[2,1536]{1,0:T(2,128)S(1)} %add_add_fusion.delta_ref, f32[2,512,1536]{2,1,0:T(8,128)S(1)} %get-tuple-element.19.probs_ref, f32[2,512,1536]{2,1,0:T(8,128)S(1)} %get-tuple-element.20.score_ref, ...), custom_call_target="tpu_custom_call" | custom-call | flops 402653184 | bytes 402653 | tf_op jit(solution)/shard_map/other_head/pallas_call | solution.py:167
  24.8 0.1 collective-permute-start.6
  24.9 0.0 copy-done
  24.9 1.9 %key_terms.1 = (bf16[512,1536]{1,0:T(8,128)(2,1)S(1)}, f32[256,512]{1,0:T(8,128)S(1)}, bf16[1,256,512]{2,1,0:T(8,128)(2,1)S(1)}) custom-call(s32[5]{0:T(128)S(1)} %stack.45.place, f32[2,1536]{1,0:T(2,128)S(1)} %add_add_fusion.delta_ref, f32[2,512,1536]{2,1,0:T(8,128)S(1)} %get-tuple-element.19.probs_ref, f32[2,512,1536]{2,1,0:T(8,128)S(1)} %get-tuple-element.20.score_ref, ...), custom_call_target="tpu_custom_call" | custom-call | flops 805306368 | bytes 805306 | tf_op jit(solution)/shard_map/key_terms/pallas_call | solution.py:167
  26.9 0.0 copy-start.2
  26.9 0.3 collective-permute-done.6.received_ref
  27.2 1.2 %own_head.1 = (f32[2,384,256]{2,1,0:T(8,128)S(1)}, bf16[2,384,256]{2,1,0:T(8,128)(2,1)S(1)}) custom-call(s32[5]{0:T(128)S(1)} %stack.45.place, bf16[512,1536]{1,0:T(8,128)(2,1)S(1)} %get-tuple-element.24.low_ref, bf16[512,512]{1,0:T(8,128)(2,1)S(1)} %get-tuple-element.21.k_ref, bf16[1536,256]{1,0:T(8,128)(2,1)S(1)} %collective-permute-done.6.received_ref), custom_call_target="tpu_custom_call" | custom-call | flops 402653184 | bytes 402653 | tf_op jit(solution)/shard_map/own_head/pallas_call | solution.py:167
  28.4 0.0 copy-done.2
  28.4 0.1 collective-permute-start.13
  28.5 0.7 collective-permute-start.7
  29.2 6.3 %collective-permute-done.13 = bf16[384,256]{1,0:T(8,128)(2,1)S(1)} collective-permute-done((bf16[384,256]{1,0:T(8,128)(2,1)S(1)}, bf16[384,256]{1,0:T(8,128)(2,1)S(1)}, u32[]{:S(2)}, u32[]{:S(2)}) %collective-permute-start.13) | collective-permute-done | bytes 196640 | tf_op jit(solution)/shard_map/ppermute | solution.py:194
  35.5 0.1 collective-permute-done.7
  35.6 0.1 bitcast_add_fusion.1
  35.6 0.0 copy-start.1
  35.7 1.7 %collective-permute-start.8 = (bf16[192,256]{1,0:T(8,128)(2,1)S(1)}, bf16[192,256]{1,0:T(8,128)(2,1)S(1)}, u32[]{:S(2)}, u32[]{:S(2)}) collective-permute-start(bf16[192,256]{1,0:T(8,128)(2,1)S(1)} %fusion), channel_id=1, source_target_pairs={{0,8},{2,10},{4,12},{6,14},{8,0},{10,2},{12,4},{14,6},{16,24},{18,... | collective-permute-start | bytes 294920 | tf_op jit(solution)/shard_map/ppermute | solution.py:194
  37.4 0.7 collective-permute-start.14
  38.2 2.2 %collective-permute-done.8 = bf16[192,256]{1,0:T(8,128)(2,1)S(1)} collective-permute-done((bf16[192,256]{1,0:T(8,128)(2,1)S(1)}, bf16[192,256]{1,0:T(8,128)(2,1)S(1)}, u32[]{:S(2)}, u32[]{:S(2)}) %collective-permute-start.8) | collective-permute-done | bytes 98336 | tf_op jit(solution)/shard_map/ppermute | solution.py:194
  40.4 0.4 collective-permute-start.9
  40.8 1.3 %collective-permute-done.14 = bf16[192,256]{1,0:T(8,128)(2,1)S(1)} collective-permute-done((bf16[192,256]{1,0:T(8,128)(2,1)S(1)}, bf16[192,256]{1,0:T(8,128)(2,1)S(1)}, u32[]{:S(2)}, u32[]{:S(2)}) %collective-permute-start.14) | collective-permute-done | bytes 98336 | tf_op jit(solution)/shard_map/ppermute | solution.py:194
  42.2 1.4 %collective-permute-start.15 = (bf16[96,256]{1,0:T(8,128)(2,1)S(1)}, bf16[96,256]{1,0:T(8,128)(2,1)S(1)}, u32[]{:S(2)}, u32[]{:S(2)}) collective-permute-start(bf16[96,256]{1,0:T(8,128)(2,1)S(1)} %fusion.5), channel_id=1, source_target_pairs={{0,16},{2,18},{4,20},{6,22},{8,24},{10,26},{12,28},{14,30},{16,0},... | collective-permute-start | bytes 147464 | tf_op jit(solution)/shard_map/ppermute | solution.py:194
  43.5 1.9 %collective-permute-done.9 = bf16[96,256]{1,0:T(8,128)(2,1)S(1)} collective-permute-done((bf16[96,256]{1,0:T(8,128)(2,1)S(1)}, bf16[96,256]{1,0:T(8,128)(2,1)S(1)}, u32[]{:S(2)}, u32[]{:S(2)}) %collective-permute-start.9) | collective-permute-done | bytes 49184 | tf_op jit(solution)/shard_map/ppermute | solution.py:194
  45.5 0.7 collective-permute-start.10
  46.2 3.5 %collective-permute-done.15 = bf16[96,256]{1,0:T(8,128)(2,1)S(1)} collective-permute-done((bf16[96,256]{1,0:T(8,128)(2,1)S(1)}, bf16[96,256]{1,0:T(8,128)(2,1)S(1)}, u32[]{:S(2)}, u32[]{:S(2)}) %collective-permute-start.15) | collective-permute-done | bytes 49184 | tf_op jit(solution)/shard_map/ppermute | solution.py:194
  49.8 0.1 collective-permute-start.16
  49.8 0.7 collective-permute-done.10
  50.5 2.6 %collective-permute-start.11 = (bf16[192,256]{1,0:T(8,128)(2,1)S(1)}, bf16[192,256]{1,0:T(8,128)(2,1)S(1)}, u32[]{:S(2)}, u32[]{:S(2)}) collective-permute-start(bf16[192,256]{1,0:T(8,128)(2,1)S(1)} %pad_maximum_fusion.5), channel_id=1, source_target_pairs={{0,8},{2,10},{4,12},{6,14},{8,0},{10,2},{12,4},{14,6},{16,24},{18,... | collective-permute-start | bytes 294920 | tf_op jit(solution)/shard_map/ppermute | solution.py:194
  53.2 1.7 %collective-permute-done.16 = bf16[96,256]{1,0:T(8,128)(2,1)S(1)} collective-permute-done((bf16[96,256]{1,0:T(8,128)(2,1)S(1)}, bf16[96,256]{1,0:T(8,128)(2,1)S(1)}, u32[]{:S(2)}, u32[]{:S(2)}) %collective-permute-start.16) | collective-permute-done | bytes 49184 | tf_op jit(solution)/shard_map/ppermute | solution.py:194
  54.8 0.7 collective-permute-start.17
  55.5 0.7 collective-permute-done.11
  56.3 0.7 collective-permute-start.12
  57.0 2.5 %collective-permute-done.17 = bf16[192,256]{1,0:T(8,128)(2,1)S(1)} collective-permute-done((bf16[192,256]{1,0:T(8,128)(2,1)S(1)}, bf16[192,256]{1,0:T(8,128)(2,1)S(1)}, u32[]{:S(2)}, u32[]{:S(2)}) %collective-permute-start.17) | collective-permute-done | bytes 98336 | tf_op jit(solution)/shard_map/ppermute | solution.py:194
  59.5 0.1 collective-permute-start.18
  59.6 2.4 %collective-permute-done.12 = bf16[384,256]{1,0:T(8,128)(2,1)S(1)} collective-permute-done((bf16[384,256]{1,0:T(8,128)(2,1)S(1)}, bf16[384,256]{1,0:T(8,128)(2,1)S(1)}, u32[]{:S(2)}, u32[]{:S(2)}) %collective-permute-start.12) | collective-permute-done | bytes 196640 | tf_op jit(solution)/shard_map/ppermute | solution.py:194
  62.0 3.2 %collective-permute-done.18 = bf16[384,256]{1,0:T(8,128)(2,1)S(1)} collective-permute-done((bf16[384,256]{1,0:T(8,128)(2,1)S(1)}, bf16[384,256]{1,0:T(8,128)(2,1)S(1)}, u32[]{:S(2)}, u32[]{:S(2)}) %collective-permute-start.18) | collective-permute-done | bytes 196640 | tf_op jit(solution)/shard_map/ppermute | solution.py:194
  65.3 0.1 pad_maximum_fusion.mine_ref
  65.4 0.1 collective-permute-start.19
  65.5 0.0 copy-done.1
  65.5 2.2 %value_terms.1 = (f32[256,512]{1,0:T(8,128)S(1)}, bf16[1,256,512]{2,1,0:T(8,128)(2,1)}) custom-call(s32[5]{0:T(128)S(1)} %stack.45.place, f32[2,512,1536]{2,1,0:T(8,128)S(1)} %copy-done.1, bf16[1536,512]{1,0:T(8,128)(2,1)S(1)} %get-tuple-element.30.g_ref), custom_call_target="tpu_custom_call" | custom-call | flops 805306368 | bytes 805306 | tf_op jit(solution)/shard_map/value_terms/pallas_call | solution.py:167
  67.7 0.0 copy-start.3
  67.7 0.8 copy-done.3
  68.5 1.1 %collective-permute-start.21 = (bf16[256,512]{1,0:T(8,128)(2,1)}, bf16[256,512]{1,0:T(8,128)(2,1)S(1)}, u32[]{:S(2)}, u32[]{:S(2)}) collective-permute-start(bf16[256,512]{1,0:T(8,128)(2,1)} %bitcast.27), channel_id=1, source_target_pairs={{0,1},{1,0},{2,3},{3,2},{4,5},{5,4},{6,7},{7,6},{8,9},{9,8},{10,11... | collective-permute-start | bytes 786440 | tf_op jit(solution)/shard_map/ppermute | solution.py:198
  69.6 0.9 %collective-permute-start.20 = (bf16[256,512]{1,0:T(8,128)(2,1)S(1)}, bf16[256,512]{1,0:T(8,128)(2,1)S(1)}, u32[]{:S(2)}, u32[]{:S(2)}) collective-permute-start(bf16[256,512]{1,0:T(8,128)(2,1)S(1)} %bitcast.44), channel_id=1, source_target_pairs={{0,1},{1,0},{2,3},{3,2},{4,5},{5,4},{6,7},{7,6},{8,9},{9,8},{10,11... | collective-permute-start | bytes 786440 | tf_op jit(solution)/shard_map/ppermute | solution.py:198
  70.5 0.1 pad_add_fusion.place
  70.6 7.2 %collective-permute-done.21 = bf16[256,512]{1,0:T(8,128)(2,1)S(1)} collective-permute-done((bf16[256,512]{1,0:T(8,128)(2,1)}, bf16[256,512]{1,0:T(8,128)(2,1)S(1)}, u32[]{:S(2)}, u32[]{:S(2)}) %collective-permute-start.21) | collective-permute-done | bytes 262176 | tf_op jit(solution)/shard_map/ppermute | solution.py:198
  77.8 1.8 %add_convert_fusion = bf16[256,512]{1,0:T(8,128)(2,1)} fusion(f32[256,512]{1,0:T(8,128)} %copy-done.3, bf16[256,512]{1,0:T(8,128)(2,1)S(1)} %collective-permute-done.21), kind=kLoop, calls=%fused_computation.1 | loop fusion | flops 393216 | bytes 1048576 | tf_op jit(solution)/shard_map/convert_element_type | solution.py:324
  79.6 3.4 %collective-permute-done.20 = bf16[256,512]{1,0:T(8,128)(2,1)S(1)} collective-permute-done((bf16[256,512]{1,0:T(8,128)(2,1)S(1)}, bf16[256,512]{1,0:T(8,128)(2,1)S(1)}, u32[]{:S(2)}, u32[]{:S(2)}) %collective-permute-start.20) | collective-permute-done | bytes 262176 | tf_op jit(solution)/shard_map/ppermute | solution.py:198
  83.0 1.8 %add_convert_fusion.1 = bf16[256,512]{1,0:T(8,128)(2,1)} fusion(f32[256,512]{1,0:T(8,128)} %copy-done.2, bf16[256,512]{1,0:T(8,128)(2,1)S(1)} %collective-permute-done.20), kind=kLoop, calls=%fused_computation.2 | loop fusion | flops 393216 | bytes 1048576 | tf_op jit(solution)/shard_map/convert_element_type | solution.py:325
  84.8 0.0 collective-permute-done.19.theirs_ref
  84.8 1.9 %assemble.1 = bf16[1536,512]{1,0:T(8,128)(2,1)} custom-call(s32[3]{0:T(128)S(1)} %pad_add_fusion.place, bf16[2,8,96,256]{3,2,1,0:T(8,128)(2,1)S(1)} %pad_maximum_fusion.mine_ref, bf16[2,8,96,256]{3,2,1,0:T(8,128)(2,1)S(1)} %collective-permute-done.19.theirs_ref), custom_call_target="tpu_custom_call" | custom-call | flops 786432000 | bytes 786432 | tf_op jit(solution)/shard_map/assemble/pallas_call | solution.py:167
  (17 shorter events, 0.3 us)
Async XLA Ops:
  7.9 17.0 %copy-start = (f32[2,512,1536]{2,1,0:T(8,128)}, f32[2,512,1536]{2,1,0:T(8,128)S(1)}, u32[]{:S(2)}) copy-start(f32[2,512,1536]{2,1,0:T(8,128)S(1)} %get-tuple-element.19.probs_ref) | copy-start | bytes 18874372
  7.9 2.2 %collective-permute-start = (f32[2,1536]{1,0:T(2,128)S(1)}, f32[2,1536]{1,0:T(2,128)S(1)}, u32[]{:S(2)}, u32[]{:S(2)}) collective-permute-start(f32[2,1536]{1,0:T(2,128)S(1)} %get-tuple-element.18), channel_id=1, source_target_pairs={{0,2},{2,0},{4,6},{6,4},{8,10},{10,8},{12,14},{14,12},{16,18},{18,... | collective-permute-start | bytes 36872 | tf_op jit(solution)/shard_map/ppermute | solution.py:194
  8.0 3.8 %collective-permute-start.1 = (f32[2,1536]{1,0:T(2,128)S(1)}, f32[2,1536]{1,0:T(2,128)S(1)}, u32[]{:S(2)}, u32[]{:S(2)}) collective-permute-start(f32[2,1536]{1,0:T(2,128)S(1)} %get-tuple-element.18), channel_id=1, source_target_pairs={{0,4},{2,6},{4,0},{6,2},{8,12},{10,14},{12,8},{14,10},{16,20},{18,... | collective-permute-start | bytes 36872 | tf_op jit(solution)/shard_map/ppermute | solution.py:194
  10.1 3.1 %collective-permute-start.2 = (f32[2,1536]{1,0:T(2,128)S(1)}, f32[2,1536]{1,0:T(2,128)S(1)}, u32[]{:S(2)}, u32[]{:S(2)}) collective-permute-start(f32[2,1536]{1,0:T(2,128)S(1)} %get-tuple-element.18), channel_id=1, source_target_pairs={{0,6},{2,4},{4,2},{6,0},{8,14},{10,12},{12,10},{14,8},{16,22},{18,... | collective-permute-start | bytes 36872 | tf_op jit(solution)/shard_map/ppermute | solution.py:194
  13.2 4.5 %collective-permute-start.3 = (f32[2,1536]{1,0:T(2,128)S(1)}, f32[2,1536]{1,0:T(2,128)S(1)}, u32[]{:S(2)}, u32[]{:S(2)}) collective-permute-start(f32[2,1536]{1,0:T(2,128)S(1)} %add_add_fusion.1), channel_id=1, source_target_pairs={{0,8},{2,10},{4,12},{6,14},{8,0},{10,2},{12,4},{14,6},{16,24},{18,... | collective-permute-start | bytes 36872 | tf_op jit(solution)/shard_map/ppermute | solution.py:194
  14.2 5.1 %collective-permute-start.4 = (f32[2,1536]{1,0:T(2,128)S(1)}, f32[2,1536]{1,0:T(2,128)S(1)}, u32[]{:S(2)}, u32[]{:S(2)}) collective-permute-start(f32[2,1536]{1,0:T(2,128)S(1)} %add_add_fusion.1), channel_id=1, source_target_pairs={{0,16},{2,18},{4,20},{6,22},{8,24},{10,26},{12,28},{14,30},{16,0},... | collective-permute-start | bytes 36872 | tf_op jit(solution)/shard_map/ppermute | solution.py:194
  17.6 5.5 %collective-permute-start.5 = (f32[2,1536]{1,0:T(2,128)S(1)}, f32[2,1536]{1,0:T(2,128)S(1)}, u32[]{:S(2)}, u32[]{:S(2)}) collective-permute-start(f32[2,1536]{1,0:T(2,128)S(1)} %add_add_fusion.1), channel_id=1, source_target_pairs={{0,24},{2,26},{4,28},{6,30},{8,16},{10,18},{12,20},{14,22},{16,8},... | collective-permute-start | bytes 36872 | tf_op jit(solution)/shard_map/ppermute | solution.py:194
  24.8 2.4 %collective-permute-start.6 = (bf16[1536,256]{1,0:T(8,128)(2,1)S(1)}, bf16[1536,256]{1,0:T(8,128)(2,1)S(1)}, u32[]{:S(2)}, u32[]{:S(2)}) collective-permute-start(bf16[1536,256]{1,0:T(8,128)(2,1)S(1)} %get-tuple-element.25), channel_id=1, source_target_pairs={{0,2},{2,0},{4,6},{6,4},{8,10},{10,8},{12,14},{14,12},{16,18},{18,... | collective-permute-start | bytes 2359304 | tf_op jit(solution)/shard_map/ppermute | solution.py:194
  26.9 1.5 %copy-start.2 = (f32[256,512]{1,0:T(8,128)}, f32[256,512]{1,0:T(8,128)S(1)}, u32[]{:S(2)}) copy-start(f32[256,512]{1,0:T(8,128)S(1)} %get-tuple-element.28) | copy-start | bytes 1572868
  28.4 7.1 %collective-permute-start.13 = (bf16[384,256]{1,0:T(8,128)(2,1)S(1)}, bf16[384,256]{1,0:T(8,128)(2,1)S(1)}, u32[]{:S(2)}, u32[]{:S(2)}) collective-permute-start(bf16[384,256]{1,0:T(8,128)(2,1)S(1)} %get-tuple-element.36), channel_id=1, source_target_pairs={{0,8},{2,10},{4,12},{6,14},{8,0},{10,2},{12,4},{14,6},{16,24},{18,... | collective-permute-start | bytes 589832 | tf_op jit(solution)/shard_map/ppermute | solution.py:194
  28.5 7.1 %collective-permute-start.7 = (bf16[384,256]{1,0:T(8,128)(2,1)S(1)}, bf16[384,256]{1,0:T(8,128)(2,1)S(1)}, u32[]{:S(2)}, u32[]{:S(2)}) collective-permute-start(bf16[384,256]{1,0:T(8,128)(2,1)S(1)} %get-tuple-element.35), channel_id=1, source_target_pairs={{0,4},{2,6},{4,0},{6,2},{8,12},{10,14},{12,8},{14,10},{16,20},{18,... | collective-permute-start | bytes 589832 | tf_op jit(solution)/shard_map/ppermute | solution.py:194
  35.6 29.8 %copy-start.1 = (f32[2,512,1536]{2,1,0:T(8,128)S(1)}, f32[2,512,1536]{2,1,0:T(8,128)}, u32[]{:S(2)}) copy-start(f32[2,512,1536]{2,1,0:T(8,128)} %copy-done) | copy-start | bytes 18874372
  35.7 4.7 %collective-permute-start.8 = (bf16[192,256]{1,0:T(8,128)(2,1)S(1)}, bf16[192,256]{1,0:T(8,128)(2,1)S(1)}, u32[]{:S(2)}, u32[]{:S(2)}) collective-permute-start(bf16[192,256]{1,0:T(8,128)(2,1)S(1)} %fusion), channel_id=1, source_target_pairs={{0,8},{2,10},{4,12},{6,14},{8,0},{10,2},{12,4},{14,6},{16,24},{18,... | collective-permute-start | bytes 294920 | tf_op jit(solution)/shard_map/ppermute | solution.py:194
  37.4 4.7 %collective-permute-start.14 = (bf16[192,256]{1,0:T(8,128)(2,1)S(1)}, bf16[192,256]{1,0:T(8,128)(2,1)S(1)}, u32[]{:S(2)}, u32[]{:S(2)}) collective-permute-start(bf16[192,256]{1,0:T(8,128)(2,1)S(1)} %fusion.1), channel_id=1, source_target_pairs={{0,4},{2,6},{4,0},{6,2},{8,12},{10,14},{12,8},{14,10},{16,20},{18,... | collective-permute-start | bytes 294920 | tf_op jit(solution)/shard_map/ppermute | solution.py:194
  40.4 5.1 %collective-permute-start.9 = (bf16[96,256]{1,0:T(8,128)(2,1)S(1)}, bf16[96,256]{1,0:T(8,128)(2,1)S(1)}, u32[]{:S(2)}, u32[]{:S(2)}) collective-permute-start(bf16[96,256]{1,0:T(8,128)(2,1)S(1)} %fusion.4), channel_id=1, source_target_pairs={{0,16},{2,18},{4,20},{6,22},{8,24},{10,26},{12,28},{14,30},{16,0},... | collective-permute-start | bytes 147464 | tf_op jit(solution)/shard_map/ppermute | solution.py:194
  42.2 7.6 %collective-permute-start.15 = (bf16[96,256]{1,0:T(8,128)(2,1)S(1)}, bf16[96,256]{1,0:T(8,128)(2,1)S(1)}, u32[]{:S(2)}, u32[]{:S(2)}) collective-permute-start(bf16[96,256]{1,0:T(8,128)(2,1)S(1)} %fusion.5), channel_id=1, source_target_pairs={{0,16},{2,18},{4,20},{6,22},{8,24},{10,26},{12,28},{14,30},{16,0},... | collective-permute-start | bytes 147464 | tf_op jit(solution)/shard_map/ppermute | solution.py:194
  45.5 5.1 %collective-permute-start.10 = (bf16[96,256]{1,0:T(8,128)(2,1)S(1)}, bf16[96,256]{1,0:T(8,128)(2,1)S(1)}, u32[]{:S(2)}, u32[]{:S(2)}) collective-permute-start(bf16[96,256]{1,0:T(8,128)(2,1)S(1)} %fusion.3), channel_id=1, source_target_pairs={{0,16},{2,18},{4,20},{6,22},{8,24},{10,26},{12,28},{14,30},{16,0},... | collective-permute-start | bytes 147464 | tf_op jit(solution)/shard_map/ppermute | solution.py:194
  49.8 5.1 %collective-permute-start.16 = (bf16[96,256]{1,0:T(8,128)(2,1)S(1)}, bf16[96,256]{1,0:T(8,128)(2,1)S(1)}, u32[]{:S(2)}, u32[]{:S(2)}) collective-permute-start(bf16[96,256]{1,0:T(8,128)(2,1)S(1)} %fusion.2), channel_id=1, source_target_pairs={{0,16},{2,18},{4,20},{6,22},{8,24},{10,26},{12,28},{14,30},{16,0},... | collective-permute-start | bytes 147464 | tf_op jit(solution)/shard_map/ppermute | solution.py:194
  50.5 5.7 %collective-permute-start.11 = (bf16[192,256]{1,0:T(8,128)(2,1)S(1)}, bf16[192,256]{1,0:T(8,128)(2,1)S(1)}, u32[]{:S(2)}, u32[]{:S(2)}) collective-permute-start(bf16[192,256]{1,0:T(8,128)(2,1)S(1)} %pad_maximum_fusion.5), channel_id=1, source_target_pairs={{0,8},{2,10},{4,12},{6,14},{8,0},{10,2},{12,4},{14,6},{16,24},{18,... | collective-permute-start | bytes 294920 | tf_op jit(solution)/shard_map/ppermute | solution.py:194
  54.8 4.7 %collective-permute-start.17 = (bf16[192,256]{1,0:T(8,128)(2,1)S(1)}, bf16[192,256]{1,0:T(8,128)(2,1)S(1)}, u32[]{:S(2)}, u32[]{:S(2)}) collective-permute-start(bf16[192,256]{1,0:T(8,128)(2,1)S(1)} %pad_maximum_fusion.6), channel_id=1, source_target_pairs={{0,4},{2,6},{4,0},{6,2},{8,12},{10,14},{12,8},{14,10},{16,20},{18,... | collective-permute-start | bytes 294920 | tf_op jit(solution)/shard_map/ppermute | solution.py:194
  56.3 5.7 %collective-permute-start.12 = (bf16[384,256]{1,0:T(8,128)(2,1)S(1)}, bf16[384,256]{1,0:T(8,128)(2,1)S(1)}, u32[]{:S(2)}, u32[]{:S(2)}) collective-permute-start(bf16[384,256]{1,0:T(8,128)(2,1)S(1)} %pad_maximum_fusion.3), channel_id=1, source_target_pairs={{0,4},{2,6},{4,0},{6,2},{8,12},{10,14},{12,8},{14,10},{16,20},{18,... | collective-permute-start | bytes 589832 | tf_op jit(solution)/shard_map/ppermute | solution.py:194
  59.5 5.7 %collective-permute-start.18 = (bf16[384,256]{1,0:T(8,128)(2,1)S(1)}, bf16[384,256]{1,0:T(8,128)(2,1)S(1)}, u32[]{:S(2)}, u32[]{:S(2)}) collective-permute-start(bf16[384,256]{1,0:T(8,128)(2,1)S(1)} %pad_maximum_fusion.4), channel_id=1, source_target_pairs={{0,8},{2,10},{4,12},{6,14},{8,0},{10,2},{12,4},{14,6},{16,24},{18,... | collective-permute-start | bytes 589832 | tf_op jit(solution)/shard_map/ppermute | solution.py:194
  65.4 19.5 %collective-permute-start.19 = (bf16[2,8,96,256]{3,2,1,0:T(8,128)(2,1)S(1)}, bf16[2,8,96,256]{3,2,1,0:T(8,128)(2,1)S(1)}, u32[]{:S(2)}, u32[]{:S(2)}) collective-permute-start(bf16[2,8,96,256]{3,2,1,0:T(8,128)(2,1)S(1)} %pad_maximum_fusion.mine_ref), channel_id=1, source_target_pairs={{0,2},{2,0},{4,6},{6,4},{8,10},{10,8},{12,14},{14,12},{16,18},{18,... | collective-permute-start | bytes 2359304 | tf_op jit(solution)/shard_map/ppermute | solution.py:194
  67.7 0.8 copy-start.3
  68.5 9.3 %collective-permute-start.21 = (bf16[256,512]{1,0:T(8,128)(2,1)}, bf16[256,512]{1,0:T(8,128)(2,1)S(1)}, u32[]{:S(2)}, u32[]{:S(2)}) collective-permute-start(bf16[256,512]{1,0:T(8,128)(2,1)} %bitcast.27), channel_id=1, source_target_pairs={{0,1},{1,0},{2,3},{3,2},{4,5},{5,4},{6,7},{7,6},{8,9},{9,8},{10,11... | collective-permute-start | bytes 786440 | tf_op jit(solution)/shard_map/ppermute | solution.py:198
  69.6 13.4 %collective-permute-start.20 = (bf16[256,512]{1,0:T(8,128)(2,1)S(1)}, bf16[256,512]{1,0:T(8,128)(2,1)S(1)}, u32[]{:S(2)}, u32[]{:S(2)}) collective-permute-start(bf16[256,512]{1,0:T(8,128)(2,1)S(1)} %bitcast.44), channel_id=1, source_target_pairs={{0,1},{1,0},{2,3},{3,2},{4,5},{5,4},{6,7},{7,6},{8,9},{9,8},{10,11... | collective-permute-start | bytes 786440 | tf_op jit(solution)/shard_map/ppermute | solution.py:198

commit v4 on v3

v4 whole, which is shorter than its diff:
```python
import math
from functools import partial

import jax
import jax.numpy as jnp
from jax import lax
from jax.experimental import pallas as pl
from jax.experimental.pallas import tpu as pltpu
from jax.sharding import PartitionSpec as P

LOG2E = math.log2(math.e)
MASKED = 1e30
NT = (((1,), (1,)), ((), ()))
NN = (((1,), (0,)), ((), ()))
TN = (((0,), (0,)), ((), ()))
PARAMS = pltpu.CompilerParams(vmem_limit_bytes=24 * 1024 * 1024)
IN_VMEM = pl.BlockSpec(memory_space=pltpu.VMEM)
IN_SMEM = pl.BlockSpec(memory_space=pltpu.SMEM)
IN_HBM = pl.BlockSpec(memory_space=pl.ANY)


def dot(a, b, dims):
    return lax.dot_general(a, b, dims, preferred_element_type=jnp.float32)


def ways(start, size):
    return pl.ds(pl.multiple_of(start, size), size)


def forward_kernel(
    place, compat, q_hbm, g_hbm, k_hbm, v_hbm, lse_ref, targets_ref,
    delta_ref, probs_ref, dprobs_ref, q_ref, g_ref, k_ref, v_ref, sems, *, heads, blocks, scale,
):
    value_count, width = k_ref.shape[0], k_ref.shape[1] // heads
    block = q_ref.shape[0] // blocks
    copies = [
        pltpu.make_async_copy(k_hbm, k_ref, sems.at[0]),
        pltpu.make_async_copy(v_hbm, v_ref, sems.at[1]),
    ]
    for index in range(blocks):
        rows = pl.ds(index * block, block)
        for half, (source, target) in enumerate(((q_hbm, q_ref), (g_hbm, g_ref))):
            copies.append(
                pltpu.make_async_copy(source.at[rows], target.at[rows], sems.at[2 + 2 * index + half])
            )
    for copy in copies:
        copy.start()
    copies[0].wait()
    copies[1].wait()
    for index in range(blocks):
        rows = slice(index * block, (index + 1) * block)
        copies[2 + 2 * index].wait()
        copies[3 + 2 * index].wait()
        for head in range(heads):
            columns = slice(head * width, (head + 1) * width)
            local = targets_ref[head : head + 1, rows] - place[0] * value_count
            hit = (local >= 0) & (local < value_count)
            compatible = compat[head, 0, index] == 1
            live = compatible | (jnp.max(jnp.where(hit, 1.0, 0.0)) > 0.0)

            @pl.when(live)
            def _():
                lse_rows = jnp.where(hit | compatible, lse_ref[head : head + 1, rows], MASKED) * LOG2E
                scores = dot(k_ref[:, columns], q_ref[rows, columns], NT)
                dprobs = dot(v_ref[:, columns], g_ref[rows, columns], NT)
                probs = jnp.exp2(scores * (scale * LOG2E) - lse_rows)
                delta_ref[head : head + 1, rows] = jnp.sum(probs * dprobs, axis=0, keepdims=True)
                probs_ref[head, :, rows] = probs
                dprobs_ref[head, :, rows] = dprobs

            @pl.when(jnp.logical_not(live))
            def _():
                delta_ref[head : head + 1, rows] = jnp.zeros((1, block), jnp.float32)
                probs_ref[head, :, rows] = jnp.zeros((value_count, block), jnp.float32)
                dprobs_ref[head, :, rows] = jnp.zeros((value_count, block), jnp.float32)


def value_kernel(place, probs_ref, g_ref, own_ref, send_ref):
    heads, _, _ = probs_ref.shape
    width = g_ref.shape[1] // heads
    share = own_ref.shape[0]
    parts = send_ref.shape[0] + 1
    for step in range(parts):
        rows = ways(lax.rem(place[1] + step, parts) * share, share)
        for head in range(heads):
            columns = slice(head * width, (head + 1) * width)
            term = dot(probs_ref[head, rows, :].astype(jnp.bfloat16), g_ref[:, columns], NN)
            if step == 0:
                own_ref[:, columns] = term
            else:
                send_ref[step - 1, :, columns] = term.astype(jnp.bfloat16)


def onehot_less(terms, place, targets_ref, head, rows):
    local = targets_ref[pl.ds(head, 1), rows] - place[0] * terms.shape[0]
    slots = lax.broadcasted_iota(jnp.int32, terms.shape, 0)
    return jnp.where(slots == local, terms - 1.0, terms)


def pair_dot(terms, keys):
    high = terms.astype(jnp.bfloat16)
    rest = (terms - high.astype(jnp.float32)).astype(jnp.bfloat16)
    return jnp.transpose(dot(keys, high, TN) + dot(keys, rest, TN))


def query_kernel(place, probs_ref, dprobs_ref, targets_ref, k_ref, out_ref, *, own, chunk):
    head = place[2] if own else 1 - place[2]
    width = out_ref.shape[2]
    keys = k_ref[:, ways(head * width, width)]
    for start in range(0, out_ref.shape[1], chunk):
        rows = slice(start, start + chunk)
        probs = probs_ref[head, :, rows]
        terms = onehot_less(
            probs * (dprobs_ref[head, :, rows] + 1.0), place, targets_ref, head, rows
        )
        out_ref[0, rows, :] = pair_dot(terms, keys)
        out_ref[1, rows, :] = pair_dot(probs, keys)


def delta_kernel(own_ref, received_ref, terms_ref, out_ref, same_terms_ref):
    out_ref[...] = own_ref[...] + received_ref[...]


def combine_kernel(
    place, delta_ref, gone_ref, own_ref, received_ref, keep_ref, sum_ref, *send_refs, scale
):
    chains, rows, width = keep_ref.shape
    sum_ref[...] = delta_ref[...] + gone_ref[...]
    for other in (1, 0):
        for chain in range(chains):
            target = send_refs[chain] if other else keep_ref.at[chain]
            span = ways((2 * chain + (place[3 + chain] ^ other)) * rows, rows)
            delta = sum_ref[pl.ds(place[2], 1), span] * scale
            delta = jnp.transpose(jnp.broadcast_to(delta, (128, rows)))
            for start in range(0, width, 128):
                columns = slice(start, start + 128)
                direct = own_ref[0, span, columns] + received_ref[0, span, columns]
                weighted = own_ref[1, span, columns] + received_ref[1, span, columns]
                total = scale * direct - delta * weighted
                target[:, columns] = total.astype(target.dtype)


def key_kernel(
    place, delta_ref, probs_ref, dprobs_ref, targets_ref, q_ref, values_ref, own_ref, send_ref,
    low_ref, *, chunk, scale,
):
    heads = probs_ref.shape[0]
    width = own_ref.shape[1] // heads
    share = own_ref.shape[0]
    parts = send_ref.shape[0] + 1
    send_ref[:, :, heads * width :] = values_ref[...]
    for head in range(heads):
        columns = slice(head * width, (head + 1) * width)
        for start in range(0, q_ref.shape[0], chunk):
            rows = slice(start, start + chunk)
            gap = dprobs_ref[head, :, rows] - (delta_ref[head : head + 1, rows] - 1.0)
            terms = onehot_less(probs_ref[head, :, rows] * gap, place, targets_ref, head, rows)
            low_ref[head, :, rows] = terms.astype(jnp.bfloat16)
        for step in range(parts):
            rows = ways(lax.rem(place[1] + step, parts) * share, share)
            term = scale * dot(low_ref[head, rows, :], q_ref[:, columns], NN)
            if step == 0:
                own_ref[:, columns] = term
            else:
                send_ref[step - 1, :, columns] = term.astype(jnp.bfloat16)


def place_pieces(place, source, out_ref, sems, side):
    chains = len(source)
    pieces, piece, width = source[0].shape
    columns = ways((place[0] ^ side) * width, width)
    copies = []
    for chain in range(chains):
        for index in range(pieces):
            rows = ways((chain * pieces + (index ^ place[1 + chain])) * piece, piece)
            copies.append(
                pltpu.make_async_copy(
                    source[chain].at[index], out_ref.at[rows, columns], sems.at[len(copies)]
                )
            )
            copies[-1].start()
    return copies


def split_kernel(place, keep_ref, *rest):
    chains = keep_ref.shape[0]
    came_refs, kept_ref, sent_refs = rest[:chains], rest[chains + 1], rest[chains + 2 :]
    rows = kept_ref.shape[1]
    for chain in range(chains):
        for other in (1, 0):
            target = sent_refs[chain] if other else kept_ref.at[chain]
            span = ways((place[3 + chains + chain] ^ other) * rows, rows)
            total = keep_ref[chain, span, :] + came_refs[chain][span, :].astype(jnp.float32)
            target[...] = total.astype(target.dtype)


def middle_kernel(
    total_ref, came_ref, key_ref, value_ref, received_ref, key_out, value_out, *out_refs
):
    rows = total_ref.shape[1]
    for chain, out_ref in enumerate(out_refs):
        out_ref[:rows] = total_ref[chain]
        out_ref[rows:] = came_ref[chain]
    wide = key_ref.shape[1]
    key_sum, value_sum = key_ref[...], value_ref[...]
    for step in range(received_ref.shape[0]):
        key_sum += received_ref[step, :, :wide].astype(jnp.float32)
        value_sum += received_ref[step, :, wide:].astype(jnp.float32)
    key_out[...] = key_sum.astype(jnp.bfloat16)
    value_out[...] = value_sum.astype(jnp.bfloat16)


def own_columns_kernel(place, *rest):
    *mine, out_ref, sems = rest
    for copy in place_pieces(place, mine, out_ref, sems, 0):
        copy.wait()


def other_columns_kernel(place, begun_ref, *rest):
    *theirs, out_ref, sems = rest
    for copy in place_pieces(place, theirs, out_ref, sems, 1):
        copy.wait()


def call(kernel, name, inputs, in_specs, outputs, flops, scratch=(), out_specs=None, aliases={}):
    return pl.pallas_call(
        kernel,
        in_specs=in_specs,
        out_specs=[IN_VMEM] * len(outputs) if out_specs is None else out_specs,
        out_shape=outputs,
        scratch_shapes=list(scratch),
        input_output_aliases=aliases,
        cost_estimate=pl.CostEstimate(flops=flops, bytes_accessed=flops // 1000, transcendentals=0),
        compiler_params=PARAMS,
        name=name,
    )(*inputs)


def on_device(queries, pool_keys, pool_values, out_grad, lse, compat, targets):
    heads, value_blocks, blocks = compat.shape
    query_count, wide = queries.shape
    value_count = pool_keys.shape[0]
    width = wide // heads
    scale = width ** -0.5
    value_devices, parts = lax.axis_size("val"), lax.axis_size("qry")
    bits = value_devices.bit_length() - 1
    assert heads == 2 and value_blocks == 1 and value_devices == 1 << bits and bits >= 4
    val, qry = lax.axis_index("val"), lax.axis_index("qry")
    core = lax.rem(val, 2)
    share = value_count // parts
    f32, bf16 = jnp.float32, jnp.bfloat16

    def flip(array, mask):
        return lax.ppermute(array, "val", [(i, i ^ mask) for i in range(value_devices)])

    def swap_shares(send):
        return jnp.stack([
            lax.ppermute(send[step - 1], "qry", [(i, (i + step) % parts) for i in range(parts)])
            for step in range(1, parts)
        ])

    def add(own, received):
        for array in received:
            own = own + array.astype(f32)
        return own

    def bit_of(bit):
        return lax.rem(val // (1 << bit), 2)

    chains = 2 if query_count % (2 * value_devices // 2 * 16) == 0 else 1
    orders = [[1, 2], [2, 1]][:chains]
    orders = [order + list(range(3, bits)) for order in orders]
    place = jnp.stack([val, qry, core] + [bit_of(order[stage]) for stage in range(2) for order in orders]).astype(jnp.int32)
    work = 2 * query_count * value_count * width

    delta, probs, dprobs, q_near, g_near, k_near = call(
        partial(forward_kernel, heads=heads, blocks=blocks, scale=scale),
        "forward_pass",
        (place,)
        + tuple(
            pltpu.with_memory_space_constraint(array, pltpu.HBM)
            for array in (
                compat, queries, out_grad, pool_keys, pool_values, lse, jnp.transpose(targets)
            )
        ),
        [IN_SMEM, IN_SMEM] + [IN_HBM] * 4 + [IN_VMEM] * 2,
        [
            pltpu.VMEM((heads, query_count), f32),
            pltpu.VMEM((heads, value_count, query_count), f32),
            pltpu.VMEM((heads, value_count, query_count), f32),
            pltpu.VMEM(queries.shape, bf16),
            pltpu.VMEM(queries.shape, bf16),
            pltpu.VMEM(pool_keys.shape, bf16),
        ],
        4 * work,
        [
            pltpu.VMEM(pool_values.shape, bf16),
            pltpu.SemaphoreType.DMA((2 + 2 * blocks,)),
        ],
    )
    shares = [
        pltpu.VMEM((share, wide), f32),
        pltpu.VMEM((parts - 1, share, wide), bf16),
    ]
    value_own, value_send = call(
        value_kernel, "value_terms", (place, probs, g_near), [IN_SMEM] + [IN_VMEM] * 2, shares, 2 * work
    )
    chunk = query_count // 3 if query_count % 384 == 0 else query_count
    rows_of = pltpu.VMEM((2, query_count, width), f32)
    targets = jnp.transpose(targets)

    def query_terms(own, name):
        return call(
            partial(query_kernel, own=own, chunk=chunk),
            name,
            (place, probs, dprobs, targets, k_near),
            [IN_SMEM] + [IN_VMEM] * 4,
            [rows_of],
            4 * work,
        )[0]

    other = query_terms(False, "other_head")
    mine = query_terms(True, "own_head")
    received = None
    for bit in range(bits):
        came = flip(delta, 1 << bit)
        if bit < bits - 1:
            carried = {0: other, bits - 2: mine}.get(bit)
            if carried is None:
                delta = delta + came
                continue
            delta, carried = call(
                delta_kernel,
                "delta_sum",
                (delta, came, carried),
                [IN_VMEM] * 2 + [IN_HBM],
                [pltpu.VMEM((heads, query_count), f32), rows_of],
                heads * query_count,
                out_specs=[IN_VMEM, IN_HBM],
                aliases={2: 1},
            )
            if bit == 0:
                received = flip(carried, 1)
            else:
                mine = carried
    half = query_count // (2 * chains)
    keep, delta, *send = call(
        partial(combine_kernel, scale=scale),
        "combine",
        (place, delta, came, mine, received),
        [IN_SMEM] + [IN_VMEM] * 4,
        [
            pltpu.VMEM((chains, half, width), f32),
            pltpu.VMEM((heads, query_count), f32),
        ]
        + [pltpu.VMEM((half, width), bf16)] * chains,
        work // 4,
    )
    key_own, pool_send = call(
        partial(key_kernel, chunk=chunk, scale=scale),
        "key_terms",
        (place, delta, probs, dprobs, targets, q_near, value_send),
        [IN_SMEM] + [IN_VMEM] * 6,
        [shares[0], pltpu.VMEM((parts - 1, share, 2 * wide), bf16)],
        2 * work,
        [pltpu.VMEM((heads, value_count, query_count), bf16)],
    )
    pool_received = swap_shares(pool_send)

    came = [flip(send[chain], 1 << order[0]) for chain, order in enumerate(orders)]
    kept, *sent = call(
        split_kernel,
        "split",
        (place, keep, *came, pool_send),
        [IN_SMEM] + [IN_VMEM] * (1 + chains) + [IN_HBM],
        [pltpu.VMEM((chains, half // 2, width), f32)]
        + [pltpu.VMEM((half // 2, width), bf16)] * chains,
        work // 8,
    )
    total = jnp.stack(
        [
            kept[chain] + flip(sent[chain], 1 << order[1]).astype(f32)
            for chain, order in enumerate(orders)
        ]
    )
    for bit in range(3, bits):
        split = total.reshape(chains, 2, -1, width)
        pick = partial(lax.dynamic_index_in_dim, split, axis=1, keepdims=False)
        came = flip(pick(1 - bit_of(bit)).astype(bf16), 1 << bit)
        total = pick(bit_of(bit)) + came.astype(f32)
    total = total.astype(bf16)
    for bit in range(bits - 1, 3, -1):
        total = jnp.concatenate([total, flip(total, 1 << bit)], axis=1)
    key_grad, value_grad, *parts_of = call(
        middle_kernel,
        "middle",
        (total, flip(total, 8), key_own, value_own, pool_received),
        [IN_VMEM] * 5,
        [
            jax.ShapeDtypeStruct((share, wide), bf16),
            jax.ShapeDtypeStruct((share, wide), bf16),
        ]
        + [pltpu.VMEM((half // 2, width), bf16)] * chains,
        work // 8,
    )
    gathered = []
    own_piece = []
    for chain, order in enumerate(orders):
        part = parts_of[chain]
        for bit in order[1::-1]:
            part = jnp.concatenate([part, flip(part, 1 << bit)], axis=0)
        gathered.append(part)
        index = 0
        for bit in order:
            index = 2 * index + bit_of(bit)
        own_piece.append(index)
    pieces = value_devices // 2
    near = partial(pltpu.with_memory_space_constraint, memory_space=pltpu.VMEM)
    gathered = [near(part.reshape(pieces, -1, width)) for part in gathered]
    theirs = [near(flip(part, 1)) for part in gathered]
    order_place = jnp.stack([core] + own_piece).astype(jnp.int32)
    query_shape = jax.ShapeDtypeStruct((query_count, wide), bf16)
    sems = [pltpu.SemaphoreType.DMA((chains * pieces,))]
    (begun,) = call(
        own_columns_kernel,
        "own_columns",
        (order_place, *gathered),
        [IN_SMEM] + [IN_VMEM] * chains,
        [query_shape],
        work // 4,
        sems,
        [IN_HBM],
    )
    (query_grad,) = call(
        other_columns_kernel,
        "other_columns",
        (order_place, begun, *theirs),
        [IN_SMEM, IN_HBM] + [IN_VMEM] * chains,
        [query_shape],
        work // 4,
        sems,
        [IN_HBM],
        {1: 0},
    )
    return query_grad, key_grad, value_grad


def solution(mesh):
    placed = (
        P("qry", None),
        P("val", None),
        P("val", None),
        P("qry", None),
        P(None, "qry"),
        P(None, "val", "qry"),
        P("qry", None),
    )
    return jax.shard_map(
        on_device,
        mesh=mesh,
        in_specs=placed,
        out_specs=(P("qry", None), P(("val", "qry"), None), P(("val", "qry"), None)),
        check_vma=False,
    )
```

time: 87.7 us -> 69.6 us (0.79)
  waiting for transfers between devices: 46 us -> 28.5 us
  Pallas kernels: 16.1 us -> 22.6 us
  other arithmetic: 4.03 us -> 0.24 us
  starting transfers between devices: 18.8 us -> 16.6 us
  local copies, waits for them, and re-layouts: 1 us -> 0.09 us
    ppermute x2 -> x1, waiting for transfers between devices: 10.6 us -> 0.01 us  [swap_shares(): lax.ppermute(send[step - 1], 'qry', [(i, (i + step) % parts) for i in ran...]
    ppermute x20 -> x17, waiting for transfers between devices: 35.4 us -> 28.5 us  [flip(): lax.ppermute(array, 'val', [(i, i ^ mask) for i in range(value_devices)])]
    pallas_call x6 -> x12, Pallas kernels: 16.1 us -> 22.6 us  [call(): pl.pallas_call(kernel, in_specs=in_specs, out_specs=[IN_VMEM] * len(outpu...]
    convert_element_type x4 -> x2, other arithmetic: 3.64 us -> 0.04 us  [the longest x1 0.02 us: on_device(): came = flip(pick(1 - bit_of(bit)).astype(bf16), 1 << bit)]
    ppermute x20 -> x17, starting transfers between devices: 16.7 us -> 15.4 us  [flip(): lax.ppermute(array, 'val', [(i, i ^ mask) for i in range(value_devices)])]
    ppermute x2 -> x1, starting transfers between devices: 2.03 us -> 1.16 us  [swap_shares(): lax.ppermute(send[step - 1], 'qry', [(i, (i + step) % parts) for i in ran...]
  transfers between devices with their start and end apart: 22 -> 18, of which waited for: 19 -> 12; matrix products, arithmetic and copies ran while one was open for 4% -> 0% of each run, Pallas kernels for 5% -> 16%
where the time goes in v4:
time: 69.6 us; the launch traced here: 69.1 us
  waiting for transfers between devices  28.5 us (41%)
  Pallas kernels  22.6 us (32%)
  starting transfers between devices  16.6 us (24%)
  between operations  1 us (1%)
    ppermute x17, waiting for transfers between devices, flip(): lax.ppermute(array, 'val', [(i, i ^ mask) for i in range(value_devices)])  28.5 us
    pallas_call x12, Pallas kernels, call(): pl.pallas_call(kernel, in_specs=in_specs, out_specs=[IN_VMEM] * len(outpu...  22.6 us
    ppermute x17, starting transfers between devices, flip(): lax.ppermute(array, 'val', [(i, i ^ mask) for i in range(value_devices)])  15.4 us
  transfers between devices with their start and end apart: 18, of which 12 were waited for; matrix products, arithmetic and copies ran while one was open for 0% of the time, Pallas kernels for 16%

profile of v4, /device:TPU:0, one launch (start us, length us, event | category | flops | bytes accessed | tf_op | source)
XLA Modules:
  0.0 69.1 jit_solution(13952408892369927085)
XLA Ops:
  0.6 0.0 copy-start
  0.7 0.1 stack.50.place
  0.8 7.2 %forward_pass.1 = (f32[2,1536]{1,0:T(2,128)S(1)}, f32[2,512,1536]{2,1,0:T(8,128)S(1)}, f32[2,512,1536]{2,1,0:T(8,128)S(1)}, bf16[1536,512]{1,0:T(8,128)(2,1)S(1)...) custom-call(s32[7]{0:T(128)S(1)} %stack.50.place, s32[2,1,6]{2,1,0:T(1,128)} %compat.1, ...), custom_call_target="tpu_custom_call" | custom-call | flops 1610612736 | bytes 1610612 | tf_op jit(solution)/shard_map/forward_pass/pallas_call | solution.py:226
  8.0 0.1 collective-permute-start
  8.1 0.0 copy-done
  8.1 3.0 %other_head.1.terms_ref = f32[2,1536,256]{2,1,0:T(8,128)S(1)} custom-call(s32[7]{0:T(128)S(1)} %stack.50.place, f32[2,512,1536]{2,1,0:T(8,128)S(1)} %get-tuple-element.29.probs_ref, f32[2,512,1536]{2,1,0:T(8,128)S(1)} %get-tuple-element.30.dprobs_ref, s32[2,1536]{1,0:T(2,128)S(1)} %bitcast.33, bf16[512,512]{1,0:T(8,128)(2,1)S(1)} %get-tuple-element.31.k_ref), custom_call_target="tpu_custom_call" | custom-call | flops 1610612736 | bytes 1610612 | tf_op jit(solution)/shard_map/other_head/pallas_call | solution.py:226
  11.1 0.0 collective-permute-done.received_ref
  11.1 0.6 collective-permute-start.4
  11.7 1.6 %collective-permute-start.1 = (f32[2,1536]{1,0:T(2,128)S(1)}, f32[2,1536]{1,0:T(2,128)S(1)}, u32[]{:S(2)}, u32[]{:S(2)}) collective-permute-start(f32[2,1536]{1,0:T(2,128)S(1)} %get-tuple-element.32), channel_id=1, source_target_pairs={{0,4},{2,6},{4,0},{6,2},{8,12},{10,14},{12,8},{14,10},{16,20},{18,... | collective-permute-start | bytes 36872 | tf_op jit(solution)/shard_map/ppermute | solution.py:254
  13.3 2.1 %collective-permute-done.1 = f32[2,1536]{1,0:T(2,128)S(1)} collective-permute-done((f32[2,1536]{1,0:T(2,128)S(1)}, f32[2,1536]{1,0:T(2,128)S(1)}, u32[]{:S(2)}, u32[]{:S(2)}) %collective-permute-start.1) | collective-permute-done | bytes 12320 | tf_op jit(solution)/shard_map/ppermute | solution.py:254
  15.4 2.5 %collective-permute-start.2 = (f32[2,1536]{1,0:T(2,128)S(1)}, f32[2,1536]{1,0:T(2,128)S(1)}, u32[]{:S(2)}, u32[]{:S(2)}) collective-permute-start(f32[2,1536]{1,0:T(2,128)S(1)} %add.39.own_ref), channel_id=1, source_target_pairs={{0,8},{2,10},{4,12},{6,14},{8,0},{10,2},{12,4},{14,6},{16,24},{18,... | collective-permute-start | bytes 36872 | tf_op jit(solution)/shard_map/ppermute | solution.py:254
  17.9 3.0 %own_head.1.terms_ref = f32[2,1536,256]{2,1,0:T(8,128)S(1)} custom-call(s32[7]{0:T(128)S(1)} %stack.50.place, f32[2,512,1536]{2,1,0:T(8,128)S(1)} %get-tuple-element.29.probs_ref, f32[2,512,1536]{2,1,0:T(8,128)S(1)} %get-tuple-element.30.dprobs_ref, s32[2,1536]{1,0:T(2,128)S(1)} %bitcast.34, bf16[512,512]{1,0:T(8,128)(2,1)S(1)} %get-tuple-element.31.k_ref), custom_call_target="tpu_custom_call" | custom-call | flops 1610612736 | bytes 1610612 | tf_op jit(solution)/shard_map/own_head/pallas_call | solution.py:226
  20.8 0.0 collective-permute-done.2.received_ref
  20.9 1.3 %collective-permute-start.3 = (f32[2,1536]{1,0:T(2,128)S(1)}, f32[2,1536]{1,0:T(2,128)S(1)}, u32[]{:S(2)}, u32[]{:S(2)}) collective-permute-start(f32[2,1536]{1,0:T(2,128)S(1)} %get-tuple-element.33.delta_ref), channel_id=1, source_target_pairs={{0,16},{2,18},{4,20},{6,22},{8,24},{10,26},{12,28},{14,30},{16,0},... | collective-permute-start | bytes 36872 | tf_op jit(solution)/shard_map/ppermute | solution.py:254
  22.2 3.4 %collective-permute-done.3.gone_ref = f32[2,1536]{1,0:T(2,128)S(1)} collective-permute-done((f32[2,1536]{1,0:T(2,128)S(1)}, f32[2,1536]{1,0:T(2,128)S(1)}, u32[]{:S(2)}, u32[]{:S(2)}) %collective-permute-start.3) | collective-permute-done | bytes 12320 | tf_op jit(solution)/shard_map/ppermute | solution.py:254
  25.5 0.0 collective-permute-done.4.received_ref
  25.5 1.1 %combine.1 = (f32[2,384,256]{2,1,0:T(8,128)S(1)}, f32[2,1536]{1,0:T(2,128)S(1)}, bf16[384,256]{1,0:T(8,128)(2,1)S(1)}, bf16[384,256]{1,0:T(8,128)(2,1)S(1)}) custom-call(s32[7]{0:T(128)S(1)} %stack.50.place, f32[2,1536]{1,0:T(2,128)S(1)} %get-tuple-element.33.delta_ref, f32[2,1536]{1,0:T(2,128)S(1)} %collective-permute-done.3.gone_ref, ...), custom_call_target="tpu_custom_call" | custom-call | flops 100663296 | bytes 100663 | tf_op jit(solution)/shard_map/combine/pallas_call | solution.py:226
  26.6 0.3 collective-permute-start.5
  26.9 1.0 %collective-permute-start.6 = (bf16[384,256]{1,0:T(8,128)(2,1)S(1)}, bf16[384,256]{1,0:T(8,128)(2,1)S(1)}, u32[]{:S(2)}, u32[]{:S(2)}) collective-permute-start(bf16[384,256]{1,0:T(8,128)(2,1)S(1)} %get-tuple-element.38), channel_id=1, source_target_pairs={{0,8},{2,10},{4,12},{6,14},{8,0},{10,2},{12,4},{14,6},{16,24},{18,... | collective-permute-start | bytes 589832 | tf_op jit(solution)/shard_map/ppermute | solution.py:254
  27.9 1.5 %value_terms.1 = (f32[256,512]{1,0:T(8,128)S(1)}, bf16[1,256,512]{2,1,0:T(8,128)(2,1)S(1)}) custom-call(s32[7]{0:T(128)S(1)} %stack.50.place, f32[2,512,1536]{2,1,0:T(8,128)S(1)} %get-tuple-element.29.probs_ref, bf16[1536,512]{1,0:T(8,128)(2,1)S(1)} %get-tuple-element.41.g_ref), custom_call_target="tpu_custom_call" | custom-call | flops 805306368 | bytes 805306 | tf_op jit(solution)/shard_map/value_terms/pallas_call | solution.py:226
  29.4 2.3 %key_terms.1 = (f32[256,512]{1,0:T(8,128)S(1)}, bf16[1,256,1024]{2,1,0:T(8,128)(2,1)S(1)}) custom-call(s32[7]{0:T(128)S(1)} %stack.50.place, f32[2,1536]{1,0:T(2,128)S(1)} %get-tuple-element.39.delta_ref, f32[2,512,1536]{2,1,0:T(8,128)S(1)} %get-tuple-element.29.probs_ref, f32[2,512,1536]{2,1,0:T(8,128)S(1)} %get-tuple-element.30.dprobs_ref, ...), custom_call_target="tpu_custom_call" | custom-call | flops 805306368 | bytes 805306 | tf_op jit(solution)/shard_map/key_terms/pallas_call | solution.py:226
  31.7 0.7 collective-permute-done.5.rest_0_
  32.3 0.3 collective-permute-done.6.rest_1_
  32.6 0.6 split.1
  33.2 1.1 %collective-permute-start.7 = (bf16[192,256]{1,0:T(8,128)(2,1)S(1)}, bf16[192,256]{1,0:T(8,128)(2,1)S(1)}, u32[]{:S(2)}, u32[]{:S(2)}) collective-permute-start(bf16[192,256]{1,0:T(8,128)(2,1)S(1)} %get-tuple-element.45), channel_id=1, source_target_pairs={{0,8},{2,10},{4,12},{6,14},{8,0},{10,2},{12,4},{14,6},{16,24},{18,... | collective-permute-start | bytes 294920 | tf_op jit(solution)/shard_map/ppermute | solution.py:254
  34.3 1.4 %collective-permute-start.8 = (bf16[192,256]{1,0:T(8,128)(2,1)S(1)}, bf16[192,256]{1,0:T(8,128)(2,1)S(1)}, u32[]{:S(2)}, u32[]{:S(2)}) collective-permute-start(bf16[192,256]{1,0:T(8,128)(2,1)S(1)} %get-tuple-element.46), channel_id=1, source_target_pairs={{0,4},{2,6},{4,0},{6,2},{8,12},{10,14},{12,8},{14,10},{16,20},{18,... | collective-permute-start | bytes 294920 | tf_op jit(solution)/shard_map/ppermute | solution.py:254
  35.7 1.2 %collective-permute-start.11 = (bf16[256,1024]{1,0:T(8,128)(2,1)S(1)}, bf16[256,1024]{1,0:T(8,128)(2,1)S(1)}, u32[]{:S(2)}, u32[]{:S(2)}) collective-permute-start(bf16[256,1024]{1,0:T(8,128)(2,1)S(1)} %bitcast.31), channel_id=1, source_target_pairs={{0,1},{1,0},{2,3},{3,2},{4,5},{5,4},{6,7},{7,6},{8,9},{9,8},{10,11... | collective-permute-start | bytes 1572872 | tf_op jit(solution)/shard_map/ppermute | solution.py:258
  36.9 1.8 %collective-permute-done.7 = bf16[192,256]{1,0:T(8,128)(2,1)S(1)} collective-permute-done((bf16[192,256]{1,0:T(8,128)(2,1)S(1)}, bf16[192,256]{1,0:T(8,128)(2,1)S(1)}, u32[]{:S(2)}, u32[]{:S(2)}) %collective-permute-start.7) | collective-permute-done | bytes 98336 | tf_op jit(solution)/shard_map/ppermute | solution.py:254
  38.7 0.2 collective-permute-done.8
  39.0 2.9 %collective-permute-start.9 = (bf16[2,96,256]{2,1,0:T(8,128)(2,1)S(1)}, bf16[2,96,256]{2,1,0:T(8,128)(2,1)S(1)}, u32[]{:S(2)}, u32[]{:S(2)}) collective-permute-start(bf16[2,96,256]{2,1,0:T(8,128)(2,1)S(1)} %fusion.6), channel_id=1, source_target_pairs={{0,16},{2,18},{4,20},{6,22},{8,24},{10,26},{12,28},{14,30},{16,0},... | collective-permute-start | bytes 294920 | tf_op jit(solution)/shard_map/ppermute | solution.py:254
  41.9 5.5 %collective-permute-done.9 = bf16[2,96,256]{2,1,0:T(8,128)(2,1)S(1)} collective-permute-done((bf16[2,96,256]{2,1,0:T(8,128)(2,1)S(1)}, bf16[2,96,256]{2,1,0:T(8,128)(2,1)S(1)}, u32[]{:S(2)}, u32[]{:S(2)}) %collective-permute-start.9) | collective-permute-done | bytes 98336 | tf_op jit(solution)/shard_map/ppermute | solution.py:254
  47.4 0.2 collective-permute-start.10
  47.6 6.2 %collective-permute-done.10.came_ref = bf16[2,96,256]{2,1,0:T(8,128)(2,1)S(1)} collective-permute-done((bf16[2,96,256]{2,1,0:T(8,128)(2,1)S(1)}, bf16[2,96,256]{2,1,0:T(8,128)(2,1)S(1)}, u32[]{:S(2)}, u32[]{:S(2)}) %collective-permute-start.10) | collective-permute-done | bytes 98336 | tf_op jit(solution)/shard_map/ppermute | solution.py:254
  53.7 0.0 collective-permute-done.11
  53.7 0.9 %middle.1 = (bf16[256,512]{1,0:T(8,128)(2,1)}, bf16[256,512]{1,0:T(8,128)(2,1)}, bf16[192,256]{1,0:T(8,128)(2,1)S(1)}, bf16[192,256]{1,0:T(8,128)(2,1)S(1)}) custom-call(bf16[2,96,256]{2,1,0:T(8,128)(2,1)S(1)} %fusion.5.total_ref, bf16[2,96,256]{2,1,0:T(8,128)(2,1)S(1)} %collective-permute-done.10.came_ref, f32[256,512]{1,0:T(8,128)S(1)} %get-tuple-element.47.key_ref, ...), custom_call_target="tpu_custom_call" | custom-call | flops 50331648 | bytes 50331 | tf_op jit(solution)/shard_map/middle/pallas_call | solution.py:226
  54.6 0.5 collective-permute-start.14
  55.1 0.0 collective-permute-start.12
  55.2 4.1 %collective-permute-done.14 = bf16[192,256]{1,0:T(8,128)(2,1)S(1)} collective-permute-done((bf16[192,256]{1,0:T(8,128)(2,1)S(1)}, bf16[192,256]{1,0:T(8,128)(2,1)S(1)}, u32[]{:S(2)}, u32[]{:S(2)}) %collective-permute-start.14) | collective-permute-done | bytes 98336 | tf_op jit(solution)/shard_map/ppermute | solution.py:254
  59.2 0.3 collective-permute-start.15
  59.5 0.3 collective-permute-done.12
  59.8 1.6 %collective-permute-start.13 = (bf16[384,256]{1,0:T(8,128)(2,1)S(1)}, bf16[384,256]{1,0:T(8,128)(2,1)S(1)}, u32[]{:S(2)}, u32[]{:S(2)}) collective-permute-start(bf16[384,256]{1,0:T(8,128)(2,1)S(1)} %pad_maximum_fusion.2), channel_id=1, source_target_pairs={{0,4},{2,6},{4,0},{6,2},{8,12},{10,14},{12,8},{14,10},{16,20},{18,... | collective-permute-start | bytes 589832 | tf_op jit(solution)/shard_map/ppermute | solution.py:254
  61.3 3.6 %collective-permute-done.15 = bf16[384,256]{1,0:T(8,128)(2,1)S(1)} collective-permute-done((bf16[384,256]{1,0:T(8,128)(2,1)S(1)}, bf16[384,256]{1,0:T(8,128)(2,1)S(1)}, u32[]{:S(2)}, u32[]{:S(2)}) %collective-permute-start.15) | collective-permute-done | bytes 196640 | tf_op jit(solution)/shard_map/ppermute | solution.py:254
  65.0 0.1 collective-permute-start.17
  65.1 0.4 collective-permute-done.13
  65.5 0.1 collective-permute-start.16
  65.7 0.1 pad_add_fusion.place
  65.8 1.5 %own_columns.1.begun_ref = bf16[1536,512]{1,0:T(8,128)(2,1)} custom-call(s32[3]{0:T(128)S(1)} %pad_add_fusion.place, bf16[8,96,256]{2,1,0:T(8,128)(2,1)S(1)} %bitcast.29, bf16[8,96,256]{2,1,0:T(8,128)(2,1)S(1)} %bitcast.27), custom_call_target="tpu_custom_call" | custom-call | flops 100663296 | bytes 100663 | tf_op jit(solution)/shard_map/own_columns/pallas_call | solution.py:226
  67.3 0.0 collective-permute-done.17.rest_1_
  67.3 0.0 collective-permute-done.16.rest_0_
  67.4 1.5 %other_columns.1 = bf16[1536,512]{1,0:T(8,128)(2,1)} custom-call(s32[3]{0:T(128)S(1)} %pad_add_fusion.place, bf16[1536,512]{1,0:T(8,128)(2,1)} %own_columns.1.begun_ref, bf16[8,96,256]{2,1,0:T(8,128)(2,1)S(1)} %collective-permute-done.16.rest_0_, bf16[8,96,256]{2,1,0:T(8,128)(2,1)S(1)} %collective-permute-done.17.rest_1_), custom_call_target="tpu_custom_call", output_to_operand_aliasing={{}: (1, {})} | custom-call | flops 100663296 | bytes 100663 | tf_op jit(solution)/shard_map/other_columns/pallas_call | solution.py:226
  (10 shorter events, 0.2 us)
Async XLA Ops:
  0.6 7.4 %copy-start = (s32[1536,2]{0,1:T(2,128)S(1)}, s32[1536,2]{0,1:T(2,128)}, u32[]{:S(2)}) copy-start(s32[1536,2]{0,1:T(2,128)} %param.13) | copy-start | bytes 36868
  8.0 3.1 %collective-permute-start = (f32[2,1536]{1,0:T(2,128)S(1)}, f32[2,1536]{1,0:T(2,128)S(1)}, u32[]{:S(2)}, u32[]{:S(2)}) collective-permute-start(f32[2,1536]{1,0:T(2,128)S(1)} %get-tuple-element.28.own_ref), channel_id=1, source_target_pairs={{0,2},{2,0},{4,6},{6,4},{8,10},{10,8},{12,14},{14,12},{16,18},{18,... | collective-permute-start | bytes 36872 | tf_op jit(solution)/shard_map/ppermute | solution.py:254
  11.1 14.5 %collective-permute-start.4 = (f32[2,1536,256]{2,1,0:T(8,128)S(1)}, f32[2,1536,256]{2,1,0:T(8,128)S(1)}, u32[]{:S(2)}, u32[]{:S(2)}) collective-permute-start(f32[2,1536,256]{2,1,0:T(8,128)S(1)} %get-tuple-element.35), channel_id=1, source_target_pairs={{0,2},{2,0},{4,6},{6,4},{8,10},{10,8},{12,14},{14,12},{16,18},{18,... | collective-permute-start | bytes 9437192 | tf_op jit(solution)/shard_map/ppermute | solution.py:254
  11.7 3.7 %collective-permute-start.1 = (f32[2,1536]{1,0:T(2,128)S(1)}, f32[2,1536]{1,0:T(2,128)S(1)}, u32[]{:S(2)}, u32[]{:S(2)}) collective-permute-start(f32[2,1536]{1,0:T(2,128)S(1)} %get-tuple-element.32), channel_id=1, source_target_pairs={{0,4},{2,6},{4,0},{6,2},{8,12},{10,14},{12,8},{14,10},{16,20},{18,... | collective-permute-start | bytes 36872 | tf_op jit(solution)/shard_map/ppermute | solution.py:254
  15.4 5.5 %collective-permute-start.2 = (f32[2,1536]{1,0:T(2,128)S(1)}, f32[2,1536]{1,0:T(2,128)S(1)}, u32[]{:S(2)}, u32[]{:S(2)}) collective-permute-start(f32[2,1536]{1,0:T(2,128)S(1)} %add.39.own_ref), channel_id=1, source_target_pairs={{0,8},{2,10},{4,12},{6,14},{8,0},{10,2},{12,4},{14,6},{16,24},{18,... | collective-permute-start | bytes 36872 | tf_op jit(solution)/shard_map/ppermute | solution.py:254
  20.9 4.7 %collective-permute-start.3 = (f32[2,1536]{1,0:T(2,128)S(1)}, f32[2,1536]{1,0:T(2,128)S(1)}, u32[]{:S(2)}, u32[]{:S(2)}) collective-permute-start(f32[2,1536]{1,0:T(2,128)S(1)} %get-tuple-element.33.delta_ref), channel_id=1, source_target_pairs={{0,16},{2,18},{4,20},{6,22},{8,24},{10,26},{12,28},{14,30},{16,0},... | collective-permute-start | bytes 36872 | tf_op jit(solution)/shard_map/ppermute | solution.py:254
  26.6 5.7 %collective-permute-start.5 = (bf16[384,256]{1,0:T(8,128)(2,1)S(1)}, bf16[384,256]{1,0:T(8,128)(2,1)S(1)}, u32[]{:S(2)}, u32[]{:S(2)}) collective-permute-start(bf16[384,256]{1,0:T(8,128)(2,1)S(1)} %get-tuple-element.37), channel_id=1, source_target_pairs={{0,4},{2,6},{4,0},{6,2},{8,12},{10,14},{12,8},{14,10},{16,20},{18,... | collective-permute-start | bytes 589832 | tf_op jit(solution)/shard_map/ppermute | solution.py:254
  26.9 5.8 %collective-permute-start.6 = (bf16[384,256]{1,0:T(8,128)(2,1)S(1)}, bf16[384,256]{1,0:T(8,128)(2,1)S(1)}, u32[]{:S(2)}, u32[]{:S(2)}) collective-permute-start(bf16[384,256]{1,0:T(8,128)(2,1)S(1)} %get-tuple-element.38), channel_id=1, source_target_pairs={{0,8},{2,10},{4,12},{6,14},{8,0},{10,2},{12,4},{14,6},{16,24},{18,... | collective-permute-start | bytes 589832 | tf_op jit(solution)/shard_map/ppermute | solution.py:254
  33.2 5.4 %collective-permute-start.7 = (bf16[192,256]{1,0:T(8,128)(2,1)S(1)}, bf16[192,256]{1,0:T(8,128)(2,1)S(1)}, u32[]{:S(2)}, u32[]{:S(2)}) collective-permute-start(bf16[192,256]{1,0:T(8,128)(2,1)S(1)} %get-tuple-element.45), channel_id=1, source_target_pairs={{0,8},{2,10},{4,12},{6,14},{8,0},{10,2},{12,4},{14,6},{16,24},{18,... | collective-permute-start | bytes 294920 | tf_op jit(solution)/shard_map/ppermute | solution.py:254
  34.3 4.6 %collective-permute-start.8 = (bf16[192,256]{1,0:T(8,128)(2,1)S(1)}, bf16[192,256]{1,0:T(8,128)(2,1)S(1)}, u32[]{:S(2)}, u32[]{:S(2)}) collective-permute-start(bf16[192,256]{1,0:T(8,128)(2,1)S(1)} %get-tuple-element.46), channel_id=1, source_target_pairs={{0,4},{2,6},{4,0},{6,2},{8,12},{10,14},{12,8},{14,10},{16,20},{18,... | collective-permute-start | bytes 294920 | tf_op jit(solution)/shard_map/ppermute | solution.py:254
  35.7 18.0 %collective-permute-start.11 = (bf16[256,1024]{1,0:T(8,128)(2,1)S(1)}, bf16[256,1024]{1,0:T(8,128)(2,1)S(1)}, u32[]{:S(2)}, u32[]{:S(2)}) collective-permute-start(bf16[256,1024]{1,0:T(8,128)(2,1)S(1)} %bitcast.31), channel_id=1, source_target_pairs={{0,1},{1,0},{2,3},{3,2},{4,5},{5,4},{6,7},{7,6},{8,9},{9,8},{10,11... | collective-permute-start | bytes 1572872 | tf_op jit(solution)/shard_map/ppermute | solution.py:258
  39.0 8.4 %collective-permute-start.9 = (bf16[2,96,256]{2,1,0:T(8,128)(2,1)S(1)}, bf16[2,96,256]{2,1,0:T(8,128)(2,1)S(1)}, u32[]{:S(2)}, u32[]{:S(2)}) collective-permute-start(bf16[2,96,256]{2,1,0:T(8,128)(2,1)S(1)} %fusion.6), channel_id=1, source_target_pairs={{0,16},{2,18},{4,20},{6,22},{8,24},{10,26},{12,28},{14,30},{16,0},... | collective-permute-start | bytes 294920 | tf_op jit(solution)/shard_map/ppermute | solution.py:254
  47.4 6.3 %collective-permute-start.10 = (bf16[2,96,256]{2,1,0:T(8,128)(2,1)S(1)}, bf16[2,96,256]{2,1,0:T(8,128)(2,1)S(1)}, u32[]{:S(2)}, u32[]{:S(2)}) collective-permute-start(bf16[2,96,256]{2,1,0:T(8,128)(2,1)S(1)} %fusion.5.total_ref), channel_id=1, source_target_pairs={{0,16},{2,18},{4,20},{6,22},{8,24},{10,26},{12,28},{14,30},{16,0},... | collective-permute-start | bytes 294920 | tf_op jit(solution)/shard_map/ppermute | solution.py:254
  54.6 4.6 %collective-permute-start.14 = (bf16[192,256]{1,0:T(8,128)(2,1)S(1)}, bf16[192,256]{1,0:T(8,128)(2,1)S(1)}, u32[]{:S(2)}, u32[]{:S(2)}) collective-permute-start(bf16[192,256]{1,0:T(8,128)(2,1)S(1)} %get-tuple-element.50), channel_id=1, source_target_pairs={{0,4},{2,6},{4,0},{6,2},{8,12},{10,14},{12,8},{14,10},{16,20},{18,... | collective-permute-start | bytes 294920 | tf_op jit(solution)/shard_map/ppermute | solution.py:254
  55.1 4.6 %collective-permute-start.12 = (bf16[192,256]{1,0:T(8,128)(2,1)S(1)}, bf16[192,256]{1,0:T(8,128)(2,1)S(1)}, u32[]{:S(2)}, u32[]{:S(2)}) collective-permute-start(bf16[192,256]{1,0:T(8,128)(2,1)S(1)} %get-tuple-element.49), channel_id=1, source_target_pairs={{0,8},{2,10},{4,12},{6,14},{8,0},{10,2},{12,4},{14,6},{16,24},{18,... | collective-permute-start | bytes 294920 | tf_op jit(solution)/shard_map/ppermute | solution.py:254
  59.2 5.7 %collective-permute-start.15 = (bf16[384,256]{1,0:T(8,128)(2,1)S(1)}, bf16[384,256]{1,0:T(8,128)(2,1)S(1)}, u32[]{:S(2)}, u32[]{:S(2)}) collective-permute-start(bf16[384,256]{1,0:T(8,128)(2,1)S(1)} %pad_maximum_fusion.3), channel_id=1, source_target_pairs={{0,8},{2,10},{4,12},{6,14},{8,0},{10,2},{12,4},{14,6},{16,24},{18,... | collective-permute-start | bytes 589832 | tf_op jit(solution)/shard_map/ppermute | solution.py:254
  59.8 5.7 %collective-permute-start.13 = (bf16[384,256]{1,0:T(8,128)(2,1)S(1)}, bf16[384,256]{1,0:T(8,128)(2,1)S(1)}, u32[]{:S(2)}, u32[]{:S(2)}) collective-permute-start(bf16[384,256]{1,0:T(8,128)(2,1)S(1)} %pad_maximum_fusion.2), channel_id=1, source_target_pairs={{0,4},{2,6},{4,0},{6,2},{8,12},{10,14},{12,8},{14,10},{16,20},{18,... | collective-permute-start | bytes 589832 | tf_op jit(solution)/shard_map/ppermute | solution.py:254
  65.0 2.3 %collective-permute-start.17 = (bf16[8,96,256]{2,1,0:T(8,128)(2,1)S(1)}, bf16[8,96,256]{2,1,0:T(8,128)(2,1)S(1)}, u32[]{:S(2)}, u32[]{:S(2)}) collective-permute-start(bf16[8,96,256]{2,1,0:T(8,128)(2,1)S(1)} %bitcast.26), channel_id=1, source_target_pairs={{0,2},{2,0},{4,6},{6,4},{8,10},{10,8},{12,14},{14,12},{16,18},{18,... | collective-permute-start | bytes 1179656 | tf_op jit(solution)/shard_map/ppermute | solution.py:254
  65.5 1.8 %collective-permute-start.16 = (bf16[8,96,256]{2,1,0:T(8,128)(2,1)S(1)}, bf16[8,96,256]{2,1,0:T(8,128)(2,1)S(1)}, u32[]{:S(2)}, u32[]{:S(2)}) collective-permute-start(bf16[8,96,256]{2,1,0:T(8,128)(2,1)S(1)} %bitcast.28), channel_id=1, source_target_pairs={{0,2},{2,0},{4,6},{6,4},{8,10},{10,8},{12,14},{14,12},{16,18},{18,... | collective-permute-start | bytes 1179656 | tf_op jit(solution)/shard_map/ppermute | solution.py:254

commit v5 on v4

--- a/solution.py
+++ b/solution.py
@@ -12,7 +12,6 @@
 MASKED = 1e30
 NT = (((1,), (1,)), ((), ()))
 NN = (((1,), (0,)), ((), ()))
-TN = (((0,), (0,)), ((), ()))
 PARAMS = pltpu.CompilerParams(vmem_limit_bytes=24 * 1024 * 1024)
 IN_VMEM = pl.BlockSpec(memory_space=pltpu.VMEM)
 IN_SMEM = pl.BlockSpec(memory_space=pltpu.SMEM)
@@ -51,16 +50,20 @@
         rows = slice(index * block, (index + 1) * block)
         copies[2 + 2 * index].wait()
         copies[3 + 2 * index].wait()
+        hits = []
+        live = False
         for head in range(heads):
-            columns = slice(head * width, (head + 1) * width)
             local = targets_ref[head : head + 1, rows] - place[0] * value_count
             hit = (local >= 0) & (local < value_count)
             compatible = compat[head, 0, index] == 1
-            live = compatible | (jnp.max(jnp.where(hit, 1.0, 0.0)) > 0.0)
-
-            @pl.when(live)
-            def _():
-                lse_rows = jnp.where(hit | compatible, lse_ref[head : head + 1, rows], MASKED) * LOG2E
+            hits.append(hit | compatible)
+            live = live | compatible | (jnp.max(jnp.where(hit, 1.0, 0.0)) > 0.0)
+
+        @pl.when(live)
+        def _():
+            for head in range(heads):
+                columns = slice(head * width, (head + 1) * width)
+                lse_rows = jnp.where(hits[head], lse_ref[head : head + 1, rows], MASKED) * LOG2E
                 scores = dot(k_ref[:, columns], q_ref[rows, columns], NT)
                 dprobs = dot(v_ref[:, columns], g_ref[rows, columns], NT)
                 probs = jnp.exp2(scores * (scale * LOG2E) - lse_rows)
@@ -68,8 +71,9 @@
                 probs_ref[head, :, rows] = probs
                 dprobs_ref[head, :, rows] = dprobs
 
-            @pl.when(jnp.logical_not(live))
-            def _():
+        @pl.when(jnp.logical_not(live))
+        def _():
+            for head in range(heads):
                 delta_ref[head : head + 1, rows] = jnp.zeros((1, block), jnp.float32)
                 probs_ref[head, :, rows] = jnp.zeros((value_count, block), jnp.float32)
                 dprobs_ref[head, :, rows] = jnp.zeros((value_count, block), jnp.float32)
@@ -100,13 +104,13 @@
 def pair_dot(terms, keys):
     high = terms.astype(jnp.bfloat16)
     rest = (terms - high.astype(jnp.float32)).astype(jnp.bfloat16)
-    return jnp.transpose(dot(keys, high, TN) + dot(keys, rest, TN))
+    return jnp.transpose(dot(keys, high, NN) + dot(keys, rest, NN))
 
 
 def query_kernel(place, probs_ref, dprobs_ref, targets_ref, k_ref, out_ref, *, own, chunk):
     head = place[2] if own else 1 - place[2]
     width = out_ref.shape[2]
-    keys = k_ref[:, ways(head * width, width)]
+    keys = jnp.transpose(k_ref[:, ways(head * width, width)])
     for start in range(0, out_ref.shape[1], chunk):
         rows = slice(start, start + chunk)
         probs = probs_ref[head, :, rows]
@@ -122,22 +126,19 @@
 
 
 def combine_kernel(
-    place, delta_ref, gone_ref, own_ref, received_ref, keep_ref, sum_ref, *send_refs, scale
+    place, delta_ref, gone_ref, own_ref, received_ref, keep_ref, sum_ref, send_ref, *, scale
 ):
-    chains, rows, width = keep_ref.shape
+    rows, width = keep_ref.shape
     sum_ref[...] = delta_ref[...] + gone_ref[...]
-    for other in (1, 0):
-        for chain in range(chains):
-            target = send_refs[chain] if other else keep_ref.at[chain]
-            span = ways((2 * chain + (place[3 + chain] ^ other)) * rows, rows)
-            delta = sum_ref[pl.ds(place[2], 1), span] * scale
-            delta = jnp.transpose(jnp.broadcast_to(delta, (128, rows)))
-            for start in range(0, width, 128):
-                columns = slice(start, start + 128)
-                direct = own_ref[0, span, columns] + received_ref[0, span, columns]
-                weighted = own_ref[1, span, columns] + received_ref[1, span, columns]
-                total = scale * direct - delta * weighted
-                target[:, columns] = total.astype(target.dtype)
+    for target, other in ((send_ref, 1), (keep_ref, 0)):
+        span = ways((place[3] ^ other) * rows, rows)
+        delta = sum_ref[pl.ds(place[2], 1), span] * scale
+        delta = jnp.transpose(jnp.broadcast_to(delta, (128, rows)))
+        for start in range(0, width, 128):
+            columns = slice(start, start + 128)
+            direct = own_ref[0, span, columns] + received_ref[0, span, columns]
+            weighted = own_ref[1, span, columns] + received_ref[1, span, columns]
+            target[:, columns] = (scale * direct - delta * weighted).astype(target.dtype)
 
 
 def key_kernel(
@@ -165,42 +166,19 @@
                 send_ref[step - 1, :, columns] = term.astype(jnp.bfloat16)
 
 
-def place_pieces(place, source, out_ref, sems, side):
-    chains = len(source)
-    pieces, piece, width = source[0].shape
-    columns = ways((place[0] ^ side) * width, width)
-    copies = []
-    for chain in range(chains):
-        for index in range(pieces):
-            rows = ways((chain * pieces + (index ^ place[1 + chain])) * piece, piece)
-            copies.append(
-                pltpu.make_async_copy(
-                    source[chain].at[index], out_ref.at[rows, columns], sems.at[len(copies)]
-                )
-            )
-            copies[-1].start()
-    return copies
-
-
-def split_kernel(place, keep_ref, *rest):
-    chains = keep_ref.shape[0]
-    came_refs, kept_ref, sent_refs = rest[:chains], rest[chains + 1], rest[chains + 2 :]
-    rows = kept_ref.shape[1]
-    for chain in range(chains):
-        for other in (1, 0):
-            target = sent_refs[chain] if other else kept_ref.at[chain]
-            span = ways((place[3 + chains + chain] ^ other) * rows, rows)
-            total = keep_ref[chain, span, :] + came_refs[chain][span, :].astype(jnp.float32)
-            target[...] = total.astype(target.dtype)
+def split_kernel(place, keep_ref, came_ref, after_ref, kept_ref, sent_ref):
+    rows = kept_ref.shape[0]
+    for target, other in ((sent_ref, 1), (kept_ref, 0)):
+        span = ways((place[4] ^ other) * rows, rows)
+        total = keep_ref[span, :] + came_ref[span, :].astype(jnp.float32)
+        target[...] = total.astype(target.dtype)
 
 
 def middle_kernel(
-    total_ref, came_ref, key_ref, value_ref, received_ref, key_out, value_out, *out_refs
+    total_ref, came_ref, key_ref, value_ref, received_ref, key_out, value_out, out_ref
 ):
-    rows = total_ref.shape[1]
-    for chain, out_ref in enumerate(out_refs):
-        out_ref[:rows] = total_ref[chain]
-        out_ref[rows:] = came_ref[chain]
+    total = total_ref[...].astype(jnp.float32) + came_ref[...].astype(jnp.float32)
+    out_ref[...] = total.astype(jnp.bfloat16)
     wide = key_ref.shape[1]
     key_sum, value_sum = key_ref[...], value_ref[...]
     for step in range(received_ref.shape[0]):
@@ -210,15 +188,21 @@
     value_out[...] = value_sum.astype(jnp.bfloat16)
 
 
-def own_columns_kernel(place, *rest):
-    *mine, out_ref, sems = rest
-    for copy in place_pieces(place, mine, out_ref, sems, 0):
-        copy.wait()
-
-
-def other_columns_kernel(place, begun_ref, *rest):
-    *theirs, out_ref, sems = rest
-    for copy in place_pieces(place, theirs, out_ref, sems, 1):
+def place_kernel(place, *rest, sources, piece):
+    out_ref, sems = rest[-2:]
+    copies = []
+    for ref, (side, first) in zip(rest, sources):
+        width = ref.shape[1]
+        columns = ways((place[0] ^ side) * width, width)
+        for index in range(ref.shape[0] // piece):
+            rows = ways(((first + index) ^ place[1 + side]) * piece, piece)
+            copies.append(
+                pltpu.make_async_copy(
+                    ref.at[pl.ds(index * piece, piece)], out_ref.at[rows, columns], sems.at[len(copies)]
+                )
+            )
+            copies[-1].start()
+    for copy in copies:
         copy.wait()
 
 
@@ -250,8 +234,9 @@
     share = value_count // parts
     f32, bf16 = jnp.float32, jnp.bfloat16
 
-    def flip(array, mask):
-        return lax.ppermute(array, "val", [(i, i ^ mask) for i in range(value_devices)])
+    def flip(array, *masks):
+        pairs = [(i, i ^ masks[i % len(masks)]) for i in range(value_devices)]
+        return lax.ppermute(array, "val", pairs)
 
     def swap_shares(send):
         return jnp.stack([
@@ -267,10 +252,17 @@
     def bit_of(bit):
         return lax.rem(val // (1 << bit), 2)
 
-    chains = 2 if query_count % (2 * value_devices // 2 * 16) == 0 else 1
-    orders = [[1, 2], [2, 1]][:chains]
-    orders = [order + list(range(3, bits)) for order in orders]
-    place = jnp.stack([val, qry, core] + [bit_of(order[stage]) for stage in range(2) for order in orders]).astype(jnp.int32)
+    orders = [[1, 2], [2, 1]]
+    orders = [order + list(range(3, bits - 1)) for order in orders]
+    last = 1 << (bits - 1)
+
+    def own_bits(turn):
+        first, second = orders[turn], orders[1 - turn]
+        return [jnp.where(core == 0, bit_of(a), bit_of(b)) for a, b in zip(first, second)]
+
+    stages = [(1 << a, 1 << b) for a, b in zip(*orders)]
+    stage_bits = own_bits(0)
+    place = jnp.stack([val, qry, core] + stage_bits[:2]).astype(jnp.int32)
     work = 2 * query_count * value_count * width
 
     delta, probs, dprobs, q_near, g_near, k_near = call(
@@ -325,7 +317,7 @@
     for bit in range(bits):
         came = flip(delta, 1 << bit)
         if bit < bits - 1:
-            carried = {0: other, bits - 2: mine}.get(bit)
+            carried = {1: other, bits - 2: mine}.get(bit)
             if carried is None:
                 delta = delta + came
                 continue
@@ -339,21 +331,21 @@
                 out_specs=[IN_VMEM, IN_HBM],
                 aliases={2: 1},
             )
-            if bit == 0:
+            if bit == 1:
                 received = flip(carried, 1)
             else:
                 mine = carried
-    half = query_count // (2 * chains)
-    keep, delta, *send = call(
+    half = query_count // 2
+    keep, delta, send = call(
         partial(combine_kernel, scale=scale),
         "combine",
         (place, delta, came, mine, received),
         [IN_SMEM] + [IN_VMEM] * 4,
         [
-            pltpu.VMEM((chains, half, width), f32),
+            pltpu.VMEM((half, width), f32),
             pltpu.VMEM((heads, query_count), f32),
-        ]
-        + [pltpu.VMEM((half, width), bf16)] * chains,
+            pltpu.VMEM((half, width), bf16),
+        ],
         work // 4,
     )
     key_own, pool_send = call(
@@ -367,82 +359,64 @@
     )
     pool_received = swap_shares(pool_send)
 
-    came = [flip(send[chain], 1 << order[0]) for chain, order in enumerate(orders)]
-    kept, *sent = call(
+    kept, sent = call(
         split_kernel,
         "split",
-        (place, keep, *came, pool_send),
-        [IN_SMEM] + [IN_VMEM] * (1 + chains) + [IN_HBM],
-        [pltpu.VMEM((chains, half // 2, width), f32)]
-        + [pltpu.VMEM((half // 2, width), bf16)] * chains,
+        (place, keep, flip(send, *stages[0]), pool_send),
+        [IN_SMEM] + [IN_VMEM] * 2 + [IN_HBM],
+        [pltpu.VMEM((half // 2, width), f32), pltpu.VMEM((half // 2, width), bf16)],
         work // 8,
     )
-    total = jnp.stack(
-        [
-            kept[chain] + flip(sent[chain], 1 << order[1]).astype(f32)
-            for chain, order in enumerate(orders)
-        ]
-    )
-    for bit in range(3, bits):
-        split = total.reshape(chains, 2, -1, width)
-        pick = partial(lax.dynamic_index_in_dim, split, axis=1, keepdims=False)
-        came = flip(pick(1 - bit_of(bit)).astype(bf16), 1 << bit)
-        total = pick(bit_of(bit)) + came.astype(f32)
+    total = kept + flip(sent, *stages[1]).astype(f32)
+    for stage in range(2, bits - 2):
+        split = total.reshape(2, -1, width)
+        pick = partial(lax.dynamic_index_in_dim, split, axis=0, keepdims=False)
+        came = flip(pick(1 - stage_bits[stage]).astype(bf16), *stages[stage])
+        total = pick(stage_bits[stage]) + came.astype(f32)
     total = total.astype(bf16)
-    for bit in range(bits - 1, 3, -1):
-        total = jnp.concatenate([total, flip(total, 1 << bit)], axis=1)
-    key_grad, value_grad, *parts_of = call(
+    piece = total.shape[0]
+    key_grad, value_grad, total = call(
         middle_kernel,
         "middle",
-        (total, flip(total, 8), key_own, value_own, pool_received),
+        (total, flip(total, last), key_own, value_own, pool_received),
         [IN_VMEM] * 5,
         [
             jax.ShapeDtypeStruct((share, wide), bf16),
             jax.ShapeDtypeStruct((share, wide), bf16),
-        ]
-        + [pltpu.VMEM((half // 2, width), bf16)] * chains,
+            pltpu.VMEM((piece, width), bf16),
+        ],
         work // 8,
     )
-    gathered = []
-    own_piece = []
-    for chain, order in enumerate(orders):
-        part = parts_of[chain]
-        for bit in order[1::-1]:
-            part = jnp.concatenate([part, flip(part, 1 << bit)], axis=0)
-        gathered.append(part)
+    for masks in stages[:0:-1]:
+        total = jnp.concatenate([total, flip(total, *masks)], axis=0)
+
+    def index_of(bits_of):
         index = 0
-        for bit in order:
-            index = 2 * index + bit_of(bit)
-        own_piece.append(index)
-    pieces = value_devices // 2
+        for bit in bits_of:
+            index = 2 * index + bit
+        return index
+
+    pieces_place = jnp.stack([core, index_of(own_bits(0)), index_of(own_bits(1))]).astype(jnp.int32)
     near = partial(pltpu.with_memory_space_constraint, memory_space=pltpu.VMEM)
-    gathered = [near(part.reshape(pieces, -1, width)) for part in gathered]
-    theirs = [near(flip(part, 1)) for part in gathered]
-    order_place = jnp.stack([core] + own_piece).astype(jnp.int32)
-    query_shape = jax.ShapeDtypeStruct((query_count, wide), bf16)
-    sems = [pltpu.SemaphoreType.DMA((chains * pieces,))]
-    (begun,) = call(
-        own_columns_kernel,
-        "own_columns",
-        (order_place, *gathered),
-        [IN_SMEM] + [IN_VMEM] * chains,
-        [query_shape],
-        work // 4,
-        sems,
-        [IN_HBM],
-    )
-    (query_grad,) = call(
-        other_columns_kernel,
-        "other_columns",
-        (order_place, begun, *theirs),
-        [IN_SMEM, IN_HBM] + [IN_VMEM] * chains,
-        [query_shape],
-        work // 4,
-        sems,
-        [IN_HBM],
-        {1: 0},
-    )
-    return query_grad, key_grad, value_grad
+    pieces = half // piece
+    rest = flip(total, *stages[0])
+    begun = ()
+    for name, parts_of in (
+        ("own_columns", [(total, 0, 0), (rest, 0, pieces), (flip(total, 1), 1, 0)]),
+        ("other_columns", [(flip(rest, 1), 1, pieces)]),
+    ):
+        begun = call(
+            partial(place_kernel, sources=[source[1:] for source in parts_of], piece=piece),
+            name,
+            (pieces_place, *[near(source[0]) for source in parts_of], *begun),
+            [IN_SMEM] + [IN_VMEM] * len(parts_of) + [IN_HBM] * len(begun),
+            [jax.ShapeDtypeStruct((query_count, wide), bf16)],
+            work // 4,
+            [pltpu.SemaphoreType.DMA((len(parts_of) * pieces,))],
+            [IN_HBM],
+            {1 + len(parts_of): 0} if begun else {},
+        )
+    return begun[0], key_grad, value_grad
 
 
 def solution(mesh):

time: 69.6 us -> 67 us (0.963)
  starting transfers between devices: 16.6 us -> 14 us
  waiting for transfers between devices: 28.5 us -> 30.8 us
  Pallas kernels: 22.6 us -> 20.6 us
    ppermute x1, waiting for transfers between devices: 0.01 us -> 3.72 us  [swap_shares(): lax.ppermute(send[step - 1], 'qry', [(i, (i + step) % parts) for i in ran...]
    ppermute x17 -> x12, starting transfers between devices: 15.4 us -> 12.2 us  [flip(): return lax.ppermute(array, 'val', pairs)]
    pallas_call x12, Pallas kernels: 22.6 us -> 20.6 us  [call(): pl.pallas_call(kernel, in_specs=in_specs, out_specs=[IN_VMEM] * len(outpu...]
    ppermute x17 -> x12, waiting for transfers between devices: 28.5 us -> 27.1 us  [flip(): return lax.ppermute(array, 'val', pairs)]
  transfers between devices with their start and end apart: 18 -> 13, of which waited for: 12 -> 8; matrix products, arithmetic and copies ran while one was open for 0% -> 0% of each run, Pallas kernels for 16% -> 17%
where the time goes in v5:
time: 67 us; the launch traced here: 66.7 us
  waiting for transfers between devices  30.8 us (46%)
  Pallas kernels  20.6 us (31%)
  starting transfers between devices  14 us (21%)
  between operations  0.94 us (1%)
    ppermute x12, waiting for transfers between devices, flip(): return lax.ppermute(array, 'val', pairs)  27.1 us
    pallas_call x12, Pallas kernels, call(): pl.pallas_call(kernel, in_specs=in_specs, out_specs=[IN_VMEM] * len(outpu...  20.6 us
    ppermute x12, starting transfers between devices, flip(): return lax.ppermute(array, 'val', pairs)  12.2 us
    ppermute x1, waiting for transfers between devices, swap_shares(): lax.ppermute(send[step - 1], 'qry', [(i, (i + step) % parts) for i in ran...  3.72 us
    ppermute x1, starting transfers between devices, swap_shares(): lax.ppermute(send[step - 1], 'qry', [(i, (i + step) % parts) for i in ran...  1.84 us
  transfers between devices with their start and end apart: 13, of which 8 were waited for; matrix products, arithmetic and copies ran while one was open for 0% of the time, Pallas kernels for 17%

profile of v5, /device:TPU:0, one launch (start us, length us, event | category | flops | bytes accessed | tf_op | source)
XLA Modules:
  0.0 66.7 jit_solution(12897415181038000172)
XLA Ops:
  0.6 0.0 copy-start
  0.7 0.1 stack.39.place
  0.8 5.4 %forward_pass.1 = (f32[2,1536]{1,0:T(2,128)S(1)}, f32[2,512,1536]{2,1,0:T(8,128)S(1)}, f32[2,512,1536]{2,1,0:T(8,128)S(1)}, bf16[1536,512]{1,0:T(8,128)(2,1)S(1)...) custom-call(s32[5]{0:T(128)S(1)} %stack.39.place, s32[2,1,6]{2,1,0:T(1,128)} %compat.1, ...), custom_call_target="tpu_custom_call" | custom-call | flops 1610612736 | bytes 1610612 | tf_op jit(solution)/shard_map/forward_pass/pallas_call | solution.py:210
  6.2 0.5 collective-permute-start
  6.7 0.8 %collective-permute-done = f32[2,1536]{1,0:T(2,128)S(1)} collective-permute-done((f32[2,1536]{1,0:T(2,128)S(1)}, f32[2,1536]{1,0:T(2,128)S(1)}, u32[]{:S(2)}, u32[]{:S(2)}) %collective-permute-start) | collective-permute-done | bytes 12320 | tf_op jit(solution)/shard_map/ppermute | solution.py:239
  7.5 2.4 %collective-permute-start.1 = (f32[2,1536]{1,0:T(2,128)S(1)}, f32[2,1536]{1,0:T(2,128)S(1)}, u32[]{:S(2)}, u32[]{:S(2)}) collective-permute-start(f32[2,1536]{1,0:T(2,128)S(1)} %add.16.own_ref), channel_id=1, source_target_pairs={{0,4},{2,6},{4,0},{6,2},{8,12},{10,14},{12,8},{14,10},{16,20},{18,... | collective-permute-start | bytes 36872 | tf_op jit(solution)/shard_map/ppermute | solution.py:239
  9.9 0.0 copy-done
  9.9 3.0 %other_head.1.terms_ref = f32[2,1536,256]{2,1,0:T(8,128)S(1)} custom-call(s32[5]{0:T(128)S(1)} %stack.39.place, f32[2,512,1536]{2,1,0:T(8,128)S(1)} %get-tuple-element.26.probs_ref, f32[2,512,1536]{2,1,0:T(8,128)S(1)} %get-tuple-element.27.dprobs_ref, s32[2,1536]{1,0:T(2,128)S(1)} %bitcast.13, bf16[512,512]{1,0:T(8,128)(2,1)S(1)} %get-tuple-element.28.k_ref), custom_call_target="tpu_custom_call" | custom-call | flops 1610612736 | bytes 1610612 | tf_op jit(solution)/shard_map/other_head/pallas_call | solution.py:210
  12.9 0.0 collective-permute-done.1.received_ref
  12.9 0.2 collective-permute-start.4
  13.1 2.1 %collective-permute-start.2 = (f32[2,1536]{1,0:T(2,128)S(1)}, f32[2,1536]{1,0:T(2,128)S(1)}, u32[]{:S(2)}, u32[]{:S(2)}) collective-permute-start(f32[2,1536]{1,0:T(2,128)S(1)} %get-tuple-element.29.own_ref), channel_id=1, source_target_pairs={{0,8},{2,10},{4,12},{6,14},{8,0},{10,2},{12,4},{14,6},{16,24},{18,... | collective-permute-start | bytes 36872 | tf_op jit(solution)/shard_map/ppermute | solution.py:239
  15.2 3.0 %own_head.1.terms_ref = f32[2,1536,256]{2,1,0:T(8,128)S(1)} custom-call(s32[5]{0:T(128)S(1)} %stack.39.place, f32[2,512,1536]{2,1,0:T(8,128)S(1)} %get-tuple-element.26.probs_ref, f32[2,512,1536]{2,1,0:T(8,128)S(1)} %get-tuple-element.27.dprobs_ref, s32[2,1536]{1,0:T(2,128)S(1)} %bitcast.14, bf16[512,512]{1,0:T(8,128)(2,1)S(1)} %get-tuple-element.28.k_ref), custom_call_target="tpu_custom_call" | custom-call | flops 1610612736 | bytes 1610612 | tf_op jit(solution)/shard_map/own_head/pallas_call | solution.py:210
  18.2 0.0 collective-permute-done.2.received_ref
  18.2 2.0 %collective-permute-start.3 = (f32[2,1536]{1,0:T(2,128)S(1)}, f32[2,1536]{1,0:T(2,128)S(1)}, u32[]{:S(2)}, u32[]{:S(2)}) collective-permute-start(f32[2,1536]{1,0:T(2,128)S(1)} %get-tuple-element.30.delta_ref), channel_id=1, source_target_pairs={{0,16},{2,18},{4,20},{6,22},{8,24},{10,26},{12,28},{14,30},{16,0},... | collective-permute-start | bytes 36872 | tf_op jit(solution)/shard_map/ppermute | solution.py:239
  20.2 2.7 %collective-permute-done.3.gone_ref = f32[2,1536]{1,0:T(2,128)S(1)} collective-permute-done((f32[2,1536]{1,0:T(2,128)S(1)}, f32[2,1536]{1,0:T(2,128)S(1)}, u32[]{:S(2)}, u32[]{:S(2)}) %collective-permute-start.3) | collective-permute-done | bytes 12320 | tf_op jit(solution)/shard_map/ppermute | solution.py:239
  22.9 0.0 collective-permute-done.4.received_ref
  22.9 1.1 %combine.1 = (f32[768,256]{1,0:T(8,128)S(1)}, f32[2,1536]{1,0:T(2,128)S(1)}, bf16[768,256]{1,0:T(8,128)(2,1)S(1)}) custom-call(s32[5]{0:T(128)S(1)} %stack.39.place, f32[2,1536]{1,0:T(2,128)S(1)} %get-tuple-element.30.delta_ref, f32[2,1536]{1,0:T(2,128)S(1)} %collective-permute-done.3.gone_ref, f32[2,1536,256]{2,1,0:T(8,128)S(1)} %get-tuple-element.31.own_ref, ...), custom_call_target="tpu_custom_call" | custom-call | flops 100663296 | bytes 100663 | tf_op jit(solution)/shard_map/combine/pallas_call | solution.py:210
  23.9 0.6 collective-permute-start.5
  24.6 1.5 %value_terms.1 = (f32[256,512]{1,0:T(8,128)S(1)}, bf16[1,256,512]{2,1,0:T(8,128)(2,1)S(1)}) custom-call(s32[5]{0:T(128)S(1)} %stack.39.place, f32[2,512,1536]{2,1,0:T(8,128)S(1)} %get-tuple-element.26.probs_ref, bf16[1536,512]{1,0:T(8,128)(2,1)S(1)} %get-tuple-element.37.g_ref), custom_call_target="tpu_custom_call" | custom-call | flops 805306368 | bytes 805306 | tf_op jit(solution)/shard_map/value_terms/pallas_call | solution.py:210
  26.1 2.3 %key_terms.1 = (f32[256,512]{1,0:T(8,128)S(1)}, bf16[1,256,1024]{2,1,0:T(8,128)(2,1)S(1)}) custom-call(s32[5]{0:T(128)S(1)} %stack.39.place, f32[2,1536]{1,0:T(2,128)S(1)} %get-tuple-element.35.delta_ref, f32[2,512,1536]{2,1,0:T(8,128)S(1)} %get-tuple-element.26.probs_ref, f32[2,512,1536]{2,1,0:T(8,128)S(1)} %get-tuple-element.27.dprobs_ref, ...), custom_call_target="tpu_custom_call" | custom-call | flops 805306368 | bytes 805306 | tf_op jit(solution)/shard_map/key_terms/pallas_call | solution.py:210
  28.4 3.4 %collective-permute-done.5.came_ref = bf16[768,256]{1,0:T(8,128)(2,1)S(1)} collective-permute-done((bf16[768,256]{1,0:T(8,128)(2,1)S(1)}, bf16[768,256]{1,0:T(8,128)(2,1)S(1)}, u32[]{:S(2)}, u32[]{:S(2)}) %collective-permute-start.5) | collective-permute-done | bytes 393248 | tf_op jit(solution)/shard_map/ppermute | solution.py:239
  31.8 0.6 split.1
  32.4 0.7 %collective-permute-start.6 = (bf16[384,256]{1,0:T(8,128)(2,1)S(1)}, bf16[384,256]{1,0:T(8,128)(2,1)S(1)}, u32[]{:S(2)}, u32[]{:S(2)}) collective-permute-start(bf16[384,256]{1,0:T(8,128)(2,1)S(1)} %get-tuple-element.41), channel_id=1, source_target_pairs={{0,8},{2,6},{4,12},{6,2},{8,0},{10,14},{12,4},{14,10},{16,24},{18,... | collective-permute-start | bytes 589832 | tf_op jit(solution)/shard_map/ppermute | solution.py:239
  33.1 1.8 %collective-permute-start.8 = (bf16[256,1024]{1,0:T(8,128)(2,1)S(1)}, bf16[256,1024]{1,0:T(8,128)(2,1)S(1)}, u32[]{:S(2)}, u32[]{:S(2)}) collective-permute-start(bf16[256,1024]{1,0:T(8,128)(2,1)S(1)} %bitcast.10), channel_id=1, source_target_pairs={{0,1},{1,0},{2,3},{3,2},{4,5},{5,4},{6,7},{7,6},{8,9},{9,8},{10,11... | collective-permute-start | bytes 1572872 | tf_op jit(solution)/shard_map/ppermute | solution.py:243
  35.0 3.1 %collective-permute-done.6 = bf16[384,256]{1,0:T(8,128)(2,1)S(1)} collective-permute-done((bf16[384,256]{1,0:T(8,128)(2,1)S(1)}, bf16[384,256]{1,0:T(8,128)(2,1)S(1)}, u32[]{:S(2)}, u32[]{:S(2)}) %collective-permute-start.6) | collective-permute-done | bytes 196640 | tf_op jit(solution)/shard_map/ppermute | solution.py:239
  38.1 0.1 add_convert_fusion.total_ref
  38.2 2.9 %collective-permute-start.7 = (bf16[384,256]{1,0:T(8,128)(2,1)S(1)}, bf16[384,256]{1,0:T(8,128)(2,1)S(1)}, u32[]{:S(2)}, u32[]{:S(2)}) collective-permute-start(bf16[384,256]{1,0:T(8,128)(2,1)S(1)} %add_convert_fusion.total_ref), channel_id=1, source_target_pairs={{0,16},{2,18},{4,20},{6,22},{8,24},{10,26},{12,28},{14,30},{16,0},... | collective-permute-start | bytes 589832 | tf_op jit(solution)/shard_map/ppermute | solution.py:239
  41.1 3.7 %collective-permute-done.8 = bf16[256,1024]{1,0:T(8,128)(2,1)S(1)} collective-permute-done((bf16[256,1024]{1,0:T(8,128)(2,1)S(1)}, bf16[256,1024]{1,0:T(8,128)(2,1)S(1)}, u32[]{:S(2)}, u32[]{:S(2)}) %collective-permute-start.8) | collective-permute-done | bytes 524320 | tf_op jit(solution)/shard_map/ppermute | solution.py:243
  44.9 2.2 %collective-permute-done.7.came_ref = bf16[384,256]{1,0:T(8,128)(2,1)S(1)} collective-permute-done((bf16[384,256]{1,0:T(8,128)(2,1)S(1)}, bf16[384,256]{1,0:T(8,128)(2,1)S(1)}, u32[]{:S(2)}, u32[]{:S(2)}) %collective-permute-start.7) | collective-permute-done | bytes 196640 | tf_op jit(solution)/shard_map/ppermute | solution.py:239
  47.0 0.9 %middle.1 = (bf16[256,512]{1,0:T(8,128)(2,1)}, bf16[256,512]{1,0:T(8,128)(2,1)}, bf16[384,256]{1,0:T(8,128)(2,1)S(1)}) custom-call(bf16[384,256]{1,0:T(8,128)(2,1)S(1)} %add_convert_fusion.total_ref, bf16[384,256]{1,0:T(8,128)(2,1)S(1)} %collective-permute-done.7.came_ref, f32[256,512]{1,0:T(8,128)S(1)} %get-tuple-element.42.key_ref, ...), custom_call_target="tpu_custom_call" | custom-call | flops 50331648 | bytes 50331 | tf_op jit(solution)/shard_map/middle/pallas_call | solution.py:210
  47.9 0.0 collective-permute-start.9
  48.0 7.7 %collective-permute-done.9 = bf16[384,256]{1,0:T(8,128)(2,1)S(1)} collective-permute-done((bf16[384,256]{1,0:T(8,128)(2,1)S(1)}, bf16[384,256]{1,0:T(8,128)(2,1)S(1)}, u32[]{:S(2)}, u32[]{:S(2)}) %collective-permute-start.9) | collective-permute-done | bytes 196640 | tf_op jit(solution)/shard_map/ppermute | solution.py:239
  55.6 0.7 %collective-permute-start.10 = (bf16[768,256]{1,0:T(8,128)(2,1)S(1)}, bf16[768,256]{1,0:T(8,128)(2,1)S(1)}, u32[]{:S(2)}, u32[]{:S(2)}) collective-permute-start(bf16[768,256]{1,0:T(8,128)(2,1)S(1)} %constant_dynamic-update-slice_fusion.rest_0_), channel_id=1, source_target_pairs={{0,4},{2,10},{4,0},{6,14},{8,12},{10,2},{12,8},{14,6},{16,20},{18,... | collective-permute-start | bytes 1179656 | tf_op jit(solution)/shard_map/ppermute | solution.py:239
  56.3 0.0 collective-permute-start.12
  56.3 7.1 %collective-permute-done.10.rest_1_ = bf16[768,256]{1,0:T(8,128)(2,1)S(1)} collective-permute-done((bf16[768,256]{1,0:T(8,128)(2,1)S(1)}, bf16[768,256]{1,0:T(8,128)(2,1)S(1)}, u32[]{:S(2)}, u32[]{:S(2)}) %collective-permute-start.10) | collective-permute-done | bytes 393248 | tf_op jit(solution)/shard_map/ppermute | solution.py:239
  63.5 0.0 collective-permute-start.11
  63.5 0.1 pad_add_fusion.place
  63.6 0.0 collective-permute-done.12.rest_2_
  63.6 1.6 %own_columns.1.rest_1_ = bf16[1536,512]{1,0:T(8,128)(2,1)} custom-call(s32[3]{0:T(128)S(1)} %pad_add_fusion.place, bf16[768,256]{1,0:T(8,128)(2,1)S(1)} %constant_dynamic-update-slice_fusion.rest_0_, bf16[768,256]{1,0:T(8,128)(2,1)S(1)} %collective-permute-done.10.rest_1_, bf16[768,256]{1,0:T(8,128)(2,1)S(1)} %collective-permute-done.12.rest_2_), custom_call_target="tpu_custom_call" | custom-call | flops 100663296 | bytes 100663 | tf_op jit(solution)/shard_map/own_columns/pallas_call | solution.py:210
  65.2 0.0 collective-permute-done.11.rest_0_
  65.2 1.3 %other_columns.1 = bf16[1536,512]{1,0:T(8,128)(2,1)} custom-call(s32[3]{0:T(128)S(1)} %pad_add_fusion.place, bf16[768,256]{1,0:T(8,128)(2,1)S(1)} %collective-permute-done.11.rest_0_, bf16[1536,512]{1,0:T(8,128)(2,1)} %own_columns.1.rest_1_), custom_call_target="tpu_custom_call", output_to_operand_aliasing={{}: (2, {})} | custom-call | flops 100663296 | bytes 100663 | tf_op jit(solution)/shard_map/other_columns/pallas_call | solution.py:210
  (5 shorter events, 0.0 us)
Async XLA Ops:
  0.6 9.3 %copy-start = (s32[1536,2]{0,1:T(2,128)S(1)}, s32[1536,2]{0,1:T(2,128)}, u32[]{:S(2)}) copy-start(s32[1536,2]{0,1:T(2,128)} %param.13) | copy-start | bytes 36868
  6.2 1.4 %collective-permute-start = (f32[2,1536]{1,0:T(2,128)S(1)}, f32[2,1536]{1,0:T(2,128)S(1)}, u32[]{:S(2)}, u32[]{:S(2)}) collective-permute-start(f32[2,1536]{1,0:T(2,128)S(1)} %get-tuple-element.25), channel_id=1, source_target_pairs={{0,2},{2,0},{4,6},{6,4},{8,10},{10,8},{12,14},{14,12},{16,18},{18,... | collective-permute-start | bytes 36872 | tf_op jit(solution)/shard_map/ppermute | solution.py:239
  7.5 5.4 %collective-permute-start.1 = (f32[2,1536]{1,0:T(2,128)S(1)}, f32[2,1536]{1,0:T(2,128)S(1)}, u32[]{:S(2)}, u32[]{:S(2)}) collective-permute-start(f32[2,1536]{1,0:T(2,128)S(1)} %add.16.own_ref), channel_id=1, source_target_pairs={{0,4},{2,6},{4,0},{6,2},{8,12},{10,14},{12,8},{14,10},{16,20},{18,... | collective-permute-start | bytes 36872 | tf_op jit(solution)/shard_map/ppermute | solution.py:239
  12.9 9.9 %collective-permute-start.4 = (f32[2,1536,256]{2,1,0:T(8,128)S(1)}, f32[2,1536,256]{2,1,0:T(8,128)S(1)}, u32[]{:S(2)}, u32[]{:S(2)}) collective-permute-start(f32[2,1536,256]{2,1,0:T(8,128)S(1)} %get-tuple-element.32), channel_id=1, source_target_pairs={{0,2},{2,0},{4,6},{6,4},{8,10},{10,8},{12,14},{14,12},{16,18},{18,... | collective-permute-start | bytes 9437192 | tf_op jit(solution)/shard_map/ppermute | solution.py:239
  13.1 5.1 %collective-permute-start.2 = (f32[2,1536]{1,0:T(2,128)S(1)}, f32[2,1536]{1,0:T(2,128)S(1)}, u32[]{:S(2)}, u32[]{:S(2)}) collective-permute-start(f32[2,1536]{1,0:T(2,128)S(1)} %get-tuple-element.29.own_ref), channel_id=1, source_target_pairs={{0,8},{2,10},{4,12},{6,14},{8,0},{10,2},{12,4},{14,6},{16,24},{18,... | collective-permute-start | bytes 36872 | tf_op jit(solution)/shard_map/ppermute | solution.py:239
  18.2 4.7 %collective-permute-start.3 = (f32[2,1536]{1,0:T(2,128)S(1)}, f32[2,1536]{1,0:T(2,128)S(1)}, u32[]{:S(2)}, u32[]{:S(2)}) collective-permute-start(f32[2,1536]{1,0:T(2,128)S(1)} %get-tuple-element.30.delta_ref), channel_id=1, source_target_pairs={{0,16},{2,18},{4,20},{6,22},{8,24},{10,26},{12,28},{14,30},{16,0},... | collective-permute-start | bytes 36872 | tf_op jit(solution)/shard_map/ppermute | solution.py:239
  23.9 7.8 %collective-permute-start.5 = (bf16[768,256]{1,0:T(8,128)(2,1)S(1)}, bf16[768,256]{1,0:T(8,128)(2,1)S(1)}, u32[]{:S(2)}, u32[]{:S(2)}) collective-permute-start(bf16[768,256]{1,0:T(8,128)(2,1)S(1)} %get-tuple-element.34), channel_id=1, source_target_pairs={{0,4},{2,10},{4,0},{6,14},{8,12},{10,2},{12,8},{14,6},{16,20},{18,... | collective-permute-start | bytes 1179656 | tf_op jit(solution)/shard_map/ppermute | solution.py:239
  32.4 5.7 %collective-permute-start.6 = (bf16[384,256]{1,0:T(8,128)(2,1)S(1)}, bf16[384,256]{1,0:T(8,128)(2,1)S(1)}, u32[]{:S(2)}, u32[]{:S(2)}) collective-permute-start(bf16[384,256]{1,0:T(8,128)(2,1)S(1)} %get-tuple-element.41), channel_id=1, source_target_pairs={{0,8},{2,6},{4,12},{6,2},{8,0},{10,14},{12,4},{14,10},{16,24},{18,... | collective-permute-start | bytes 589832 | tf_op jit(solution)/shard_map/ppermute | solution.py:239
  33.1 11.7 %collective-permute-start.8 = (bf16[256,1024]{1,0:T(8,128)(2,1)S(1)}, bf16[256,1024]{1,0:T(8,128)(2,1)S(1)}, u32[]{:S(2)}, u32[]{:S(2)}) collective-permute-start(bf16[256,1024]{1,0:T(8,128)(2,1)S(1)} %bitcast.10), channel_id=1, source_target_pairs={{0,1},{1,0},{2,3},{3,2},{4,5},{5,4},{6,7},{7,6},{8,9},{9,8},{10,11... | collective-permute-start | bytes 1572872 | tf_op jit(solution)/shard_map/ppermute | solution.py:243
  38.2 8.8 %collective-permute-start.7 = (bf16[384,256]{1,0:T(8,128)(2,1)S(1)}, bf16[384,256]{1,0:T(8,128)(2,1)S(1)}, u32[]{:S(2)}, u32[]{:S(2)}) collective-permute-start(bf16[384,256]{1,0:T(8,128)(2,1)S(1)} %add_convert_fusion.total_ref), channel_id=1, source_target_pairs={{0,16},{2,18},{4,20},{6,22},{8,24},{10,26},{12,28},{14,30},{16,0},... | collective-permute-start | bytes 589832 | tf_op jit(solution)/shard_map/ppermute | solution.py:239
  47.9 7.7 %collective-permute-start.9 = (bf16[384,256]{1,0:T(8,128)(2,1)S(1)}, bf16[384,256]{1,0:T(8,128)(2,1)S(1)}, u32[]{:S(2)}, u32[]{:S(2)}) collective-permute-start(bf16[384,256]{1,0:T(8,128)(2,1)S(1)} %get-tuple-element.44), channel_id=1, source_target_pairs={{0,8},{2,6},{4,12},{6,2},{8,0},{10,14},{12,4},{14,10},{16,24},{18,... | collective-permute-start | bytes 589832 | tf_op jit(solution)/shard_map/ppermute | solution.py:239
  55.6 7.8 %collective-permute-start.10 = (bf16[768,256]{1,0:T(8,128)(2,1)S(1)}, bf16[768,256]{1,0:T(8,128)(2,1)S(1)}, u32[]{:S(2)}, u32[]{:S(2)}) collective-permute-start(bf16[768,256]{1,0:T(8,128)(2,1)S(1)} %constant_dynamic-update-slice_fusion.rest_0_), channel_id=1, source_target_pairs={{0,4},{2,10},{4,0},{6,14},{8,12},{10,2},{12,8},{14,6},{16,20},{18,... | collective-permute-start | bytes 1179656 | tf_op jit(solution)/shard_map/ppermute | solution.py:239
  56.3 7.2 %collective-permute-start.12 = (bf16[768,256]{1,0:T(8,128)(2,1)S(1)}, bf16[768,256]{1,0:T(8,128)(2,1)S(1)}, u32[]{:S(2)}, u32[]{:S(2)}) collective-permute-start(bf16[768,256]{1,0:T(8,128)(2,1)S(1)} %constant_dynamic-update-slice_fusion.rest_0_), channel_id=1, source_target_pairs={{0,2},{2,0},{4,6},{6,4},{8,10},{10,8},{12,14},{14,12},{16,18},{18,... | collective-permute-start | bytes 1179656 | tf_op jit(solution)/shard_map/ppermute | solution.py:239
  63.5 1.7 %collective-permute-start.11 = (bf16[768,256]{1,0:T(8,128)(2,1)S(1)}, bf16[768,256]{1,0:T(8,128)(2,1)S(1)}, u32[]{:S(2)}, u32[]{:S(2)}) collective-permute-start(bf16[768,256]{1,0:T(8,128)(2,1)S(1)} %collective-permute-done.10.rest_1_), channel_id=1, source_target_pairs={{0,2},{2,0},{4,6},{6,4},{8,10},{10,8},{12,14},{14,12},{16,18},{18,... | collective-permute-start | bytes 1179656 | tf_op jit(solution)/shard_map/ppermute | solution.py:239

commit v6 on v4

--- a/solution.py
+++ b/solution.py
@@ -12,7 +12,6 @@
 MASKED = 1e30
 NT = (((1,), (1,)), ((), ()))
 NN = (((1,), (0,)), ((), ()))
-TN = (((0,), (0,)), ((), ()))
 PARAMS = pltpu.CompilerParams(vmem_limit_bytes=24 * 1024 * 1024)
 IN_VMEM = pl.BlockSpec(memory_space=pltpu.VMEM)
 IN_SMEM = pl.BlockSpec(memory_space=pltpu.SMEM)
@@ -51,16 +50,20 @@
         rows = slice(index * block, (index + 1) * block)
         copies[2 + 2 * index].wait()
         copies[3 + 2 * index].wait()
+        hits = []
+        live = False
         for head in range(heads):
-            columns = slice(head * width, (head + 1) * width)
             local = targets_ref[head : head + 1, rows] - place[0] * value_count
             hit = (local >= 0) & (local < value_count)
             compatible = compat[head, 0, index] == 1
-            live = compatible | (jnp.max(jnp.where(hit, 1.0, 0.0)) > 0.0)
-
-            @pl.when(live)
-            def _():
-                lse_rows = jnp.where(hit | compatible, lse_ref[head : head + 1, rows], MASKED) * LOG2E
+            hits.append(hit | compatible)
+            live = live | compatible | (jnp.max(jnp.where(hit, 1.0, 0.0)) > 0.0)
+
+        @pl.when(live)
+        def _():
+            for head in range(heads):
+                columns = slice(head * width, (head + 1) * width)
+                lse_rows = jnp.where(hits[head], lse_ref[head : head + 1, rows], MASKED) * LOG2E
                 scores = dot(k_ref[:, columns], q_ref[rows, columns], NT)
                 dprobs = dot(v_ref[:, columns], g_ref[rows, columns], NT)
                 probs = jnp.exp2(scores * (scale * LOG2E) - lse_rows)
@@ -68,8 +71,9 @@
                 probs_ref[head, :, rows] = probs
                 dprobs_ref[head, :, rows] = dprobs
 
-            @pl.when(jnp.logical_not(live))
-            def _():
+        @pl.when(jnp.logical_not(live))
+        def _():
+            for head in range(heads):
                 delta_ref[head : head + 1, rows] = jnp.zeros((1, block), jnp.float32)
                 probs_ref[head, :, rows] = jnp.zeros((value_count, block), jnp.float32)
                 dprobs_ref[head, :, rows] = jnp.zeros((value_count, block), jnp.float32)
@@ -100,13 +104,13 @@
 def pair_dot(terms, keys):
     high = terms.astype(jnp.bfloat16)
     rest = (terms - high.astype(jnp.float32)).astype(jnp.bfloat16)
-    return jnp.transpose(dot(keys, high, TN) + dot(keys, rest, TN))
+    return jnp.transpose(dot(keys, high, NN) + dot(keys, rest, NN))
 
 
 def query_kernel(place, probs_ref, dprobs_ref, targets_ref, k_ref, out_ref, *, own, chunk):
     head = place[2] if own else 1 - place[2]
     width = out_ref.shape[2]
-    keys = k_ref[:, ways(head * width, width)]
+    keys = jnp.transpose(k_ref[:, ways(head * width, width)])
     for start in range(0, out_ref.shape[1], chunk):
         rows = slice(start, start + chunk)
         probs = probs_ref[head, :, rows]
@@ -117,15 +121,15 @@
         out_ref[1, rows, :] = pair_dot(probs, keys)
 
 
-def delta_kernel(own_ref, received_ref, terms_ref, out_ref, same_terms_ref):
-    out_ref[...] = own_ref[...] + received_ref[...]
-
-
-def combine_kernel(
-    place, delta_ref, gone_ref, own_ref, received_ref, keep_ref, sum_ref, *send_refs, scale
-):
+def delta_kernel(*refs):
+    *added, terms_ref, out_ref, same_terms_ref = refs
+    out_ref[...] = sum(ref[...] for ref in added)
+
+
+def combine_kernel(place, own_ref, received_ref, *rest, deltas, scale):
+    added, (keep_ref, sum_ref, *send_refs) = rest[:deltas], rest[deltas:]
     chains, rows, width = keep_ref.shape
-    sum_ref[...] = delta_ref[...] + gone_ref[...]
+    sum_ref[...] = sum(ref[...] for ref in added)
     for other in (1, 0):
         for chain in range(chains):
             target = send_refs[chain] if other else keep_ref.at[chain]
@@ -136,8 +140,7 @@
                 columns = slice(start, start + 128)
                 direct = own_ref[0, span, columns] + received_ref[0, span, columns]
                 weighted = own_ref[1, span, columns] + received_ref[1, span, columns]
-                total = scale * direct - delta * weighted
-                target[:, columns] = total.astype(target.dtype)
+                target[:, columns] = (scale * direct - delta * weighted).astype(target.dtype)
 
 
 def key_kernel(
@@ -165,23 +168,6 @@
                 send_ref[step - 1, :, columns] = term.astype(jnp.bfloat16)
 
 
-def place_pieces(place, source, out_ref, sems, side):
-    chains = len(source)
-    pieces, piece, width = source[0].shape
-    columns = ways((place[0] ^ side) * width, width)
-    copies = []
-    for chain in range(chains):
-        for index in range(pieces):
-            rows = ways((chain * pieces + (index ^ place[1 + chain])) * piece, piece)
-            copies.append(
-                pltpu.make_async_copy(
-                    source[chain].at[index], out_ref.at[rows, columns], sems.at[len(copies)]
-                )
-            )
-            copies[-1].start()
-    return copies
-
-
 def split_kernel(place, keep_ref, *rest):
     chains = keep_ref.shape[0]
     came_refs, kept_ref, sent_refs = rest[:chains], rest[chains + 1], rest[chains + 2 :]
@@ -194,13 +180,13 @@
             target[...] = total.astype(target.dtype)
 
 
-def middle_kernel(
-    total_ref, came_ref, key_ref, value_ref, received_ref, key_out, value_out, *out_refs
-):
-    rows = total_ref.shape[1]
+def join_kernel(total_ref, came_ref, after_ref, *out_refs):
     for chain, out_ref in enumerate(out_refs):
-        out_ref[:rows] = total_ref[chain]
-        out_ref[rows:] = came_ref[chain]
+        total = total_ref[chain].astype(jnp.float32) + came_ref[chain].astype(jnp.float32)
+        out_ref[...] = total.astype(jnp.bfloat16)
+
+
+def pool_kernel(key_ref, value_ref, received_ref, key_out, value_out):
     wide = key_ref.shape[1]
     key_sum, value_sum = key_ref[...], value_ref[...]
     for step in range(received_ref.shape[0]):
@@ -210,15 +196,22 @@
     value_out[...] = value_sum.astype(jnp.bfloat16)
 
 
-def own_columns_kernel(place, *rest):
-    *mine, out_ref, sems = rest
-    for copy in place_pieces(place, mine, out_ref, sems, 0):
-        copy.wait()
-
-
-def other_columns_kernel(place, begun_ref, *rest):
-    *theirs, out_ref, sems = rest
-    for copy in place_pieces(place, theirs, out_ref, sems, 1):
+def place_kernel(place, *rest, sources, pieces, piece):
+    out_ref, sems = rest[-2:]
+    copies = []
+    for ref, (side, chain, first) in zip(rest, sources):
+        width = ref.shape[1]
+        columns = ways((place[0] ^ side) * width, width)
+        for index in range(ref.shape[0] // piece):
+            natural = chain * pieces + ((first + index) ^ place[1 + chain])
+            rows = ways(natural * piece, piece)
+            copies.append(
+                pltpu.make_async_copy(
+                    ref.at[pl.ds(index * piece, piece)], out_ref.at[rows, columns], sems.at[len(copies)]
+                )
+            )
+            copies[-1].start()
+    for copy in copies:
         copy.wait()
 
 
@@ -267,10 +260,12 @@
     def bit_of(bit):
         return lax.rem(val // (1 << bit), 2)
 
-    chains = 2 if query_count % (2 * value_devices // 2 * 16) == 0 else 1
+    pieces = 1 << (bits - 2)
+    chains = 2 if query_count % (2 * pieces * 16) == 0 else 1
     orders = [[1, 2], [2, 1]][:chains]
-    orders = [order + list(range(3, bits)) for order in orders]
-    place = jnp.stack([val, qry, core] + [bit_of(order[stage]) for stage in range(2) for order in orders]).astype(jnp.int32)
+    place = jnp.stack(
+        [val, qry, core] + [bit_of(order[stage]) for stage in range(2) for order in orders]
+    ).astype(jnp.int32)
     work = 2 * query_count * value_count * width
 
     delta, probs, dprobs, q_near, g_near, k_near = call(
@@ -320,35 +315,32 @@
         )[0]
 
     other = query_terms(False, "other_head")
-    mine = query_terms(True, "own_head")
     received = None
-    for bit in range(bits):
-        came = flip(delta, 1 << bit)
-        if bit < bits - 1:
-            carried = {0: other, bits - 2: mine}.get(bit)
-            if carried is None:
-                delta = delta + came
-                continue
-            delta, carried = call(
+    stride = 1
+    added = [delta]
+    while stride < value_devices:
+        if stride > 1:
+            terms = other if received is None else received
+            delta, terms = call(
                 delta_kernel,
                 "delta_sum",
-                (delta, came, carried),
-                [IN_VMEM] * 2 + [IN_HBM],
+                (*added, terms),
+                [IN_VMEM] * len(added) + [IN_HBM],
                 [pltpu.VMEM((heads, query_count), f32), rows_of],
                 heads * query_count,
                 out_specs=[IN_VMEM, IN_HBM],
-                aliases={2: 1},
+                aliases={len(added): 1},
             )
-            if bit == 0:
-                received = flip(carried, 1)
-            else:
-                mine = carried
+            received = flip(terms, 1) if received is None else terms
+        steps = min(4, value_devices // stride)
+        added = [delta] + [flip(delta, stride * step) for step in range(1, steps)]
+        stride *= steps
     half = query_count // (2 * chains)
     keep, delta, *send = call(
-        partial(combine_kernel, scale=scale),
+        partial(combine_kernel, deltas=len(added), scale=scale),
         "combine",
-        (place, delta, came, mine, received),
-        [IN_SMEM] + [IN_VMEM] * 4,
+        (place, query_terms(True, "own_head"), received, *added),
+        [IN_SMEM] + [IN_VMEM] * (2 + len(added)),
         [
             pltpu.VMEM((chains, half, width), f32),
             pltpu.VMEM((heads, query_count), f32),
@@ -383,66 +375,68 @@
             for chain, order in enumerate(orders)
         ]
     )
-    for bit in range(3, bits):
+    for bit in range(3, bits - 1):
         split = total.reshape(chains, 2, -1, width)
         pick = partial(lax.dynamic_index_in_dim, split, axis=1, keepdims=False)
         came = flip(pick(1 - bit_of(bit)).astype(bf16), 1 << bit)
         total = pick(bit_of(bit)) + came.astype(f32)
     total = total.astype(bf16)
-    for bit in range(bits - 1, 3, -1):
-        total = jnp.concatenate([total, flip(total, 1 << bit)], axis=1)
-    key_grad, value_grad, *parts_of = call(
-        middle_kernel,
-        "middle",
-        (total, flip(total, 8), key_own, value_own, pool_received),
-        [IN_VMEM] * 5,
-        [
-            jax.ShapeDtypeStruct((share, wide), bf16),
-            jax.ShapeDtypeStruct((share, wide), bf16),
-        ]
-        + [pltpu.VMEM((half // 2, width), bf16)] * chains,
+    piece = total.shape[1]
+    joined = call(
+        join_kernel,
+        "join",
+        (total, flip(total, 1 << (bits - 1)), pool_received),
+        [IN_VMEM] * 2 + [IN_HBM],
+        [pltpu.VMEM((piece, width), bf16)] * chains,
+        work // 16,
+    )
+    key_grad, value_grad = call(
+        pool_kernel,
+        "pool_sum",
+        (key_own, value_own, pool_received),
+        [IN_VMEM] * 3,
+        [pltpu.HBM((share, wide), bf16)] * 2,
         work // 8,
     )
-    gathered = []
-    own_piece = []
+    first_half, second_half, own_piece = [], [], []
     for chain, order in enumerate(orders):
-        part = parts_of[chain]
-        for bit in order[1::-1]:
+        part = joined[chain]
+        for bit in list(range(bits - 2, 2, -1)) + [order[1]]:
             part = jnp.concatenate([part, flip(part, 1 << bit)], axis=0)
-        gathered.append(part)
+        first_half.append(part)
+        second_half.append(flip(part, 1 << order[0]))
         index = 0
-        for bit in order:
+        for bit in order + list(range(3, bits - 1)):
             index = 2 * index + bit_of(bit)
         own_piece.append(index)
-    pieces = value_devices // 2
+    pieces_place = jnp.stack([core] + own_piece).astype(jnp.int32)
     near = partial(pltpu.with_memory_space_constraint, memory_space=pltpu.VMEM)
-    gathered = [near(part.reshape(pieces, -1, width)) for part in gathered]
-    theirs = [near(flip(part, 1)) for part in gathered]
-    order_place = jnp.stack([core] + own_piece).astype(jnp.int32)
-    query_shape = jax.ShapeDtypeStruct((query_count, wide), bf16)
-    sems = [pltpu.SemaphoreType.DMA((chains * pieces,))]
-    (begun,) = call(
-        own_columns_kernel,
-        "own_columns",
-        (order_place, *gathered),
-        [IN_SMEM] + [IN_VMEM] * chains,
-        [query_shape],
-        work // 4,
-        sems,
-        [IN_HBM],
-    )
-    (query_grad,) = call(
-        other_columns_kernel,
-        "other_columns",
-        (order_place, begun, *theirs),
-        [IN_SMEM, IN_HBM] + [IN_VMEM] * chains,
-        [query_shape],
-        work // 4,
-        sems,
-        [IN_HBM],
-        {1: 0},
-    )
-    return query_grad, key_grad, value_grad
+    early, late = [], []
+    for chain in range(chains):
+        early.append((first_half[chain], 0, chain, 0))
+        early.append((second_half[chain], 0, chain, pieces // 2))
+        early.append((flip(first_half[chain], 1), 1, chain, 0))
+        late.append((flip(second_half[chain], 1), 1, chain, pieces // 2))
+    before = (pltpu.with_memory_space_constraint(key_grad, pltpu.HBM),)
+    for name, sources in (("own_columns", early), ("other_columns", late)):
+        copied = len(sources)
+        before = call(
+            partial(
+                place_kernel,
+                sources=[source[1:] for source in sources],
+                pieces=pieces,
+                piece=piece,
+            ),
+            name,
+            (pieces_place, *[near(source[0]) for source in sources], *before),
+            [IN_SMEM] + [IN_VMEM] * copied + [IN_HBM],
+            [jax.ShapeDtypeStruct((query_count, wide), bf16)],
+            work // 4,
+            [pltpu.SemaphoreType.DMA((copied * pieces // 2,))],
+            [IN_HBM],
+            {1 + copied: 0} if name == "other_columns" else {},
+        )
+    return before[0], key_grad, value_grad
 
 
 def solution(mesh):

time: 69.6 us -> 61.8 us (0.89)
  waiting for transfers between devices: 28.5 us -> 23.2 us
  Pallas kernels: 22.6 us -> 20.9 us
  starting transfers between devices: 16.6 us -> 15.9 us
    ppermute x17 -> x20, waiting for transfers between devices: 28.5 us -> 23.2 us  [flip(): lax.ppermute(array, 'val', [(i, i ^ mask) for i in range(value_devices)])]
    ppermute x17 -> x20, starting transfers between devices: 15.4 us -> 13.6 us  [flip(): lax.ppermute(array, 'val', [(i, i ^ mask) for i in range(value_devices)])]
    pallas_call x12, Pallas kernels: 22.6 us -> 20.9 us  [call(): pl.pallas_call(kernel, in_specs=in_specs, out_specs=[IN_VMEM] * len(outpu...]
    ppermute x1, starting transfers between devices: 1.16 us -> 2.28 us  [swap_shares(): lax.ppermute(send[step - 1], 'qry', [(i, (i + step) % parts) for i in ran...]
  transfers between devices with their start and end apart: 18 -> 21, of which waited for: 12 -> 11; matrix products, arithmetic and copies ran while one was open for 0% -> 0% of each run, Pallas kernels for 16% -> 20%
where the time goes in v6:
time: 61.8 us; the launch traced here: 61.2 us
  waiting for transfers between devices  23.2 us (38%)
  Pallas kernels  20.9 us (34%)
  starting transfers between devices  15.9 us (26%)
  between operations  0.99 us (2%)
    ppermute x20, waiting for transfers between devices, flip(): lax.ppermute(array, 'val', [(i, i ^ mask) for i in range(value_devices)])  23.2 us
    pallas_call x12, Pallas kernels, call(): pl.pallas_call(kernel, in_specs=in_specs, out_specs=[IN_VMEM] * len(outpu...  20.9 us
    ppermute x20, starting transfers between devices, flip(): lax.ppermute(array, 'val', [(i, i ^ mask) for i in range(value_devices)])  13.6 us
    ppermute x1, starting transfers between devices, swap_shares(): lax.ppermute(send[step - 1], 'qry', [(i, (i + step) % parts) for i in ran...  2.28 us
  transfers between devices with their start and end apart: 21, of which 11 were waited for; matrix products, arithmetic and copies ran while one was open for 0% of the time, Pallas kernels for 20%

profile of v6, /device:TPU:0, one launch (start us, length us, event | category | flops | bytes accessed | tf_op | source)
XLA Modules:
  0.0 61.2 jit_solution(2801482888592669887)
XLA Ops:
  0.6 0.0 copy-start
  0.7 0.1 stack.53.place
  0.8 5.7 %forward_pass.1 = (f32[2,1536]{1,0:T(2,128)S(1)}, f32[2,512,1536]{2,1,0:T(8,128)S(1)}, f32[2,512,1536]{2,1,0:T(8,128)S(1)}, bf16[1536,512]{1,0:T(8,128)(2,1)S(1)...) custom-call(s32[7]{0:T(128)S(1)} %stack.53.place, s32[2,1,6]{2,1,0:T(1,128)} %compat.1, ...), custom_call_target="tpu_custom_call" | custom-call | flops 1610612736 | bytes 1610612 | tf_op jit(solution)/shard_map/forward_pass/pallas_call | solution.py:219
  6.5 0.5 collective-permute-start
  7.0 2.4 %collective-permute-start.1 = (f32[2,1536]{1,0:T(2,128)S(1)}, f32[2,1536]{1,0:T(2,128)S(1)}, u32[]{:S(2)}, u32[]{:S(2)}) collective-permute-start(f32[2,1536]{1,0:T(2,128)S(1)} %get-tuple-element.29.refs_0_), channel_id=1, source_target_pairs={{0,4},{2,6},{4,0},{6,2},{8,12},{10,14},{12,8},{14,10},{16,20},{18,... | collective-permute-start | bytes 36872 | tf_op jit(solution)/shard_map/ppermute | solution.py:247
  9.4 0.0 collective-permute-start.2
  9.4 0.0 copy-done
  9.4 3.0 %other_head.1.refs_4_ = f32[2,1536,256]{2,1,0:T(8,128)S(1)} custom-call(s32[7]{0:T(128)S(1)} %stack.53.place, f32[2,512,1536]{2,1,0:T(8,128)S(1)} %get-tuple-element.26.probs_ref, f32[2,512,1536]{2,1,0:T(8,128)S(1)} %get-tuple-element.27.dprobs_ref, s32[2,1536]{1,0:T(2,128)S(1)} %bitcast.30, bf16[512,512]{1,0:T(8,128)(2,1)S(1)} %get-tuple-element.28.k_ref), custom_call_target="tpu_custom_call" | custom-call | flops 1610612736 | bytes 1610612 | tf_op jit(solution)/shard_map/other_head/pallas_call | solution.py:219
  12.4 0.0 collective-permute-done.refs_1_
  12.4 0.0 collective-permute-done.1.refs_2_
  12.4 0.1 collective-permute-done.2.refs_3_
  12.5 0.1 collective-permute-start.3
  12.6 1.5 %collective-permute-start.4 = (f32[2,1536]{1,0:T(2,128)S(1)}, f32[2,1536]{1,0:T(2,128)S(1)}, u32[]{:S(2)}, u32[]{:S(2)}) collective-permute-start(f32[2,1536]{1,0:T(2,128)S(1)} %get-tuple-element.31.rest_0_), channel_id=1, source_target_pairs={{0,8},{2,10},{4,12},{6,14},{8,0},{10,2},{12,4},{14,6},{16,24},{18,... | collective-permute-start | bytes 36872 | tf_op jit(solution)/shard_map/ppermute | solution.py:247
  14.2 2.8 %collective-permute-start.5 = (f32[2,1536]{1,0:T(2,128)S(1)}, f32[2,1536]{1,0:T(2,128)S(1)}, u32[]{:S(2)}, u32[]{:S(2)}) collective-permute-start(f32[2,1536]{1,0:T(2,128)S(1)} %get-tuple-element.31.rest_0_), channel_id=1, source_target_pairs={{0,16},{2,18},{4,20},{6,22},{8,24},{10,26},{12,28},{14,30},{16,0},... | collective-permute-start | bytes 36872 | tf_op jit(solution)/shard_map/ppermute | solution.py:247
  16.9 0.4 collective-permute-start.6
  17.3 3.0 %own_head.1.own_ref = f32[2,1536,256]{2,1,0:T(8,128)S(1)} custom-call(s32[7]{0:T(128)S(1)} %stack.53.place, f32[2,512,1536]{2,1,0:T(8,128)S(1)} %get-tuple-element.26.probs_ref, f32[2,512,1536]{2,1,0:T(8,128)S(1)} %get-tuple-element.27.dprobs_ref, s32[2,1536]{1,0:T(2,128)S(1)} %bitcast.31, bf16[512,512]{1,0:T(8,128)(2,1)S(1)} %get-tuple-element.28.k_ref), custom_call_target="tpu_custom_call" | custom-call | flops 1610612736 | bytes 1610612 | tf_op jit(solution)/shard_map/own_head/pallas_call | solution.py:219
  20.3 0.0 collective-permute-done.4.rest_1_
  20.3 0.0 collective-permute-done.5.rest_2_
  20.4 2.1 %collective-permute-done.6.rest_3_ = f32[2,1536]{1,0:T(2,128)S(1)} collective-permute-done((f32[2,1536]{1,0:T(2,128)S(1)}, f32[2,1536]{1,0:T(2,128)S(1)}, u32[]{:S(2)}, u32[]{:S(2)}) %collective-permute-start.6) | collective-permute-done | bytes 12320 | tf_op jit(solution)/shard_map/ppermute | solution.py:247
  22.4 0.0 collective-permute-done.3.received_ref
  22.4 0.9 %combine.1 = (f32[2,384,256]{2,1,0:T(8,128)S(1)}, f32[2,1536]{1,0:T(2,128)S(1)}, bf16[384,256]{1,0:T(8,128)(2,1)S(1)}, bf16[384,256]{1,0:T(8,128)(2,1)S(1)}) custom-call(s32[7]{0:T(128)S(1)} %stack.53.place, f32[2,1536,256]{2,1,0:T(8,128)S(1)} %own_head.1.own_ref, f32[2,1536,256]{2,1,0:T(8,128)S(1)} %collective-permute-done.3.received_ref, ...), custom_call_target="tpu_custom_call" | custom-call | flops 100663296 | bytes 100663 | tf_op jit(solution)/shard_map/combine/pallas_call | solution.py:219
  23.3 1.6 %collective-permute-start.7 = (bf16[384,256]{1,0:T(8,128)(2,1)S(1)}, bf16[384,256]{1,0:T(8,128)(2,1)S(1)}, u32[]{:S(2)}, u32[]{:S(2)}) collective-permute-start(bf16[384,256]{1,0:T(8,128)(2,1)S(1)} %get-tuple-element.33), channel_id=1, source_target_pairs={{0,4},{2,6},{4,0},{6,2},{8,12},{10,14},{12,8},{14,10},{16,20},{18,... | collective-permute-start | bytes 589832 | tf_op jit(solution)/shard_map/ppermute | solution.py:247
  24.9 0.0 collective-permute-start.8
  24.9 1.5 %value_terms.1 = (f32[256,512]{1,0:T(8,128)S(1)}, bf16[1,256,512]{2,1,0:T(8,128)(2,1)S(1)}) custom-call(s32[7]{0:T(128)S(1)} %stack.53.place, f32[2,512,1536]{2,1,0:T(8,128)S(1)} %get-tuple-element.26.probs_ref, bf16[1536,512]{1,0:T(8,128)(2,1)S(1)} %get-tuple-element.37.g_ref), custom_call_target="tpu_custom_call" | custom-call | flops 805306368 | bytes 805306 | tf_op jit(solution)/shard_map/value_terms/pallas_call | solution.py:219
  26.4 2.3 %key_terms.1 = (f32[256,512]{1,0:T(8,128)S(1)}, bf16[1,256,1024]{2,1,0:T(8,128)(2,1)S(1)}) custom-call(s32[7]{0:T(128)S(1)} %stack.53.place, f32[2,1536]{1,0:T(2,128)S(1)} %get-tuple-element.35.delta_ref, f32[2,512,1536]{2,1,0:T(8,128)S(1)} %get-tuple-element.26.probs_ref, f32[2,512,1536]{2,1,0:T(8,128)S(1)} %get-tuple-element.27.dprobs_ref, ...), custom_call_target="tpu_custom_call" | custom-call | flops 805306368 | bytes 805306 | tf_op jit(solution)/shard_map/key_terms/pallas_call | solution.py:219
  28.7 0.4 collective-permute-done.7.rest_0_
  29.1 1.5 %collective-permute-done.8.rest_1_ = bf16[384,256]{1,0:T(8,128)(2,1)S(1)} collective-permute-done((bf16[384,256]{1,0:T(8,128)(2,1)S(1)}, bf16[384,256]{1,0:T(8,128)(2,1)S(1)}, u32[]{:S(2)}, u32[]{:S(2)}) %collective-permute-start.8) | collective-permute-done | bytes 196640 | tf_op jit(solution)/shard_map/ppermute | solution.py:247
  30.6 0.6 %split.1 = (f32[2,192,256]{2,1,0:T(8,128)S(1)}, bf16[192,256]{1,0:T(8,128)(2,1)S(1)}, bf16[192,256]{1,0:T(8,128)(2,1)S(1)}) custom-call(s32[7]{0:T(128)S(1)} %stack.53.place, f32[2,384,256]{2,1,0:T(8,128)S(1)} %get-tuple-element.32.keep_ref, bf16[384,256]{1,0:T(8,128)(2,1)S(1)} %collective-permute-done.7.rest_0_, ...), custom_call_target="tpu_custom_call" | custom-call | flops 50331648 | bytes 50331 | tf_op jit(solution)/shard_map/split/pallas_call | solution.py:219
  31.2 0.6 collective-permute-start.10
  31.8 0.2 collective-permute-start.9
  32.0 2.3 %collective-permute-start.12 = (bf16[256,1024]{1,0:T(8,128)(2,1)S(1)}, bf16[256,1024]{1,0:T(8,128)(2,1)S(1)}, u32[]{:S(2)}, u32[]{:S(2)}) collective-permute-start(bf16[256,1024]{1,0:T(8,128)(2,1)S(1)} %bitcast.28), channel_id=1, source_target_pairs={{0,1},{1,0},{2,3},{3,2},{4,5},{5,4},{6,7},{7,6},{8,9},{9,8},{10,11... | collective-permute-start | bytes 1572872 | tf_op jit(solution)/shard_map/ppermute | solution.py:251
  34.2 1.7 %collective-permute-done.10 = bf16[192,256]{1,0:T(8,128)(2,1)S(1)} collective-permute-done((bf16[192,256]{1,0:T(8,128)(2,1)S(1)}, bf16[192,256]{1,0:T(8,128)(2,1)S(1)}, u32[]{:S(2)}, u32[]{:S(2)}) %collective-permute-start.10) | collective-permute-done | bytes 98336 | tf_op jit(solution)/shard_map/ppermute | solution.py:247
  35.9 1.0 %collective-permute-done.9 = bf16[192,256]{1,0:T(8,128)(2,1)S(1)} collective-permute-done((bf16[192,256]{1,0:T(8,128)(2,1)S(1)}, bf16[192,256]{1,0:T(8,128)(2,1)S(1)}, u32[]{:S(2)}, u32[]{:S(2)}) %collective-permute-start.9) | collective-permute-done | bytes 98336 | tf_op jit(solution)/shard_map/ppermute | solution.py:247
  36.9 0.1 fusion.2
  37.0 0.1 collective-permute-start.11
  37.2 7.9 %collective-permute-done.11.came_ref = bf16[2,192,256]{2,1,0:T(8,128)(2,1)S(1)} collective-permute-done((bf16[2,192,256]{2,1,0:T(8,128)(2,1)S(1)}, bf16[2,192,256]{2,1,0:T(8,128)(2,1)S(1)}, u32[]{:S(2)}, u32[]{:S(2)}) %collective-permute-start.11) | collective-permute-done | bytes 196640 | tf_op jit(solution)/shard_map/ppermute | solution.py:247
  45.1 0.0 collective-permute-done.12
  45.1 1.6 %collective-permute-start.16 = (bf16[192,256]{1,0:T(8,128)(2,1)S(1)}, bf16[192,256]{1,0:T(8,128)(2,1)S(1)}, u32[]{:S(2)}, u32[]{:S(2)}) collective-permute-start(bf16[192,256]{1,0:T(8,128)(2,1)S(1)} %get-tuple-element.44), channel_id=1, source_target_pairs={{0,4},{2,6},{4,0},{6,2},{8,12},{10,14},{12,8},{14,10},{16,20},{18,... | collective-permute-start | bytes 294920 | tf_op jit(solution)/shard_map/ppermute | solution.py:247
  46.7 0.0 collective-permute-start.13
  46.7 4.1 %collective-permute-done.16 = bf16[192,256]{1,0:T(8,128)(2,1)S(1)} collective-permute-done((bf16[192,256]{1,0:T(8,128)(2,1)S(1)}, bf16[192,256]{1,0:T(8,128)(2,1)S(1)}, u32[]{:S(2)}, u32[]{:S(2)}) %collective-permute-start.16) | collective-permute-done | bytes 98336 | tf_op jit(solution)/shard_map/ppermute | solution.py:247
  50.9 0.1 collective-permute-start.17
  51.0 0.4 collective-permute-done.13
  51.4 1.2 %collective-permute-start.14 = (bf16[384,256]{1,0:T(8,128)(2,1)S(1)}, bf16[384,256]{1,0:T(8,128)(2,1)S(1)}, u32[]{:S(2)}, u32[]{:S(2)}) collective-permute-start(bf16[384,256]{1,0:T(8,128)(2,1)S(1)} %constant_dynamic-update-slice_fusion.rest_0_), channel_id=1, source_target_pairs={{0,4},{2,6},{4,0},{6,2},{8,12},{10,14},{12,8},{14,10},{16,20},{18,... | collective-permute-start | bytes 589832 | tf_op jit(solution)/shard_map/ppermute | solution.py:247
  52.6 0.0 collective-permute-start.20
  52.6 0.5 collective-permute-start.19
  53.1 3.5 %collective-permute-done.17.rest_4_ = bf16[384,256]{1,0:T(8,128)(2,1)S(1)} collective-permute-done((bf16[384,256]{1,0:T(8,128)(2,1)S(1)}, bf16[384,256]{1,0:T(8,128)(2,1)S(1)}, u32[]{:S(2)}, u32[]{:S(2)}) %collective-permute-start.17) | collective-permute-done | bytes 196640 | tf_op jit(solution)/shard_map/ppermute | solution.py:247
  56.6 0.0 collective-permute-start.18
  56.6 0.5 collective-permute-done.14.rest_1_
  57.1 0.0 collective-permute-start.15
  57.1 0.1 pad_add_fusion.place
  57.2 0.9 %pool_sum.1 = (bf16[256,512]{1,0:T(8,128)(2,1)}, bf16[256,512]{1,0:T(8,128)(2,1)}) custom-call(f32[256,512]{1,0:T(8,128)S(1)} %get-tuple-element.45.key_ref, f32[256,512]{1,0:T(8,128)S(1)} %get-tuple-element.46.value_ref, bf16[1,256,1024]{2,1,0:T(8,128)(2,1)S(1)} %bitcast.27), custom_call_target="tpu_custom_call" | custom-call | flops 50331648 | bytes 50331 | tf_op jit(solution)/shard_map/pool_sum/pallas_call | solution.py:219
  58.1 0.0 collective-permute-done.20.rest_5_
  58.1 0.0 collective-permute-done.19.rest_2_
  58.1 1.6 %own_columns.1.rest_2_ = bf16[1536,512]{1,0:T(8,128)(2,1)} custom-call(s32[3]{0:T(128)S(1)} %pad_add_fusion.place, bf16[384,256]{1,0:T(8,128)(2,1)S(1)} %constant_dynamic-update-slice_fusion.rest_0_, bf16[384,256]{1,0:T(8,128)(2,1)S(1)} %collective-permute-done.14.rest_1_, bf16[384,256]{1,0:T(8,128)(2,1)S(1)} %collective-permute-done.19.rest_2_, ...), custom_call_target="tpu_custom_call" | custom-call | flops 100663296 | bytes 100663 | tf_op jit(solution)/shard_map/own_columns/pallas_call | solution.py:219
  59.7 0.0 collective-permute-done.18.rest_1_
  59.7 0.0 collective-permute-done.15.rest_0_
  59.8 1.3 %other_columns.1 = bf16[1536,512]{1,0:T(8,128)(2,1)} custom-call(s32[3]{0:T(128)S(1)} %pad_add_fusion.place, bf16[384,256]{1,0:T(8,128)(2,1)S(1)} %collective-permute-done.15.rest_0_, bf16[384,256]{1,0:T(8,128)(2,1)S(1)} %collective-permute-done.18.rest_1_, bf16[1536,512]{1,0:T(8,128)(2,1)} %own_columns.1.rest_2_), custom_call_target="tpu_custom_call", output_to_operand_aliasing={{}: (3, {})} | custom-call | flops 100663296 | bytes 100663 | tf_op jit(solution)/shard_map/other_columns/pallas_call | solution.py:219
  (7 shorter events, 0.1 us)
Async XLA Ops:
  0.6 8.7 %copy-start = (s32[1536,2]{0,1:T(2,128)S(1)}, s32[1536,2]{0,1:T(2,128)}, u32[]{:S(2)}) copy-start(s32[1536,2]{0,1:T(2,128)} %param.13) | copy-start | bytes 36868
  6.5 5.9 %collective-permute-start = (f32[2,1536]{1,0:T(2,128)S(1)}, f32[2,1536]{1,0:T(2,128)S(1)}, u32[]{:S(2)}, u32[]{:S(2)}) collective-permute-start(f32[2,1536]{1,0:T(2,128)S(1)} %get-tuple-element.29.refs_0_), channel_id=1, source_target_pairs={{0,2},{2,0},{4,6},{6,4},{8,10},{10,8},{12,14},{14,12},{16,18},{18,... | collective-permute-start | bytes 36872 | tf_op jit(solution)/shard_map/ppermute | solution.py:247
  7.0 5.4 %collective-permute-start.1 = (f32[2,1536]{1,0:T(2,128)S(1)}, f32[2,1536]{1,0:T(2,128)S(1)}, u32[]{:S(2)}, u32[]{:S(2)}) collective-permute-start(f32[2,1536]{1,0:T(2,128)S(1)} %get-tuple-element.29.refs_0_), channel_id=1, source_target_pairs={{0,4},{2,6},{4,0},{6,2},{8,12},{10,14},{12,8},{14,10},{16,20},{18,... | collective-permute-start | bytes 36872 | tf_op jit(solution)/shard_map/ppermute | solution.py:247
  9.4 3.1 %collective-permute-start.2 = (f32[2,1536]{1,0:T(2,128)S(1)}, f32[2,1536]{1,0:T(2,128)S(1)}, u32[]{:S(2)}, u32[]{:S(2)}) collective-permute-start(f32[2,1536]{1,0:T(2,128)S(1)} %get-tuple-element.29.refs_0_), channel_id=1, source_target_pairs={{0,6},{2,4},{4,2},{6,0},{8,14},{10,12},{12,10},{14,8},{16,22},{18,... | collective-permute-start | bytes 36872 | tf_op jit(solution)/shard_map/ppermute | solution.py:247
  12.5 9.9 %collective-permute-start.3 = (f32[2,1536,256]{2,1,0:T(8,128)S(1)}, f32[2,1536,256]{2,1,0:T(8,128)S(1)}, u32[]{:S(2)}, u32[]{:S(2)}) collective-permute-start(f32[2,1536,256]{2,1,0:T(8,128)S(1)} %get-tuple-element.30), channel_id=1, source_target_pairs={{0,2},{2,0},{4,6},{6,4},{8,10},{10,8},{12,14},{14,12},{16,18},{18,... | collective-permute-start | bytes 9437192 | tf_op jit(solution)/shard_map/ppermute | solution.py:247
  12.6 7.7 %collective-permute-start.4 = (f32[2,1536]{1,0:T(2,128)S(1)}, f32[2,1536]{1,0:T(2,128)S(1)}, u32[]{:S(2)}, u32[]{:S(2)}) collective-permute-start(f32[2,1536]{1,0:T(2,128)S(1)} %get-tuple-element.31.rest_0_), channel_id=1, source_target_pairs={{0,8},{2,10},{4,12},{6,14},{8,0},{10,2},{12,4},{14,6},{16,24},{18,... | collective-permute-start | bytes 36872 | tf_op jit(solution)/shard_map/ppermute | solution.py:247
  14.2 6.2 %collective-permute-start.5 = (f32[2,1536]{1,0:T(2,128)S(1)}, f32[2,1536]{1,0:T(2,128)S(1)}, u32[]{:S(2)}, u32[]{:S(2)}) collective-permute-start(f32[2,1536]{1,0:T(2,128)S(1)} %get-tuple-element.31.rest_0_), channel_id=1, source_target_pairs={{0,16},{2,18},{4,20},{6,22},{8,24},{10,26},{12,28},{14,30},{16,0},... | collective-permute-start | bytes 36872 | tf_op jit(solution)/shard_map/ppermute | solution.py:247
  16.9 5.5 %collective-permute-start.6 = (f32[2,1536]{1,0:T(2,128)S(1)}, f32[2,1536]{1,0:T(2,128)S(1)}, u32[]{:S(2)}, u32[]{:S(2)}) collective-permute-start(f32[2,1536]{1,0:T(2,128)S(1)} %get-tuple-element.31.rest_0_), channel_id=1, source_target_pairs={{0,24},{2,26},{4,28},{6,30},{8,16},{10,18},{12,20},{14,22},{16,8},... | collective-permute-start | bytes 36872 | tf_op jit(solution)/shard_map/ppermute | solution.py:247
  23.3 5.7 %collective-permute-start.7 = (bf16[384,256]{1,0:T(8,128)(2,1)S(1)}, bf16[384,256]{1,0:T(8,128)(2,1)S(1)}, u32[]{:S(2)}, u32[]{:S(2)}) collective-permute-start(bf16[384,256]{1,0:T(8,128)(2,1)S(1)} %get-tuple-element.33), channel_id=1, source_target_pairs={{0,4},{2,6},{4,0},{6,2},{8,12},{10,14},{12,8},{14,10},{16,20},{18,... | collective-permute-start | bytes 589832 | tf_op jit(solution)/shard_map/ppermute | solution.py:247
  24.9 5.7 %collective-permute-start.8 = (bf16[384,256]{1,0:T(8,128)(2,1)S(1)}, bf16[384,256]{1,0:T(8,128)(2,1)S(1)}, u32[]{:S(2)}, u32[]{:S(2)}) collective-permute-start(bf16[384,256]{1,0:T(8,128)(2,1)S(1)} %get-tuple-element.34), channel_id=1, source_target_pairs={{0,8},{2,10},{4,12},{6,14},{8,0},{10,2},{12,4},{14,6},{16,24},{18,... | collective-permute-start | bytes 589832 | tf_op jit(solution)/shard_map/ppermute | solution.py:247
  31.2 4.7 %collective-permute-start.10 = (bf16[192,256]{1,0:T(8,128)(2,1)S(1)}, bf16[192,256]{1,0:T(8,128)(2,1)S(1)}, u32[]{:S(2)}, u32[]{:S(2)}) collective-permute-start(bf16[192,256]{1,0:T(8,128)(2,1)S(1)} %get-tuple-element.42), channel_id=1, source_target_pairs={{0,4},{2,6},{4,0},{6,2},{8,12},{10,14},{12,8},{14,10},{16,20},{18,... | collective-permute-start | bytes 294920 | tf_op jit(solution)/shard_map/ppermute | solution.py:247
  31.8 5.1 %collective-permute-start.9 = (bf16[192,256]{1,0:T(8,128)(2,1)S(1)}, bf16[192,256]{1,0:T(8,128)(2,1)S(1)}, u32[]{:S(2)}, u32[]{:S(2)}) collective-permute-start(bf16[192,256]{1,0:T(8,128)(2,1)S(1)} %get-tuple-element.41), channel_id=1, source_target_pairs={{0,8},{2,10},{4,12},{6,14},{8,0},{10,2},{12,4},{14,6},{16,24},{18,... | collective-permute-start | bytes 294920 | tf_op jit(solution)/shard_map/ppermute | solution.py:247
  32.0 13.1 %collective-permute-start.12 = (bf16[256,1024]{1,0:T(8,128)(2,1)S(1)}, bf16[256,1024]{1,0:T(8,128)(2,1)S(1)}, u32[]{:S(2)}, u32[]{:S(2)}) collective-permute-start(bf16[256,1024]{1,0:T(8,128)(2,1)S(1)} %bitcast.28), channel_id=1, source_target_pairs={{0,1},{1,0},{2,3},{3,2},{4,5},{5,4},{6,7},{7,6},{8,9},{9,8},{10,11... | collective-permute-start | bytes 1572872 | tf_op jit(solution)/shard_map/ppermute | solution.py:251
  37.0 8.0 %collective-permute-start.11 = (bf16[2,192,256]{2,1,0:T(8,128)(2,1)S(1)}, bf16[2,192,256]{2,1,0:T(8,128)(2,1)S(1)}, u32[]{:S(2)}, u32[]{:S(2)}) collective-permute-start(bf16[2,192,256]{2,1,0:T(8,128)(2,1)S(1)} %pad_maximum_fusion.total_ref), channel_id=1, source_target_pairs={{0,16},{2,18},{4,20},{6,22},{8,24},{10,26},{12,28},{14,30},{16,0},... | collective-permute-start | bytes 589832 | tf_op jit(solution)/shard_map/ppermute | solution.py:247
  45.1 5.7 %collective-permute-start.16 = (bf16[192,256]{1,0:T(8,128)(2,1)S(1)}, bf16[192,256]{1,0:T(8,128)(2,1)S(1)}, u32[]{:S(2)}, u32[]{:S(2)}) collective-permute-start(bf16[192,256]{1,0:T(8,128)(2,1)S(1)} %get-tuple-element.44), channel_id=1, source_target_pairs={{0,4},{2,6},{4,0},{6,2},{8,12},{10,14},{12,8},{14,10},{16,20},{18,... | collective-permute-start | bytes 294920 | tf_op jit(solution)/shard_map/ppermute | solution.py:247
  46.7 4.6 %collective-permute-start.13 = (bf16[192,256]{1,0:T(8,128)(2,1)S(1)}, bf16[192,256]{1,0:T(8,128)(2,1)S(1)}, u32[]{:S(2)}, u32[]{:S(2)}) collective-permute-start(bf16[192,256]{1,0:T(8,128)(2,1)S(1)} %get-tuple-element.43), channel_id=1, source_target_pairs={{0,8},{2,10},{4,12},{6,14},{8,0},{10,2},{12,4},{14,6},{16,24},{18,... | collective-permute-start | bytes 294920 | tf_op jit(solution)/shard_map/ppermute | solution.py:247
  50.9 5.7 %collective-permute-start.17 = (bf16[384,256]{1,0:T(8,128)(2,1)S(1)}, bf16[384,256]{1,0:T(8,128)(2,1)S(1)}, u32[]{:S(2)}, u32[]{:S(2)}) collective-permute-start(bf16[384,256]{1,0:T(8,128)(2,1)S(1)} %constant_dynamic-update-slice_fusion.2.rest_3_), channel_id=1, source_target_pairs={{0,8},{2,10},{4,12},{6,14},{8,0},{10,2},{12,4},{14,6},{16,24},{18,... | collective-permute-start | bytes 589832 | tf_op jit(solution)/shard_map/ppermute | solution.py:247
  51.4 5.7 %collective-permute-start.14 = (bf16[384,256]{1,0:T(8,128)(2,1)S(1)}, bf16[384,256]{1,0:T(8,128)(2,1)S(1)}, u32[]{:S(2)}, u32[]{:S(2)}) collective-permute-start(bf16[384,256]{1,0:T(8,128)(2,1)S(1)} %constant_dynamic-update-slice_fusion.rest_0_), channel_id=1, source_target_pairs={{0,4},{2,6},{4,0},{6,2},{8,12},{10,14},{12,8},{14,10},{16,20},{18,... | collective-permute-start | bytes 589832 | tf_op jit(solution)/shard_map/ppermute | solution.py:247
  52.6 5.5 %collective-permute-start.20 = (bf16[384,256]{1,0:T(8,128)(2,1)S(1)}, bf16[384,256]{1,0:T(8,128)(2,1)S(1)}, u32[]{:S(2)}, u32[]{:S(2)}) collective-permute-start(bf16[384,256]{1,0:T(8,128)(2,1)S(1)} %constant_dynamic-update-slice_fusion.2.rest_3_), channel_id=1, source_target_pairs={{0,2},{2,0},{4,6},{6,4},{8,10},{10,8},{12,14},{14,12},{16,18},{18,... | collective-permute-start | bytes 589832 | tf_op jit(solution)/shard_map/ppermute | solution.py:247
  52.6 5.5 %collective-permute-start.19 = (bf16[384,256]{1,0:T(8,128)(2,1)S(1)}, bf16[384,256]{1,0:T(8,128)(2,1)S(1)}, u32[]{:S(2)}, u32[]{:S(2)}) collective-permute-start(bf16[384,256]{1,0:T(8,128)(2,1)S(1)} %constant_dynamic-update-slice_fusion.rest_0_), channel_id=1, source_target_pairs={{0,2},{2,0},{4,6},{6,4},{8,10},{10,8},{12,14},{14,12},{16,18},{18,... | collective-permute-start | bytes 589832 | tf_op jit(solution)/shard_map/ppermute | solution.py:247
  56.6 3.1 %collective-permute-start.18 = (bf16[384,256]{1,0:T(8,128)(2,1)S(1)}, bf16[384,256]{1,0:T(8,128)(2,1)S(1)}, u32[]{:S(2)}, u32[]{:S(2)}) collective-permute-start(bf16[384,256]{1,0:T(8,128)(2,1)S(1)} %collective-permute-done.17.rest_4_), channel_id=1, source_target_pairs={{0,2},{2,0},{4,6},{6,4},{8,10},{10,8},{12,14},{14,12},{16,18},{18,... | collective-permute-start | bytes 589832 | tf_op jit(solution)/shard_map/ppermute | solution.py:247
  57.1 2.7 %collective-permute-start.15 = (bf16[384,256]{1,0:T(8,128)(2,1)S(1)}, bf16[384,256]{1,0:T(8,128)(2,1)S(1)}, u32[]{:S(2)}, u32[]{:S(2)}) collective-permute-start(bf16[384,256]{1,0:T(8,128)(2,1)S(1)} %collective-permute-done.14.rest_1_), channel_id=1, source_target_pairs={{0,2},{2,0},{4,6},{6,4},{8,10},{10,8},{12,14},{14,12},{16,18},{18,... | collective-permute-start | bytes 589832 | tf_op jit(solution)/shard_map/ppermute | solution.py:247

commit v7 on v6

--- a/solution.py
+++ b/solution.py
@@ -27,54 +27,63 @@
 
 
 def forward_kernel(
-    place, compat, q_hbm, g_hbm, k_hbm, v_hbm, lse_ref, targets_ref,
-    delta_ref, probs_ref, dprobs_ref, q_ref, g_ref, k_ref, v_ref, sems, *, heads, blocks, scale,
+    compat_hbm, q_hbm, g_hbm, k_hbm, v_hbm, lse_hbm, targets_hbm,
+    delta_ref, probs_ref, dprobs_ref, q_ref, g_ref, k_ref,
+    v_ref, lse_ref, targets_ref, compat, sems, *, heads, blocks, scale,
 ):
     value_count, width = k_ref.shape[0], k_ref.shape[1] // heads
     block = q_ref.shape[0] // blocks
-    copies = [
-        pltpu.make_async_copy(k_hbm, k_ref, sems.at[0]),
-        pltpu.make_async_copy(v_hbm, v_ref, sems.at[1]),
+    pairs = [
+        (compat_hbm, compat), (targets_hbm, targets_ref), (lse_hbm, lse_ref),
+        (k_hbm, k_ref), (v_hbm, v_ref),
     ]
+    small = len(pairs)
     for index in range(blocks):
         rows = pl.ds(index * block, block)
-        for half, (source, target) in enumerate(((q_hbm, q_ref), (g_hbm, g_ref))):
-            copies.append(
-                pltpu.make_async_copy(source.at[rows], target.at[rows], sems.at[2 + 2 * index + half])
-            )
+        pairs += [(q_hbm.at[rows], q_ref.at[rows]), (g_hbm.at[rows], g_ref.at[rows])]
+    copies = [pltpu.make_async_copy(*pair, sems.at[n]) for n, pair in enumerate(pairs)]
     for copy in copies:
         copy.start()
-    copies[0].wait()
-    copies[1].wait()
+    for copy in copies[:3]:
+        copy.wait()
+    local = targets_ref[...] - lax.axis_index("val") * value_count
+    hit = jnp.where((local >= 0) & (local < value_count), 1.0, 0.0)
+    lives = []
+    for index in range(blocks):
+        live = jnp.max(hit[:, index * block : (index + 1) * block]) > 0.0
+        for head in range(heads):
+            live = live | (compat[head, 0, index] == 1)
+        lives.append(live)
+    for copy in copies[3:small]:
+        copy.wait()
     for index in range(blocks):
         rows = slice(index * block, (index + 1) * block)
-        copies[2 + 2 * index].wait()
-        copies[3 + 2 * index].wait()
-        hits = []
-        live = False
-        for head in range(heads):
-            local = targets_ref[head : head + 1, rows] - place[0] * value_count
-            hit = (local >= 0) & (local < value_count)
-            compatible = compat[head, 0, index] == 1
-            hits.append(hit | compatible)
-            live = live | compatible | (jnp.max(jnp.where(hit, 1.0, 0.0)) > 0.0)
+        copies[small + 2 * index].wait()
+        copies[small + 2 * index + 1].wait()
+        live = lives[index]
 
         @pl.when(live)
         def _():
             for head in range(heads):
                 columns = slice(head * width, (head + 1) * width)
-                lse_rows = jnp.where(hits[head], lse_ref[head : head + 1, rows], MASKED) * LOG2E
+                usable = (hit[head : head + 1, rows] > 0.0) | (compat[head, 0, index] == 1)
+                lse_rows = jnp.where(usable, lse_ref[head : head + 1, rows], MASKED) * LOG2E
                 scores = dot(k_ref[:, columns], q_ref[rows, columns], NT)
                 dprobs = dot(v_ref[:, columns], g_ref[rows, columns], NT)
                 probs = jnp.exp2(scores * (scale * LOG2E) - lse_rows)
-                delta_ref[head : head + 1, rows] = jnp.sum(probs * dprobs, axis=0, keepdims=True)
+                delta = jnp.sum(probs * dprobs, axis=0, keepdims=True)
+                weight = jnp.sum(probs, axis=0, keepdims=True)
+                delta_ref[head : head + 1, rows] = delta
+                centre = delta / jnp.maximum(weight, 1e-30)
+                delta_ref[heads + head : heads + head + 1, rows] = centre
                 probs_ref[head, :, rows] = probs
                 dprobs_ref[head, :, rows] = dprobs
 
         @pl.when(jnp.logical_not(live))
         def _():
             for head in range(heads):
-                delta_ref[head : head + 1, rows] = jnp.zeros((1, block), jnp.float32)
+                for row in (head, heads + head):
+                    delta_ref[row : row + 1, rows] = jnp.zeros((1, block), jnp.float32)
                 probs_ref[head, :, rows] = jnp.zeros((value_count, block), jnp.float32)
                 dprobs_ref[head, :, rows] = jnp.zeros((value_count, block), jnp.float32)
 
@@ -101,46 +110,52 @@
     return jnp.where(slots == local, terms - 1.0, terms)
 
 
-def pair_dot(terms, keys):
-    high = terms.astype(jnp.bfloat16)
-    rest = (terms - high.astype(jnp.float32)).astype(jnp.bfloat16)
-    return jnp.transpose(dot(keys, high, NN) + dot(keys, rest, NN))
-
-
-def query_kernel(place, probs_ref, dprobs_ref, targets_ref, k_ref, out_ref, *, own, chunk):
+def query_kernel(
+    place, delta_ref, probs_ref, dprobs_ref, targets_ref, k_ref, out_ref, *, own, chunk
+):
     head = place[2] if own else 1 - place[2]
     width = out_ref.shape[2]
+    heads = probs_ref.shape[0]
     keys = jnp.transpose(k_ref[:, ways(head * width, width)])
     for start in range(0, out_ref.shape[1], chunk):
         rows = slice(start, start + chunk)
         probs = probs_ref[head, :, rows]
-        terms = onehot_less(
-            probs * (dprobs_ref[head, :, rows] + 1.0), place, targets_ref, head, rows
-        )
-        out_ref[0, rows, :] = pair_dot(terms, keys)
-        out_ref[1, rows, :] = pair_dot(probs, keys)
+        gap = dprobs_ref[head, :, rows] - (delta_ref[pl.ds(heads + head, 1), rows] - 1.0)
+        terms = onehot_less(probs * gap, place, targets_ref, head, rows)
+        for index, factor in enumerate((terms, probs)):
+            product = dot(keys, factor.astype(jnp.bfloat16), NN)
+            out_ref[index, rows, :] = jnp.transpose(product)
 
 
 def delta_kernel(*refs):
     *added, terms_ref, out_ref, same_terms_ref = refs
-    out_ref[...] = sum(ref[...] for ref in added)
-
-
-def combine_kernel(place, own_ref, received_ref, *rest, deltas, scale):
+    heads = out_ref.shape[0]
+    out_ref[...] = sum(ref[:heads] for ref in added)
+
+
+def combine_kernel(
+    place, own_ref, received_ref, centre_ref, came_ref, *rest, deltas, scale
+):
     added, (keep_ref, sum_ref, *send_refs) = rest[:deltas], rest[deltas:]
     chains, rows, width = keep_ref.shape
+    heads = sum_ref.shape[0]
     sum_ref[...] = sum(ref[...] for ref in added)
+
+    def column(ref, span):
+        row = sum_ref[pl.ds(place[2], 1), span] - ref[pl.ds(heads + place[2], 1), span]
+        return jnp.transpose(jnp.broadcast_to(row * scale, (128, rows)))
+
     for other in (1, 0):
         for chain in range(chains):
             target = send_refs[chain] if other else keep_ref.at[chain]
             span = ways((2 * chain + (place[3 + chain] ^ other)) * rows, rows)
-            delta = sum_ref[pl.ds(place[2], 1), span] * scale
-            delta = jnp.transpose(jnp.broadcast_to(delta, (128, rows)))
+            gaps = column(centre_ref, span), column(came_ref, span)
             for start in range(0, width, 128):
                 columns = slice(start, start + 128)
                 direct = own_ref[0, span, columns] + received_ref[0, span, columns]
-                weighted = own_ref[1, span, columns] + received_ref[1, span, columns]
-                target[:, columns] = (scale * direct - delta * weighted).astype(target.dtype)
+                weighted = own_ref[1, span, columns] * gaps[0]
+                weighted += received_ref[1, span, columns] * gaps[1]
+                target[:, columns] = (scale * direct - weighted).astype(target.dtype)
 
 
 def key_kernel(
@@ -196,6 +211,10 @@
     value_out[...] = value_sum.astype(jnp.bfloat16)
 
 
+def after_kernel(*refs):
+    pass
+
+
 def place_kernel(place, *rest, sources, pieces, piece):
     out_ref, sems = rest[-2:]
     copies = []
@@ -271,16 +290,15 @@
     delta, probs, dprobs, q_near, g_near, k_near = call(
         partial(forward_kernel, heads=heads, blocks=blocks, scale=scale),
         "forward_pass",
-        (place,)
-        + tuple(
+        tuple(
             pltpu.with_memory_space_constraint(array, pltpu.HBM)
             for array in (
                 compat, queries, out_grad, pool_keys, pool_values, lse, jnp.transpose(targets)
             )
         ),
-        [IN_SMEM, IN_SMEM] + [IN_HBM] * 4 + [IN_VMEM] * 2,
+        [IN_HBM] * 7,
         [
-            pltpu.VMEM((heads, query_count), f32),
+            pltpu.VMEM((2 * heads, query_count), f32),
             pltpu.VMEM((heads, value_count, query_count), f32),
             pltpu.VMEM((heads, value_count, query_count), f32),
             pltpu.VMEM(queries.shape, bf16),
@@ -290,7 +308,10 @@
         4 * work,
         [
             pltpu.VMEM(pool_values.shape, bf16),
-            pltpu.SemaphoreType.DMA((2 + 2 * blocks,)),
+            pltpu.VMEM((heads, query_count), f32),
+            pltpu.VMEM((heads, query_count), jnp.int32),
+            pltpu.SMEM(compat.shape, jnp.int32),
+            pltpu.SemaphoreType.DMA((5 + 2 * blocks,)),
         ],
     )
     shares = [
@@ -308,12 +329,13 @@
         return call(
             partial(query_kernel, own=own, chunk=chunk),
             name,
-            (place, probs, dprobs, targets, k_near),
-            [IN_SMEM] + [IN_VMEM] * 4,
+            (place, centre, probs, dprobs, targets, k_near),
+            [IN_SMEM] + [IN_VMEM] * 5,
             [rows_of],
-            4 * work,
+            2 * work,
         )[0]
 
+    centre = delta
     other = query_terms(False, "other_head")
     received = None
     stride = 1
@@ -334,13 +356,15 @@
             received = flip(terms, 1) if received is None else terms
         steps = min(4, value_devices // stride)
         added = [delta] + [flip(delta, stride * step) for step in range(1, steps)]
+        if stride == 1:
+            other_centre = added[1]
         stride *= steps
     half = query_count // (2 * chains)
     keep, delta, *send = call(
         partial(combine_kernel, deltas=len(added), scale=scale),
         "combine",
-        (place, query_terms(True, "own_head"), received, *added),
-        [IN_SMEM] + [IN_VMEM] * (2 + len(added)),
+        (place, query_terms(True, "own_head"), received, centre, other_centre, *added),
+        [IN_SMEM] + [IN_VMEM] * (4 + len(added)),
         [
             pltpu.VMEM((chains, half, width), f32),
             pltpu.VMEM((heads, query_count), f32),
@@ -411,16 +435,11 @@
         own_piece.append(index)
     pieces_place = jnp.stack([core] + own_piece).astype(jnp.int32)
     near = partial(pltpu.with_memory_space_constraint, memory_space=pltpu.VMEM)
-    early, late = [], []
-    for chain in range(chains):
-        early.append((first_half[chain], 0, chain, 0))
-        early.append((second_half[chain], 0, chain, pieces // 2))
-        early.append((flip(first_half[chain], 1), 1, chain, 0))
-        late.append((flip(second_half[chain], 1), 1, chain, pieces // 2))
-    before = (pltpu.with_memory_space_constraint(key_grad, pltpu.HBM),)
-    for name, sources in (("own_columns", early), ("other_columns", late)):
+    far = partial(pltpu.with_memory_space_constraint, memory_space=pltpu.HBM)
+
+    def placed(name, sources, before, aliases):
         copied = len(sources)
-        before = call(
+        return call(
             partial(
                 place_kernel,
                 sources=[source[1:] for source in sources],
@@ -428,15 +447,32 @@
                 piece=piece,
             ),
             name,
-            (pieces_place, *[near(source[0]) for source in sources], *before),
+            (pieces_place, *[near(source[0]) for source in sources], far(before)),
             [IN_SMEM] + [IN_VMEM] * copied + [IN_HBM],
-            [jax.ShapeDtypeStruct((query_count, wide), bf16)],
-            work // 4,
+            [pltpu.HBM((query_count, wide), bf16)],
+            work // 2,
             [pltpu.SemaphoreType.DMA((copied * pieces // 2,))],
             [IN_HBM],
-            {1 + copied: 0} if name == "other_columns" else {},
-        )
-    return before[0], key_grad, value_grad
+            {1 + copied: 0} if aliases else {},
+        )[0]
+
+    sources = [(part, 0, chain, 0) for chain, part in enumerate(first_half)]
+    sources += [(flip(part, 1), 1, chain, 0) for chain, part in enumerate(first_half)]
+    begun = placed("first_rows", sources, key_grad, False)
+    second_half = call(
+        after_kernel,
+        "after",
+        (*second_half, far(begun)),
+        [IN_HBM] * (chains + 1),
+        [pltpu.VMEM((half, width), bf16)] * chains,
+        work // 1000,
+        out_specs=[IN_HBM] * chains,
+        aliases={chain: chain for chain in range(chains)},
+    )
+    sources = [(part, 0, chain, pieces // 2) for chain, part in enumerate(second_half)]
+    begun = placed("own_rows", sources, begun, True)
+    sources = [(flip(part, 1), 1, chain, pieces // 2) for chain, part in enumerate(second_half)]
+    return placed("other_rows", sources, begun, True), key_grad, value_grad
 
 
 def solution(mesh):

time: 61.8 us -> 73 us (1.18)
  local copies, waits for them, and re-layouts: 0.12 us -> 12.1 us
  Pallas kernels: 20.9 us -> 18.5 us
  waiting for transfers between devices: 23.2 us -> 25.4 us
    unnamed x4 -> x22, local copies, waits for them, and re-layouts: 0.02 us -> 12 us
    pallas_call x12 -> x14, Pallas kernels: 20.9 us -> 18.5 us  [call(): pl.pallas_call(kernel, in_specs=in_specs, out_specs=[IN_VMEM] * len(outpu...]
    ppermute x20, waiting for transfers between devices: 23.2 us -> 25.4 us  [flip(): lax.ppermute(array, 'val', [(i, i ^ mask) for i in range(value_devices)])]
  transfers between devices with their start and end apart: 21 -> 21, of which waited for: 11 -> 8; matrix products, arithmetic and copies ran while one was open for 0% -> 0% of each run, Pallas kernels for 20% -> 16%
where the time goes in v7:
time: 73 us; the launch traced here: 72.8 us
  waiting for transfers between devices  25.4 us (35%)
  Pallas kernels  18.5 us (25%)
  starting transfers between devices  15.7 us (22%)
  local copies, waits for them, and re-layouts  12.1 us (17%)
  between operations  0.9 us (1%)
    ppermute x20, waiting for transfers between devices, flip(): lax.ppermute(array, 'val', [(i, i ^ mask) for i in range(value_devices)])  25.4 us
    pallas_call x14, Pallas kernels, call(): pl.pallas_call(kernel, in_specs=in_specs, out_specs=[IN_VMEM] * len(outpu...  18.5 us
    ppermute x20, starting transfers between devices, flip(): lax.ppermute(array, 'val', [(i, i ^ mask) for i in range(value_devices)])  13.8 us
    unnamed x22, local copies, waits for them, and re-layouts  12 us
    ppermute x1, starting transfers between devices, swap_shares(): lax.ppermute(send[step - 1], 'qry', [(i, (i + step) % parts) for i in ran...  1.9 us
  transfers between devices with their start and end apart: 21, of which 8 were waited for; matrix products, arithmetic and copies ran while one was open for 0% of the time, Pallas kernels for 16%

profile of v7, /device:TPU:0, one launch (start us, length us, event | category | flops | bytes accessed | tf_op | source)
XLA Modules:
  0.0 72.8 jit_solution(11999916246069598541)
XLA Ops:
  0.6 0.0 copy-start.7
  0.6 3.8 %forward_pass.1 = (f32[4,1536]{1,0:T(4,128)S(1)}, f32[2,512,1536]{2,1,0:T(8,128)S(1)}, f32[2,512,1536]{2,1,0:T(8,128)S(1)}, bf16[1536,512]{1,0:T(8,128)(2,1)S(1)...) custom-call(s32[2,1,6]{2,1,0:T(1,128)} %compat_hbm.1, bf16[1536,512]{1,0:T(8,128)(2,1)} %q_hbm.1, ...), custom_call_target="tpu_custom_call" | custom-call | flops 1610612736 | bytes 1610612 | tf_op jit(solution)/shard_map/forward_pass/pallas_call | solution.py:238
  4.5 2.6 %copy-done = f32[2,512,1536]{2,1,0:T(8,128)} copy-done((f32[2,512,1536]{2,1,0:T(8,128)}, f32[2,512,1536]{2,1,0:T(8,128)S(1)}, u32[]{:S(2)}) %copy-start) | copy-done | bytes 6291480
  7.1 2.7 %copy-done.3 = f32[2,512,1536]{2,1,0:T(8,128)} copy-done((f32[2,512,1536]{2,1,0:T(8,128)}, f32[2,512,1536]{2,1,0:T(8,128)S(1)}, u32[]{:S(2)}) %copy-start.3) | copy-done | bytes 6291480
  9.8 1.1 %copy-done.5 = bf16[1536,512]{1,0:T(8,128)(2,1)} copy-done((bf16[1536,512]{1,0:T(8,128)(2,1)}, bf16[1536,512]{1,0:T(8,128)(2,1)S(1)}, u32[]{:S(2)}) %copy-start.5) | copy-done | bytes 1572888
  10.9 0.5 collective-permute-start
  11.4 2.1 %collective-permute-start.1 = (f32[4,1536]{1,0:T(4,128)S(1)}, f32[4,1536]{1,0:T(4,128)S(1)}, u32[]{:S(2)}, u32[]{:S(2)}) collective-permute-start(f32[4,1536]{1,0:T(4,128)S(1)} %get-tuple-element.28.delta_ref.refs_0_.centre_ref), channel_id=1, source_target_pairs={{0,4},{2,6},{4,0},{6,2},{8,12},{10,14},{12,8},{14,10},{16,20},{18,... | collective-permute-start | bytes 73736 | tf_op jit(solution)/shard_map/ppermute | solution.py:266
  13.5 0.1 collective-permute-start.2
  13.7 0.1 stack.53.place
  13.8 2.8 %copy-done.1 = f32[2,512,1536]{2,1,0:T(8,128)S(1)} copy-done((f32[2,512,1536]{2,1,0:T(8,128)S(1)}, f32[2,512,1536]{2,1,0:T(8,128)}, u32[]{:S(2)}) %copy-start.1) | copy-done | bytes 6291480
  16.5 2.8 %copy-done.4 = f32[2,512,1536]{2,1,0:T(8,128)S(1)} copy-done((f32[2,512,1536]{2,1,0:T(8,128)S(1)}, f32[2,512,1536]{2,1,0:T(8,128)}, u32[]{:S(2)}) %copy-start.4) | copy-done | bytes 6291480
  19.3 2.0 %other_head.1.refs_4_ = f32[2,1536,256]{2,1,0:T(8,128)S(1)} custom-call(s32[7]{0:T(128)S(1)} %stack.53.place, f32[4,1536]{1,0:T(4,128)S(1)} %get-tuple-element.28.delta_ref.refs_0_.centre_ref, f32[2,512,1536]{2,1,0:T(8,128)S(1)} %copy-done.1, f32[2,512,1536]{2,1,0:T(8,128)S(1)} %copy-done.4, s32[2,1536]{1,0:T(2,128)S(1)} %bitcast.32, ...), custom_call_target="tpu_custom_call" | custom-call | flops 805306368 | bytes 805306 | tf_op jit(solution)/shard_map/other_head/pallas_call | solution.py:238
  21.3 0.0 collective-permute-done.refs_1_.came_ref
  21.3 0.0 collective-permute-done.1.refs_2_
  21.4 0.0 collective-permute-done.2.refs_3_
  21.4 0.2 collective-permute-start.3
  21.5 2.3 %collective-permute-start.4 = (f32[2,1536]{1,0:T(2,128)S(1)}, f32[2,1536]{1,0:T(2,128)S(1)}, u32[]{:S(2)}, u32[]{:S(2)}) collective-permute-start(f32[2,1536]{1,0:T(2,128)S(1)} %get-tuple-element.33.rest_0_), channel_id=1, source_target_pairs={{0,8},{2,10},{4,12},{6,14},{8,0},{10,2},{12,4},{14,6},{16,24},{18,... | collective-permute-start | bytes 36872 | tf_op jit(solution)/shard_map/ppermute | solution.py:266
  23.9 2.7 %collective-permute-start.5 = (f32[2,1536]{1,0:T(2,128)S(1)}, f32[2,1536]{1,0:T(2,128)S(1)}, u32[]{:S(2)}, u32[]{:S(2)}) collective-permute-start(f32[2,1536]{1,0:T(2,128)S(1)} %get-tuple-element.33.rest_0_), channel_id=1, source_target_pairs={{0,16},{2,18},{4,20},{6,22},{8,24},{10,26},{12,28},{14,30},{16,0},... | collective-permute-start | bytes 36872 | tf_op jit(solution)/shard_map/ppermute | solution.py:266
  26.5 0.2 collective-permute-start.6
  26.7 0.0 copy-done.2
  26.7 2.0 %own_head.1.own_ref = f32[2,1536,256]{2,1,0:T(8,128)S(1)} custom-call(s32[7]{0:T(128)S(1)} %stack.53.place, f32[4,1536]{1,0:T(4,128)S(1)} %get-tuple-element.28.delta_ref.refs_0_.centre_ref, f32[2,512,1536]{2,1,0:T(8,128)S(1)} %copy-done.2, f32[2,512,1536]{2,1,0:T(8,128)S(1)} %copy-done.4, s32[2,1536]{1,0:T(2,128)S(1)} %bitcast.33, ...), custom_call_target="tpu_custom_call" | custom-call | flops 805306368 | bytes 805306 | tf_op jit(solution)/shard_map/own_head/pallas_call | solution.py:238
  28.7 0.0 copy-start.6
  28.7 0.0 collective-permute-done.4.rest_1_
  28.8 0.0 collective-permute-done.5.rest_2_
  28.8 3.2 %collective-permute-done.6.rest_3_ = f32[2,1536]{1,0:T(2,128)S(1)} collective-permute-done((f32[2,1536]{1,0:T(2,128)S(1)}, f32[2,1536]{1,0:T(2,128)S(1)}, u32[]{:S(2)}, u32[]{:S(2)}) %collective-permute-start.6) | collective-permute-done | bytes 12320 | tf_op jit(solution)/shard_map/ppermute | solution.py:266
  32.0 0.0 collective-permute-done.3.received_ref
  32.0 1.2 %combine.1 = (f32[2,384,256]{2,1,0:T(8,128)S(1)}, f32[2,1536]{1,0:T(2,128)S(1)}, bf16[384,256]{1,0:T(8,128)(2,1)S(1)}, bf16[384,256]{1,0:T(8,128)(2,1)S(1)}) custom-call(s32[7]{0:T(128)S(1)} %stack.53.place, f32[2,1536,256]{2,1,0:T(8,128)S(1)} %own_head.1.own_ref, f32[2,1536,256]{2,1,0:T(8,128)S(1)} %collective-permute-done.3.received_ref, ...), custom_call_target="tpu_custom_call" | custom-call | flops 100663296 | bytes 100663 | tf_op jit(solution)/shard_map/combine/pallas_call | solution.py:238
  33.2 1.9 %collective-permute-start.7 = (bf16[384,256]{1,0:T(8,128)(2,1)S(1)}, bf16[384,256]{1,0:T(8,128)(2,1)S(1)}, u32[]{:S(2)}, u32[]{:S(2)}) collective-permute-start(bf16[384,256]{1,0:T(8,128)(2,1)S(1)} %get-tuple-element.35), channel_id=1, source_target_pairs={{0,4},{2,6},{4,0},{6,2},{8,12},{10,14},{12,8},{14,10},{16,20},{18,... | collective-permute-start | bytes 589832 | tf_op jit(solution)/shard_map/ppermute | solution.py:266
  35.1 0.0 collective-permute-start.8
  35.1 1.6 %value_terms.1 = (f32[256,512]{1,0:T(8,128)S(1)}, bf16[1,256,512]{2,1,0:T(8,128)(2,1)S(1)}) custom-call(s32[7]{0:T(128)S(1)} %stack.53.place, f32[2,512,1536]{2,1,0:T(8,128)S(1)} %copy-done.2, bf16[1536,512]{1,0:T(8,128)(2,1)S(1)} %copy-done.6), custom_call_target="tpu_custom_call" | custom-call | flops 805306368 | bytes 805306 | tf_op jit(solution)/shard_map/value_terms/pallas_call | solution.py:238
  36.8 2.3 %key_terms.1 = (f32[256,512]{1,0:T(8,128)S(1)}, bf16[1,256,1024]{2,1,0:T(8,128)(2,1)S(1)}) custom-call(s32[7]{0:T(128)S(1)} %stack.53.place, f32[2,1536]{1,0:T(2,128)S(1)} %get-tuple-element.37.delta_ref, f32[2,512,1536]{2,1,0:T(8,128)S(1)} %copy-done.2, f32[2,512,1536]{2,1,0:T(8,128)S(1)} %bitcast.27, s32[2,1536]{1,0:T(2,128)S(1)} %bitcast.34, ...), custom_call_target="tpu_custom_call" | custom-call | flops 805306368 | bytes 805306 | tf_op jit(solution)/shard_map/key_terms/pallas_call | solution.py:238
  39.1 0.0 collective-permute-done.7.rest_0_
  39.1 1.7 %collective-permute-done.8.rest_1_ = bf16[384,256]{1,0:T(8,128)(2,1)S(1)} collective-permute-done((bf16[384,256]{1,0:T(8,128)(2,1)S(1)}, bf16[384,256]{1,0:T(8,128)(2,1)S(1)}, u32[]{:S(2)}, u32[]{:S(2)}) %collective-permute-start.8) | collective-permute-done | bytes 196640 | tf_op jit(solution)/shard_map/ppermute | solution.py:266
  40.8 0.6 split.1
  41.4 0.2 collective-permute-start.10
  41.6 0.3 collective-permute-start.9
  42.0 1.9 %collective-permute-start.12 = (bf16[256,1024]{1,0:T(8,128)(2,1)S(1)}, bf16[256,1024]{1,0:T(8,128)(2,1)S(1)}, u32[]{:S(2)}, u32[]{:S(2)}) collective-permute-start(bf16[256,1024]{1,0:T(8,128)(2,1)S(1)} %bitcast.30), channel_id=1, source_target_pairs={{0,1},{1,0},{2,3},{3,2},{4,5},{5,4},{6,7},{7,6},{8,9},{9,8},{10,11... | collective-permute-start | bytes 1572872 | tf_op jit(solution)/shard_map/ppermute | solution.py:270
  43.9 2.2 %collective-permute-done.10 = bf16[192,256]{1,0:T(8,128)(2,1)S(1)} collective-permute-done((bf16[192,256]{1,0:T(8,128)(2,1)S(1)}, bf16[192,256]{1,0:T(8,128)(2,1)S(1)}, u32[]{:S(2)}, u32[]{:S(2)}) %collective-permute-start.10) | collective-permute-done | bytes 98336 | tf_op jit(solution)/shard_map/ppermute | solution.py:266
  46.1 0.6 collective-permute-done.9
  46.7 0.1 fusion.2
  46.8 0.1 collective-permute-start.11
  46.8 8.8 %collective-permute-done.11.came_ref = bf16[2,192,256]{2,1,0:T(8,128)(2,1)S(1)} collective-permute-done((bf16[2,192,256]{2,1,0:T(8,128)(2,1)S(1)}, bf16[2,192,256]{2,1,0:T(8,128)(2,1)S(1)}, u32[]{:S(2)}, u32[]{:S(2)}) %collective-permute-start.11) | collective-permute-done | bytes 196640 | tf_op jit(solution)/shard_map/ppermute | solution.py:266
  55.6 0.0 collective-permute-done.12
  55.7 1.9 %collective-permute-start.15 = (bf16[192,256]{1,0:T(8,128)(2,1)S(1)}, bf16[192,256]{1,0:T(8,128)(2,1)S(1)}, u32[]{:S(2)}, u32[]{:S(2)}) collective-permute-start(bf16[192,256]{1,0:T(8,128)(2,1)S(1)} %get-tuple-element.46), channel_id=1, source_target_pairs={{0,4},{2,6},{4,0},{6,2},{8,12},{10,14},{12,8},{14,10},{16,20},{18,... | collective-permute-start | bytes 294920 | tf_op jit(solution)/shard_map/ppermute | solution.py:266
  57.6 0.0 collective-permute-start.13
  57.6 2.8 %collective-permute-done.15 = bf16[192,256]{1,0:T(8,128)(2,1)S(1)} collective-permute-done((bf16[192,256]{1,0:T(8,128)(2,1)S(1)}, bf16[192,256]{1,0:T(8,128)(2,1)S(1)}, u32[]{:S(2)}, u32[]{:S(2)}) %collective-permute-start.15) | collective-permute-done | bytes 98336 | tf_op jit(solution)/shard_map/ppermute | solution.py:266
  60.4 0.1 collective-permute-start.18
  60.5 1.8 %collective-permute-done.13 = bf16[192,256]{1,0:T(8,128)(2,1)S(1)} collective-permute-done((bf16[192,256]{1,0:T(8,128)(2,1)S(1)}, bf16[192,256]{1,0:T(8,128)(2,1)S(1)}, u32[]{:S(2)}, u32[]{:S(2)}) %collective-permute-start.13) | collective-permute-done | bytes 98336 | tf_op jit(solution)/shard_map/ppermute | solution.py:266
  62.2 0.1 collective-permute-start.17
  62.3 0.1 collective-permute-start.16
  62.4 0.5 collective-permute-start.14
  62.9 0.1 pad_add_fusion.place
  63.0 0.9 %pool_sum.1 = (bf16[256,512]{1,0:T(8,128)(2,1)}, bf16[256,512]{1,0:T(8,128)(2,1)}) custom-call(f32[256,512]{1,0:T(8,128)S(1)} %get-tuple-element.47.key_ref, f32[256,512]{1,0:T(8,128)S(1)} %get-tuple-element.48.value_ref, bf16[1,256,1024]{2,1,0:T(8,128)(2,1)S(1)} %bitcast.29), custom_call_target="tpu_custom_call" | custom-call | flops 50331648 | bytes 50331 | tf_op jit(solution)/shard_map/pool_sum/pallas_call | solution.py:238
  63.8 0.0 collective-permute-done.18.rest_3_
  63.8 0.0 collective-permute-done.17.rest_2_
  63.8 1.5 %first_rows.1.refs_2_.rest_2_ = bf16[1536,512]{1,0:T(8,128)(2,1)} custom-call(s32[3]{0:T(128)S(1)} %pad_add_fusion.place, bf16[384,256]{1,0:T(8,128)(2,1)S(1)} %constant_dynamic-update-slice_fusion.rest_0_, bf16[384,256]{1,0:T(8,128)(2,1)S(1)} %constant_dynamic-update-slice_fusion.2.rest_1_, bf16[384,256]{1,0:T(8,128)(2,1)S(1)} %collective-permute-done.17.rest_2_, ...), custom_call_target="tpu_custom_call" | custom-call | flops 201326592 | bytes 201326 | tf_op jit(solution)/shard_map/first_rows/pallas_call | solution.py:238
  65.3 4.3 %collective-permute-done.16.refs_1_ = bf16[384,256]{1,0:T(8,128)(2,1)S(1)} collective-permute-done((bf16[384,256]{1,0:T(8,128)(2,1)S(1)}, bf16[384,256]{1,0:T(8,128)(2,1)S(1)}, u32[]{:S(2)}, u32[]{:S(2)}) %collective-permute-start.16) | collective-permute-done | bytes 196640 | tf_op jit(solution)/shard_map/ppermute | solution.py:266
  69.6 0.0 collective-permute-done.14.refs_0_
  69.6 0.0 collective-permute-start.19
  69.6 0.5 collective-permute-start.20
  70.1 1.3 %own_rows.1.rest_2_ = bf16[1536,512]{1,0:T(8,128)(2,1)} custom-call(s32[3]{0:T(128)S(1)} %pad_add_fusion.place, bf16[384,256]{1,0:T(8,128)(2,1)S(1)} %get-tuple-element.50.rest_0_, bf16[384,256]{1,0:T(8,128)(2,1)S(1)} %get-tuple-element.51.rest_1_, bf16[1536,512]{1,0:T(8,128)(2,1)} %first_rows.1.refs_2_.rest_2_), custom_call_target="tpu_custom_call", output_to_operand_aliasing={{}: (3, {})} | custom-call | flops 201326592 | bytes 201326 | tf_op jit(solution)/shard_map/own_rows/pallas_call | solution.py:238
  71.5 0.0 collective-permute-done.19.rest_0_
  71.5 0.0 collective-permute-done.20.rest_1_
  71.5 1.3 %other_rows.1 = bf16[1536,512]{1,0:T(8,128)(2,1)} custom-call(s32[3]{0:T(128)S(1)} %pad_add_fusion.place, bf16[384,256]{1,0:T(8,128)(2,1)S(1)} %collective-permute-done.19.rest_0_, bf16[384,256]{1,0:T(8,128)(2,1)S(1)} %collective-permute-done.20.rest_1_, bf16[1536,512]{1,0:T(8,128)(2,1)} %own_rows.1.rest_2_), custom_call_target="tpu_custom_call", output_to_operand_aliasing={{}: (3, {})} | custom-call | flops 201326592 | bytes 201326 | tf_op jit(solution)/shard_map/other_rows/pallas_call | solution.py:238
  (21 shorter events, 0.1 us)
Async XLA Ops:
  0.6 13.1 %copy-start.7 = (s32[1536,2]{0,1:T(2,128)S(1)}, s32[1536,2]{0,1:T(2,128)}, u32[]{:S(2)}) copy-start(s32[1536,2]{0,1:T(2,128)} %param.13) | copy-start | bytes 36868
  4.5 2.7 %copy-start = (f32[2,512,1536]{2,1,0:T(8,128)}, f32[2,512,1536]{2,1,0:T(8,128)S(1)}, u32[]{:S(2)}) copy-start(f32[2,512,1536]{2,1,0:T(8,128)S(1)} %get-tuple-element.29.probs_ref) | copy-start | bytes 18874372
  7.1 2.7 %copy-start.3 = (f32[2,512,1536]{2,1,0:T(8,128)}, f32[2,512,1536]{2,1,0:T(8,128)S(1)}, u32[]{:S(2)}) copy-start(f32[2,512,1536]{2,1,0:T(8,128)S(1)} %get-tuple-element.30.dprobs_ref) | copy-start | bytes 18874372
  9.8 1.1 %copy-start.5 = (bf16[1536,512]{1,0:T(8,128)(2,1)}, bf16[1536,512]{1,0:T(8,128)(2,1)S(1)}, u32[]{:S(2)}) copy-start(bf16[1536,512]{1,0:T(8,128)(2,1)S(1)} %get-tuple-element.39.g_ref) | copy-start | bytes 4718596
  10.9 10.4 %collective-permute-start = (f32[4,1536]{1,0:T(4,128)S(1)}, f32[4,1536]{1,0:T(4,128)S(1)}, u32[]{:S(2)}, u32[]{:S(2)}) collective-permute-start(f32[4,1536]{1,0:T(4,128)S(1)} %get-tuple-element.28.delta_ref.refs_0_.centre_ref), channel_id=1, source_target_pairs={{0,2},{2,0},{4,6},{6,4},{8,10},{10,8},{12,14},{14,12},{16,18},{18,... | collective-permute-start | bytes 73736 | tf_op jit(solution)/shard_map/ppermute | solution.py:266
  11.4 10.0 %collective-permute-start.1 = (f32[4,1536]{1,0:T(4,128)S(1)}, f32[4,1536]{1,0:T(4,128)S(1)}, u32[]{:S(2)}, u32[]{:S(2)}) collective-permute-start(f32[4,1536]{1,0:T(4,128)S(1)} %get-tuple-element.28.delta_ref.refs_0_.centre_ref), channel_id=1, source_target_pairs={{0,4},{2,6},{4,0},{6,2},{8,12},{10,14},{12,8},{14,10},{16,20},{18,... | collective-permute-start | bytes 73736 | tf_op jit(solution)/shard_map/ppermute | solution.py:266
  13.5 7.8 %collective-permute-start.2 = (f32[4,1536]{1,0:T(4,128)S(1)}, f32[4,1536]{1,0:T(4,128)S(1)}, u32[]{:S(2)}, u32[]{:S(2)}) collective-permute-start(f32[4,1536]{1,0:T(4,128)S(1)} %get-tuple-element.28.delta_ref.refs_0_.centre_ref), channel_id=1, source_target_pairs={{0,6},{2,4},{4,2},{6,0},{8,14},{10,12},{12,10},{14,8},{16,22},{18,... | collective-permute-start | bytes 73736 | tf_op jit(solution)/shard_map/ppermute | solution.py:266
  13.8 2.8 %copy-start.1 = (f32[2,512,1536]{2,1,0:T(8,128)S(1)}, f32[2,512,1536]{2,1,0:T(8,128)}, u32[]{:S(2)}) copy-start(f32[2,512,1536]{2,1,0:T(8,128)} %copy-done) | copy-start | bytes 18874372
  16.5 2.8 %copy-start.4 = (f32[2,512,1536]{2,1,0:T(8,128)S(1)}, f32[2,512,1536]{2,1,0:T(8,128)}, u32[]{:S(2)}) copy-start(f32[2,512,1536]{2,1,0:T(8,128)} %copy-done.3) | copy-start | bytes 18874372
  19.3 7.4 %copy-start.2 = (f32[2,512,1536]{2,1,0:T(8,128)S(1)}, f32[2,512,1536]{2,1,0:T(8,128)}, u32[]{:S(2)}) copy-start(f32[2,512,1536]{2,1,0:T(8,128)} %copy-done) | copy-start | bytes 18874372
  21.4 10.6 %collective-permute-start.3 = (f32[2,1536,256]{2,1,0:T(8,128)S(1)}, f32[2,1536,256]{2,1,0:T(8,128)S(1)}, u32[]{:S(2)}, u32[]{:S(2)}) collective-permute-start(f32[2,1536,256]{2,1,0:T(8,128)S(1)} %get-tuple-element.32), channel_id=1, source_target_pairs={{0,2},{2,0},{4,6},{6,4},{8,10},{10,8},{12,14},{14,12},{16,18},{18,... | collective-permute-start | bytes 9437192 | tf_op jit(solution)/shard_map/ppermute | solution.py:266
  21.5 7.2 %collective-permute-start.4 = (f32[2,1536]{1,0:T(2,128)S(1)}, f32[2,1536]{1,0:T(2,128)S(1)}, u32[]{:S(2)}, u32[]{:S(2)}) collective-permute-start(f32[2,1536]{1,0:T(2,128)S(1)} %get-tuple-element.33.rest_0_), channel_id=1, source_target_pairs={{0,8},{2,10},{4,12},{6,14},{8,0},{10,2},{12,4},{14,6},{16,24},{18,... | collective-permute-start | bytes 36872 | tf_op jit(solution)/shard_map/ppermute | solution.py:266
  23.9 4.9 %collective-permute-start.5 = (f32[2,1536]{1,0:T(2,128)S(1)}, f32[2,1536]{1,0:T(2,128)S(1)}, u32[]{:S(2)}, u32[]{:S(2)}) collective-permute-start(f32[2,1536]{1,0:T(2,128)S(1)} %get-tuple-element.33.rest_0_), channel_id=1, source_target_pairs={{0,16},{2,18},{4,20},{6,22},{8,24},{10,26},{12,28},{14,30},{16,0},... | collective-permute-start | bytes 36872 | tf_op jit(solution)/shard_map/ppermute | solution.py:266
  26.5 5.5 %collective-permute-start.6 = (f32[2,1536]{1,0:T(2,128)S(1)}, f32[2,1536]{1,0:T(2,128)S(1)}, u32[]{:S(2)}, u32[]{:S(2)}) collective-permute-start(f32[2,1536]{1,0:T(2,128)S(1)} %get-tuple-element.33.rest_0_), channel_id=1, source_target_pairs={{0,24},{2,26},{4,28},{6,30},{8,16},{10,18},{12,20},{14,22},{16,8},... | collective-permute-start | bytes 36872 | tf_op jit(solution)/shard_map/ppermute | solution.py:266
  28.7 6.4 %copy-start.6 = (bf16[1536,512]{1,0:T(8,128)(2,1)S(1)}, bf16[1536,512]{1,0:T(8,128)(2,1)}, u32[]{:S(2)}) copy-start(bf16[1536,512]{1,0:T(8,128)(2,1)} %copy-done.5) | copy-start | bytes 4718596
  32.0 4.7 %slice-start = ((s8[6291456]{0:T(1024)(128)(4,1)}), s8[4194304]{0:T(1024)(128)(4,1)S(1)}, s32[]{:S(2)}) async-start(s8[6291456]{0:T(1024)(128)(4,1)} %bitcast.26), calls=%async_computation | async-start | bytes 8388608
  33.2 5.9 %collective-permute-start.7 = (bf16[384,256]{1,0:T(8,128)(2,1)S(1)}, bf16[384,256]{1,0:T(8,128)(2,1)S(1)}, u32[]{:S(2)}, u32[]{:S(2)}) collective-permute-start(bf16[384,256]{1,0:T(8,128)(2,1)S(1)} %get-tuple-element.35), channel_id=1, source_target_pairs={{0,4},{2,6},{4,0},{6,2},{8,12},{10,14},{12,8},{14,10},{16,20},{18,... | collective-permute-start | bytes 589832 | tf_op jit(solution)/shard_map/ppermute | solution.py:266
  35.1 5.7 %collective-permute-start.8 = (bf16[384,256]{1,0:T(8,128)(2,1)S(1)}, bf16[384,256]{1,0:T(8,128)(2,1)S(1)}, u32[]{:S(2)}, u32[]{:S(2)}) collective-permute-start(bf16[384,256]{1,0:T(8,128)(2,1)S(1)} %get-tuple-element.36), channel_id=1, source_target_pairs={{0,8},{2,10},{4,12},{6,14},{8,0},{10,2},{12,4},{14,6},{16,24},{18,... | collective-permute-start | bytes 589832 | tf_op jit(solution)/shard_map/ppermute | solution.py:266
  35.1 1.7 %slice-start.1 = ((s8[6291456]{0:T(1024)(128)(4,1)}), s8[2097152]{0:T(1024)(128)(4,1)S(1)}, s32[]{:S(2)}) async-start(s8[6291456]{0:T(1024)(128)(4,1)} %bitcast.26), calls=%async_computation.1 | async-start | bytes 4194304
  41.4 4.7 %collective-permute-start.10 = (bf16[192,256]{1,0:T(8,128)(2,1)S(1)}, bf16[192,256]{1,0:T(8,128)(2,1)S(1)}, u32[]{:S(2)}, u32[]{:S(2)}) collective-permute-start(bf16[192,256]{1,0:T(8,128)(2,1)S(1)} %get-tuple-element.44), channel_id=1, source_target_pairs={{0,4},{2,6},{4,0},{6,2},{8,12},{10,14},{12,8},{14,10},{16,20},{18,... | collective-permute-start | bytes 294920 | tf_op jit(solution)/shard_map/ppermute | solution.py:266
  41.6 5.1 %collective-permute-start.9 = (bf16[192,256]{1,0:T(8,128)(2,1)S(1)}, bf16[192,256]{1,0:T(8,128)(2,1)S(1)}, u32[]{:S(2)}, u32[]{:S(2)}) collective-permute-start(bf16[192,256]{1,0:T(8,128)(2,1)S(1)} %get-tuple-element.43), channel_id=1, source_target_pairs={{0,8},{2,10},{4,12},{6,14},{8,0},{10,2},{12,4},{14,6},{16,24},{18,... | collective-permute-start | bytes 294920 | tf_op jit(solution)/shard_map/ppermute | solution.py:266
  42.0 13.7 %collective-permute-start.12 = (bf16[256,1024]{1,0:T(8,128)(2,1)S(1)}, bf16[256,1024]{1,0:T(8,128)(2,1)S(1)}, u32[]{:S(2)}, u32[]{:S(2)}) collective-permute-start(bf16[256,1024]{1,0:T(8,128)(2,1)S(1)} %bitcast.30), channel_id=1, source_target_pairs={{0,1},{1,0},{2,3},{3,2},{4,5},{5,4},{6,7},{7,6},{8,9},{9,8},{10,11... | collective-permute-start | bytes 1572872 | tf_op jit(solution)/shard_map/ppermute | solution.py:270
  46.8 8.8 %collective-permute-start.11 = (bf16[2,192,256]{2,1,0:T(8,128)(2,1)S(1)}, bf16[2,192,256]{2,1,0:T(8,128)(2,1)S(1)}, u32[]{:S(2)}, u32[]{:S(2)}) collective-permute-start(bf16[2,192,256]{2,1,0:T(8,128)(2,1)S(1)} %pad_maximum_fusion.total_ref), channel_id=1, source_target_pairs={{0,16},{2,18},{4,20},{6,22},{8,24},{10,26},{12,28},{14,30},{16,0},... | collective-permute-start | bytes 589832 | tf_op jit(solution)/shard_map/ppermute | solution.py:266
  55.7 4.7 %collective-permute-start.15 = (bf16[192,256]{1,0:T(8,128)(2,1)S(1)}, bf16[192,256]{1,0:T(8,128)(2,1)S(1)}, u32[]{:S(2)}, u32[]{:S(2)}) collective-permute-start(bf16[192,256]{1,0:T(8,128)(2,1)S(1)} %get-tuple-element.46), channel_id=1, source_target_pairs={{0,4},{2,6},{4,0},{6,2},{8,12},{10,14},{12,8},{14,10},{16,20},{18,... | collective-permute-start | bytes 294920 | tf_op jit(solution)/shard_map/ppermute | solution.py:266
  57.6 4.6 %collective-permute-start.13 = (bf16[192,256]{1,0:T(8,128)(2,1)S(1)}, bf16[192,256]{1,0:T(8,128)(2,1)S(1)}, u32[]{:S(2)}, u32[]{:S(2)}) collective-permute-start(bf16[192,256]{1,0:T(8,128)(2,1)S(1)} %get-tuple-element.45), channel_id=1, source_target_pairs={{0,8},{2,10},{4,12},{6,14},{8,0},{10,2},{12,4},{14,6},{16,24},{18,... | collective-permute-start | bytes 294920 | tf_op jit(solution)/shard_map/ppermute | solution.py:266
  60.4 3.4 %collective-permute-start.18 = (bf16[384,256]{1,0:T(8,128)(2,1)S(1)}, bf16[384,256]{1,0:T(8,128)(2,1)S(1)}, u32[]{:S(2)}, u32[]{:S(2)}) collective-permute-start(bf16[384,256]{1,0:T(8,128)(2,1)S(1)} %constant_dynamic-update-slice_fusion.2.rest_1_), channel_id=1, source_target_pairs={{0,2},{2,0},{4,6},{6,4},{8,10},{10,8},{12,14},{14,12},{16,18},{18,... | collective-permute-start | bytes 589832 | tf_op jit(solution)/shard_map/ppermute | solution.py:266
  62.2 1.6 %collective-permute-start.17 = (bf16[384,256]{1,0:T(8,128)(2,1)S(1)}, bf16[384,256]{1,0:T(8,128)(2,1)S(1)}, u32[]{:S(2)}, u32[]{:S(2)}) collective-permute-start(bf16[384,256]{1,0:T(8,128)(2,1)S(1)} %constant_dynamic-update-slice_fusion.rest_0_), channel_id=1, source_target_pairs={{0,2},{2,0},{4,6},{6,4},{8,10},{10,8},{12,14},{14,12},{16,18},{18,... | collective-permute-start | bytes 589832 | tf_op jit(solution)/shard_map/ppermute | solution.py:266
  62.3 7.3 %collective-permute-start.16 = (bf16[384,256]{1,0:T(8,128)(2,1)S(1)}, bf16[384,256]{1,0:T(8,128)(2,1)S(1)}, u32[]{:S(2)}, u32[]{:S(2)}) collective-permute-start(bf16[384,256]{1,0:T(8,128)(2,1)S(1)} %constant_dynamic-update-slice_fusion.2.rest_1_), channel_id=1, source_target_pairs={{0,8},{2,10},{4,12},{6,14},{8,0},{10,2},{12,4},{14,6},{16,24},{18,... | collective-permute-start | bytes 589832 | tf_op jit(solution)/shard_map/ppermute | solution.py:266
  62.4 7.2 %collective-permute-start.14 = (bf16[384,256]{1,0:T(8,128)(2,1)S(1)}, bf16[384,256]{1,0:T(8,128)(2,1)S(1)}, u32[]{:S(2)}, u32[]{:S(2)}) collective-permute-start(bf16[384,256]{1,0:T(8,128)(2,1)S(1)} %constant_dynamic-update-slice_fusion.rest_0_), channel_id=1, source_target_pairs={{0,4},{2,6},{4,0},{6,2},{8,12},{10,14},{12,8},{14,10},{16,20},{18,... | collective-permute-start | bytes 589832 | tf_op jit(solution)/shard_map/ppermute | solution.py:266
  69.6 1.8 %collective-permute-start.19 = (bf16[384,256]{1,0:T(8,128)(2,1)S(1)}, bf16[384,256]{1,0:T(8,128)(2,1)S(1)}, u32[]{:S(2)}, u32[]{:S(2)}) collective-permute-start(bf16[384,256]{1,0:T(8,128)(2,1)S(1)} %get-tuple-element.50.rest_0_), channel_id=1, source_target_pairs={{0,2},{2,0},{4,6},{6,4},{8,10},{10,8},{12,14},{14,12},{16,18},{18,... | collective-permute-start | bytes 589832 | tf_op jit(solution)/shard_map/ppermute | solution.py:266
  69.6 1.8 %collective-permute-start.20 = (bf16[384,256]{1,0:T(8,128)(2,1)S(1)}, bf16[384,256]{1,0:T(8,128)(2,1)S(1)}, u32[]{:S(2)}, u32[]{:S(2)}) collective-permute-start(bf16[384,256]{1,0:T(8,128)(2,1)S(1)} %get-tuple-element.51.rest_1_), channel_id=1, source_target_pairs={{0,2},{2,0},{4,6},{6,4},{8,10},{10,8},{12,14},{14,12},{16,18},{18,... | collective-permute-start | bytes 589832 | tf_op jit(solution)/shard_map/ppermute | solution.py:266

commit v8 on v7

--- a/solution.py
+++ b/solution.py
@@ -12,7 +12,7 @@
 MASKED = 1e30
 NT = (((1,), (1,)), ((), ()))
 NN = (((1,), (0,)), ((), ()))
-PARAMS = pltpu.CompilerParams(vmem_limit_bytes=24 * 1024 * 1024)
+PARAMS = pltpu.CompilerParams(vmem_limit_bytes=16 * 1024 * 1024)
 IN_VMEM = pl.BlockSpec(memory_space=pltpu.VMEM)
 IN_SMEM = pl.BlockSpec(memory_space=pltpu.SMEM)
 IN_HBM = pl.BlockSpec(memory_space=pl.ANY)
@@ -27,7 +27,7 @@
 
 
 def forward_kernel(
-    compat_hbm, q_hbm, g_hbm, k_hbm, v_hbm, lse_hbm, targets_hbm,
+    place, compat_hbm, q_hbm, g_hbm, k_hbm, v_hbm, lse_hbm, targets_hbm,
     delta_ref, probs_ref, dprobs_ref, q_ref, g_ref, k_ref,
     v_ref, lse_ref, targets_ref, compat, sems, *, heads, blocks, scale,
 ):
@@ -290,13 +290,14 @@
     delta, probs, dprobs, q_near, g_near, k_near = call(
         partial(forward_kernel, heads=heads, blocks=blocks, scale=scale),
         "forward_pass",
-        tuple(
+        (place,)
+        + tuple(
             pltpu.with_memory_space_constraint(array, pltpu.HBM)
             for array in (
                 compat, queries, out_grad, pool_keys, pool_values, lse, jnp.transpose(targets)
             )
         ),
-        [IN_HBM] * 7,
+        [IN_HBM] * 8,
         [
             pltpu.VMEM((2 * heads, query_count), f32),
             pltpu.VMEM((heads, value_count, query_count), f32),
@@ -456,22 +457,24 @@
             {1 + copied: 0} if aliases else {},
         )[0]
 
-    sources = [(part, 0, chain, 0) for chain, part in enumerate(first_half)]
-    sources += [(flip(part, 1), 1, chain, 0) for chain, part in enumerate(first_half)]
-    begun = placed("first_rows", sources, key_grad, False)
-    second_half = call(
+    def sources_of(first, second, side):
+        rows = [(part, side, chain, 0) for chain, part in enumerate(first)]
+        return rows + [(part, side, chain, pieces // 2) for chain, part in enumerate(second)]
+
+    begun = placed("first_rows", sources_of(first_half, [], 0), key_grad, False)
+    halves = call(
         after_kernel,
         "after",
-        (*second_half, far(begun)),
-        [IN_HBM] * (chains + 1),
-        [pltpu.VMEM((half, width), bf16)] * chains,
+        (*first_half, *second_half, far(begun)),
+        [IN_HBM] * (2 * chains + 1),
+        [pltpu.VMEM((half, width), bf16)] * (2 * chains),
         work // 1000,
-        out_specs=[IN_HBM] * chains,
-        aliases={chain: chain for chain in range(chains)},
-    )
-    sources = [(part, 0, chain, pieces // 2) for chain, part in enumerate(second_half)]
-    begun = placed("own_rows", sources, begun, True)
-    sources = [(flip(part, 1), 1, chain, pieces // 2) for chain, part in enumerate(second_half)]
+        out_specs=[IN_HBM] * (2 * chains),
+        aliases={index: index for index in range(2 * chains)},
+    )
+    theirs = [flip(part, 1) for part in halves]
+    begun = placed("own_rows", sources_of([], halves[chains:], 0), begun, True)
+    sources = sources_of(theirs[:chains], theirs[chains:], 1)
     return placed("other_rows", sources, begun, True), key_grad, value_grad
 
 

time: 73 us -> 60.3 us (0.83)
  local copies, waits for them, and re-layouts: 12.1 us -> 0.12 us
  starting transfers between devices: 15.7 us -> 14.7 us
  waiting for transfers between devices: 25.4 us -> 26.3 us
    unnamed x22 -> x4, local copies, waits for them, and re-layouts: 12 us -> 0.02 us
    ppermute x20, waiting for transfers between devices: 25.4 us -> 26.2 us  [flip(): lax.ppermute(array, 'val', [(i, i ^ mask) for i in range(value_devices)])]
  transfers between devices with their start and end apart: 21 -> 21, of which waited for: 8 -> 10; matrix products, arithmetic and copies ran while one was open for 0% -> 0% of each run, Pallas kernels for 16% -> 19%
where the time goes in v8:
time: 60.3 us; the launch traced here: 60.1 us
  waiting for transfers between devices  26.3 us (44%)
  Pallas kernels  18.1 us (30%)
  starting transfers between devices  14.7 us (24%)
  between operations  0.87 us (1%)
    ppermute x20, waiting for transfers between devices, flip(): lax.ppermute(array, 'val', [(i, i ^ mask) for i in range(value_devices)])  26.2 us
    pallas_call x14, Pallas kernels, call(): pl.pallas_call(kernel, in_specs=in_specs, out_specs=[IN_VMEM] * len(outpu...  18.1 us
    ppermute x20, starting transfers between devices, flip(): lax.ppermute(array, 'val', [(i, i ^ mask) for i in range(value_devices)])  13.3 us
    ppermute x1, starting transfers between devices, swap_shares(): lax.ppermute(send[step - 1], 'qry', [(i, (i + step) % parts) for i in ran...  1.31 us
  transfers between devices with their start and end apart: 21, of which 10 were waited for; matrix products, arithmetic and copies ran while one was open for 0% of the time, Pallas kernels for 19%

profile of v8, /device:TPU:0, one launch (start us, length us, event | category | flops | bytes accessed | tf_op | source)
XLA Modules:
  0.0 60.1 jit_solution(11309416442592342515)
XLA Ops:
  0.7 0.1 stack.53.place
  0.8 0.0 copy-start
  0.8 3.5 %forward_pass.1 = (f32[4,1536]{1,0:T(4,128)S(1)}, f32[2,512,1536]{2,1,0:T(8,128)S(1)}, f32[2,512,1536]{2,1,0:T(8,128)S(1)}, bf16[1536,512]{1,0:T(8,128)(2,1)S(1)...) custom-call(s32[7]{0:T(128)S(1)} %stack.53.place, s32[2,1,6]{2,1,0:T(1,128)} %compat_hbm.1, ...), custom_call_target="tpu_custom_call" | custom-call | flops 1610612736 | bytes 1610612 | tf_op jit(solution)/shard_map/forward_pass/pallas_call | solution.py:238
  4.2 0.9 %collective-permute-start = (f32[4,1536]{1,0:T(4,128)S(1)}, f32[4,1536]{1,0:T(4,128)S(1)}, u32[]{:S(2)}, u32[]{:S(2)}) collective-permute-start(f32[4,1536]{1,0:T(4,128)S(1)} %get-tuple-element.30.delta_ref.refs_0_.centre_ref), channel_id=1, source_target_pairs={{0,2},{2,0},{4,6},{6,4},{8,10},{10,8},{12,14},{14,12},{16,18},{18,... | collective-permute-start | bytes 73736 | tf_op jit(solution)/shard_map/ppermute | solution.py:266
  5.1 2.2 %collective-permute-start.1 = (f32[4,1536]{1,0:T(4,128)S(1)}, f32[4,1536]{1,0:T(4,128)S(1)}, u32[]{:S(2)}, u32[]{:S(2)}) collective-permute-start(f32[4,1536]{1,0:T(4,128)S(1)} %get-tuple-element.30.delta_ref.refs_0_.centre_ref), channel_id=1, source_target_pairs={{0,4},{2,6},{4,0},{6,2},{8,12},{10,14},{12,8},{14,10},{16,20},{18,... | collective-permute-start | bytes 73736 | tf_op jit(solution)/shard_map/ppermute | solution.py:266
  7.3 0.1 collective-permute-start.2
  7.4 0.0 copy-done
  7.4 2.0 %other_head.1.refs_4_ = f32[2,1536,256]{2,1,0:T(8,128)S(1)} custom-call(s32[7]{0:T(128)S(1)} %stack.53.place, f32[4,1536]{1,0:T(4,128)S(1)} %get-tuple-element.30.delta_ref.refs_0_.centre_ref, f32[2,512,1536]{2,1,0:T(8,128)S(1)} %get-tuple-element.31.probs_ref, f32[2,512,1536]{2,1,0:T(8,128)S(1)} %get-tuple-element.32.dprobs_ref, s32[2,1536]{1,0:T(2,128)S(1)} %bitcast.30, ...), custom_call_target="tpu_custom_call" | custom-call | flops 805306368 | bytes 805306 | tf_op jit(solution)/shard_map/other_head/pallas_call | solution.py:238
  9.4 0.0 collective-permute-done.refs_1_.came_ref
  9.4 0.0 collective-permute-done.1.refs_2_
  9.4 1.2 %collective-permute-done.2.refs_3_ = f32[4,1536]{1,0:T(4,128)S(1)} collective-permute-done((f32[4,1536]{1,0:T(4,128)S(1)}, f32[4,1536]{1,0:T(4,128)S(1)}, u32[]{:S(2)}, u32[]{:S(2)}) %collective-permute-start.2) | collective-permute-done | bytes 24608 | tf_op jit(solution)/shard_map/ppermute | solution.py:266
  10.6 0.2 collective-permute-start.3
  10.8 1.5 %collective-permute-start.4 = (f32[2,1536]{1,0:T(2,128)S(1)}, f32[2,1536]{1,0:T(2,128)S(1)}, u32[]{:S(2)}, u32[]{:S(2)}) collective-permute-start(f32[2,1536]{1,0:T(2,128)S(1)} %get-tuple-element.35.rest_0_), channel_id=1, source_target_pairs={{0,8},{2,10},{4,12},{6,14},{8,0},{10,2},{12,4},{14,6},{16,24},{18,... | collective-permute-start | bytes 36872 | tf_op jit(solution)/shard_map/ppermute | solution.py:266
  12.3 3.3 %collective-permute-start.5 = (f32[2,1536]{1,0:T(2,128)S(1)}, f32[2,1536]{1,0:T(2,128)S(1)}, u32[]{:S(2)}, u32[]{:S(2)}) collective-permute-start(f32[2,1536]{1,0:T(2,128)S(1)} %get-tuple-element.35.rest_0_), channel_id=1, source_target_pairs={{0,16},{2,18},{4,20},{6,22},{8,24},{10,26},{12,28},{14,30},{16,0},... | collective-permute-start | bytes 36872 | tf_op jit(solution)/shard_map/ppermute | solution.py:266
  15.6 0.0 collective-permute-start.6
  15.6 2.0 %own_head.1.own_ref = f32[2,1536,256]{2,1,0:T(8,128)S(1)} custom-call(s32[7]{0:T(128)S(1)} %stack.53.place, f32[4,1536]{1,0:T(4,128)S(1)} %get-tuple-element.30.delta_ref.refs_0_.centre_ref, f32[2,512,1536]{2,1,0:T(8,128)S(1)} %get-tuple-element.31.probs_ref, f32[2,512,1536]{2,1,0:T(8,128)S(1)} %get-tuple-element.32.dprobs_ref, s32[2,1536]{1,0:T(2,128)S(1)} %bitcast.31, ...), custom_call_target="tpu_custom_call" | custom-call | flops 805306368 | bytes 805306 | tf_op jit(solution)/shard_map/own_head/pallas_call | solution.py:238
  17.6 0.0 collective-permute-done.4.rest_1_
  17.6 0.0 collective-permute-done.5.rest_2_
  17.6 3.5 %collective-permute-done.6.rest_3_ = f32[2,1536]{1,0:T(2,128)S(1)} collective-permute-done((f32[2,1536]{1,0:T(2,128)S(1)}, f32[2,1536]{1,0:T(2,128)S(1)}, u32[]{:S(2)}, u32[]{:S(2)}) %collective-permute-start.6) | collective-permute-done | bytes 12320 | tf_op jit(solution)/shard_map/ppermute | solution.py:266
  21.1 0.0 collective-permute-done.3.received_ref
  21.1 1.2 %combine.1 = (f32[2,384,256]{2,1,0:T(8,128)S(1)}, f32[2,1536]{1,0:T(2,128)S(1)}, bf16[384,256]{1,0:T(8,128)(2,1)S(1)}, bf16[384,256]{1,0:T(8,128)(2,1)S(1)}) custom-call(s32[7]{0:T(128)S(1)} %stack.53.place, f32[2,1536,256]{2,1,0:T(8,128)S(1)} %own_head.1.own_ref, f32[2,1536,256]{2,1,0:T(8,128)S(1)} %collective-permute-done.3.received_ref, ...), custom_call_target="tpu_custom_call" | custom-call | flops 100663296 | bytes 100663 | tf_op jit(solution)/shard_map/combine/pallas_call | solution.py:238
  22.3 0.7 %collective-permute-start.7 = (bf16[384,256]{1,0:T(8,128)(2,1)S(1)}, bf16[384,256]{1,0:T(8,128)(2,1)S(1)}, u32[]{:S(2)}, u32[]{:S(2)}) collective-permute-start(bf16[384,256]{1,0:T(8,128)(2,1)S(1)} %get-tuple-element.37), channel_id=1, source_target_pairs={{0,4},{2,6},{4,0},{6,2},{8,12},{10,14},{12,8},{14,10},{16,20},{18,... | collective-permute-start | bytes 589832 | tf_op jit(solution)/shard_map/ppermute | solution.py:266
  23.0 0.0 collective-permute-start.8
  23.0 1.5 %value_terms.1 = (f32[256,512]{1,0:T(8,128)S(1)}, bf16[1,256,512]{2,1,0:T(8,128)(2,1)S(1)}) custom-call(s32[7]{0:T(128)S(1)} %stack.53.place, f32[2,512,1536]{2,1,0:T(8,128)S(1)} %get-tuple-element.31.probs_ref, bf16[1536,512]{1,0:T(8,128)(2,1)S(1)} %get-tuple-element.41.g_ref), custom_call_target="tpu_custom_call" | custom-call | flops 805306368 | bytes 805306 | tf_op jit(solution)/shard_map/value_terms/pallas_call | solution.py:238
  24.5 2.3 %key_terms.1 = (f32[256,512]{1,0:T(8,128)S(1)}, bf16[1,256,1024]{2,1,0:T(8,128)(2,1)S(1)}) custom-call(s32[7]{0:T(128)S(1)} %stack.53.place, f32[2,1536]{1,0:T(2,128)S(1)} %get-tuple-element.39.delta_ref, f32[2,512,1536]{2,1,0:T(8,128)S(1)} %get-tuple-element.31.probs_ref, f32[2,512,1536]{2,1,0:T(8,128)S(1)} %get-tuple-element.32.dprobs_ref, ...), custom_call_target="tpu_custom_call" | custom-call | flops 805306368 | bytes 805306 | tf_op jit(solution)/shard_map/key_terms/pallas_call | solution.py:238
  26.8 1.3 %collective-permute-done.7.rest_0_ = bf16[384,256]{1,0:T(8,128)(2,1)S(1)} collective-permute-done((bf16[384,256]{1,0:T(8,128)(2,1)S(1)}, bf16[384,256]{1,0:T(8,128)(2,1)S(1)}, u32[]{:S(2)}, u32[]{:S(2)}) %collective-permute-start.7) | collective-permute-done | bytes 196640 | tf_op jit(solution)/shard_map/ppermute | solution.py:266
  28.1 0.6 %collective-permute-done.8.rest_1_ = bf16[384,256]{1,0:T(8,128)(2,1)S(1)} collective-permute-done((bf16[384,256]{1,0:T(8,128)(2,1)S(1)}, bf16[384,256]{1,0:T(8,128)(2,1)S(1)}, u32[]{:S(2)}, u32[]{:S(2)}) %collective-permute-start.8) | collective-permute-done | bytes 196640 | tf_op jit(solution)/shard_map/ppermute | solution.py:266
  28.7 0.6 %split.1 = (f32[2,192,256]{2,1,0:T(8,128)S(1)}, bf16[192,256]{1,0:T(8,128)(2,1)S(1)}, bf16[192,256]{1,0:T(8,128)(2,1)S(1)}) custom-call(s32[7]{0:T(128)S(1)} %stack.53.place, f32[2,384,256]{2,1,0:T(8,128)S(1)} %get-tuple-element.36.keep_ref, bf16[384,256]{1,0:T(8,128)(2,1)S(1)} %collective-permute-done.7.rest_0_, ...), custom_call_target="tpu_custom_call" | custom-call | flops 50331648 | bytes 50331 | tf_op jit(solution)/shard_map/split/pallas_call | solution.py:238
  29.3 1.5 %collective-permute-start.10 = (bf16[192,256]{1,0:T(8,128)(2,1)S(1)}, bf16[192,256]{1,0:T(8,128)(2,1)S(1)}, u32[]{:S(2)}, u32[]{:S(2)}) collective-permute-start(bf16[192,256]{1,0:T(8,128)(2,1)S(1)} %get-tuple-element.46), channel_id=1, source_target_pairs={{0,4},{2,6},{4,0},{6,2},{8,12},{10,14},{12,8},{14,10},{16,20},{18,... | collective-permute-start | bytes 294920 | tf_op jit(solution)/shard_map/ppermute | solution.py:266
  30.8 0.2 collective-permute-start.9
  30.9 1.3 %collective-permute-start.12 = (bf16[256,1024]{1,0:T(8,128)(2,1)S(1)}, bf16[256,1024]{1,0:T(8,128)(2,1)S(1)}, u32[]{:S(2)}, u32[]{:S(2)}) collective-permute-start(bf16[256,1024]{1,0:T(8,128)(2,1)S(1)} %bitcast.28), channel_id=1, source_target_pairs={{0,1},{1,0},{2,3},{3,2},{4,5},{5,4},{6,7},{7,6},{8,9},{9,8},{10,11... | collective-permute-start | bytes 1572872 | tf_op jit(solution)/shard_map/ppermute | solution.py:270
  32.3 1.7 %collective-permute-done.10 = bf16[192,256]{1,0:T(8,128)(2,1)S(1)} collective-permute-done((bf16[192,256]{1,0:T(8,128)(2,1)S(1)}, bf16[192,256]{1,0:T(8,128)(2,1)S(1)}, u32[]{:S(2)}, u32[]{:S(2)}) %collective-permute-start.10) | collective-permute-done | bytes 98336 | tf_op jit(solution)/shard_map/ppermute | solution.py:266
  34.0 1.7 %collective-permute-done.9 = bf16[192,256]{1,0:T(8,128)(2,1)S(1)} collective-permute-done((bf16[192,256]{1,0:T(8,128)(2,1)S(1)}, bf16[192,256]{1,0:T(8,128)(2,1)S(1)}, u32[]{:S(2)}, u32[]{:S(2)}) %collective-permute-start.9) | collective-permute-done | bytes 98336 | tf_op jit(solution)/shard_map/ppermute | solution.py:266
  35.7 0.1 fusion.2
  35.8 0.1 collective-permute-start.11
  35.8 8.8 %collective-permute-done.11.came_ref = bf16[2,192,256]{2,1,0:T(8,128)(2,1)S(1)} collective-permute-done((bf16[2,192,256]{2,1,0:T(8,128)(2,1)S(1)}, bf16[2,192,256]{2,1,0:T(8,128)(2,1)S(1)}, u32[]{:S(2)}, u32[]{:S(2)}) %collective-permute-start.11) | collective-permute-done | bytes 196640 | tf_op jit(solution)/shard_map/ppermute | solution.py:266
  44.6 0.0 collective-permute-done.12
  44.7 0.7 %collective-permute-start.14 = (bf16[192,256]{1,0:T(8,128)(2,1)S(1)}, bf16[192,256]{1,0:T(8,128)(2,1)S(1)}, u32[]{:S(2)}, u32[]{:S(2)}) collective-permute-start(bf16[192,256]{1,0:T(8,128)(2,1)S(1)} %get-tuple-element.48), channel_id=1, source_target_pairs={{0,4},{2,6},{4,0},{6,2},{8,12},{10,14},{12,8},{14,10},{16,20},{18,... | collective-permute-start | bytes 294920 | tf_op jit(solution)/shard_map/ppermute | solution.py:266
  45.4 0.0 collective-permute-start.13
  45.4 5.0 %collective-permute-done.14 = bf16[192,256]{1,0:T(8,128)(2,1)S(1)} collective-permute-done((bf16[192,256]{1,0:T(8,128)(2,1)S(1)}, bf16[192,256]{1,0:T(8,128)(2,1)S(1)}, u32[]{:S(2)}, u32[]{:S(2)}) %collective-permute-start.14) | collective-permute-done | bytes 98336 | tf_op jit(solution)/shard_map/ppermute | solution.py:266
  50.4 0.1 collective-permute-start.16
  50.5 0.0 collective-permute-done.13
  50.5 1.0 %collective-permute-start.15 = (bf16[384,256]{1,0:T(8,128)(2,1)S(1)}, bf16[384,256]{1,0:T(8,128)(2,1)S(1)}, u32[]{:S(2)}, u32[]{:S(2)}) collective-permute-start(bf16[384,256]{1,0:T(8,128)(2,1)S(1)} %constant_dynamic-update-slice_fusion.rest_0_.refs_0_), channel_id=1, source_target_pairs={{0,4},{2,6},{4,0},{6,2},{8,12},{10,14},{12,8},{14,10},{16,20},{18,... | collective-permute-start | bytes 589832 | tf_op jit(solution)/shard_map/ppermute | solution.py:266
  51.5 0.1 pad_add_fusion.place
  51.5 0.9 %pool_sum.1 = (bf16[256,512]{1,0:T(8,128)(2,1)}, bf16[256,512]{1,0:T(8,128)(2,1)}) custom-call(f32[256,512]{1,0:T(8,128)S(1)} %get-tuple-element.49.key_ref, f32[256,512]{1,0:T(8,128)S(1)} %get-tuple-element.50.value_ref, bf16[1,256,1024]{2,1,0:T(8,128)(2,1)S(1)} %bitcast.27), custom_call_target="tpu_custom_call" | custom-call | flops 50331648 | bytes 50331 | tf_op jit(solution)/shard_map/pool_sum/pallas_call | solution.py:238
  52.4 1.3 %first_rows.1.refs_4_.rest_2_ = bf16[1536,512]{1,0:T(8,128)(2,1)} custom-call(s32[3]{0:T(128)S(1)} %pad_add_fusion.place, bf16[384,256]{1,0:T(8,128)(2,1)S(1)} %constant_dynamic-update-slice_fusion.rest_0_.refs_0_, bf16[384,256]{1,0:T(8,128)(2,1)S(1)} %constant_dynamic-update-slice_fusion.2.rest_1_.refs_1_, bf16[256,512]{1,0:T(8,128)(2,1)} %get-tuple-element.28.rest_2_), custom_call_target="tpu_custom_call" | custom-call | flops 201326592 | bytes 201326 | tf_op jit(solution)/shard_map/first_rows/pallas_call | solution.py:238
  53.7 2.4 %collective-permute-done.16.refs_3_ = bf16[384,256]{1,0:T(8,128)(2,1)S(1)} collective-permute-done((bf16[384,256]{1,0:T(8,128)(2,1)S(1)}, bf16[384,256]{1,0:T(8,128)(2,1)S(1)}, u32[]{:S(2)}, u32[]{:S(2)}) %collective-permute-start.16) | collective-permute-done | bytes 196640 | tf_op jit(solution)/shard_map/ppermute | solution.py:266
  56.1 0.1 collective-permute-done.15.refs_2_
  56.2 0.0 collective-permute-start.17
  56.2 0.5 collective-permute-start.18
  56.7 0.0 collective-permute-start.19
  56.8 0.5 collective-permute-start.20
  57.3 1.3 %own_rows.1.rest_4_ = bf16[1536,512]{1,0:T(8,128)(2,1)} custom-call(s32[3]{0:T(128)S(1)} %pad_add_fusion.place, bf16[384,256]{1,0:T(8,128)(2,1)S(1)} %get-tuple-element.54.rest_0_, bf16[384,256]{1,0:T(8,128)(2,1)S(1)} %get-tuple-element.55.rest_1_, bf16[1536,512]{1,0:T(8,128)(2,1)} %first_rows.1.refs_4_.rest_2_), custom_call_target="tpu_custom_call", output_to_operand_aliasing={{}: (3, {})} | custom-call | flops 201326592 | bytes 201326 | tf_op jit(solution)/shard_map/own_rows/pallas_call | solution.py:238
  58.6 0.0 collective-permute-done.17.rest_0_
  58.6 0.0 collective-permute-done.18.rest_1_
  58.6 0.0 collective-permute-done.19.rest_2_
  58.6 0.0 collective-permute-done.20.rest_3_
  58.6 1.5 %other_rows.1 = bf16[1536,512]{1,0:T(8,128)(2,1)} custom-call(s32[3]{0:T(128)S(1)} %pad_add_fusion.place, bf16[384,256]{1,0:T(8,128)(2,1)S(1)} %collective-permute-done.17.rest_0_, bf16[384,256]{1,0:T(8,128)(2,1)S(1)} %collective-permute-done.18.rest_1_, bf16[384,256]{1,0:T(8,128)(2,1)S(1)} %collective-permute-done.19.rest_2_, ...), custom_call_target="tpu_custom_call", output_to_operand_aliasing={{}: (5, {})} | custom-call | flops 201326592 | bytes 201326 | tf_op jit(solution)/shard_map/other_rows/pallas_call | solution.py:238
  (8 shorter events, 0.1 us)
Async XLA Ops:
  0.8 6.7 %copy-start = (s32[1536,2]{0,1:T(2,128)S(1)}, s32[1536,2]{0,1:T(2,128)}, u32[]{:S(2)}) copy-start(s32[1536,2]{0,1:T(2,128)} %param.13) | copy-start | bytes 36868
  4.2 5.2 %collective-permute-start = (f32[4,1536]{1,0:T(4,128)S(1)}, f32[4,1536]{1,0:T(4,128)S(1)}, u32[]{:S(2)}, u32[]{:S(2)}) collective-permute-start(f32[4,1536]{1,0:T(4,128)S(1)} %get-tuple-element.30.delta_ref.refs_0_.centre_ref), channel_id=1, source_target_pairs={{0,2},{2,0},{4,6},{6,4},{8,10},{10,8},{12,14},{14,12},{16,18},{18,... | collective-permute-start | bytes 73736 | tf_op jit(solution)/shard_map/ppermute | solution.py:266
  5.1 4.3 %collective-permute-start.1 = (f32[4,1536]{1,0:T(4,128)S(1)}, f32[4,1536]{1,0:T(4,128)S(1)}, u32[]{:S(2)}, u32[]{:S(2)}) collective-permute-start(f32[4,1536]{1,0:T(4,128)S(1)} %get-tuple-element.30.delta_ref.refs_0_.centre_ref), channel_id=1, source_target_pairs={{0,4},{2,6},{4,0},{6,2},{8,12},{10,14},{12,8},{14,10},{16,20},{18,... | collective-permute-start | bytes 73736 | tf_op jit(solution)/shard_map/ppermute | solution.py:266
  7.3 3.3 %collective-permute-start.2 = (f32[4,1536]{1,0:T(4,128)S(1)}, f32[4,1536]{1,0:T(4,128)S(1)}, u32[]{:S(2)}, u32[]{:S(2)}) collective-permute-start(f32[4,1536]{1,0:T(4,128)S(1)} %get-tuple-element.30.delta_ref.refs_0_.centre_ref), channel_id=1, source_target_pairs={{0,6},{2,4},{4,2},{6,0},{8,14},{10,12},{12,10},{14,8},{16,22},{18,... | collective-permute-start | bytes 73736 | tf_op jit(solution)/shard_map/ppermute | solution.py:266
  10.6 10.5 %collective-permute-start.3 = (f32[2,1536,256]{2,1,0:T(8,128)S(1)}, f32[2,1536,256]{2,1,0:T(8,128)S(1)}, u32[]{:S(2)}, u32[]{:S(2)}) collective-permute-start(f32[2,1536,256]{2,1,0:T(8,128)S(1)} %get-tuple-element.34), channel_id=1, source_target_pairs={{0,2},{2,0},{4,6},{6,4},{8,10},{10,8},{12,14},{14,12},{16,18},{18,... | collective-permute-start | bytes 9437192 | tf_op jit(solution)/shard_map/ppermute | solution.py:266
  10.8 6.8 %collective-permute-start.4 = (f32[2,1536]{1,0:T(2,128)S(1)}, f32[2,1536]{1,0:T(2,128)S(1)}, u32[]{:S(2)}, u32[]{:S(2)}) collective-permute-start(f32[2,1536]{1,0:T(2,128)S(1)} %get-tuple-element.35.rest_0_), channel_id=1, source_target_pairs={{0,8},{2,10},{4,12},{6,14},{8,0},{10,2},{12,4},{14,6},{16,24},{18,... | collective-permute-start | bytes 36872 | tf_op jit(solution)/shard_map/ppermute | solution.py:266
  12.3 5.3 %collective-permute-start.5 = (f32[2,1536]{1,0:T(2,128)S(1)}, f32[2,1536]{1,0:T(2,128)S(1)}, u32[]{:S(2)}, u32[]{:S(2)}) collective-permute-start(f32[2,1536]{1,0:T(2,128)S(1)} %get-tuple-element.35.rest_0_), channel_id=1, source_target_pairs={{0,16},{2,18},{4,20},{6,22},{8,24},{10,26},{12,28},{14,30},{16,0},... | collective-permute-start | bytes 36872 | tf_op jit(solution)/shard_map/ppermute | solution.py:266
  15.6 5.5 %collective-permute-start.6 = (f32[2,1536]{1,0:T(2,128)S(1)}, f32[2,1536]{1,0:T(2,128)S(1)}, u32[]{:S(2)}, u32[]{:S(2)}) collective-permute-start(f32[2,1536]{1,0:T(2,128)S(1)} %get-tuple-element.35.rest_0_), channel_id=1, source_target_pairs={{0,24},{2,26},{4,28},{6,30},{8,16},{10,18},{12,20},{14,22},{16,8},... | collective-permute-start | bytes 36872 | tf_op jit(solution)/shard_map/ppermute | solution.py:266
  22.3 5.7 %collective-permute-start.7 = (bf16[384,256]{1,0:T(8,128)(2,1)S(1)}, bf16[384,256]{1,0:T(8,128)(2,1)S(1)}, u32[]{:S(2)}, u32[]{:S(2)}) collective-permute-start(bf16[384,256]{1,0:T(8,128)(2,1)S(1)} %get-tuple-element.37), channel_id=1, source_target_pairs={{0,4},{2,6},{4,0},{6,2},{8,12},{10,14},{12,8},{14,10},{16,20},{18,... | collective-permute-start | bytes 589832 | tf_op jit(solution)/shard_map/ppermute | solution.py:266
  23.0 5.7 %collective-permute-start.8 = (bf16[384,256]{1,0:T(8,128)(2,1)S(1)}, bf16[384,256]{1,0:T(8,128)(2,1)S(1)}, u32[]{:S(2)}, u32[]{:S(2)}) collective-permute-start(bf16[384,256]{1,0:T(8,128)(2,1)S(1)} %get-tuple-element.38), channel_id=1, source_target_pairs={{0,8},{2,10},{4,12},{6,14},{8,0},{10,2},{12,4},{14,6},{16,24},{18,... | collective-permute-start | bytes 589832 | tf_op jit(solution)/shard_map/ppermute | solution.py:266
  29.3 4.7 %collective-permute-start.10 = (bf16[192,256]{1,0:T(8,128)(2,1)S(1)}, bf16[192,256]{1,0:T(8,128)(2,1)S(1)}, u32[]{:S(2)}, u32[]{:S(2)}) collective-permute-start(bf16[192,256]{1,0:T(8,128)(2,1)S(1)} %get-tuple-element.46), channel_id=1, source_target_pairs={{0,4},{2,6},{4,0},{6,2},{8,12},{10,14},{12,8},{14,10},{16,20},{18,... | collective-permute-start | bytes 294920 | tf_op jit(solution)/shard_map/ppermute | solution.py:266
  30.8 4.9 %collective-permute-start.9 = (bf16[192,256]{1,0:T(8,128)(2,1)S(1)}, bf16[192,256]{1,0:T(8,128)(2,1)S(1)}, u32[]{:S(2)}, u32[]{:S(2)}) collective-permute-start(bf16[192,256]{1,0:T(8,128)(2,1)S(1)} %get-tuple-element.45), channel_id=1, source_target_pairs={{0,8},{2,10},{4,12},{6,14},{8,0},{10,2},{12,4},{14,6},{16,24},{18,... | collective-permute-start | bytes 294920 | tf_op jit(solution)/shard_map/ppermute | solution.py:266
  30.9 13.7 %collective-permute-start.12 = (bf16[256,1024]{1,0:T(8,128)(2,1)S(1)}, bf16[256,1024]{1,0:T(8,128)(2,1)S(1)}, u32[]{:S(2)}, u32[]{:S(2)}) collective-permute-start(bf16[256,1024]{1,0:T(8,128)(2,1)S(1)} %bitcast.28), channel_id=1, source_target_pairs={{0,1},{1,0},{2,3},{3,2},{4,5},{5,4},{6,7},{7,6},{8,9},{9,8},{10,11... | collective-permute-start | bytes 1572872 | tf_op jit(solution)/shard_map/ppermute | solution.py:270
  35.8 8.8 %collective-permute-start.11 = (bf16[2,192,256]{2,1,0:T(8,128)(2,1)S(1)}, bf16[2,192,256]{2,1,0:T(8,128)(2,1)S(1)}, u32[]{:S(2)}, u32[]{:S(2)}) collective-permute-start(bf16[2,192,256]{2,1,0:T(8,128)(2,1)S(1)} %pad_maximum_fusion.total_ref), channel_id=1, source_target_pairs={{0,16},{2,18},{4,20},{6,22},{8,24},{10,26},{12,28},{14,30},{16,0},... | collective-permute-start | bytes 589832 | tf_op jit(solution)/shard_map/ppermute | solution.py:266
  44.7 5.7 %collective-permute-start.14 = (bf16[192,256]{1,0:T(8,128)(2,1)S(1)}, bf16[192,256]{1,0:T(8,128)(2,1)S(1)}, u32[]{:S(2)}, u32[]{:S(2)}) collective-permute-start(bf16[192,256]{1,0:T(8,128)(2,1)S(1)} %get-tuple-element.48), channel_id=1, source_target_pairs={{0,4},{2,6},{4,0},{6,2},{8,12},{10,14},{12,8},{14,10},{16,20},{18,... | collective-permute-start | bytes 294920 | tf_op jit(solution)/shard_map/ppermute | solution.py:266
  45.4 5.1 %collective-permute-start.13 = (bf16[192,256]{1,0:T(8,128)(2,1)S(1)}, bf16[192,256]{1,0:T(8,128)(2,1)S(1)}, u32[]{:S(2)}, u32[]{:S(2)}) collective-permute-start(bf16[192,256]{1,0:T(8,128)(2,1)S(1)} %get-tuple-element.47), channel_id=1, source_target_pairs={{0,8},{2,10},{4,12},{6,14},{8,0},{10,2},{12,4},{14,6},{16,24},{18,... | collective-permute-start | bytes 294920 | tf_op jit(solution)/shard_map/ppermute | solution.py:266
  50.4 5.7 %collective-permute-start.16 = (bf16[384,256]{1,0:T(8,128)(2,1)S(1)}, bf16[384,256]{1,0:T(8,128)(2,1)S(1)}, u32[]{:S(2)}, u32[]{:S(2)}) collective-permute-start(bf16[384,256]{1,0:T(8,128)(2,1)S(1)} %constant_dynamic-update-slice_fusion.2.rest_1_.refs_1_), channel_id=1, source_target_pairs={{0,8},{2,10},{4,12},{6,14},{8,0},{10,2},{12,4},{14,6},{16,24},{18,... | collective-permute-start | bytes 589832 | tf_op jit(solution)/shard_map/ppermute | solution.py:266
  50.5 5.7 %collective-permute-start.15 = (bf16[384,256]{1,0:T(8,128)(2,1)S(1)}, bf16[384,256]{1,0:T(8,128)(2,1)S(1)}, u32[]{:S(2)}, u32[]{:S(2)}) collective-permute-start(bf16[384,256]{1,0:T(8,128)(2,1)S(1)} %constant_dynamic-update-slice_fusion.rest_0_.refs_0_), channel_id=1, source_target_pairs={{0,4},{2,6},{4,0},{6,2},{8,12},{10,14},{12,8},{14,10},{16,20},{18,... | collective-permute-start | bytes 589832 | tf_op jit(solution)/shard_map/ppermute | solution.py:266
  56.2 2.4 %collective-permute-start.17 = (bf16[384,256]{1,0:T(8,128)(2,1)S(1)}, bf16[384,256]{1,0:T(8,128)(2,1)S(1)}, u32[]{:S(2)}, u32[]{:S(2)}) collective-permute-start(bf16[384,256]{1,0:T(8,128)(2,1)S(1)} %get-tuple-element.52), channel_id=1, source_target_pairs={{0,2},{2,0},{4,6},{6,4},{8,10},{10,8},{12,14},{14,12},{16,18},{18,... | collective-permute-start | bytes 589832 | tf_op jit(solution)/shard_map/ppermute | solution.py:266
  56.2 2.4 %collective-permute-start.18 = (bf16[384,256]{1,0:T(8,128)(2,1)S(1)}, bf16[384,256]{1,0:T(8,128)(2,1)S(1)}, u32[]{:S(2)}, u32[]{:S(2)}) collective-permute-start(bf16[384,256]{1,0:T(8,128)(2,1)S(1)} %get-tuple-element.53), channel_id=1, source_target_pairs={{0,2},{2,0},{4,6},{6,4},{8,10},{10,8},{12,14},{14,12},{16,18},{18,... | collective-permute-start | bytes 589832 | tf_op jit(solution)/shard_map/ppermute | solution.py:266
  56.7 1.9 %collective-permute-start.19 = (bf16[384,256]{1,0:T(8,128)(2,1)S(1)}, bf16[384,256]{1,0:T(8,128)(2,1)S(1)}, u32[]{:S(2)}, u32[]{:S(2)}) collective-permute-start(bf16[384,256]{1,0:T(8,128)(2,1)S(1)} %get-tuple-element.54.rest_0_), channel_id=1, source_target_pairs={{0,2},{2,0},{4,6},{6,4},{8,10},{10,8},{12,14},{14,12},{16,18},{18,... | collective-permute-start | bytes 589832 | tf_op jit(solution)/shard_map/ppermute | solution.py:266
  56.8 1.9 %collective-permute-start.20 = (bf16[384,256]{1,0:T(8,128)(2,1)S(1)}, bf16[384,256]{1,0:T(8,128)(2,1)S(1)}, u32[]{:S(2)}, u32[]{:S(2)}) collective-permute-start(bf16[384,256]{1,0:T(8,128)(2,1)S(1)} %get-tuple-element.55.rest_1_), channel_id=1, source_target_pairs={{0,2},{2,0},{4,6},{6,4},{8,10},{10,8},{12,14},{14,12},{16,18},{18,... | collective-permute-start | bytes 589832 | tf_op jit(solution)/shard_map/ppermute | solution.py:266

commit v9 on v8

--- a/solution.py
+++ b/solution.py
@@ -88,7 +88,7 @@
                 dprobs_ref[head, :, rows] = jnp.zeros((value_count, block), jnp.float32)
 
 
-def value_kernel(place, probs_ref, g_ref, own_ref, send_ref):
+def value_kernel(place, probs_ref, g_ref, after_ref, own_ref, send_ref):
     heads, _, _ = probs_ref.shape
     width = g_ref.shape[1] // heads
     share = own_ref.shape[0]
@@ -137,7 +137,7 @@
     place, own_ref, received_ref, centre_ref, came_ref, *rest, deltas, scale
 ):
     added, (keep_ref, sum_ref, *send_refs) = rest[:deltas], rest[deltas:]
-    chains, rows, width = keep_ref.shape
+    rows, width = keep_ref.shape
     heads = sum_ref.shape[0]
     sum_ref[...] = sum(ref[...] for ref in added)
 
@@ -145,28 +145,26 @@
         row = sum_ref[pl.ds(place[2], 1), span] - ref[pl.ds(heads + place[2], 1), span]
         return jnp.transpose(jnp.broadcast_to(row * scale, (128, rows)))
 
-    for other in (1, 0):
-        for chain in range(chains):
-            target = send_refs[chain] if other else keep_ref.at[chain]
-            span = ways((2 * chain + (place[3 + chain] ^ other)) * rows, rows)
-            gaps = column(centre_ref, span), column(came_ref, span)
-            for start in range(0, width, 128):
-                columns = slice(start, start + 128)
-                direct = own_ref[0, span, columns] + received_ref[0, span, columns]
-                weighted = own_ref[1, span, columns] * gaps[0]
-                weighted += received_ref[1, span, columns] * gaps[1]
-                target[:, columns] = (scale * direct - weighted).astype(target.dtype)
+    for step in range(4):
+        target = send_refs[step - 1] if step else keep_ref
+        span = ways((place[3] ^ step) * rows, rows)
+        gaps = column(centre_ref, span), column(came_ref, span)
+        for start in range(0, width, 128):
+            columns = slice(start, start + 128)
+            direct = own_ref[0, span, columns] + received_ref[0, span, columns]
+            weighted = own_ref[1, span, columns] * gaps[0]
+            weighted += received_ref[1, span, columns] * gaps[1]
+            target[:, columns] = (scale * direct - weighted).astype(target.dtype)
 
 
 def key_kernel(
-    place, delta_ref, probs_ref, dprobs_ref, targets_ref, q_ref, values_ref, own_ref, send_ref,
+    place, delta_ref, probs_ref, dprobs_ref, targets_ref, q_ref, own_ref, send_ref,
     low_ref, *, chunk, scale,
 ):
     heads = probs_ref.shape[0]
     width = own_ref.shape[1] // heads
     share = own_ref.shape[0]
     parts = send_ref.shape[0] + 1
-    send_ref[:, :, heads * width :] = values_ref[...]
     for head in range(heads):
         columns = slice(head * width, (head + 1) * width)
         for start in range(0, q_ref.shape[0], chunk):
@@ -183,30 +181,25 @@
                 send_ref[step - 1, :, columns] = term.astype(jnp.bfloat16)
 
 
-def split_kernel(place, keep_ref, *rest):
-    chains = keep_ref.shape[0]
-    came_refs, kept_ref, sent_refs = rest[:chains], rest[chains + 1], rest[chains + 2 :]
-    rows = kept_ref.shape[1]
-    for chain in range(chains):
-        for other in (1, 0):
-            target = sent_refs[chain] if other else kept_ref.at[chain]
-            span = ways((place[3 + chains + chain] ^ other) * rows, rows)
-            total = keep_ref[chain, span, :] + came_refs[chain][span, :].astype(jnp.float32)
-            target[...] = total.astype(target.dtype)
-
-
-def join_kernel(total_ref, came_ref, after_ref, *out_refs):
-    for chain, out_ref in enumerate(out_refs):
-        total = total_ref[chain].astype(jnp.float32) + came_ref[chain].astype(jnp.float32)
-        out_ref[...] = total.astype(jnp.bfloat16)
-
-
-def pool_kernel(key_ref, value_ref, received_ref, key_out, value_out):
-    wide = key_ref.shape[1]
+def reduce_kernel(
+    keep_ref, first_ref, second_ref, third_ref, after_value_ref, after_key_ref, out_ref
+):
+    total = keep_ref[...]
+    for ref in (first_ref, second_ref, third_ref):
+        total += ref[...].astype(jnp.float32)
+    out_ref[...] = total.astype(out_ref.dtype)
+
+
+def join_kernel(total_ref, came_ref, after_value_ref, after_key_ref, out_ref):
+    total = total_ref[...].astype(jnp.float32) + came_ref[...].astype(jnp.float32)
+    out_ref[...] = total.astype(jnp.bfloat16)
+
+
+def pool_kernel(key_ref, value_ref, key_came_ref, value_came_ref, key_out, value_out):
     key_sum, value_sum = key_ref[...], value_ref[...]
-    for step in range(received_ref.shape[0]):
-        key_sum += received_ref[step, :, :wide].astype(jnp.float32)
-        value_sum += received_ref[step, :, wide:].astype(jnp.float32)
+    for step in range(key_came_ref.shape[0]):
+        key_sum += key_came_ref[step].astype(jnp.float32)
+        value_sum += value_came_ref[step].astype(jnp.float32)
     key_out[...] = key_sum.astype(jnp.bfloat16)
     value_out[...] = value_sum.astype(jnp.bfloat16)
 
@@ -215,15 +208,15 @@
     pass
 
 
-def place_kernel(place, *rest, sources, pieces, piece):
+def place_kernel(place, *rest, sources, piece):
     out_ref, sems = rest[-2:]
     copies = []
-    for ref, (side, chain, first) in zip(rest, sources):
+    for ref, (side, step) in zip(rest, sources):
         width = ref.shape[1]
         columns = ways((place[0] ^ side) * width, width)
-        for index in range(ref.shape[0] // piece):
-            natural = chain * pieces + ((first + index) ^ place[1 + chain])
-            rows = ways(natural * piece, piece)
+        pieces = ref.shape[0] // piece
+        for index in range(pieces):
+            rows = ways(((place[1] ^ step) * pieces + (index ^ place[2])) * piece, piece)
             copies.append(
                 pltpu.make_async_copy(
                     ref.at[pl.ds(index * piece, piece)], out_ref.at[rows, columns], sems.at[len(copies)]
@@ -279,12 +272,8 @@
     def bit_of(bit):
         return lax.rem(val // (1 << bit), 2)
 
-    pieces = 1 << (bits - 2)
-    chains = 2 if query_count % (2 * pieces * 16) == 0 else 1
-    orders = [[1, 2], [2, 1]][:chains]
-    place = jnp.stack(
-        [val, qry, core] + [bit_of(order[stage]) for stage in range(2) for order in orders]
-    ).astype(jnp.int32)
+    square = lax.rem(val // 2, 4)
+    place = jnp.stack([val, qry, core, square]).astype(jnp.int32)
     work = 2 * query_count * value_count * width
 
     delta, probs, dprobs, q_near, g_near, k_near = call(
@@ -319,9 +308,6 @@
         pltpu.VMEM((share, wide), f32),
         pltpu.VMEM((parts - 1, share, wide), bf16),
     ]
-    value_own, value_send = call(
-        value_kernel, "value_terms", (place, probs, g_near), [IN_SMEM] + [IN_VMEM] * 2, shares, 2 * work
-    )
     chunk = query_count // 3 if query_count % 384 == 0 else query_count
     rows_of = pltpu.VMEM((2, query_count, width), f32)
     targets = jnp.transpose(targets)
@@ -360,122 +346,113 @@
         if stride == 1:
             other_centre = added[1]
         stride *= steps
-    half = query_count // (2 * chains)
+    quarter = query_count // 4
+    near_part = pltpu.VMEM((quarter, width), bf16)
     keep, delta, *send = call(
         partial(combine_kernel, deltas=len(added), scale=scale),
         "combine",
         (place, query_terms(True, "own_head"), received, centre, other_centre, *added),
         [IN_SMEM] + [IN_VMEM] * (4 + len(added)),
         [
-            pltpu.VMEM((chains, half, width), f32),
+            pltpu.VMEM((quarter, width), f32),
             pltpu.VMEM((heads, query_count), f32),
         ]
-        + [pltpu.VMEM((half, width), bf16)] * chains,
+        + [near_part] * 3,
         work // 4,
     )
-    key_own, pool_send = call(
+    value_own, value_send = call(
+        value_kernel,
+        "value_terms",
+        (place, probs, g_near, delta),
+        [IN_SMEM] + [IN_VMEM] * 2 + [IN_HBM],
+        shares,
+        2 * work,
+    )
+    value_came = swap_shares(value_send)
+    key_own, key_send = call(
         partial(key_kernel, chunk=chunk, scale=scale),
         "key_terms",
-        (place, delta, probs, dprobs, targets, q_near, value_send),
-        [IN_SMEM] + [IN_VMEM] * 6,
-        [shares[0], pltpu.VMEM((parts - 1, share, 2 * wide), bf16)],
+        (place, delta, probs, dprobs, targets, q_near),
+        [IN_SMEM] + [IN_VMEM] * 5,
+        shares,
         2 * work,
         [pltpu.VMEM((heads, value_count, query_count), bf16)],
     )
-    pool_received = swap_shares(pool_send)
-
-    came = [flip(send[chain], 1 << order[0]) for chain, order in enumerate(orders)]
-    kept, *sent = call(
-        split_kernel,
-        "split",
-        (place, keep, *came, pool_send),
-        [IN_SMEM] + [IN_VMEM] * (1 + chains) + [IN_HBM],
-        [pltpu.VMEM((chains, half // 2, width), f32)]
-        + [pltpu.VMEM((half // 2, width), bf16)] * chains,
+    key_came = swap_shares(key_send)
+
+    came = [flip(send[step - 1], 2 * step) for step in range(1, 4)]
+    (total,) = call(
+        reduce_kernel,
+        "reduce",
+        (keep, *came, value_send, key_send),
+        [IN_VMEM] * 4 + [IN_HBM] * 2,
+        [near_part if bits == 4 else pltpu.VMEM((quarter, width), f32)],
         work // 8,
     )
-    total = jnp.stack(
-        [
-            kept[chain] + flip(sent[chain], 1 << order[1]).astype(f32)
-            for chain, order in enumerate(orders)
-        ]
-    )
     for bit in range(3, bits - 1):
-        split = total.reshape(chains, 2, -1, width)
-        pick = partial(lax.dynamic_index_in_dim, split, axis=1, keepdims=False)
+        split = total.reshape(2, -1, width)
+        pick = partial(lax.dynamic_index_in_dim, split, axis=0, keepdims=False)
         came = flip(pick(1 - bit_of(bit)).astype(bf16), 1 << bit)
         total = pick(bit_of(bit)) + came.astype(f32)
     total = total.astype(bf16)
-    piece = total.shape[1]
-    joined = call(
+    piece = total.shape[0]
+    (part,) = call(
         join_kernel,
         "join",
-        (total, flip(total, 1 << (bits - 1)), pool_received),
-        [IN_VMEM] * 2 + [IN_HBM],
-        [pltpu.VMEM((piece, width), bf16)] * chains,
+        (total, flip(total, 1 << (bits - 1)), value_came, key_came),
+        [IN_VMEM] * 2 + [IN_HBM] * 2,
+        [pltpu.VMEM((piece, width), bf16)],
         work // 16,
     )
+    inner = 0
+    for bit in range(bits - 2, 2, -1):
+        part = jnp.concatenate([part, flip(part, 1 << bit)], axis=0)
+    for bit in range(3, bits - 1):
+        inner = 2 * inner + bit_of(bit)
+
     key_grad, value_grad = call(
         pool_kernel,
         "pool_sum",
-        (key_own, value_own, pool_received),
-        [IN_VMEM] * 3,
+        (key_own, value_own, key_came, value_came),
+        [IN_VMEM] * 4,
         [pltpu.HBM((share, wide), bf16)] * 2,
         work // 8,
     )
-    first_half, second_half, own_piece = [], [], []
-    for chain, order in enumerate(orders):
-        part = joined[chain]
-        for bit in list(range(bits - 2, 2, -1)) + [order[1]]:
-            part = jnp.concatenate([part, flip(part, 1 << bit)], axis=0)
-        first_half.append(part)
-        second_half.append(flip(part, 1 << order[0]))
-        index = 0
-        for bit in order + list(range(3, bits - 1)):
-            index = 2 * index + bit_of(bit)
-        own_piece.append(index)
-    pieces_place = jnp.stack([core] + own_piece).astype(jnp.int32)
+    others = [flip(part, 2 * step) for step in range(1, 4)]
+    pieces_place = jnp.stack([core, square, inner]).astype(jnp.int32)
     near = partial(pltpu.with_memory_space_constraint, memory_space=pltpu.VMEM)
     far = partial(pltpu.with_memory_space_constraint, memory_space=pltpu.HBM)
 
     def placed(name, sources, before, aliases):
         copied = len(sources)
         return call(
-            partial(
-                place_kernel,
-                sources=[source[1:] for source in sources],
-                pieces=pieces,
-                piece=piece,
-            ),
+            partial(place_kernel, sources=[source[1:] for source in sources], piece=piece),
             name,
             (pieces_place, *[near(source[0]) for source in sources], far(before)),
             [IN_SMEM] + [IN_VMEM] * copied + [IN_HBM],
             [pltpu.HBM((query_count, wide), bf16)],
             work // 2,
-            [pltpu.SemaphoreType.DMA((copied * pieces // 2,))],
+            [pltpu.SemaphoreType.DMA((copied * quarter // piece,))],
             [IN_HBM],
             {1 + copied: 0} if aliases else {},
         )[0]
 
-    def sources_of(first, second, side):
-        rows = [(part, side, chain, 0) for chain, part in enumerate(first)]
-        return rows + [(part, side, chain, pieces // 2) for chain, part in enumerate(second)]
-
-    begun = placed("first_rows", sources_of(first_half, [], 0), key_grad, False)
-    halves = call(
+    begun = placed("first_rows", [(part, 0, 0)], key_grad, False)
+    part, first_other = call(
         after_kernel,
         "after",
-        (*first_half, *second_half, far(begun)),
-        [IN_HBM] * (2 * chains + 1),
-        [pltpu.VMEM((half, width), bf16)] * (2 * chains),
+        (part, others[0], far(begun)),
+        [IN_HBM] * 3,
+        [near_part] * 2,
         work // 1000,
-        out_specs=[IN_HBM] * (2 * chains),
-        aliases={index: index for index in range(2 * chains)},
-    )
-    theirs = [flip(part, 1) for part in halves]
-    begun = placed("own_rows", sources_of([], halves[chains:], 0), begun, True)
-    sources = sources_of(theirs[:chains], theirs[chains:], 1)
-    return placed("other_rows", sources, begun, True), key_grad, value_grad
+        out_specs=[IN_HBM] * 2,
+        aliases={0: 0, 1: 1},
+    )
+    quarters = [part, first_other] + others[1:]
+    theirs = [(flip(array, 1), 1, step) for step, array in enumerate(quarters)]
+    mine = [(array, 0, step) for step, array in enumerate(quarters) if step]
+    begun = placed("own_rows", mine, begun, True)
+    return placed("other_rows", theirs, begun, True), key_grad, value_grad
 
 
 def solution(mesh):

time: 60.3 us -> 57.2 us (0.949)
  waiting for transfers between devices: 26.3 us -> 19.7 us
  starting transfers between devices: 14.7 us -> 18.8 us
  Pallas kernels: 18.1 us -> 17.1 us
    ppermute x20 -> x18, waiting for transfers between devices: 26.2 us -> 13.1 us  [flip(): lax.ppermute(array, 'val', [(i, i ^ mask) for i in range(value_devices)])]
    ppermute x1 -> x2, waiting for transfers between devices: 0.01 us -> 6.57 us  [swap_shares(): lax.ppermute(send[step - 1], 'qry', [(i, (i + step) % parts) for i in ran...]
    ppermute x20 -> x18, starting transfers between devices: 13.3 us -> 16.7 us  [flip(): lax.ppermute(array, 'val', [(i, i ^ mask) for i in range(value_devices)])]
    pallas_call x14, Pallas kernels: 18.1 us -> 17.1 us  [call(): pl.pallas_call(kernel, in_specs=in_specs, out_specs=[IN_VMEM] * len(outpu...]
    ppermute x1 -> x2, starting transfers between devices: 1.31 us -> 2.16 us  [swap_shares(): lax.ppermute(send[step - 1], 'qry', [(i, (i + step) % parts) for i in ran...]
  transfers between devices with their start and end apart: 21 -> 20, of which waited for: 10 -> 10; matrix products, arithmetic and copies ran while one was open for 0% -> 0% of each run, Pallas kernels for 19% -> 20%
where the time goes in v9:
time: 57.2 us; the launch traced here: 56.6 us
  waiting for transfers between devices  19.7 us (34%)
  starting transfers between devices  18.8 us (33%)
  Pallas kernels  17.1 us (30%)
  between operations  0.79 us (1%)
    pallas_call x14, Pallas kernels, call(): pl.pallas_call(kernel, in_specs=in_specs, out_specs=[IN_VMEM] * len(outpu...  17.1 us
    ppermute x18, starting transfers between devices, flip(): lax.ppermute(array, 'val', [(i, i ^ mask) for i in range(value_devices)])  16.7 us
    ppermute x18, waiting for transfers between devices, flip(): lax.ppermute(array, 'val', [(i, i ^ mask) for i in range(value_devices)])  13.1 us
    ppermute x2, waiting for transfers between devices, swap_shares(): lax.ppermute(send[step - 1], 'qry', [(i, (i + step) % parts) for i in ran...  6.57 us
    ppermute x2, starting transfers between devices, swap_shares(): lax.ppermute(send[step - 1], 'qry', [(i, (i + step) % parts) for i in ran...  2.16 us
  transfers between devices with their start and end apart: 20, of which 10 were waited for; matrix products, arithmetic and copies ran while one was open for 0% of the time, Pallas kernels for 20%

profile of v9, /device:TPU:0, one launch (start us, length us, event | category | flops | bytes accessed | tf_op | source)
XLA Modules:
  0.0 56.6 jit_solution(14938954362610835276)
XLA Ops:
  0.7 0.1 pad_add_fusion.1.place
  0.7 0.0 copy-start
  0.7 3.1 %forward_pass.1 = (f32[4,1536]{1,0:T(4,128)S(1)}, f32[2,512,1536]{2,1,0:T(8,128)S(1)}, f32[2,512,1536]{2,1,0:T(8,128)S(1)}, bf16[1536,512]{1,0:T(8,128)(2,1)S(1)...) custom-call(s32[4]{0:T(128)S(1)} %pad_add_fusion.1.place, s32[2,1,6]{2,1,0:T(1,128)} %compat_hbm.1, ...), custom_call_target="tpu_custom_call" | custom-call | flops 1610612736 | bytes 1610612 | tf_op jit(solution)/shard_map/forward_pass/pallas_call | solution.py:231
  3.9 0.2 collective-permute-start
  4.1 2.9 %collective-permute-start.1 = (f32[4,1536]{1,0:T(4,128)S(1)}, f32[4,1536]{1,0:T(4,128)S(1)}, u32[]{:S(2)}, u32[]{:S(2)}) collective-permute-start(f32[4,1536]{1,0:T(4,128)S(1)} %get-tuple-element.24.delta_ref.refs_0_.centre_ref), channel_id=1, source_target_pairs={{0,4},{2,6},{4,0},{6,2},{8,12},{10,14},{12,8},{14,10},{16,20},{18,... | collective-permute-start | bytes 73736 | tf_op jit(solution)/shard_map/ppermute | solution.py:259
  7.0 0.1 collective-permute-start.2
  7.0 0.0 copy-done
  7.0 2.0 %other_head.1.refs_4_ = f32[2,1536,256]{2,1,0:T(8,128)S(1)} custom-call(s32[4]{0:T(128)S(1)} %pad_add_fusion.1.place, f32[4,1536]{1,0:T(4,128)S(1)} %get-tuple-element.24.delta_ref.refs_0_.centre_ref, f32[2,512,1536]{2,1,0:T(8,128)S(1)} %get-tuple-element.25.probs_ref, f32[2,512,1536]{2,1,0:T(8,128)S(1)} %get-tuple-element.26.dprobs_ref, ...), custom_call_target="tpu_custom_call" | custom-call | flops 805306368 | bytes 805306 | tf_op jit(solution)/shard_map/other_head/pallas_call | solution.py:231
  9.0 0.0 collective-permute-done.refs_1_.came_ref
  9.0 0.0 collective-permute-done.1.refs_2_
  9.1 1.2 %collective-permute-done.2.refs_3_ = f32[4,1536]{1,0:T(4,128)S(1)} collective-permute-done((f32[4,1536]{1,0:T(4,128)S(1)}, f32[4,1536]{1,0:T(4,128)S(1)}, u32[]{:S(2)}, u32[]{:S(2)}) %collective-permute-start.2) | collective-permute-done | bytes 24608 | tf_op jit(solution)/shard_map/ppermute | solution.py:259
  10.2 0.2 collective-permute-start.3
  10.5 2.6 %collective-permute-start.4 = (f32[2,1536]{1,0:T(2,128)S(1)}, f32[2,1536]{1,0:T(2,128)S(1)}, u32[]{:S(2)}, u32[]{:S(2)}) collective-permute-start(f32[2,1536]{1,0:T(2,128)S(1)} %get-tuple-element.29.rest_0_), channel_id=1, source_target_pairs={{0,8},{2,10},{4,12},{6,14},{8,0},{10,2},{12,4},{14,6},{16,24},{18,... | collective-permute-start | bytes 36872 | tf_op jit(solution)/shard_map/ppermute | solution.py:259
  13.1 1.9 %collective-permute-start.5 = (f32[2,1536]{1,0:T(2,128)S(1)}, f32[2,1536]{1,0:T(2,128)S(1)}, u32[]{:S(2)}, u32[]{:S(2)}) collective-permute-start(f32[2,1536]{1,0:T(2,128)S(1)} %get-tuple-element.29.rest_0_), channel_id=1, source_target_pairs={{0,16},{2,18},{4,20},{6,22},{8,24},{10,26},{12,28},{14,30},{16,0},... | collective-permute-start | bytes 36872 | tf_op jit(solution)/shard_map/ppermute | solution.py:259
  15.0 0.5 collective-permute-start.6
  15.5 2.0 %own_head.1.own_ref = f32[2,1536,256]{2,1,0:T(8,128)S(1)} custom-call(s32[4]{0:T(128)S(1)} %pad_add_fusion.1.place, f32[4,1536]{1,0:T(4,128)S(1)} %get-tuple-element.24.delta_ref.refs_0_.centre_ref, f32[2,512,1536]{2,1,0:T(8,128)S(1)} %get-tuple-element.25.probs_ref, f32[2,512,1536]{2,1,0:T(8,128)S(1)} %get-tuple-element.26.dprobs_ref, ...), custom_call_target="tpu_custom_call" | custom-call | flops 805306368 | bytes 805306 | tf_op jit(solution)/shard_map/own_head/pallas_call | solution.py:231
  17.5 0.0 collective-permute-done.4.rest_1_
  17.5 0.2 collective-permute-done.5.rest_2_
  17.7 2.8 %collective-permute-done.6.rest_3_ = f32[2,1536]{1,0:T(2,128)S(1)} collective-permute-done((f32[2,1536]{1,0:T(2,128)S(1)}, f32[2,1536]{1,0:T(2,128)S(1)}, u32[]{:S(2)}, u32[]{:S(2)}) %collective-permute-start.6) | collective-permute-done | bytes 12320 | tf_op jit(solution)/shard_map/ppermute | solution.py:259
  20.5 0.0 collective-permute-done.3.received_ref
  20.5 1.2 %combine.1 = (f32[384,256]{1,0:T(8,128)S(1)}, f32[2,1536]{1,0:T(2,128)S(1)}, bf16[384,256]{1,0:T(8,128)(2,1)S(1)}, bf16[384,256]{1,0:T(8,128)(2,1)S(1)}, bf16[384,256]{1,0:T(8,128)(2,1)S(1)}) custom-call(s32[4]{0:T(128)S(1)} %pad_add_fusion.1.place, f32[2,1536,256]{2,1,0:T(8,128)S(1)} %own_head.1.own_ref, ...), custom_call_target="tpu_custom_call" | custom-call | flops 100663296 | bytes 100663 | tf_op jit(solution)/shard_map/combine/pallas_call | solution.py:231
  21.7 1.3 %collective-permute-start.7 = (bf16[384,256]{1,0:T(8,128)(2,1)S(1)}, bf16[384,256]{1,0:T(8,128)(2,1)S(1)}, u32[]{:S(2)}, u32[]{:S(2)}) collective-permute-start(bf16[384,256]{1,0:T(8,128)(2,1)S(1)} %get-tuple-element.31), channel_id=1, source_target_pairs={{0,4},{2,6},{4,0},{6,2},{8,12},{10,14},{12,8},{14,10},{16,20},{18,... | collective-permute-start | bytes 589832 | tf_op jit(solution)/shard_map/ppermute | solution.py:259
  23.0 0.0 collective-permute-start.8
  23.0 2.3 %collective-permute-start.9 = (bf16[384,256]{1,0:T(8,128)(2,1)S(1)}, bf16[384,256]{1,0:T(8,128)(2,1)S(1)}, u32[]{:S(2)}, u32[]{:S(2)}) collective-permute-start(bf16[384,256]{1,0:T(8,128)(2,1)S(1)} %get-tuple-element.33), channel_id=1, source_target_pairs={{0,12},{2,14},{4,8},{6,10},{8,4},{10,6},{12,0},{14,2},{16,28},{18,... | collective-permute-start | bytes 589832 | tf_op jit(solution)/shard_map/ppermute | solution.py:259
  25.2 2.2 %key_terms.1 = (f32[256,512]{1,0:T(8,128)S(1)}, bf16[1,256,512]{2,1,0:T(8,128)(2,1)S(1)}) custom-call(s32[4]{0:T(128)S(1)} %pad_add_fusion.1.place, f32[2,1536]{1,0:T(2,128)S(1)} %get-tuple-element.35.after_ref.delta_ref, f32[2,512,1536]{2,1,0:T(8,128)S(1)} %get-tuple-element.25.probs_ref, f32[2,512,1536]{2,1,0:T(8,128)S(1)} %get-tuple-element.26.dprobs_ref, ...), custom_call_target="tpu_custom_call" | custom-call | flops 805306368 | bytes 805306 | tf_op jit(solution)/shard_map/key_terms/pallas_call | solution.py:231
  27.5 1.7 %collective-permute-start.12 = (bf16[256,512]{1,0:T(8,128)(2,1)S(1)}, bf16[256,512]{1,0:T(8,128)(2,1)S(1)}, u32[]{:S(2)}, u32[]{:S(2)}) collective-permute-start(bf16[256,512]{1,0:T(8,128)(2,1)S(1)} %bitcast.13), channel_id=1, source_target_pairs={{0,1},{1,0},{2,3},{3,2},{4,5},{5,4},{6,7},{7,6},{8,9},{9,8},{10,11... | collective-permute-start | bytes 786440 | tf_op jit(solution)/shard_map/ppermute | solution.py:263
  29.1 1.5 %value_terms.1 = (f32[256,512]{1,0:T(8,128)S(1)}, bf16[1,256,512]{2,1,0:T(8,128)(2,1)S(1)}) custom-call(s32[4]{0:T(128)S(1)} %pad_add_fusion.1.place, f32[2,512,1536]{2,1,0:T(8,128)S(1)} %get-tuple-element.25.probs_ref, bf16[1536,512]{1,0:T(8,128)(2,1)S(1)} %get-tuple-element.34.g_ref, f32[2,1536]{1,0:T(2,128)S(1)} %get-tuple-element.35.after_ref.delta_ref), custom_call_target="tpu_custom_call" | custom-call | flops 805306368 | bytes 805306 | tf_op jit(solution)/shard_map/value_terms/pallas_call | solution.py:231
  30.6 0.5 collective-permute-start.11
  31.2 0.0 collective-permute-done.7.first_ref
  31.2 0.0 collective-permute-done.8.second_ref
  31.2 1.4 %collective-permute-done.9.third_ref = bf16[384,256]{1,0:T(8,128)(2,1)S(1)} collective-permute-done((bf16[384,256]{1,0:T(8,128)(2,1)S(1)}, bf16[384,256]{1,0:T(8,128)(2,1)S(1)}, u32[]{:S(2)}, u32[]{:S(2)}) %collective-permute-start.9) | collective-permute-done | bytes 196640 | tf_op jit(solution)/shard_map/ppermute | solution.py:259
  32.6 0.1 reduce.1.total_ref
  32.7 0.1 collective-permute-start.10
  32.8 3.8 %collective-permute-done.12 = bf16[256,512]{1,0:T(8,128)(2,1)S(1)} collective-permute-done((bf16[256,512]{1,0:T(8,128)(2,1)S(1)}, bf16[256,512]{1,0:T(8,128)(2,1)S(1)}, u32[]{:S(2)}, u32[]{:S(2)}) %collective-permute-start.12) | collective-permute-done | bytes 262176 | tf_op jit(solution)/shard_map/ppermute | solution.py:263
  36.6 2.8 %collective-permute-done.11 = bf16[256,512]{1,0:T(8,128)(2,1)S(1)} collective-permute-done((bf16[256,512]{1,0:T(8,128)(2,1)S(1)}, bf16[256,512]{1,0:T(8,128)(2,1)S(1)}, u32[]{:S(2)}, u32[]{:S(2)}) %collective-permute-start.11) | collective-permute-done | bytes 262176 | tf_op jit(solution)/shard_map/ppermute | solution.py:263
  39.4 2.5 %collective-permute-done.10.came_ref = bf16[384,256]{1,0:T(8,128)(2,1)S(1)} collective-permute-done((bf16[384,256]{1,0:T(8,128)(2,1)S(1)}, bf16[384,256]{1,0:T(8,128)(2,1)S(1)}, u32[]{:S(2)}, u32[]{:S(2)}) %collective-permute-start.10) | collective-permute-done | bytes 196640 | tf_op jit(solution)/shard_map/ppermute | solution.py:259
  41.9 1.2 %collective-permute-start.13 = (bf16[384,256]{1,0:T(8,128)(2,1)S(1)}, bf16[384,256]{1,0:T(8,128)(2,1)S(1)}, u32[]{:S(2)}, u32[]{:S(2)}) collective-permute-start(bf16[384,256]{1,0:T(8,128)(2,1)S(1)} %join.1.rest_0_.refs_0_), channel_id=1, source_target_pairs={{0,4},{2,6},{4,0},{6,2},{8,12},{10,14},{12,8},{14,10},{16,20},{18,... | collective-permute-start | bytes 589832 | tf_op jit(solution)/shard_map/ppermute | solution.py:259
  43.1 0.0 collective-permute-start.16
  43.1 2.3 %collective-permute-start.18 = (bf16[384,256]{1,0:T(8,128)(2,1)S(1)}, bf16[384,256]{1,0:T(8,128)(2,1)S(1)}, u32[]{:S(2)}, u32[]{:S(2)}) collective-permute-start(bf16[384,256]{1,0:T(8,128)(2,1)S(1)} %join.1.rest_0_.refs_0_), channel_id=1, source_target_pairs={{0,12},{2,14},{4,8},{6,10},{8,4},{10,6},{12,0},{14,2},{16,28},{18,... | collective-permute-start | bytes 589832 | tf_op jit(solution)/shard_map/ppermute | solution.py:259
  45.4 0.1 pad_add_fusion.place
  45.5 0.9 %pool_sum.1 = (bf16[256,512]{1,0:T(8,128)(2,1)}, bf16[256,512]{1,0:T(8,128)(2,1)}) custom-call(f32[256,512]{1,0:T(8,128)S(1)} %get-tuple-element.39.key_ref, f32[256,512]{1,0:T(8,128)S(1)} %get-tuple-element.40.value_ref, bf16[1,256,512]{2,1,0:T(8,128)(2,1)S(1)} %bitcast.10, bf16[1,256,512]{2,1,0:T(8,128)(2,1)S(1)} %bitcast.12), custom_call_target="tpu_custom_call" | custom-call | flops 50331648 | bytes 50331 | tf_op jit(solution)/shard_map/pool_sum/pallas_call | solution.py:231
  46.4 1.2 %first_rows.1.refs_2_.rest_3_ = bf16[1536,512]{1,0:T(8,128)(2,1)} custom-call(s32[3]{0:T(128)S(1)} %pad_add_fusion.place, bf16[384,256]{1,0:T(8,128)(2,1)S(1)} %join.1.rest_0_.refs_0_, bf16[256,512]{1,0:T(8,128)(2,1)} %get-tuple-element.22.rest_1_), custom_call_target="tpu_custom_call" | custom-call | flops 201326592 | bytes 201326 | tf_op jit(solution)/shard_map/first_rows/pallas_call | solution.py:231
  47.6 1.9 %collective-permute-done.13.refs_1_ = bf16[384,256]{1,0:T(8,128)(2,1)S(1)} collective-permute-done((bf16[384,256]{1,0:T(8,128)(2,1)S(1)}, bf16[384,256]{1,0:T(8,128)(2,1)S(1)}, u32[]{:S(2)}, u32[]{:S(2)}) %collective-permute-start.13) | collective-permute-done | bytes 196640 | tf_op jit(solution)/shard_map/ppermute | solution.py:259
  49.6 0.7 %collective-permute-done.16.rest_1_ = bf16[384,256]{1,0:T(8,128)(2,1)S(1)} collective-permute-done((bf16[384,256]{1,0:T(8,128)(2,1)S(1)}, bf16[384,256]{1,0:T(8,128)(2,1)S(1)}, u32[]{:S(2)}, u32[]{:S(2)}) %collective-permute-start.16) | collective-permute-done | bytes 196640 | tf_op jit(solution)/shard_map/ppermute | solution.py:259
  50.3 2.4 %collective-permute-done.18.rest_2_ = bf16[384,256]{1,0:T(8,128)(2,1)S(1)} collective-permute-done((bf16[384,256]{1,0:T(8,128)(2,1)S(1)}, bf16[384,256]{1,0:T(8,128)(2,1)S(1)}, u32[]{:S(2)}, u32[]{:S(2)}) %collective-permute-start.18) | collective-permute-done | bytes 196640 | tf_op jit(solution)/shard_map/ppermute | solution.py:259
  52.7 0.0 collective-permute-start.14
  52.7 0.5 collective-permute-start.15
  53.2 0.0 collective-permute-start.17
  53.2 0.5 collective-permute-start.19
  53.7 1.4 %own_rows.1.rest_4_ = bf16[1536,512]{1,0:T(8,128)(2,1)} custom-call(s32[3]{0:T(128)S(1)} %pad_add_fusion.place, bf16[384,256]{1,0:T(8,128)(2,1)S(1)} %get-tuple-element.43.rest_0_, bf16[384,256]{1,0:T(8,128)(2,1)S(1)} %collective-permute-done.16.rest_1_, bf16[384,256]{1,0:T(8,128)(2,1)S(1)} %collective-permute-done.18.rest_2_, ...), custom_call_target="tpu_custom_call", output_to_operand_aliasing={{}: (4, {})} | custom-call | flops 201326592 | bytes 201326 | tf_op jit(solution)/shard_map/own_rows/pallas_call | solution.py:231
  55.1 0.0 collective-permute-done.14.rest_0_
  55.1 0.0 collective-permute-done.15.rest_1_
  55.1 0.0 collective-permute-done.17.rest_2_
  55.1 0.0 collective-permute-done.19.rest_3_
  55.1 1.5 %other_rows.1 = bf16[1536,512]{1,0:T(8,128)(2,1)} custom-call(s32[3]{0:T(128)S(1)} %pad_add_fusion.place, bf16[384,256]{1,0:T(8,128)(2,1)S(1)} %collective-permute-done.14.rest_0_, bf16[384,256]{1,0:T(8,128)(2,1)S(1)} %collective-permute-done.15.rest_1_, bf16[384,256]{1,0:T(8,128)(2,1)S(1)} %collective-permute-done.17.rest_2_, ...), custom_call_target="tpu_custom_call", output_to_operand_aliasing={{}: (5, {})} | custom-call | flops 201326592 | bytes 201326 | tf_op jit(solution)/shard_map/other_rows/pallas_call | solution.py:231
  (3 shorter events, 0.1 us)
Async XLA Ops:
  0.7 6.3 %copy-start = (s32[1536,2]{0,1:T(2,128)S(1)}, s32[1536,2]{0,1:T(2,128)}, u32[]{:S(2)}) copy-start(s32[1536,2]{0,1:T(2,128)} %param.13) | copy-start | bytes 36868
  3.9 5.2 %collective-permute-start = (f32[4,1536]{1,0:T(4,128)S(1)}, f32[4,1536]{1,0:T(4,128)S(1)}, u32[]{:S(2)}, u32[]{:S(2)}) collective-permute-start(f32[4,1536]{1,0:T(4,128)S(1)} %get-tuple-element.24.delta_ref.refs_0_.centre_ref), channel_id=1, source_target_pairs={{0,2},{2,0},{4,6},{6,4},{8,10},{10,8},{12,14},{14,12},{16,18},{18,... | collective-permute-start | bytes 73736 | tf_op jit(solution)/shard_map/ppermute | solution.py:259
  4.1 5.0 %collective-permute-start.1 = (f32[4,1536]{1,0:T(4,128)S(1)}, f32[4,1536]{1,0:T(4,128)S(1)}, u32[]{:S(2)}, u32[]{:S(2)}) collective-permute-start(f32[4,1536]{1,0:T(4,128)S(1)} %get-tuple-element.24.delta_ref.refs_0_.centre_ref), channel_id=1, source_target_pairs={{0,4},{2,6},{4,0},{6,2},{8,12},{10,14},{12,8},{14,10},{16,20},{18,... | collective-permute-start | bytes 73736 | tf_op jit(solution)/shard_map/ppermute | solution.py:259
  7.0 3.3 %collective-permute-start.2 = (f32[4,1536]{1,0:T(4,128)S(1)}, f32[4,1536]{1,0:T(4,128)S(1)}, u32[]{:S(2)}, u32[]{:S(2)}) collective-permute-start(f32[4,1536]{1,0:T(4,128)S(1)} %get-tuple-element.24.delta_ref.refs_0_.centre_ref), channel_id=1, source_target_pairs={{0,6},{2,4},{4,2},{6,0},{8,14},{10,12},{12,10},{14,8},{16,22},{18,... | collective-permute-start | bytes 73736 | tf_op jit(solution)/shard_map/ppermute | solution.py:259
  10.2 10.2 %collective-permute-start.3 = (f32[2,1536,256]{2,1,0:T(8,128)S(1)}, f32[2,1536,256]{2,1,0:T(8,128)S(1)}, u32[]{:S(2)}, u32[]{:S(2)}) collective-permute-start(f32[2,1536,256]{2,1,0:T(8,128)S(1)} %get-tuple-element.28), channel_id=1, source_target_pairs={{0,2},{2,0},{4,6},{6,4},{8,10},{10,8},{12,14},{14,12},{16,18},{18,... | collective-permute-start | bytes 9437192 | tf_op jit(solution)/shard_map/ppermute | solution.py:259
  10.5 7.0 %collective-permute-start.4 = (f32[2,1536]{1,0:T(2,128)S(1)}, f32[2,1536]{1,0:T(2,128)S(1)}, u32[]{:S(2)}, u32[]{:S(2)}) collective-permute-start(f32[2,1536]{1,0:T(2,128)S(1)} %get-tuple-element.29.rest_0_), channel_id=1, source_target_pairs={{0,8},{2,10},{4,12},{6,14},{8,0},{10,2},{12,4},{14,6},{16,24},{18,... | collective-permute-start | bytes 36872 | tf_op jit(solution)/shard_map/ppermute | solution.py:259
  13.1 4.6 %collective-permute-start.5 = (f32[2,1536]{1,0:T(2,128)S(1)}, f32[2,1536]{1,0:T(2,128)S(1)}, u32[]{:S(2)}, u32[]{:S(2)}) collective-permute-start(f32[2,1536]{1,0:T(2,128)S(1)} %get-tuple-element.29.rest_0_), channel_id=1, source_target_pairs={{0,16},{2,18},{4,20},{6,22},{8,24},{10,26},{12,28},{14,30},{16,0},... | collective-permute-start | bytes 36872 | tf_op jit(solution)/shard_map/ppermute | solution.py:259
  15.0 5.5 %collective-permute-start.6 = (f32[2,1536]{1,0:T(2,128)S(1)}, f32[2,1536]{1,0:T(2,128)S(1)}, u32[]{:S(2)}, u32[]{:S(2)}) collective-permute-start(f32[2,1536]{1,0:T(2,128)S(1)} %get-tuple-element.29.rest_0_), channel_id=1, source_target_pairs={{0,24},{2,26},{4,28},{6,30},{8,16},{10,18},{12,20},{14,22},{16,8},... | collective-permute-start | bytes 36872 | tf_op jit(solution)/shard_map/ppermute | solution.py:259
  21.7 9.5 %collective-permute-start.7 = (bf16[384,256]{1,0:T(8,128)(2,1)S(1)}, bf16[384,256]{1,0:T(8,128)(2,1)S(1)}, u32[]{:S(2)}, u32[]{:S(2)}) collective-permute-start(bf16[384,256]{1,0:T(8,128)(2,1)S(1)} %get-tuple-element.31), channel_id=1, source_target_pairs={{0,4},{2,6},{4,0},{6,2},{8,12},{10,14},{12,8},{14,10},{16,20},{18,... | collective-permute-start | bytes 589832 | tf_op jit(solution)/shard_map/ppermute | solution.py:259
  23.0 8.2 %collective-permute-start.8 = (bf16[384,256]{1,0:T(8,128)(2,1)S(1)}, bf16[384,256]{1,0:T(8,128)(2,1)S(1)}, u32[]{:S(2)}, u32[]{:S(2)}) collective-permute-start(bf16[384,256]{1,0:T(8,128)(2,1)S(1)} %get-tuple-element.32), channel_id=1, source_target_pairs={{0,8},{2,10},{4,12},{6,14},{8,0},{10,2},{12,4},{14,6},{16,24},{18,... | collective-permute-start | bytes 589832 | tf_op jit(solution)/shard_map/ppermute | solution.py:259
  23.0 9.6 %collective-permute-start.9 = (bf16[384,256]{1,0:T(8,128)(2,1)S(1)}, bf16[384,256]{1,0:T(8,128)(2,1)S(1)}, u32[]{:S(2)}, u32[]{:S(2)}) collective-permute-start(bf16[384,256]{1,0:T(8,128)(2,1)S(1)} %get-tuple-element.33), channel_id=1, source_target_pairs={{0,12},{2,14},{4,8},{6,10},{8,4},{10,6},{12,0},{14,2},{16,28},{18,... | collective-permute-start | bytes 589832 | tf_op jit(solution)/shard_map/ppermute | solution.py:259
  27.5 9.1 %collective-permute-start.12 = (bf16[256,512]{1,0:T(8,128)(2,1)S(1)}, bf16[256,512]{1,0:T(8,128)(2,1)S(1)}, u32[]{:S(2)}, u32[]{:S(2)}) collective-permute-start(bf16[256,512]{1,0:T(8,128)(2,1)S(1)} %bitcast.13), channel_id=1, source_target_pairs={{0,1},{1,0},{2,3},{3,2},{4,5},{5,4},{6,7},{7,6},{8,9},{9,8},{10,11... | collective-permute-start | bytes 786440 | tf_op jit(solution)/shard_map/ppermute | solution.py:263
  30.6 8.7 %collective-permute-start.11 = (bf16[256,512]{1,0:T(8,128)(2,1)S(1)}, bf16[256,512]{1,0:T(8,128)(2,1)S(1)}, u32[]{:S(2)}, u32[]{:S(2)}) collective-permute-start(bf16[256,512]{1,0:T(8,128)(2,1)S(1)} %bitcast.14), channel_id=1, source_target_pairs={{0,1},{1,0},{2,3},{3,2},{4,5},{5,4},{6,7},{7,6},{8,9},{9,8},{10,11... | collective-permute-start | bytes 786440 | tf_op jit(solution)/shard_map/ppermute | solution.py:263
  32.7 9.1 %collective-permute-start.10 = (bf16[384,256]{1,0:T(8,128)(2,1)S(1)}, bf16[384,256]{1,0:T(8,128)(2,1)S(1)}, u32[]{:S(2)}, u32[]{:S(2)}) collective-permute-start(bf16[384,256]{1,0:T(8,128)(2,1)S(1)} %reduce.1.total_ref), channel_id=1, source_target_pairs={{0,16},{2,18},{4,20},{6,22},{8,24},{10,26},{12,28},{14,30},{16,0},... | collective-permute-start | bytes 589832 | tf_op jit(solution)/shard_map/ppermute | solution.py:259
  41.9 7.7 %collective-permute-start.13 = (bf16[384,256]{1,0:T(8,128)(2,1)S(1)}, bf16[384,256]{1,0:T(8,128)(2,1)S(1)}, u32[]{:S(2)}, u32[]{:S(2)}) collective-permute-start(bf16[384,256]{1,0:T(8,128)(2,1)S(1)} %join.1.rest_0_.refs_0_), channel_id=1, source_target_pairs={{0,4},{2,6},{4,0},{6,2},{8,12},{10,14},{12,8},{14,10},{16,20},{18,... | collective-permute-start | bytes 589832 | tf_op jit(solution)/shard_map/ppermute | solution.py:259
  43.1 7.1 %collective-permute-start.16 = (bf16[384,256]{1,0:T(8,128)(2,1)S(1)}, bf16[384,256]{1,0:T(8,128)(2,1)S(1)}, u32[]{:S(2)}, u32[]{:S(2)}) collective-permute-start(bf16[384,256]{1,0:T(8,128)(2,1)S(1)} %join.1.rest_0_.refs_0_), channel_id=1, source_target_pairs={{0,8},{2,10},{4,12},{6,14},{8,0},{10,2},{12,4},{14,6},{16,24},{18,... | collective-permute-start | bytes 589832 | tf_op jit(solution)/shard_map/ppermute | solution.py:259
  43.1 9.5 %collective-permute-start.18 = (bf16[384,256]{1,0:T(8,128)(2,1)S(1)}, bf16[384,256]{1,0:T(8,128)(2,1)S(1)}, u32[]{:S(2)}, u32[]{:S(2)}) collective-permute-start(bf16[384,256]{1,0:T(8,128)(2,1)S(1)} %join.1.rest_0_.refs_0_), channel_id=1, source_target_pairs={{0,12},{2,14},{4,8},{6,10},{8,4},{10,6},{12,0},{14,2},{16,28},{18,... | collective-permute-start | bytes 589832 | tf_op jit(solution)/shard_map/ppermute | solution.py:259
  52.7 2.4 %collective-permute-start.14 = (bf16[384,256]{1,0:T(8,128)(2,1)S(1)}, bf16[384,256]{1,0:T(8,128)(2,1)S(1)}, u32[]{:S(2)}, u32[]{:S(2)}) collective-permute-start(bf16[384,256]{1,0:T(8,128)(2,1)S(1)} %get-tuple-element.42), channel_id=1, source_target_pairs={{0,2},{2,0},{4,6},{6,4},{8,10},{10,8},{12,14},{14,12},{16,18},{18,... | collective-permute-start | bytes 589832 | tf_op jit(solution)/shard_map/ppermute | solution.py:259
  52.7 2.4 %collective-permute-start.15 = (bf16[384,256]{1,0:T(8,128)(2,1)S(1)}, bf16[384,256]{1,0:T(8,128)(2,1)S(1)}, u32[]{:S(2)}, u32[]{:S(2)}) collective-permute-start(bf16[384,256]{1,0:T(8,128)(2,1)S(1)} %get-tuple-element.43.rest_0_), channel_id=1, source_target_pairs={{0,2},{2,0},{4,6},{6,4},{8,10},{10,8},{12,14},{14,12},{16,18},{18,... | collective-permute-start | bytes 589832 | tf_op jit(solution)/shard_map/ppermute | solution.py:259
  53.2 1.9 %collective-permute-start.17 = (bf16[384,256]{1,0:T(8,128)(2,1)S(1)}, bf16[384,256]{1,0:T(8,128)(2,1)S(1)}, u32[]{:S(2)}, u32[]{:S(2)}) collective-permute-start(bf16[384,256]{1,0:T(8,128)(2,1)S(1)} %collective-permute-done.16.rest_1_), channel_id=1, source_target_pairs={{0,2},{2,0},{4,6},{6,4},{8,10},{10,8},{12,14},{14,12},{16,18},{18,... | collective-permute-start | bytes 589832 | tf_op jit(solution)/shard_map/ppermute | solution.py:259
  53.2 1.9 %collective-permute-start.19 = (bf16[384,256]{1,0:T(8,128)(2,1)S(1)}, bf16[384,256]{1,0:T(8,128)(2,1)S(1)}, u32[]{:S(2)}, u32[]{:S(2)}) collective-permute-start(bf16[384,256]{1,0:T(8,128)(2,1)S(1)} %collective-permute-done.18.rest_2_), channel_id=1, source_target_pairs={{0,2},{2,0},{4,6},{6,4},{8,10},{10,8},{12,14},{14,12},{16,18},{18,... | collective-permute-start | bytes 589832 | tf_op jit(solution)/shard_map/ppermute | solution.py:259

commit v10 on v9

--- a/solution.py
+++ b/solution.py
@@ -137,28 +137,31 @@
     place, own_ref, received_ref, centre_ref, came_ref, *rest, deltas, scale
 ):
     added, (keep_ref, sum_ref, *send_refs) = rest[:deltas], rest[deltas:]
-    rows, width = keep_ref.shape
+    _, rows, width = keep_ref.shape
     heads = sum_ref.shape[0]
     sum_ref[...] = sum(ref[...] for ref in added)
 
     def column(ref, span):
         row = sum_ref[pl.ds(place[2], 1), span] - ref[pl.ds(heads + place[2], 1), span]
-        return jnp.transpose(jnp.broadcast_to(row * scale, (128, rows)))
-
-    for step in range(4):
-        target = send_refs[step - 1] if step else keep_ref
-        span = ways((place[3] ^ step) * rows, rows)
-        gaps = column(centre_ref, span), column(came_ref, span)
-        for start in range(0, width, 128):
-            columns = slice(start, start + 128)
-            direct = own_ref[0, span, columns] + received_ref[0, span, columns]
-            weighted = own_ref[1, span, columns] * gaps[0]
-            weighted += received_ref[1, span, columns] * gaps[1]
-            target[:, columns] = (scale * direct - weighted).astype(target.dtype)
+        return jnp.transpose(jnp.broadcast_to(row * scale, (128, 2 * rows)))
+
+    for step in (3, 1, 2, 0):
+        span = ways((place[3] ^ step) * 2 * rows, 2 * rows)
+        own_gap, came_gap = column(centre_ref, span), column(came_ref, span)
+        for part in range(2):
+            target = send_refs[3 * part + step - 1] if step else keep_ref.at[part]
+            span = ways((2 * (place[3] ^ step) + part) * rows, rows)
+            inside = slice(part * rows, (part + 1) * rows)
+            for start in range(0, width, 128):
+                columns = slice(start, start + 128)
+                direct = own_ref[0, span, columns] + received_ref[0, span, columns]
+                weighted = own_ref[1, span, columns] * own_gap[inside]
+                weighted += received_ref[1, span, columns] * came_gap[inside]
+                target[:, columns] = (scale * direct - weighted).astype(target.dtype)
 
 
 def key_kernel(
-    place, delta_ref, probs_ref, dprobs_ref, targets_ref, q_ref, own_ref, send_ref,
+    place, delta_ref, probs_ref, dprobs_ref, targets_ref, q_ref, after_ref, own_ref, send_ref,
     low_ref, *, chunk, scale,
 ):
     heads = probs_ref.shape[0]
@@ -181,18 +184,23 @@
                 send_ref[step - 1, :, columns] = term.astype(jnp.bfloat16)
 
 
-def reduce_kernel(
-    keep_ref, first_ref, second_ref, third_ref, after_value_ref, after_key_ref, out_ref
-):
-    total = keep_ref[...]
+def reduce_kernel(keep_ref, first_ref, second_ref, third_ref, *rest, part):
+    total = keep_ref[part]
     for ref in (first_ref, second_ref, third_ref):
         total += ref[...].astype(jnp.float32)
-    out_ref[...] = total.astype(out_ref.dtype)
-
-
-def join_kernel(total_ref, came_ref, after_value_ref, after_key_ref, out_ref):
+    rest[-1][...] = total.astype(rest[-1].dtype)
+
+
+def join_kernel(total_ref, came_ref, out_ref):
     total = total_ref[...].astype(jnp.float32) + came_ref[...].astype(jnp.float32)
     out_ref[...] = total.astype(jnp.bfloat16)
+
+
+def gather_kernel(*refs):
+    out_ref = refs[-1]
+    rows = refs[0].shape[0]
+    for ref, step in zip(refs, (0, 3, 1, 2)):
+        out_ref[step * rows : (step + 1) * rows] = ref[...]
 
 
 def pool_kernel(key_ref, value_ref, key_came_ref, value_came_ref, key_out, value_out):
@@ -204,22 +212,21 @@
     value_out[...] = value_sum.astype(jnp.bfloat16)
 
 
-def after_kernel(*refs):
-    pass
-
-
 def place_kernel(place, *rest, sources, piece):
     out_ref, sems = rest[-2:]
     copies = []
-    for ref, (side, step) in zip(rest, sources):
+    for ref, (side, part) in zip(rest, sources):
         width = ref.shape[1]
         columns = ways((place[0] ^ side) * width, width)
-        pieces = ref.shape[0] // piece
-        for index in range(pieces):
-            rows = ways(((place[1] ^ step) * pieces + (index ^ place[2])) * piece, piece)
+        pieces = ref.shape[0] // (4 * piece)
+        for index in range(4 * pieces):
+            step, inner = divmod(index, pieces)
+            block = (2 * (place[1] ^ step) + part) * pieces + (inner ^ place[2])
             copies.append(
                 pltpu.make_async_copy(
-                    ref.at[pl.ds(index * piece, piece)], out_ref.at[rows, columns], sems.at[len(copies)]
+                    ref.at[pl.ds(index * piece, piece)],
+                    out_ref.at[ways(block * piece, piece), columns],
+                    sems.at[len(copies)],
                 )
             )
             copies[-1].start()
@@ -346,24 +353,55 @@
         if stride == 1:
             other_centre = added[1]
         stride *= steps
-    quarter = query_count // 4
-    near_part = pltpu.VMEM((quarter, width), bf16)
+    eighth = query_count // 8
+    near_part = pltpu.VMEM((eighth, width), bf16)
     keep, delta, *send = call(
         partial(combine_kernel, deltas=len(added), scale=scale),
         "combine",
         (place, query_terms(True, "own_head"), received, centre, other_centre, *added),
         [IN_SMEM] + [IN_VMEM] * (4 + len(added)),
         [
-            pltpu.VMEM((quarter, width), f32),
+            pltpu.VMEM((2, eighth, width), f32),
             pltpu.VMEM((heads, query_count), f32),
         ]
-        + [near_part] * 3,
+        + [near_part] * 6,
         work // 4,
     )
+    def reduced(part, after):
+        came = {step: flip(send[3 * part + step - 1], 2 * step) for step in (3, 1, 2)}
+        return call(
+            partial(reduce_kernel, part=part),
+            "reduce",
+            (keep, came[3], came[1], came[2], *after),
+            [IN_VMEM] * 4 + [IN_HBM] * len(after),
+            [near_part if bits == 4 else pltpu.VMEM((eighth, width), f32)],
+            work // 16,
+        )[0]
+
+    def joined(total):
+        for bit in range(3, bits - 1):
+            split = total.reshape(2, -1, width)
+            pick = partial(lax.dynamic_index_in_dim, split, axis=0, keepdims=False)
+            came = flip(pick(1 - bit_of(bit)).astype(bf16), 1 << bit)
+            total = pick(bit_of(bit)) + came.astype(f32)
+        total = total.astype(bf16)
+        (whole,) = call(
+            join_kernel,
+            "join",
+            (total, flip(total, 1 << (bits - 1))),
+            [IN_VMEM] * 2,
+            [pltpu.VMEM(total.shape, bf16)],
+            work // 16,
+        )
+        for bit in range(bits - 2, 2, -1):
+            whole = jnp.concatenate([whole, flip(whole, 1 << bit)], axis=0)
+        return whole
+
+    totals = [reduced(0, ())]
     value_own, value_send = call(
         value_kernel,
         "value_terms",
-        (place, probs, g_near, delta),
+        (place, probs, g_near, totals[0]),
         [IN_SMEM] + [IN_VMEM] * 2 + [IN_HBM],
         shares,
         2 * work,
@@ -372,41 +410,17 @@
     key_own, key_send = call(
         partial(key_kernel, chunk=chunk, scale=scale),
         "key_terms",
-        (place, delta, probs, dprobs, targets, q_near),
-        [IN_SMEM] + [IN_VMEM] * 5,
+        (place, delta, probs, dprobs, targets, q_near, totals[0]),
+        [IN_SMEM] + [IN_VMEM] * 5 + [IN_HBM],
         shares,
         2 * work,
         [pltpu.VMEM((heads, value_count, query_count), bf16)],
     )
     key_came = swap_shares(key_send)
 
-    came = [flip(send[step - 1], 2 * step) for step in range(1, 4)]
-    (total,) = call(
-        reduce_kernel,
-        "reduce",
-        (keep, *came, value_send, key_send),
-        [IN_VMEM] * 4 + [IN_HBM] * 2,
-        [near_part if bits == 4 else pltpu.VMEM((quarter, width), f32)],
-        work // 8,
-    )
-    for bit in range(3, bits - 1):
-        split = total.reshape(2, -1, width)
-        pick = partial(lax.dynamic_index_in_dim, split, axis=0, keepdims=False)
-        came = flip(pick(1 - bit_of(bit)).astype(bf16), 1 << bit)
-        total = pick(bit_of(bit)) + came.astype(f32)
-    total = total.astype(bf16)
-    piece = total.shape[0]
-    (part,) = call(
-        join_kernel,
-        "join",
-        (total, flip(total, 1 << (bits - 1)), value_came, key_came),
-        [IN_VMEM] * 2 + [IN_HBM] * 2,
-        [pltpu.VMEM((piece, width), bf16)],
-        work // 16,
-    )
+    totals.append(reduced(1, (value_send, key_send)))
+    piece = eighth >> (bits - 4)
     inner = 0
-    for bit in range(bits - 2, 2, -1):
-        part = jnp.concatenate([part, flip(part, 1 << bit)], axis=0)
     for bit in range(3, bits - 1):
         inner = 2 * inner + bit_of(bit)
 
@@ -418,8 +432,20 @@
         [pltpu.HBM((share, wide), bf16)] * 2,
         work // 8,
     )
-    others = [flip(part, 2 * step) for step in range(1, 4)]
     pieces_place = jnp.stack([core, square, inner]).astype(jnp.int32)
+
+    def gathered(total, after):
+        whole = joined(total)
+        others = {step: flip(whole, 2 * step) for step in (3, 1, 2)}
+        return call(
+            gather_kernel,
+            "gather",
+            (whole, others[3], others[1], others[2], *after),
+            [IN_VMEM] * 4 + [IN_HBM] * len(after),
+            [pltpu.VMEM((4 * eighth, width), bf16)],
+            work // 16,
+        )[0]
+
     near = partial(pltpu.with_memory_space_constraint, memory_space=pltpu.VMEM)
     far = partial(pltpu.with_memory_space_constraint, memory_space=pltpu.HBM)
 
@@ -432,27 +458,17 @@
             [IN_SMEM] + [IN_VMEM] * copied + [IN_HBM],
             [pltpu.HBM((query_count, wide), bf16)],
             work // 2,
-            [pltpu.SemaphoreType.DMA((copied * quarter // piece,))],
+            [pltpu.SemaphoreType.DMA((copied * 4 * eighth // piece,))],
             [IN_HBM],
             {1 + copied: 0} if aliases else {},
         )[0]
 
-    begun = placed("first_rows", [(part, 0, 0)], key_grad, False)
-    part, first_other = call(
-        after_kernel,
-        "after",
-        (part, others[0], far(begun)),
-        [IN_HBM] * 3,
-        [near_part] * 2,
-        work // 1000,
-        out_specs=[IN_HBM] * 2,
-        aliases={0: 0, 1: 1},
-    )
-    quarters = [part, first_other] + others[1:]
-    theirs = [(flip(array, 1), 1, step) for step, array in enumerate(quarters)]
-    mine = [(array, 0, step) for step, array in enumerate(quarters) if step]
-    begun = placed("own_rows", mine, begun, True)
-    return placed("other_rows", theirs, begun, True), key_grad, value_grad
+    mine = [gathered(totals[0], ())]
+    begun = placed("first_rows", [(mine[0], 0, 0)], key_grad, False)
+    mine.append(gathered(totals[1], (far(begun),)))
+    theirs = [flip(array, 1) for array in mine]
+    begun = placed("own_rows", [(mine[1], 0, 1), (theirs[0], 1, 0)], begun, True)
+    return placed("other_rows", [(theirs[1], 1, 1)], begun, True), key_grad, value_grad
 
 
 def solution(mesh):

time: 57.2 us -> 57.1 us (level)
  waiting for transfers between devices: 19.7 us -> 12.9 us
  starting transfers between devices: 18.8 us -> 24.8 us
  Pallas kernels: 17.1 us -> 18 us
    ppermute x2, waiting for transfers between devices: 6.57 us -> 0.01 us  [swap_shares(): lax.ppermute(send[step - 1], 'qry', [(i, (i + step) % parts) for i in ran...]
    ppermute x18 -> x23, starting transfers between devices: 16.7 us -> 22.8 us  [flip(): lax.ppermute(array, 'val', [(i, i ^ mask) for i in range(value_devices)])]
    pallas_call x14 -> x17, Pallas kernels: 17.1 us -> 18 us  [call(): pl.pallas_call(kernel, in_specs=in_specs, out_specs=[IN_VMEM] * len(outpu...]
    ppermute x18 -> x23, waiting for transfers between devices: 13.1 us -> 12.9 us  [flip(): lax.ppermute(array, 'val', [(i, i ^ mask) for i in range(value_devices)])]
  transfers between devices with their start and end apart: 20 -> 25, of which waited for: 10 -> 11; matrix products, arithmetic and copies ran while one was open for 0% -> 0% of each run, Pallas kernels for 20% -> 20%
where the time goes in v10:
time: 57.1 us; the launch traced here: 56.7 us
  starting transfers between devices  24.8 us (43%)
  Pallas kernels  18 us (32%)
  waiting for transfers between devices  12.9 us (23%)
  between operations  0.86 us (2%)
    ppermute x23, starting transfers between devices, flip(): lax.ppermute(array, 'val', [(i, i ^ mask) for i in range(value_devices)])  22.8 us
    pallas_call x17, Pallas kernels, call(): pl.pallas_call(kernel, in_specs=in_specs, out_specs=[IN_VMEM] * len(outpu...  18 us
    ppermute x23, waiting for transfers between devices, flip(): lax.ppermute(array, 'val', [(i, i ^ mask) for i in range(value_devices)])  12.9 us
    ppermute x2, starting transfers between devices, swap_shares(): lax.ppermute(send[step - 1], 'qry', [(i, (i + step) % parts) for i in ran...  2.03 us
  transfers between devices with their start and end apart: 25, of which 11 were waited for; matrix products, arithmetic and copies ran while one was open for 0% of the time, Pallas kernels for 20%

profile of v10, /device:TPU:0, one launch (start us, length us, event | category | flops | bytes accessed | tf_op | source)
XLA Modules:
  0.0 56.7 jit_solution(9626442720958894743)
XLA Ops:
  0.7 0.1 pad_add_fusion.1.place
  0.7 3.8 %forward_pass.1 = (f32[4,1536]{1,0:T(4,128)S(1)}, f32[2,512,1536]{2,1,0:T(8,128)S(1)}, f32[2,512,1536]{2,1,0:T(8,128)S(1)}, bf16[1536,512]{1,0:T(8,128)(2,1)S(1)...) custom-call(s32[4]{0:T(128)S(1)} %pad_add_fusion.1.place, s32[2,1,6]{2,1,0:T(1,128)} %compat_hbm.1, ...), custom_call_target="tpu_custom_call" | custom-call | flops 1610612736 | bytes 1610612 | tf_op jit(solution)/shard_map/forward_pass/pallas_call | solution.py:238
  4.6 0.2 collective-permute-start
  4.7 2.3 %collective-permute-start.1 = (f32[4,1536]{1,0:T(4,128)S(1)}, f32[4,1536]{1,0:T(4,128)S(1)}, u32[]{:S(2)}, u32[]{:S(2)}) collective-permute-start(f32[4,1536]{1,0:T(4,128)S(1)} %get-tuple-element.25.delta_ref.refs_0_.centre_ref), channel_id=1, source_target_pairs={{0,4},{2,6},{4,0},{6,2},{8,12},{10,14},{12,8},{14,10},{16,20},{18,... | collective-permute-start | bytes 73736 | tf_op jit(solution)/shard_map/ppermute | solution.py:266
  7.0 0.1 collective-permute-start.2
  7.1 2.0 %other_head.1.refs_4_ = f32[2,1536,256]{2,1,0:T(8,128)S(1)} custom-call(s32[4]{0:T(128)S(1)} %pad_add_fusion.1.place, f32[4,1536]{1,0:T(4,128)S(1)} %get-tuple-element.25.delta_ref.refs_0_.centre_ref, f32[2,512,1536]{2,1,0:T(8,128)S(1)} %get-tuple-element.26.probs_ref, f32[2,512,1536]{2,1,0:T(8,128)S(1)} %get-tuple-element.27.dprobs_ref, ...), custom_call_target="tpu_custom_call" | custom-call | flops 805306368 | bytes 805306 | tf_op jit(solution)/shard_map/other_head/pallas_call | solution.py:238
  9.1 0.0 collective-permute-done.refs_1_.came_ref
  9.1 0.0 collective-permute-done.1.refs_2_
  9.1 1.2 %collective-permute-done.2.refs_3_ = f32[4,1536]{1,0:T(4,128)S(1)} collective-permute-done((f32[4,1536]{1,0:T(4,128)S(1)}, f32[4,1536]{1,0:T(4,128)S(1)}, u32[]{:S(2)}, u32[]{:S(2)}) %collective-permute-start.2) | collective-permute-done | bytes 24608 | tf_op jit(solution)/shard_map/ppermute | solution.py:266
  10.3 0.2 collective-permute-start.3
  10.5 3.0 %collective-permute-start.4 = (f32[2,1536]{1,0:T(2,128)S(1)}, f32[2,1536]{1,0:T(2,128)S(1)}, u32[]{:S(2)}, u32[]{:S(2)}) collective-permute-start(f32[2,1536]{1,0:T(2,128)S(1)} %get-tuple-element.30.rest_0_), channel_id=1, source_target_pairs={{0,8},{2,10},{4,12},{6,14},{8,0},{10,2},{12,4},{14,6},{16,24},{18,... | collective-permute-start | bytes 36872 | tf_op jit(solution)/shard_map/ppermute | solution.py:266
  13.5 1.9 %collective-permute-start.5 = (f32[2,1536]{1,0:T(2,128)S(1)}, f32[2,1536]{1,0:T(2,128)S(1)}, u32[]{:S(2)}, u32[]{:S(2)}) collective-permute-start(f32[2,1536]{1,0:T(2,128)S(1)} %get-tuple-element.30.rest_0_), channel_id=1, source_target_pairs={{0,16},{2,18},{4,20},{6,22},{8,24},{10,26},{12,28},{14,30},{16,0},... | collective-permute-start | bytes 36872 | tf_op jit(solution)/shard_map/ppermute | solution.py:266
  15.3 0.5 collective-permute-start.6
  15.8 2.0 %own_head.1.own_ref = f32[2,1536,256]{2,1,0:T(8,128)S(1)} custom-call(s32[4]{0:T(128)S(1)} %pad_add_fusion.1.place, f32[4,1536]{1,0:T(4,128)S(1)} %get-tuple-element.25.delta_ref.refs_0_.centre_ref, f32[2,512,1536]{2,1,0:T(8,128)S(1)} %get-tuple-element.26.probs_ref, f32[2,512,1536]{2,1,0:T(8,128)S(1)} %get-tuple-element.27.dprobs_ref, ...), custom_call_target="tpu_custom_call" | custom-call | flops 805306368 | bytes 805306 | tf_op jit(solution)/shard_map/own_head/pallas_call | solution.py:238
  17.8 0.0 collective-permute-done.4.rest_1_
  17.8 0.2 collective-permute-done.5.rest_2_
  18.1 2.8 %collective-permute-done.6.rest_3_ = f32[2,1536]{1,0:T(2,128)S(1)} collective-permute-done((f32[2,1536]{1,0:T(2,128)S(1)}, f32[2,1536]{1,0:T(2,128)S(1)}, u32[]{:S(2)}, u32[]{:S(2)}) %collective-permute-start.6) | collective-permute-done | bytes 12320 | tf_op jit(solution)/shard_map/ppermute | solution.py:266
  20.8 0.0 collective-permute-done.3.received_ref
  20.8 1.2 %combine.1 = (f32[2,192,256]{2,1,0:T(8,128)S(1)}, f32[2,1536]{1,0:T(2,128)S(1)}, bf16[192,256]{1,0:T(8,128)(2,1)S(1)}, bf16[192,256]{1,0:T(8,128)(2,1)S(1)}, bf1...) custom-call(s32[4]{0:T(128)S(1)} %pad_add_fusion.1.place, ...), custom_call_target="tpu_custom_call" | custom-call | flops 100663296 | bytes 100663 | tf_op jit(solution)/shard_map/combine/pallas_call | solution.py:238
  22.0 0.1 collective-permute-start.10
  22.1 0.8 %collective-permute-start.11 = (bf16[192,256]{1,0:T(8,128)(2,1)S(1)}, bf16[192,256]{1,0:T(8,128)(2,1)S(1)}, u32[]{:S(2)}, u32[]{:S(2)}) collective-permute-start(bf16[192,256]{1,0:T(8,128)(2,1)S(1)} %get-tuple-element.37), channel_id=1, source_target_pairs={{0,4},{2,6},{4,0},{6,2},{8,12},{10,14},{12,8},{14,10},{16,20},{18,... | collective-permute-start | bytes 294920 | tf_op jit(solution)/shard_map/ppermute | solution.py:266
  23.0 2.6 %collective-permute-start.12 = (bf16[192,256]{1,0:T(8,128)(2,1)S(1)}, bf16[192,256]{1,0:T(8,128)(2,1)S(1)}, u32[]{:S(2)}, u32[]{:S(2)}) collective-permute-start(bf16[192,256]{1,0:T(8,128)(2,1)S(1)} %get-tuple-element.38), channel_id=1, source_target_pairs={{0,8},{2,10},{4,12},{6,14},{8,0},{10,2},{12,4},{14,6},{16,24},{18,... | collective-permute-start | bytes 294920 | tf_op jit(solution)/shard_map/ppermute | solution.py:266
  25.6 0.2 collective-permute-start.7
  25.8 1.2 %collective-permute-start.8 = (bf16[192,256]{1,0:T(8,128)(2,1)S(1)}, bf16[192,256]{1,0:T(8,128)(2,1)S(1)}, u32[]{:S(2)}, u32[]{:S(2)}) collective-permute-start(bf16[192,256]{1,0:T(8,128)(2,1)S(1)} %get-tuple-element.33), channel_id=1, source_target_pairs={{0,4},{2,6},{4,0},{6,2},{8,12},{10,14},{12,8},{14,10},{16,20},{18,... | collective-permute-start | bytes 294920 | tf_op jit(solution)/shard_map/ppermute | solution.py:266
  27.1 1.4 %collective-permute-done.10.first_ref = bf16[192,256]{1,0:T(8,128)(2,1)S(1)} collective-permute-done((bf16[192,256]{1,0:T(8,128)(2,1)S(1)}, bf16[192,256]{1,0:T(8,128)(2,1)S(1)}, u32[]{:S(2)}, u32[]{:S(2)}) %collective-permute-start.10) | collective-permute-done | bytes 98336 | tf_op jit(solution)/shard_map/ppermute | solution.py:266
  28.5 0.6 %collective-permute-start.9 = (bf16[192,256]{1,0:T(8,128)(2,1)S(1)}, bf16[192,256]{1,0:T(8,128)(2,1)S(1)}, u32[]{:S(2)}, u32[]{:S(2)}) collective-permute-start(bf16[192,256]{1,0:T(8,128)(2,1)S(1)} %get-tuple-element.34), channel_id=1, source_target_pairs={{0,8},{2,10},{4,12},{6,14},{8,0},{10,2},{12,4},{14,6},{16,24},{18,... | collective-permute-start | bytes 294920 | tf_op jit(solution)/shard_map/ppermute | solution.py:266
  29.1 0.6 collective-permute-done.11.second_ref
  29.6 1.4 %collective-permute-done.12.third_ref = bf16[192,256]{1,0:T(8,128)(2,1)S(1)} collective-permute-done((bf16[192,256]{1,0:T(8,128)(2,1)S(1)}, bf16[192,256]{1,0:T(8,128)(2,1)S(1)}, u32[]{:S(2)}, u32[]{:S(2)}) %collective-permute-start.12) | collective-permute-done | bytes 98336 | tf_op jit(solution)/shard_map/ppermute | solution.py:266
  31.1 0.1 reduce.2.after_ref.total_ref
  31.1 0.1 collective-permute-start.17
  31.2 1.5 %value_terms.1 = (f32[256,512]{1,0:T(8,128)S(1)}, bf16[1,256,512]{2,1,0:T(8,128)(2,1)S(1)}) custom-call(s32[4]{0:T(128)S(1)} %pad_add_fusion.1.place, f32[2,512,1536]{2,1,0:T(8,128)S(1)} %get-tuple-element.26.probs_ref, bf16[1536,512]{1,0:T(8,128)(2,1)S(1)} %get-tuple-element.35.g_ref, bf16[192,256]{1,0:T(8,128)(2,1)S(1)} %reduce.2.after_ref.total_ref), custom_call_target="tpu_custom_call" | custom-call | flops 805306368 | bytes 805306 | tf_op jit(solution)/shard_map/value_terms/pallas_call | solution.py:238
  32.7 2.2 %key_terms.1 = (f32[256,512]{1,0:T(8,128)S(1)}, bf16[1,256,512]{2,1,0:T(8,128)(2,1)S(1)}) custom-call(s32[4]{0:T(128)S(1)} %pad_add_fusion.1.place, f32[2,1536]{1,0:T(2,128)S(1)} %get-tuple-element.40.delta_ref, f32[2,512,1536]{2,1,0:T(8,128)S(1)} %get-tuple-element.26.probs_ref, f32[2,512,1536]{2,1,0:T(8,128)S(1)} %get-tuple-element.27.dprobs_ref, ...), custom_call_target="tpu_custom_call" | custom-call | flops 805306368 | bytes 805306 | tf_op jit(solution)/shard_map/key_terms/pallas_call | solution.py:238
  35.0 0.0 collective-permute-done.7.first_ref
  35.0 0.0 collective-permute-done.8.second_ref
  35.0 0.0 collective-permute-done.9.third_ref
  35.0 0.1 reduce.3.total_ref
  35.1 3.0 %collective-permute-start.13 = (bf16[192,256]{1,0:T(8,128)(2,1)S(1)}, bf16[192,256]{1,0:T(8,128)(2,1)S(1)}, u32[]{:S(2)}, u32[]{:S(2)}) collective-permute-start(bf16[192,256]{1,0:T(8,128)(2,1)S(1)} %reduce.3.total_ref), channel_id=1, source_target_pairs={{0,16},{2,18},{4,20},{6,22},{8,24},{10,26},{12,28},{14,30},{16,0},... | collective-permute-start | bytes 294920 | tf_op jit(solution)/shard_map/ppermute | solution.py:266
  38.1 1.8 %collective-permute-start.21 = (bf16[256,512]{1,0:T(8,128)(2,1)S(1)}, bf16[256,512]{1,0:T(8,128)(2,1)S(1)}, u32[]{:S(2)}, u32[]{:S(2)}) collective-permute-start(bf16[256,512]{1,0:T(8,128)(2,1)S(1)} %bitcast.10), channel_id=1, source_target_pairs={{0,1},{1,0},{2,3},{3,2},{4,5},{5,4},{6,7},{7,6},{8,9},{9,8},{10,11... | collective-permute-start | bytes 786440 | tf_op jit(solution)/shard_map/ppermute | solution.py:270
  39.9 0.2 collective-permute-start.22
  40.1 0.0 collective-permute-done.17.came_ref
  40.1 0.7 %collective-permute-start.18 = (bf16[192,256]{1,0:T(8,128)(2,1)S(1)}, bf16[192,256]{1,0:T(8,128)(2,1)S(1)}, u32[]{:S(2)}, u32[]{:S(2)}) collective-permute-start(bf16[192,256]{1,0:T(8,128)(2,1)S(1)} %join.3.refs_0_), channel_id=1, source_target_pairs={{0,12},{2,14},{4,8},{6,10},{8,4},{10,6},{12,0},{14,2},{16,28},{18,... | collective-permute-start | bytes 294920 | tf_op jit(solution)/shard_map/ppermute | solution.py:266
  40.8 1.0 %collective-permute-start.19 = (bf16[192,256]{1,0:T(8,128)(2,1)S(1)}, bf16[192,256]{1,0:T(8,128)(2,1)S(1)}, u32[]{:S(2)}, u32[]{:S(2)}) collective-permute-start(bf16[192,256]{1,0:T(8,128)(2,1)S(1)} %join.3.refs_0_), channel_id=1, source_target_pairs={{0,4},{2,6},{4,0},{6,2},{8,12},{10,14},{12,8},{14,10},{16,20},{18,... | collective-permute-start | bytes 294920 | tf_op jit(solution)/shard_map/ppermute | solution.py:266
  41.8 0.0 collective-permute-done.13.came_ref
  41.8 1.9 %collective-permute-start.20 = (bf16[192,256]{1,0:T(8,128)(2,1)S(1)}, bf16[192,256]{1,0:T(8,128)(2,1)S(1)}, u32[]{:S(2)}, u32[]{:S(2)}) collective-permute-start(bf16[192,256]{1,0:T(8,128)(2,1)S(1)} %join.3.refs_0_), channel_id=1, source_target_pairs={{0,8},{2,10},{4,12},{6,14},{8,0},{10,2},{12,4},{14,6},{16,24},{18,... | collective-permute-start | bytes 294920 | tf_op jit(solution)/shard_map/ppermute | solution.py:266
  43.7 3.1 %collective-permute-done.18.refs_1_ = bf16[192,256]{1,0:T(8,128)(2,1)S(1)} collective-permute-done((bf16[192,256]{1,0:T(8,128)(2,1)S(1)}, bf16[192,256]{1,0:T(8,128)(2,1)S(1)}, u32[]{:S(2)}, u32[]{:S(2)}) %collective-permute-start.18) | collective-permute-done | bytes 98336 | tf_op jit(solution)/shard_map/ppermute | solution.py:266
  46.8 0.5 collective-permute-start.14
  47.3 1.2 %collective-permute-done.19.refs_2_ = bf16[192,256]{1,0:T(8,128)(2,1)S(1)} collective-permute-done((bf16[192,256]{1,0:T(8,128)(2,1)S(1)}, bf16[192,256]{1,0:T(8,128)(2,1)S(1)}, u32[]{:S(2)}, u32[]{:S(2)}) %collective-permute-start.19) | collective-permute-done | bytes 98336 | tf_op jit(solution)/shard_map/ppermute | solution.py:266
  48.5 0.4 collective-permute-start.15
  48.9 0.0 collective-permute-done.20.refs_3_
  48.9 1.4 %collective-permute-start.16 = (bf16[192,256]{1,0:T(8,128)(2,1)S(1)}, bf16[192,256]{1,0:T(8,128)(2,1)S(1)}, u32[]{:S(2)}, u32[]{:S(2)}) collective-permute-start(bf16[192,256]{1,0:T(8,128)(2,1)S(1)} %join.2.refs_0_), channel_id=1, source_target_pairs={{0,8},{2,10},{4,12},{6,14},{8,0},{10,2},{12,4},{14,6},{16,24},{18,... | collective-permute-start | bytes 294920 | tf_op jit(solution)/shard_map/ppermute | solution.py:266
  50.3 0.1 pad_add_fusion.place
  50.4 0.0 collective-permute-done.21
  50.4 0.1 collective-permute-start.24
  50.5 0.0 collective-permute-done.22
  50.5 0.9 %pool_sum.1 = (bf16[256,512]{1,0:T(8,128)(2,1)}, bf16[256,512]{1,0:T(8,128)(2,1)}) custom-call(f32[256,512]{1,0:T(8,128)S(1)} %get-tuple-element.43.key_ref, f32[256,512]{1,0:T(8,128)S(1)} %get-tuple-element.44.value_ref, bf16[1,256,512]{2,1,0:T(8,128)(2,1)S(1)} %bitcast.11, bf16[1,256,512]{2,1,0:T(8,128)(2,1)S(1)} %bitcast.12), custom_call_target="tpu_custom_call" | custom-call | flops 50331648 | bytes 50331 | tf_op jit(solution)/shard_map/pool_sum/pallas_call | solution.py:238
  51.4 1.3 %first_rows.1.refs_4_.rest_2_ = bf16[1536,512]{1,0:T(8,128)(2,1)} custom-call(s32[3]{0:T(128)S(1)} %pad_add_fusion.place, bf16[768,256]{1,0:T(8,128)(2,1)S(1)} %gather.2.rest_0_, bf16[256,512]{1,0:T(8,128)(2,1)} %get-tuple-element.23.rest_1_), custom_call_target="tpu_custom_call" | custom-call | flops 201326592 | bytes 201326 | tf_op jit(solution)/shard_map/first_rows/pallas_call | solution.py:238
  52.7 0.0 collective-permute-done.14.refs_1_
  52.7 0.7 %collective-permute-done.15.refs_2_ = bf16[192,256]{1,0:T(8,128)(2,1)S(1)} collective-permute-done((bf16[192,256]{1,0:T(8,128)(2,1)S(1)}, bf16[192,256]{1,0:T(8,128)(2,1)S(1)}, u32[]{:S(2)}, u32[]{:S(2)}) %collective-permute-start.15) | collective-permute-done | bytes 98336 | tf_op jit(solution)/shard_map/ppermute | solution.py:266
  53.4 0.1 collective-permute-done.16.refs_3_
  53.6 0.1 collective-permute-start.23
  53.6 0.0 collective-permute-done.24.rest_1_
  53.7 1.5 %own_rows.1.rest_1_ = bf16[1536,512]{1,0:T(8,128)(2,1)} custom-call(s32[3]{0:T(128)S(1)} %pad_add_fusion.place, bf16[768,256]{1,0:T(8,128)(2,1)S(1)} %gather.3.rest_0_, bf16[768,256]{1,0:T(8,128)(2,1)S(1)} %collective-permute-done.24.rest_1_, bf16[1536,512]{1,0:T(8,128)(2,1)} %first_rows.1.refs_4_.rest_2_), custom_call_target="tpu_custom_call", output_to_operand_aliasing={{}: (3, {})} | custom-call | flops 201326592 | bytes 201326 | tf_op jit(solution)/shard_map/own_rows/pallas_call | solution.py:238
  55.1 0.2 collective-permute-done.23.rest_0_
  55.4 1.3 %other_rows.1 = bf16[1536,512]{1,0:T(8,128)(2,1)} custom-call(s32[3]{0:T(128)S(1)} %pad_add_fusion.place, bf16[768,256]{1,0:T(8,128)(2,1)S(1)} %collective-permute-done.23.rest_0_, bf16[1536,512]{1,0:T(8,128)(2,1)} %own_rows.1.rest_1_), custom_call_target="tpu_custom_call", output_to_operand_aliasing={{}: (2, {})} | custom-call | flops 201326592 | bytes 201326 | tf_op jit(solution)/shard_map/other_rows/pallas_call | solution.py:238
  (7 shorter events, 0.1 us)
Async XLA Ops:
  0.7 6.3 %copy-start = (s32[1536,2]{0,1:T(2,128)S(1)}, s32[1536,2]{0,1:T(2,128)}, u32[]{:S(2)}) copy-start(s32[1536,2]{0,1:T(2,128)} %param.13) | copy-start | bytes 36868
  4.6 4.5 %collective-permute-start = (f32[4,1536]{1,0:T(4,128)S(1)}, f32[4,1536]{1,0:T(4,128)S(1)}, u32[]{:S(2)}, u32[]{:S(2)}) collective-permute-start(f32[4,1536]{1,0:T(4,128)S(1)} %get-tuple-element.25.delta_ref.refs_0_.centre_ref), channel_id=1, source_target_pairs={{0,2},{2,0},{4,6},{6,4},{8,10},{10,8},{12,14},{14,12},{16,18},{18,... | collective-permute-start | bytes 73736 | tf_op jit(solution)/shard_map/ppermute | solution.py:266
  4.7 4.3 %collective-permute-start.1 = (f32[4,1536]{1,0:T(4,128)S(1)}, f32[4,1536]{1,0:T(4,128)S(1)}, u32[]{:S(2)}, u32[]{:S(2)}) collective-permute-start(f32[4,1536]{1,0:T(4,128)S(1)} %get-tuple-element.25.delta_ref.refs_0_.centre_ref), channel_id=1, source_target_pairs={{0,4},{2,6},{4,0},{6,2},{8,12},{10,14},{12,8},{14,10},{16,20},{18,... | collective-permute-start | bytes 73736 | tf_op jit(solution)/shard_map/ppermute | solution.py:266
  7.0 3.3 %collective-permute-start.2 = (f32[4,1536]{1,0:T(4,128)S(1)}, f32[4,1536]{1,0:T(4,128)S(1)}, u32[]{:S(2)}, u32[]{:S(2)}) collective-permute-start(f32[4,1536]{1,0:T(4,128)S(1)} %get-tuple-element.25.delta_ref.refs_0_.centre_ref), channel_id=1, source_target_pairs={{0,6},{2,4},{4,2},{6,0},{8,14},{10,12},{12,10},{14,8},{16,22},{18,... | collective-permute-start | bytes 73736 | tf_op jit(solution)/shard_map/ppermute | solution.py:266
  10.3 10.6 %collective-permute-start.3 = (f32[2,1536,256]{2,1,0:T(8,128)S(1)}, f32[2,1536,256]{2,1,0:T(8,128)S(1)}, u32[]{:S(2)}, u32[]{:S(2)}) collective-permute-start(f32[2,1536,256]{2,1,0:T(8,128)S(1)} %get-tuple-element.29), channel_id=1, source_target_pairs={{0,2},{2,0},{4,6},{6,4},{8,10},{10,8},{12,14},{14,12},{16,18},{18,... | collective-permute-start | bytes 9437192 | tf_op jit(solution)/shard_map/ppermute | solution.py:266
  10.5 7.3 %collective-permute-start.4 = (f32[2,1536]{1,0:T(2,128)S(1)}, f32[2,1536]{1,0:T(2,128)S(1)}, u32[]{:S(2)}, u32[]{:S(2)}) collective-permute-start(f32[2,1536]{1,0:T(2,128)S(1)} %get-tuple-element.30.rest_0_), channel_id=1, source_target_pairs={{0,8},{2,10},{4,12},{6,14},{8,0},{10,2},{12,4},{14,6},{16,24},{18,... | collective-permute-start | bytes 36872 | tf_op jit(solution)/shard_map/ppermute | solution.py:266
  13.5 4.6 %collective-permute-start.5 = (f32[2,1536]{1,0:T(2,128)S(1)}, f32[2,1536]{1,0:T(2,128)S(1)}, u32[]{:S(2)}, u32[]{:S(2)}) collective-permute-start(f32[2,1536]{1,0:T(2,128)S(1)} %get-tuple-element.30.rest_0_), channel_id=1, source_target_pairs={{0,16},{2,18},{4,20},{6,22},{8,24},{10,26},{12,28},{14,30},{16,0},... | collective-permute-start | bytes 36872 | tf_op jit(solution)/shard_map/ppermute | solution.py:266
  15.3 5.5 %collective-permute-start.6 = (f32[2,1536]{1,0:T(2,128)S(1)}, f32[2,1536]{1,0:T(2,128)S(1)}, u32[]{:S(2)}, u32[]{:S(2)}) collective-permute-start(f32[2,1536]{1,0:T(2,128)S(1)} %get-tuple-element.30.rest_0_), channel_id=1, source_target_pairs={{0,24},{2,26},{4,28},{6,30},{8,16},{10,18},{12,20},{14,22},{16,8},... | collective-permute-start | bytes 36872 | tf_op jit(solution)/shard_map/ppermute | solution.py:266
  22.0 6.4 %collective-permute-start.10 = (bf16[192,256]{1,0:T(8,128)(2,1)S(1)}, bf16[192,256]{1,0:T(8,128)(2,1)S(1)}, u32[]{:S(2)}, u32[]{:S(2)}) collective-permute-start(bf16[192,256]{1,0:T(8,128)(2,1)S(1)} %get-tuple-element.36), channel_id=1, source_target_pairs={{0,12},{2,14},{4,8},{6,10},{8,4},{10,6},{12,0},{14,2},{16,28},{18,... | collective-permute-start | bytes 294920 | tf_op jit(solution)/shard_map/ppermute | solution.py:266
  22.1 7.5 %collective-permute-start.11 = (bf16[192,256]{1,0:T(8,128)(2,1)S(1)}, bf16[192,256]{1,0:T(8,128)(2,1)S(1)}, u32[]{:S(2)}, u32[]{:S(2)}) collective-permute-start(bf16[192,256]{1,0:T(8,128)(2,1)S(1)} %get-tuple-element.37), channel_id=1, source_target_pairs={{0,4},{2,6},{4,0},{6,2},{8,12},{10,14},{12,8},{14,10},{16,20},{18,... | collective-permute-start | bytes 294920 | tf_op jit(solution)/shard_map/ppermute | solution.py:266
  23.0 8.1 %collective-permute-start.12 = (bf16[192,256]{1,0:T(8,128)(2,1)S(1)}, bf16[192,256]{1,0:T(8,128)(2,1)S(1)}, u32[]{:S(2)}, u32[]{:S(2)}) collective-permute-start(bf16[192,256]{1,0:T(8,128)(2,1)S(1)} %get-tuple-element.38), channel_id=1, source_target_pairs={{0,8},{2,10},{4,12},{6,14},{8,0},{10,2},{12,4},{14,6},{16,24},{18,... | collective-permute-start | bytes 294920 | tf_op jit(solution)/shard_map/ppermute | solution.py:266
  25.6 9.4 %collective-permute-start.7 = (bf16[192,256]{1,0:T(8,128)(2,1)S(1)}, bf16[192,256]{1,0:T(8,128)(2,1)S(1)}, u32[]{:S(2)}, u32[]{:S(2)}) collective-permute-start(bf16[192,256]{1,0:T(8,128)(2,1)S(1)} %get-tuple-element.32), channel_id=1, source_target_pairs={{0,12},{2,14},{4,8},{6,10},{8,4},{10,6},{12,0},{14,2},{16,28},{18,... | collective-permute-start | bytes 294920 | tf_op jit(solution)/shard_map/ppermute | solution.py:266
  25.8 9.2 %collective-permute-start.8 = (bf16[192,256]{1,0:T(8,128)(2,1)S(1)}, bf16[192,256]{1,0:T(8,128)(2,1)S(1)}, u32[]{:S(2)}, u32[]{:S(2)}) collective-permute-start(bf16[192,256]{1,0:T(8,128)(2,1)S(1)} %get-tuple-element.33), channel_id=1, source_target_pairs={{0,4},{2,6},{4,0},{6,2},{8,12},{10,14},{12,8},{14,10},{16,20},{18,... | collective-permute-start | bytes 294920 | tf_op jit(solution)/shard_map/ppermute | solution.py:266
  28.5 6.6 %collective-permute-start.9 = (bf16[192,256]{1,0:T(8,128)(2,1)S(1)}, bf16[192,256]{1,0:T(8,128)(2,1)S(1)}, u32[]{:S(2)}, u32[]{:S(2)}) collective-permute-start(bf16[192,256]{1,0:T(8,128)(2,1)S(1)} %get-tuple-element.34), channel_id=1, source_target_pairs={{0,8},{2,10},{4,12},{6,14},{8,0},{10,2},{12,4},{14,6},{16,24},{18,... | collective-permute-start | bytes 294920 | tf_op jit(solution)/shard_map/ppermute | solution.py:266
  31.1 9.0 %collective-permute-start.17 = (bf16[192,256]{1,0:T(8,128)(2,1)S(1)}, bf16[192,256]{1,0:T(8,128)(2,1)S(1)}, u32[]{:S(2)}, u32[]{:S(2)}) collective-permute-start(bf16[192,256]{1,0:T(8,128)(2,1)S(1)} %reduce.2.after_ref.total_ref), channel_id=1, source_target_pairs={{0,16},{2,18},{4,20},{6,22},{8,24},{10,26},{12,28},{14,30},{16,0},... | collective-permute-start | bytes 294920 | tf_op jit(solution)/shard_map/ppermute | solution.py:266
  35.1 6.8 %collective-permute-start.13 = (bf16[192,256]{1,0:T(8,128)(2,1)S(1)}, bf16[192,256]{1,0:T(8,128)(2,1)S(1)}, u32[]{:S(2)}, u32[]{:S(2)}) collective-permute-start(bf16[192,256]{1,0:T(8,128)(2,1)S(1)} %reduce.3.total_ref), channel_id=1, source_target_pairs={{0,16},{2,18},{4,20},{6,22},{8,24},{10,26},{12,28},{14,30},{16,0},... | collective-permute-start | bytes 294920 | tf_op jit(solution)/shard_map/ppermute | solution.py:266
  38.1 12.4 %collective-permute-start.21 = (bf16[256,512]{1,0:T(8,128)(2,1)S(1)}, bf16[256,512]{1,0:T(8,128)(2,1)S(1)}, u32[]{:S(2)}, u32[]{:S(2)}) collective-permute-start(bf16[256,512]{1,0:T(8,128)(2,1)S(1)} %bitcast.10), channel_id=1, source_target_pairs={{0,1},{1,0},{2,3},{3,2},{4,5},{5,4},{6,7},{7,6},{8,9},{9,8},{10,11... | collective-permute-start | bytes 786440 | tf_op jit(solution)/shard_map/ppermute | solution.py:270
  39.9 10.6 %collective-permute-start.22 = (bf16[256,512]{1,0:T(8,128)(2,1)S(1)}, bf16[256,512]{1,0:T(8,128)(2,1)S(1)}, u32[]{:S(2)}, u32[]{:S(2)}) collective-permute-start(bf16[256,512]{1,0:T(8,128)(2,1)S(1)} %bitcast.9), channel_id=1, source_target_pairs={{0,1},{1,0},{2,3},{3,2},{4,5},{5,4},{6,7},{7,6},{8,9},{9,8},{10,11... | collective-permute-start | bytes 786440 | tf_op jit(solution)/shard_map/ppermute | solution.py:270
  40.1 6.7 %collective-permute-start.18 = (bf16[192,256]{1,0:T(8,128)(2,1)S(1)}, bf16[192,256]{1,0:T(8,128)(2,1)S(1)}, u32[]{:S(2)}, u32[]{:S(2)}) collective-permute-start(bf16[192,256]{1,0:T(8,128)(2,1)S(1)} %join.3.refs_0_), channel_id=1, source_target_pairs={{0,12},{2,14},{4,8},{6,10},{8,4},{10,6},{12,0},{14,2},{16,28},{18,... | collective-permute-start | bytes 294920 | tf_op jit(solution)/shard_map/ppermute | solution.py:266
  40.8 7.7 %collective-permute-start.19 = (bf16[192,256]{1,0:T(8,128)(2,1)S(1)}, bf16[192,256]{1,0:T(8,128)(2,1)S(1)}, u32[]{:S(2)}, u32[]{:S(2)}) collective-permute-start(bf16[192,256]{1,0:T(8,128)(2,1)S(1)} %join.3.refs_0_), channel_id=1, source_target_pairs={{0,4},{2,6},{4,0},{6,2},{8,12},{10,14},{12,8},{14,10},{16,20},{18,... | collective-permute-start | bytes 294920 | tf_op jit(solution)/shard_map/ppermute | solution.py:266
  41.8 7.1 %collective-permute-start.20 = (bf16[192,256]{1,0:T(8,128)(2,1)S(1)}, bf16[192,256]{1,0:T(8,128)(2,1)S(1)}, u32[]{:S(2)}, u32[]{:S(2)}) collective-permute-start(bf16[192,256]{1,0:T(8,128)(2,1)S(1)} %join.3.refs_0_), channel_id=1, source_target_pairs={{0,8},{2,10},{4,12},{6,14},{8,0},{10,2},{12,4},{14,6},{16,24},{18,... | collective-permute-start | bytes 294920 | tf_op jit(solution)/shard_map/ppermute | solution.py:266
  46.8 5.9 %collective-permute-start.14 = (bf16[192,256]{1,0:T(8,128)(2,1)S(1)}, bf16[192,256]{1,0:T(8,128)(2,1)S(1)}, u32[]{:S(2)}, u32[]{:S(2)}) collective-permute-start(bf16[192,256]{1,0:T(8,128)(2,1)S(1)} %join.2.refs_0_), channel_id=1, source_target_pairs={{0,12},{2,14},{4,8},{6,10},{8,4},{10,6},{12,0},{14,2},{16,28},{18,... | collective-permute-start | bytes 294920 | tf_op jit(solution)/shard_map/ppermute | solution.py:266
  48.5 4.9 %collective-permute-start.15 = (bf16[192,256]{1,0:T(8,128)(2,1)S(1)}, bf16[192,256]{1,0:T(8,128)(2,1)S(1)}, u32[]{:S(2)}, u32[]{:S(2)}) collective-permute-start(bf16[192,256]{1,0:T(8,128)(2,1)S(1)} %join.2.refs_0_), channel_id=1, source_target_pairs={{0,4},{2,6},{4,0},{6,2},{8,12},{10,14},{12,8},{14,10},{16,20},{18,... | collective-permute-start | bytes 294920 | tf_op jit(solution)/shard_map/ppermute | solution.py:266
  48.9 4.6 %collective-permute-start.16 = (bf16[192,256]{1,0:T(8,128)(2,1)S(1)}, bf16[192,256]{1,0:T(8,128)(2,1)S(1)}, u32[]{:S(2)}, u32[]{:S(2)}) collective-permute-start(bf16[192,256]{1,0:T(8,128)(2,1)S(1)} %join.2.refs_0_), channel_id=1, source_target_pairs={{0,8},{2,10},{4,12},{6,14},{8,0},{10,2},{12,4},{14,6},{16,24},{18,... | collective-permute-start | bytes 294920 | tf_op jit(solution)/shard_map/ppermute | solution.py:266
  50.4 3.2 %collective-permute-start.24 = (bf16[768,256]{1,0:T(8,128)(2,1)S(1)}, bf16[768,256]{1,0:T(8,128)(2,1)S(1)}, u32[]{:S(2)}, u32[]{:S(2)}) collective-permute-start(bf16[768,256]{1,0:T(8,128)(2,1)S(1)} %gather.2.rest_0_), channel_id=1, source_target_pairs={{0,2},{2,0},{4,6},{6,4},{8,10},{10,8},{12,14},{14,12},{16,18},{18,... | collective-permute-start | bytes 1179656 | tf_op jit(solution)/shard_map/ppermute | solution.py:266
  53.6 1.8 %collective-permute-start.23 = (bf16[768,256]{1,0:T(8,128)(2,1)S(1)}, bf16[768,256]{1,0:T(8,128)(2,1)S(1)}, u32[]{:S(2)}, u32[]{:S(2)}) collective-permute-start(bf16[768,256]{1,0:T(8,128)(2,1)S(1)} %gather.3.rest_0_), channel_id=1, source_target_pairs={{0,2},{2,0},{4,6},{6,4},{8,10},{10,8},{12,14},{14,12},{16,18},{18,... | collective-permute-start | bytes 1179656 | tf_op jit(solution)/shard_map/ppermute | solution.py:266

commit v11 on v10

--- a/solution.py
+++ b/solution.py
@@ -137,31 +137,28 @@
     place, own_ref, received_ref, centre_ref, came_ref, *rest, deltas, scale
 ):
     added, (keep_ref, sum_ref, *send_refs) = rest[:deltas], rest[deltas:]
-    _, rows, width = keep_ref.shape
+    rows, width = keep_ref.shape
     heads = sum_ref.shape[0]
     sum_ref[...] = sum(ref[...] for ref in added)
 
     def column(ref, span):
         row = sum_ref[pl.ds(place[2], 1), span] - ref[pl.ds(heads + place[2], 1), span]
-        return jnp.transpose(jnp.broadcast_to(row * scale, (128, 2 * rows)))
+        return jnp.transpose(jnp.broadcast_to(row * scale, (128, rows)))
 
     for step in (3, 1, 2, 0):
-        span = ways((place[3] ^ step) * 2 * rows, 2 * rows)
+        target = send_refs[step - 1] if step else keep_ref
+        span = ways((place[3] ^ step) * rows, rows)
         own_gap, came_gap = column(centre_ref, span), column(came_ref, span)
-        for part in range(2):
-            target = send_refs[3 * part + step - 1] if step else keep_ref.at[part]
-            span = ways((2 * (place[3] ^ step) + part) * rows, rows)
-            inside = slice(part * rows, (part + 1) * rows)
-            for start in range(0, width, 128):
-                columns = slice(start, start + 128)
-                direct = own_ref[0, span, columns] + received_ref[0, span, columns]
-                weighted = own_ref[1, span, columns] * own_gap[inside]
-                weighted += received_ref[1, span, columns] * came_gap[inside]
-                target[:, columns] = (scale * direct - weighted).astype(target.dtype)
+        for start in range(0, width, 128):
+            columns = slice(start, start + 128)
+            direct = own_ref[0, span, columns] + received_ref[0, span, columns]
+            weighted = own_ref[1, span, columns] * own_gap
+            weighted += received_ref[1, span, columns] * came_gap
+            target[:, columns] = (scale * direct - weighted).astype(target.dtype)
 
 
 def key_kernel(
-    place, delta_ref, probs_ref, dprobs_ref, targets_ref, q_ref, after_ref, own_ref, send_ref,
+    place, delta_ref, probs_ref, dprobs_ref, targets_ref, q_ref, own_ref, send_ref,
     low_ref, *, chunk, scale,
 ):
     heads = probs_ref.shape[0]
@@ -184,11 +181,14 @@
                 send_ref[step - 1, :, columns] = term.astype(jnp.bfloat16)
 
 
-def reduce_kernel(keep_ref, first_ref, second_ref, third_ref, *rest, part):
-    total = keep_ref[part]
-    for ref in (first_ref, second_ref, third_ref):
-        total += ref[...].astype(jnp.float32)
-    rest[-1][...] = total.astype(rest[-1].dtype)
+def reduce_kernel(keep_ref, first_ref, second_ref, third_ref, after_value, after_key, *out_refs):
+    rows = out_refs[0].shape[0]
+    for part, out_ref in enumerate(out_refs):
+        span = slice(part * rows, (part + 1) * rows)
+        total = keep_ref[span]
+        for ref in (first_ref, second_ref, third_ref):
+            total += ref[span].astype(jnp.float32)
+        out_ref[...] = total.astype(out_ref.dtype)
 
 
 def join_kernel(total_ref, came_ref, out_ref):
@@ -354,30 +354,19 @@
             other_centre = added[1]
         stride *= steps
     eighth = query_count // 8
-    near_part = pltpu.VMEM((eighth, width), bf16)
+    quarter = 2 * eighth
     keep, delta, *send = call(
         partial(combine_kernel, deltas=len(added), scale=scale),
         "combine",
         (place, query_terms(True, "own_head"), received, centre, other_centre, *added),
         [IN_SMEM] + [IN_VMEM] * (4 + len(added)),
         [
-            pltpu.VMEM((2, eighth, width), f32),
+            pltpu.VMEM((quarter, width), f32),
             pltpu.VMEM((heads, query_count), f32),
         ]
-        + [near_part] * 6,
+        + [pltpu.VMEM((quarter, width), bf16)] * 3,
         work // 4,
     )
-    def reduced(part, after):
-        came = {step: flip(send[3 * part + step - 1], 2 * step) for step in (3, 1, 2)}
-        return call(
-            partial(reduce_kernel, part=part),
-            "reduce",
-            (keep, came[3], came[1], came[2], *after),
-            [IN_VMEM] * 4 + [IN_HBM] * len(after),
-            [near_part if bits == 4 else pltpu.VMEM((eighth, width), f32)],
-            work // 16,
-        )[0]
-
     def joined(total):
         for bit in range(3, bits - 1):
             split = total.reshape(2, -1, width)
@@ -397,11 +386,10 @@
             whole = jnp.concatenate([whole, flip(whole, 1 << bit)], axis=0)
         return whole
 
-    totals = [reduced(0, ())]
     value_own, value_send = call(
         value_kernel,
         "value_terms",
-        (place, probs, g_near, totals[0]),
+        (place, probs, g_near, delta),
         [IN_SMEM] + [IN_VMEM] * 2 + [IN_HBM],
         shares,
         2 * work,
@@ -410,15 +398,23 @@
     key_own, key_send = call(
         partial(key_kernel, chunk=chunk, scale=scale),
         "key_terms",
-        (place, delta, probs, dprobs, targets, q_near, totals[0]),
-        [IN_SMEM] + [IN_VMEM] * 5 + [IN_HBM],
+        (place, delta, probs, dprobs, targets, q_near),
+        [IN_SMEM] + [IN_VMEM] * 5,
         shares,
         2 * work,
         [pltpu.VMEM((heads, value_count, query_count), bf16)],
     )
     key_came = swap_shares(key_send)
 
-    totals.append(reduced(1, (value_send, key_send)))
+    came = {step: flip(send[step - 1], 2 * step) for step in (3, 1, 2)}
+    totals = call(
+        reduce_kernel,
+        "reduce",
+        (keep, came[3], came[1], came[2], value_send, key_send),
+        [IN_VMEM] * 4 + [IN_HBM] * 2,
+        [pltpu.VMEM((eighth, width), bf16 if bits == 4 else f32)] * 2,
+        work // 8,
+    )
     piece = eighth >> (bits - 4)
     inner = 0
     for bit in range(3, bits - 1):

time: 57.1 us -> 56.1 us (0.982)
  starting transfers between devices: 24.8 us -> 22.2 us
  waiting for transfers between devices: 12.9 us -> 14.3 us
    ppermute x23 -> x20, starting transfers between devices: 22.8 us -> 20.1 us  [flip(): lax.ppermute(array, 'val', [(i, i ^ mask) for i in range(value_devices)])]
    ppermute x23 -> x20, waiting for transfers between devices: 12.9 us -> 14.3 us  [flip(): lax.ppermute(array, 'val', [(i, i ^ mask) for i in range(value_devices)])]
    pallas_call x17 -> x16, Pallas kernels: 18 us -> 18.3 us  [call(): pl.pallas_call(kernel, in_specs=in_specs, out_specs=[IN_VMEM] * len(outpu...]
  transfers between devices with their start and end apart: 25 -> 22, of which waited for: 11 -> 9; matrix products, arithmetic and copies ran while one was open for 0% -> 0% of each run, Pallas kernels for 20% -> 21%
where the time goes in v11:
time: 56.1 us; the launch traced here: 55.9 us
  starting transfers between devices  22.2 us (40%)
  Pallas kernels  18.3 us (33%)
  waiting for transfers between devices  14.3 us (25%)
  between operations  0.83 us (1%)
    ppermute x20, starting transfers between devices, flip(): lax.ppermute(array, 'val', [(i, i ^ mask) for i in range(value_devices)])  20.1 us
    pallas_call x16, Pallas kernels, call(): pl.pallas_call(kernel, in_specs=in_specs, out_specs=[IN_VMEM] * len(outpu...  18.3 us
    ppermute x20, waiting for transfers between devices, flip(): lax.ppermute(array, 'val', [(i, i ^ mask) for i in range(value_devices)])  14.3 us
    ppermute x2, starting transfers between devices, swap_shares(): lax.ppermute(send[step - 1], 'qry', [(i, (i + step) % parts) for i in ran...  2.16 us
  transfers between devices with their start and end apart: 22, of which 9 were waited for; matrix products, arithmetic and copies ran while one was open for 0% of the time, Pallas kernels for 21%

profile of v11, /device:TPU:0, one launch (start us, length us, event | category | flops | bytes accessed | tf_op | source)
XLA Modules:
  0.0 55.9 jit_solution(12258358349641467737)
XLA Ops:
  0.7 0.1 pad_add_fusion.1.place
  0.7 0.0 copy-start
  0.7 4.2 %forward_pass.1 = (f32[4,1536]{1,0:T(4,128)S(1)}, f32[2,512,1536]{2,1,0:T(8,128)S(1)}, f32[2,512,1536]{2,1,0:T(8,128)S(1)}, bf16[1536,512]{1,0:T(8,128)(2,1)S(1)...) custom-call(s32[4]{0:T(128)S(1)} %pad_add_fusion.1.place, s32[2,1,6]{2,1,0:T(1,128)} %compat_hbm.1, ...), custom_call_target="tpu_custom_call" | custom-call | flops 1610612736 | bytes 1610612 | tf_op jit(solution)/shard_map/forward_pass/pallas_call | solution.py:238
  4.9 0.1 collective-permute-start
  5.0 2.8 %collective-permute-start.1 = (f32[4,1536]{1,0:T(4,128)S(1)}, f32[4,1536]{1,0:T(4,128)S(1)}, u32[]{:S(2)}, u32[]{:S(2)}) collective-permute-start(f32[4,1536]{1,0:T(4,128)S(1)} %get-tuple-element.24.delta_ref.refs_0_.centre_ref), channel_id=1, source_target_pairs={{0,4},{2,6},{4,0},{6,2},{8,12},{10,14},{12,8},{14,10},{16,20},{18,... | collective-permute-start | bytes 73736 | tf_op jit(solution)/shard_map/ppermute | solution.py:266
  7.8 0.0 collective-permute-start.2
  7.8 0.0 copy-done
  7.8 2.0 %other_head.1.refs_4_ = f32[2,1536,256]{2,1,0:T(8,128)S(1)} custom-call(s32[4]{0:T(128)S(1)} %pad_add_fusion.1.place, f32[4,1536]{1,0:T(4,128)S(1)} %get-tuple-element.24.delta_ref.refs_0_.centre_ref, f32[2,512,1536]{2,1,0:T(8,128)S(1)} %get-tuple-element.25.probs_ref, f32[2,512,1536]{2,1,0:T(8,128)S(1)} %get-tuple-element.26.dprobs_ref, ...), custom_call_target="tpu_custom_call" | custom-call | flops 805306368 | bytes 805306 | tf_op jit(solution)/shard_map/other_head/pallas_call | solution.py:238
  9.8 0.0 collective-permute-done.refs_1_.came_ref
  9.8 0.0 collective-permute-done.1.refs_2_
  9.8 1.3 %collective-permute-done.2.refs_3_ = f32[4,1536]{1,0:T(4,128)S(1)} collective-permute-done((f32[4,1536]{1,0:T(4,128)S(1)}, f32[4,1536]{1,0:T(4,128)S(1)}, u32[]{:S(2)}, u32[]{:S(2)}) %collective-permute-start.2) | collective-permute-done | bytes 24608 | tf_op jit(solution)/shard_map/ppermute | solution.py:266
  11.1 0.2 collective-permute-start.3
  11.3 1.4 %collective-permute-start.4 = (f32[2,1536]{1,0:T(2,128)S(1)}, f32[2,1536]{1,0:T(2,128)S(1)}, u32[]{:S(2)}, u32[]{:S(2)}) collective-permute-start(f32[2,1536]{1,0:T(2,128)S(1)} %get-tuple-element.29.rest_0_), channel_id=1, source_target_pairs={{0,8},{2,10},{4,12},{6,14},{8,0},{10,2},{12,4},{14,6},{16,24},{18,... | collective-permute-start | bytes 36872 | tf_op jit(solution)/shard_map/ppermute | solution.py:266
  12.7 3.2 %collective-permute-start.5 = (f32[2,1536]{1,0:T(2,128)S(1)}, f32[2,1536]{1,0:T(2,128)S(1)}, u32[]{:S(2)}, u32[]{:S(2)}) collective-permute-start(f32[2,1536]{1,0:T(2,128)S(1)} %get-tuple-element.29.rest_0_), channel_id=1, source_target_pairs={{0,16},{2,18},{4,20},{6,22},{8,24},{10,26},{12,28},{14,30},{16,0},... | collective-permute-start | bytes 36872 | tf_op jit(solution)/shard_map/ppermute | solution.py:266
  15.8 0.0 collective-permute-start.6
  15.8 2.0 %own_head.1.own_ref = f32[2,1536,256]{2,1,0:T(8,128)S(1)} custom-call(s32[4]{0:T(128)S(1)} %pad_add_fusion.1.place, f32[4,1536]{1,0:T(4,128)S(1)} %get-tuple-element.24.delta_ref.refs_0_.centre_ref, f32[2,512,1536]{2,1,0:T(8,128)S(1)} %get-tuple-element.25.probs_ref, f32[2,512,1536]{2,1,0:T(8,128)S(1)} %get-tuple-element.26.dprobs_ref, ...), custom_call_target="tpu_custom_call" | custom-call | flops 805306368 | bytes 805306 | tf_op jit(solution)/shard_map/own_head/pallas_call | solution.py:238
  17.8 0.0 collective-permute-done.4.rest_1_
  17.8 0.0 collective-permute-done.5.rest_2_
  17.8 3.5 %collective-permute-done.6.rest_3_ = f32[2,1536]{1,0:T(2,128)S(1)} collective-permute-done((f32[2,1536]{1,0:T(2,128)S(1)}, f32[2,1536]{1,0:T(2,128)S(1)}, u32[]{:S(2)}, u32[]{:S(2)}) %collective-permute-start.6) | collective-permute-done | bytes 12320 | tf_op jit(solution)/shard_map/ppermute | solution.py:266
  21.3 0.0 collective-permute-done.3.received_ref
  21.3 1.2 %combine.1 = (f32[384,256]{1,0:T(8,128)S(1)}, f32[2,1536]{1,0:T(2,128)S(1)}, bf16[384,256]{1,0:T(8,128)(2,1)S(1)}, bf16[384,256]{1,0:T(8,128)(2,1)S(1)}, bf16[384,256]{1,0:T(8,128)(2,1)S(1)}) custom-call(s32[4]{0:T(128)S(1)} %pad_add_fusion.1.place, f32[2,1536,256]{2,1,0:T(8,128)S(1)} %own_head.1.own_ref, ...), custom_call_target="tpu_custom_call" | custom-call | flops 100663296 | bytes 100663 | tf_op jit(solution)/shard_map/combine/pallas_call | solution.py:238
  22.5 0.1 collective-permute-start.7
  22.6 0.8 %collective-permute-start.8 = (bf16[384,256]{1,0:T(8,128)(2,1)S(1)}, bf16[384,256]{1,0:T(8,128)(2,1)S(1)}, u32[]{:S(2)}, u32[]{:S(2)}) collective-permute-start(bf16[384,256]{1,0:T(8,128)(2,1)S(1)} %get-tuple-element.32), channel_id=1, source_target_pairs={{0,4},{2,6},{4,0},{6,2},{8,12},{10,14},{12,8},{14,10},{16,20},{18,... | collective-permute-start | bytes 589832 | tf_op jit(solution)/shard_map/ppermute | solution.py:266
  23.4 2.7 %collective-permute-start.9 = (bf16[384,256]{1,0:T(8,128)(2,1)S(1)}, bf16[384,256]{1,0:T(8,128)(2,1)S(1)}, u32[]{:S(2)}, u32[]{:S(2)}) collective-permute-start(bf16[384,256]{1,0:T(8,128)(2,1)S(1)} %get-tuple-element.33), channel_id=1, source_target_pairs={{0,8},{2,10},{4,12},{6,14},{8,0},{10,2},{12,4},{14,6},{16,24},{18,... | collective-permute-start | bytes 589832 | tf_op jit(solution)/shard_map/ppermute | solution.py:266
  26.1 2.2 %key_terms.1 = (f32[256,512]{1,0:T(8,128)S(1)}, bf16[1,256,512]{2,1,0:T(8,128)(2,1)S(1)}) custom-call(s32[4]{0:T(128)S(1)} %pad_add_fusion.1.place, f32[2,1536]{1,0:T(2,128)S(1)} %get-tuple-element.35.after_ref.delta_ref, f32[2,512,1536]{2,1,0:T(8,128)S(1)} %get-tuple-element.25.probs_ref, f32[2,512,1536]{2,1,0:T(8,128)S(1)} %get-tuple-element.26.dprobs_ref, ...), custom_call_target="tpu_custom_call" | custom-call | flops 805306368 | bytes 805306 | tf_op jit(solution)/shard_map/key_terms/pallas_call | solution.py:238
  28.3 0.4 collective-permute-start.18
  28.8 1.5 %value_terms.1 = (f32[256,512]{1,0:T(8,128)S(1)}, bf16[1,256,512]{2,1,0:T(8,128)(2,1)S(1)}) custom-call(s32[4]{0:T(128)S(1)} %pad_add_fusion.1.place, f32[2,512,1536]{2,1,0:T(8,128)S(1)} %get-tuple-element.25.probs_ref, bf16[1536,512]{1,0:T(8,128)(2,1)S(1)} %get-tuple-element.34.g_ref, f32[2,1536]{1,0:T(2,128)S(1)} %get-tuple-element.35.after_ref.delta_ref), custom_call_target="tpu_custom_call" | custom-call | flops 805306368 | bytes 805306 | tf_op jit(solution)/shard_map/value_terms/pallas_call | solution.py:238
  30.3 1.7 %collective-permute-start.19 = (bf16[256,512]{1,0:T(8,128)(2,1)S(1)}, bf16[256,512]{1,0:T(8,128)(2,1)S(1)}, u32[]{:S(2)}, u32[]{:S(2)}) collective-permute-start(bf16[256,512]{1,0:T(8,128)(2,1)S(1)} %bitcast.12), channel_id=1, source_target_pairs={{0,1},{1,0},{2,3},{3,2},{4,5},{5,4},{6,7},{7,6},{8,9},{9,8},{10,11... | collective-permute-start | bytes 786440 | tf_op jit(solution)/shard_map/ppermute | solution.py:270
  32.0 0.0 collective-permute-done.7.first_ref
  32.0 0.3 collective-permute-done.8.second_ref
  32.3 0.0 collective-permute-done.9.third_ref
  32.3 0.1 reduce.1
  32.4 0.4 collective-permute-start.14
  32.9 2.5 %collective-permute-start.10 = (bf16[192,256]{1,0:T(8,128)(2,1)S(1)}, bf16[192,256]{1,0:T(8,128)(2,1)S(1)}, u32[]{:S(2)}, u32[]{:S(2)}) collective-permute-start(bf16[192,256]{1,0:T(8,128)(2,1)S(1)} %get-tuple-element.39.total_ref), channel_id=1, source_target_pairs={{0,16},{2,18},{4,20},{6,22},{8,24},{10,26},{12,28},{14,30},{16,0},... | collective-permute-start | bytes 294920 | tf_op jit(solution)/shard_map/ppermute | solution.py:266
  35.4 6.0 %collective-permute-done.14.came_ref = bf16[192,256]{1,0:T(8,128)(2,1)S(1)} collective-permute-done((bf16[192,256]{1,0:T(8,128)(2,1)S(1)}, bf16[192,256]{1,0:T(8,128)(2,1)S(1)}, u32[]{:S(2)}, u32[]{:S(2)}) %collective-permute-start.14) | collective-permute-done | bytes 98336 | tf_op jit(solution)/shard_map/ppermute | solution.py:266
  41.4 0.1 collective-permute-start.15
  41.5 1.6 %collective-permute-start.16 = (bf16[192,256]{1,0:T(8,128)(2,1)S(1)}, bf16[192,256]{1,0:T(8,128)(2,1)S(1)}, u32[]{:S(2)}, u32[]{:S(2)}) collective-permute-start(bf16[192,256]{1,0:T(8,128)(2,1)S(1)} %join.3.refs_0_), channel_id=1, source_target_pairs={{0,4},{2,6},{4,0},{6,2},{8,12},{10,14},{12,8},{14,10},{16,20},{18,... | collective-permute-start | bytes 294920 | tf_op jit(solution)/shard_map/ppermute | solution.py:266
  43.1 0.0 collective-permute-done.10.came_ref
  43.1 1.9 %collective-permute-start.17 = (bf16[192,256]{1,0:T(8,128)(2,1)S(1)}, bf16[192,256]{1,0:T(8,128)(2,1)S(1)}, u32[]{:S(2)}, u32[]{:S(2)}) collective-permute-start(bf16[192,256]{1,0:T(8,128)(2,1)S(1)} %join.3.refs_0_), channel_id=1, source_target_pairs={{0,8},{2,10},{4,12},{6,14},{8,0},{10,2},{12,4},{14,6},{16,24},{18,... | collective-permute-start | bytes 294920 | tf_op jit(solution)/shard_map/ppermute | solution.py:266
  45.0 0.0 collective-permute-done.18
  45.0 1.0 %collective-permute-start.11 = (bf16[192,256]{1,0:T(8,128)(2,1)S(1)}, bf16[192,256]{1,0:T(8,128)(2,1)S(1)}, u32[]{:S(2)}, u32[]{:S(2)}) collective-permute-start(bf16[192,256]{1,0:T(8,128)(2,1)S(1)} %join.2.refs_0_), channel_id=1, source_target_pairs={{0,12},{2,14},{4,8},{6,10},{8,4},{10,6},{12,0},{14,2},{16,28},{18,... | collective-permute-start | bytes 294920 | tf_op jit(solution)/shard_map/ppermute | solution.py:266
  46.0 0.0 collective-permute-done.19
  46.0 0.6 %collective-permute-start.12 = (bf16[192,256]{1,0:T(8,128)(2,1)S(1)}, bf16[192,256]{1,0:T(8,128)(2,1)S(1)}, u32[]{:S(2)}, u32[]{:S(2)}) collective-permute-start(bf16[192,256]{1,0:T(8,128)(2,1)S(1)} %join.2.refs_0_), channel_id=1, source_target_pairs={{0,4},{2,6},{4,0},{6,2},{8,12},{10,14},{12,8},{14,10},{16,20},{18,... | collective-permute-start | bytes 294920 | tf_op jit(solution)/shard_map/ppermute | solution.py:266
  46.7 1.3 %collective-permute-done.15.refs_1_ = bf16[192,256]{1,0:T(8,128)(2,1)S(1)} collective-permute-done((bf16[192,256]{1,0:T(8,128)(2,1)S(1)}, bf16[192,256]{1,0:T(8,128)(2,1)S(1)}, u32[]{:S(2)}, u32[]{:S(2)}) %collective-permute-start.15) | collective-permute-done | bytes 98336 | tf_op jit(solution)/shard_map/ppermute | solution.py:266
  48.0 0.6 %collective-permute-start.13 = (bf16[192,256]{1,0:T(8,128)(2,1)S(1)}, bf16[192,256]{1,0:T(8,128)(2,1)S(1)}, u32[]{:S(2)}, u32[]{:S(2)}) collective-permute-start(bf16[192,256]{1,0:T(8,128)(2,1)S(1)} %join.2.refs_0_), channel_id=1, source_target_pairs={{0,8},{2,10},{4,12},{6,14},{8,0},{10,2},{12,4},{14,6},{16,24},{18,... | collective-permute-start | bytes 294920 | tf_op jit(solution)/shard_map/ppermute | solution.py:266
  48.6 0.1 pad_add_fusion.place
  48.7 0.9 %pool_sum.1 = (bf16[256,512]{1,0:T(8,128)(2,1)}, bf16[256,512]{1,0:T(8,128)(2,1)}) custom-call(f32[256,512]{1,0:T(8,128)S(1)} %get-tuple-element.41.key_ref, f32[256,512]{1,0:T(8,128)S(1)} %get-tuple-element.42.value_ref, bf16[1,256,512]{2,1,0:T(8,128)(2,1)S(1)} %bitcast.9, bf16[1,256,512]{2,1,0:T(8,128)(2,1)S(1)} %bitcast.10), custom_call_target="tpu_custom_call" | custom-call | flops 50331648 | bytes 50331 | tf_op jit(solution)/shard_map/pool_sum/pallas_call | solution.py:238
  49.6 0.0 collective-permute-done.16.refs_2_
  49.6 0.6 %collective-permute-done.17.refs_3_ = bf16[192,256]{1,0:T(8,128)(2,1)S(1)} collective-permute-done((bf16[192,256]{1,0:T(8,128)(2,1)S(1)}, bf16[192,256]{1,0:T(8,128)(2,1)S(1)}, u32[]{:S(2)}, u32[]{:S(2)}) %collective-permute-start.17) | collective-permute-done | bytes 98336 | tf_op jit(solution)/shard_map/ppermute | solution.py:266
  50.2 0.1 collective-permute-start.21
  50.3 1.3 %first_rows.1.refs_4_.rest_2_ = bf16[1536,512]{1,0:T(8,128)(2,1)} custom-call(s32[3]{0:T(128)S(1)} %pad_add_fusion.place, bf16[768,256]{1,0:T(8,128)(2,1)S(1)} %gather.2.rest_0_, bf16[256,512]{1,0:T(8,128)(2,1)} %get-tuple-element.22.rest_1_), custom_call_target="tpu_custom_call" | custom-call | flops 201326592 | bytes 201326 | tf_op jit(solution)/shard_map/first_rows/pallas_call | solution.py:238
  51.6 0.2 collective-permute-done.11.refs_1_
  51.8 0.0 collective-permute-done.12.refs_2_
  51.8 0.9 %collective-permute-done.13.refs_3_ = bf16[192,256]{1,0:T(8,128)(2,1)S(1)} collective-permute-done((bf16[192,256]{1,0:T(8,128)(2,1)S(1)}, bf16[192,256]{1,0:T(8,128)(2,1)S(1)}, u32[]{:S(2)}, u32[]{:S(2)}) %collective-permute-start.13) | collective-permute-done | bytes 98336 | tf_op jit(solution)/shard_map/ppermute | solution.py:266
  52.8 0.1 collective-permute-start.20
  52.8 0.0 collective-permute-done.21.rest_1_
  52.8 1.5 %own_rows.1.rest_1_ = bf16[1536,512]{1,0:T(8,128)(2,1)} custom-call(s32[3]{0:T(128)S(1)} %pad_add_fusion.place, bf16[768,256]{1,0:T(8,128)(2,1)S(1)} %gather.3.rest_0_, bf16[768,256]{1,0:T(8,128)(2,1)S(1)} %collective-permute-done.21.rest_1_, bf16[1536,512]{1,0:T(8,128)(2,1)} %first_rows.1.refs_4_.rest_2_), custom_call_target="tpu_custom_call", output_to_operand_aliasing={{}: (3, {})} | custom-call | flops 201326592 | bytes 201326 | tf_op jit(solution)/shard_map/own_rows/pallas_call | solution.py:238
  54.3 0.2 collective-permute-done.20.rest_0_
  54.5 1.3 %other_rows.1 = bf16[1536,512]{1,0:T(8,128)(2,1)} custom-call(s32[3]{0:T(128)S(1)} %pad_add_fusion.place, bf16[768,256]{1,0:T(8,128)(2,1)S(1)} %collective-permute-done.20.rest_0_, bf16[1536,512]{1,0:T(8,128)(2,1)} %own_rows.1.rest_1_), custom_call_target="tpu_custom_call", output_to_operand_aliasing={{}: (2, {})} | custom-call | flops 201326592 | bytes 201326 | tf_op jit(solution)/shard_map/other_rows/pallas_call | solution.py:238
  (5 shorter events, 0.1 us)
Async XLA Ops:
  0.7 7.1 %copy-start = (s32[1536,2]{0,1:T(2,128)S(1)}, s32[1536,2]{0,1:T(2,128)}, u32[]{:S(2)}) copy-start(s32[1536,2]{0,1:T(2,128)} %param.13) | copy-start | bytes 36868
  4.9 4.9 %collective-permute-start = (f32[4,1536]{1,0:T(4,128)S(1)}, f32[4,1536]{1,0:T(4,128)S(1)}, u32[]{:S(2)}, u32[]{:S(2)}) collective-permute-start(f32[4,1536]{1,0:T(4,128)S(1)} %get-tuple-element.24.delta_ref.refs_0_.centre_ref), channel_id=1, source_target_pairs={{0,2},{2,0},{4,6},{6,4},{8,10},{10,8},{12,14},{14,12},{16,18},{18,... | collective-permute-start | bytes 73736 | tf_op jit(solution)/shard_map/ppermute | solution.py:266
  5.0 4.8 %collective-permute-start.1 = (f32[4,1536]{1,0:T(4,128)S(1)}, f32[4,1536]{1,0:T(4,128)S(1)}, u32[]{:S(2)}, u32[]{:S(2)}) collective-permute-start(f32[4,1536]{1,0:T(4,128)S(1)} %get-tuple-element.24.delta_ref.refs_0_.centre_ref), channel_id=1, source_target_pairs={{0,4},{2,6},{4,0},{6,2},{8,12},{10,14},{12,8},{14,10},{16,20},{18,... | collective-permute-start | bytes 73736 | tf_op jit(solution)/shard_map/ppermute | solution.py:266
  7.8 3.3 %collective-permute-start.2 = (f32[4,1536]{1,0:T(4,128)S(1)}, f32[4,1536]{1,0:T(4,128)S(1)}, u32[]{:S(2)}, u32[]{:S(2)}) collective-permute-start(f32[4,1536]{1,0:T(4,128)S(1)} %get-tuple-element.24.delta_ref.refs_0_.centre_ref), channel_id=1, source_target_pairs={{0,6},{2,4},{4,2},{6,0},{8,14},{10,12},{12,10},{14,8},{16,22},{18,... | collective-permute-start | bytes 73736 | tf_op jit(solution)/shard_map/ppermute | solution.py:266
  11.1 10.2 %collective-permute-start.3 = (f32[2,1536,256]{2,1,0:T(8,128)S(1)}, f32[2,1536,256]{2,1,0:T(8,128)S(1)}, u32[]{:S(2)}, u32[]{:S(2)}) collective-permute-start(f32[2,1536,256]{2,1,0:T(8,128)S(1)} %get-tuple-element.28), channel_id=1, source_target_pairs={{0,2},{2,0},{4,6},{6,4},{8,10},{10,8},{12,14},{14,12},{16,18},{18,... | collective-permute-start | bytes 9437192 | tf_op jit(solution)/shard_map/ppermute | solution.py:266
  11.3 6.5 %collective-permute-start.4 = (f32[2,1536]{1,0:T(2,128)S(1)}, f32[2,1536]{1,0:T(2,128)S(1)}, u32[]{:S(2)}, u32[]{:S(2)}) collective-permute-start(f32[2,1536]{1,0:T(2,128)S(1)} %get-tuple-element.29.rest_0_), channel_id=1, source_target_pairs={{0,8},{2,10},{4,12},{6,14},{8,0},{10,2},{12,4},{14,6},{16,24},{18,... | collective-permute-start | bytes 36872 | tf_op jit(solution)/shard_map/ppermute | solution.py:266
  12.7 5.2 %collective-permute-start.5 = (f32[2,1536]{1,0:T(2,128)S(1)}, f32[2,1536]{1,0:T(2,128)S(1)}, u32[]{:S(2)}, u32[]{:S(2)}) collective-permute-start(f32[2,1536]{1,0:T(2,128)S(1)} %get-tuple-element.29.rest_0_), channel_id=1, source_target_pairs={{0,16},{2,18},{4,20},{6,22},{8,24},{10,26},{12,28},{14,30},{16,0},... | collective-permute-start | bytes 36872 | tf_op jit(solution)/shard_map/ppermute | solution.py:266
  15.8 5.5 %collective-permute-start.6 = (f32[2,1536]{1,0:T(2,128)S(1)}, f32[2,1536]{1,0:T(2,128)S(1)}, u32[]{:S(2)}, u32[]{:S(2)}) collective-permute-start(f32[2,1536]{1,0:T(2,128)S(1)} %get-tuple-element.29.rest_0_), channel_id=1, source_target_pairs={{0,24},{2,26},{4,28},{6,30},{8,16},{10,18},{12,20},{14,22},{16,8},... | collective-permute-start | bytes 36872 | tf_op jit(solution)/shard_map/ppermute | solution.py:266
  22.5 9.5 %collective-permute-start.7 = (bf16[384,256]{1,0:T(8,128)(2,1)S(1)}, bf16[384,256]{1,0:T(8,128)(2,1)S(1)}, u32[]{:S(2)}, u32[]{:S(2)}) collective-permute-start(bf16[384,256]{1,0:T(8,128)(2,1)S(1)} %get-tuple-element.31), channel_id=1, source_target_pairs={{0,12},{2,14},{4,8},{6,10},{8,4},{10,6},{12,0},{14,2},{16,28},{18,... | collective-permute-start | bytes 589832 | tf_op jit(solution)/shard_map/ppermute | solution.py:266
  22.6 9.7 %collective-permute-start.8 = (bf16[384,256]{1,0:T(8,128)(2,1)S(1)}, bf16[384,256]{1,0:T(8,128)(2,1)S(1)}, u32[]{:S(2)}, u32[]{:S(2)}) collective-permute-start(bf16[384,256]{1,0:T(8,128)(2,1)S(1)} %get-tuple-element.32), channel_id=1, source_target_pairs={{0,4},{2,6},{4,0},{6,2},{8,12},{10,14},{12,8},{14,10},{16,20},{18,... | collective-permute-start | bytes 589832 | tf_op jit(solution)/shard_map/ppermute | solution.py:266
  23.4 8.9 %collective-permute-start.9 = (bf16[384,256]{1,0:T(8,128)(2,1)S(1)}, bf16[384,256]{1,0:T(8,128)(2,1)S(1)}, u32[]{:S(2)}, u32[]{:S(2)}) collective-permute-start(bf16[384,256]{1,0:T(8,128)(2,1)S(1)} %get-tuple-element.33), channel_id=1, source_target_pairs={{0,8},{2,10},{4,12},{6,14},{8,0},{10,2},{12,4},{14,6},{16,24},{18,... | collective-permute-start | bytes 589832 | tf_op jit(solution)/shard_map/ppermute | solution.py:266
  28.3 16.7 %collective-permute-start.18 = (bf16[256,512]{1,0:T(8,128)(2,1)S(1)}, bf16[256,512]{1,0:T(8,128)(2,1)S(1)}, u32[]{:S(2)}, u32[]{:S(2)}) collective-permute-start(bf16[256,512]{1,0:T(8,128)(2,1)S(1)} %bitcast.11), channel_id=1, source_target_pairs={{0,1},{1,0},{2,3},{3,2},{4,5},{5,4},{6,7},{7,6},{8,9},{9,8},{10,11... | collective-permute-start | bytes 786440 | tf_op jit(solution)/shard_map/ppermute | solution.py:270
  30.3 15.7 %collective-permute-start.19 = (bf16[256,512]{1,0:T(8,128)(2,1)S(1)}, bf16[256,512]{1,0:T(8,128)(2,1)S(1)}, u32[]{:S(2)}, u32[]{:S(2)}) collective-permute-start(bf16[256,512]{1,0:T(8,128)(2,1)S(1)} %bitcast.12), channel_id=1, source_target_pairs={{0,1},{1,0},{2,3},{3,2},{4,5},{5,4},{6,7},{7,6},{8,9},{9,8},{10,11... | collective-permute-start | bytes 786440 | tf_op jit(solution)/shard_map/ppermute | solution.py:270
  32.4 9.0 %collective-permute-start.14 = (bf16[192,256]{1,0:T(8,128)(2,1)S(1)}, bf16[192,256]{1,0:T(8,128)(2,1)S(1)}, u32[]{:S(2)}, u32[]{:S(2)}) collective-permute-start(bf16[192,256]{1,0:T(8,128)(2,1)S(1)} %get-tuple-element.40.total_ref), channel_id=1, source_target_pairs={{0,16},{2,18},{4,20},{6,22},{8,24},{10,26},{12,28},{14,30},{16,0},... | collective-permute-start | bytes 294920 | tf_op jit(solution)/shard_map/ppermute | solution.py:266
  32.9 10.2 %collective-permute-start.10 = (bf16[192,256]{1,0:T(8,128)(2,1)S(1)}, bf16[192,256]{1,0:T(8,128)(2,1)S(1)}, u32[]{:S(2)}, u32[]{:S(2)}) collective-permute-start(bf16[192,256]{1,0:T(8,128)(2,1)S(1)} %get-tuple-element.39.total_ref), channel_id=1, source_target_pairs={{0,16},{2,18},{4,20},{6,22},{8,24},{10,26},{12,28},{14,30},{16,0},... | collective-permute-start | bytes 294920 | tf_op jit(solution)/shard_map/ppermute | solution.py:266
  41.4 6.6 %collective-permute-start.15 = (bf16[192,256]{1,0:T(8,128)(2,1)S(1)}, bf16[192,256]{1,0:T(8,128)(2,1)S(1)}, u32[]{:S(2)}, u32[]{:S(2)}) collective-permute-start(bf16[192,256]{1,0:T(8,128)(2,1)S(1)} %join.3.refs_0_), channel_id=1, source_target_pairs={{0,12},{2,14},{4,8},{6,10},{8,4},{10,6},{12,0},{14,2},{16,28},{18,... | collective-permute-start | bytes 294920 | tf_op jit(solution)/shard_map/ppermute | solution.py:266
  41.5 8.0 %collective-permute-start.16 = (bf16[192,256]{1,0:T(8,128)(2,1)S(1)}, bf16[192,256]{1,0:T(8,128)(2,1)S(1)}, u32[]{:S(2)}, u32[]{:S(2)}) collective-permute-start(bf16[192,256]{1,0:T(8,128)(2,1)S(1)} %join.3.refs_0_), channel_id=1, source_target_pairs={{0,4},{2,6},{4,0},{6,2},{8,12},{10,14},{12,8},{14,10},{16,20},{18,... | collective-permute-start | bytes 294920 | tf_op jit(solution)/shard_map/ppermute | solution.py:266
  43.1 7.1 %collective-permute-start.17 = (bf16[192,256]{1,0:T(8,128)(2,1)S(1)}, bf16[192,256]{1,0:T(8,128)(2,1)S(1)}, u32[]{:S(2)}, u32[]{:S(2)}) collective-permute-start(bf16[192,256]{1,0:T(8,128)(2,1)S(1)} %join.3.refs_0_), channel_id=1, source_target_pairs={{0,8},{2,10},{4,12},{6,14},{8,0},{10,2},{12,4},{14,6},{16,24},{18,... | collective-permute-start | bytes 294920 | tf_op jit(solution)/shard_map/ppermute | solution.py:266
  45.0 6.8 %collective-permute-start.11 = (bf16[192,256]{1,0:T(8,128)(2,1)S(1)}, bf16[192,256]{1,0:T(8,128)(2,1)S(1)}, u32[]{:S(2)}, u32[]{:S(2)}) collective-permute-start(bf16[192,256]{1,0:T(8,128)(2,1)S(1)} %join.2.refs_0_), channel_id=1, source_target_pairs={{0,12},{2,14},{4,8},{6,10},{8,4},{10,6},{12,0},{14,2},{16,28},{18,... | collective-permute-start | bytes 294920 | tf_op jit(solution)/shard_map/ppermute | solution.py:266
  46.0 5.8 %collective-permute-start.12 = (bf16[192,256]{1,0:T(8,128)(2,1)S(1)}, bf16[192,256]{1,0:T(8,128)(2,1)S(1)}, u32[]{:S(2)}, u32[]{:S(2)}) collective-permute-start(bf16[192,256]{1,0:T(8,128)(2,1)S(1)} %join.2.refs_0_), channel_id=1, source_target_pairs={{0,4},{2,6},{4,0},{6,2},{8,12},{10,14},{12,8},{14,10},{16,20},{18,... | collective-permute-start | bytes 294920 | tf_op jit(solution)/shard_map/ppermute | solution.py:266
  48.0 4.7 %collective-permute-start.13 = (bf16[192,256]{1,0:T(8,128)(2,1)S(1)}, bf16[192,256]{1,0:T(8,128)(2,1)S(1)}, u32[]{:S(2)}, u32[]{:S(2)}) collective-permute-start(bf16[192,256]{1,0:T(8,128)(2,1)S(1)} %join.2.refs_0_), channel_id=1, source_target_pairs={{0,8},{2,10},{4,12},{6,14},{8,0},{10,2},{12,4},{14,6},{16,24},{18,... | collective-permute-start | bytes 294920 | tf_op jit(solution)/shard_map/ppermute | solution.py:266
  50.2 2.7 %collective-permute-start.21 = (bf16[768,256]{1,0:T(8,128)(2,1)S(1)}, bf16[768,256]{1,0:T(8,128)(2,1)S(1)}, u32[]{:S(2)}, u32[]{:S(2)}) collective-permute-start(bf16[768,256]{1,0:T(8,128)(2,1)S(1)} %gather.2.rest_0_), channel_id=1, source_target_pairs={{0,2},{2,0},{4,6},{6,4},{8,10},{10,8},{12,14},{14,12},{16,18},{18,... | collective-permute-start | bytes 1179656 | tf_op jit(solution)/shard_map/ppermute | solution.py:266
  52.8 1.8 %collective-permute-start.20 = (bf16[768,256]{1,0:T(8,128)(2,1)S(1)}, bf16[768,256]{1,0:T(8,128)(2,1)S(1)}, u32[]{:S(2)}, u32[]{:S(2)}) collective-permute-start(bf16[768,256]{1,0:T(8,128)(2,1)S(1)} %gather.3.rest_0_), channel_id=1, source_target_pairs={{0,2},{2,0},{4,6},{6,4},{8,10},{10,8},{12,14},{14,12},{16,18},{18,... | collective-permute-start | bytes 1179656 | tf_op jit(solution)/shard_map/ppermute | solution.py:266

commit v12 on v11

--- a/solution.py
+++ b/solution.py
@@ -181,14 +181,11 @@
                 send_ref[step - 1, :, columns] = term.astype(jnp.bfloat16)
 
 
-def reduce_kernel(keep_ref, first_ref, second_ref, third_ref, after_value, after_key, *out_refs):
-    rows = out_refs[0].shape[0]
-    for part, out_ref in enumerate(out_refs):
-        span = slice(part * rows, (part + 1) * rows)
-        total = keep_ref[span]
-        for ref in (first_ref, second_ref, third_ref):
-            total += ref[span].astype(jnp.float32)
-        out_ref[...] = total.astype(out_ref.dtype)
+def reduce_kernel(keep_ref, first_ref, second_ref, third_ref, after_value, after_key, out_ref):
+    total = keep_ref[...]
+    for ref in (first_ref, second_ref, third_ref):
+        total += ref[...].astype(jnp.float32)
+    out_ref[...] = total.astype(out_ref.dtype)
 
 
 def join_kernel(total_ref, came_ref, out_ref):
@@ -199,8 +196,8 @@
 def gather_kernel(*refs):
     out_ref = refs[-1]
     rows = refs[0].shape[0]
-    for ref, step in zip(refs, (0, 3, 1, 2)):
-        out_ref[step * rows : (step + 1) * rows] = ref[...]
+    for index, ref in enumerate(refs[:3]):
+        out_ref[index * rows : (index + 1) * rows] = ref[...]
 
 
 def pool_kernel(key_ref, value_ref, key_came_ref, value_came_ref, key_out, value_out):
@@ -212,16 +209,20 @@
     value_out[...] = value_sum.astype(jnp.bfloat16)
 
 
-def place_kernel(place, *rest, sources, piece):
+def after_kernel(*refs):
+    pass
+
+
+def place_kernel(place, *rest, sources, quarter, piece):
     out_ref, sems = rest[-2:]
+    pieces = quarter // piece
     copies = []
-    for ref, (side, part) in zip(rest, sources):
+    for ref, (side, steps) in zip(rest, sources):
         width = ref.shape[1]
         columns = ways((place[0] ^ side) * width, width)
-        pieces = ref.shape[0] // (4 * piece)
-        for index in range(4 * pieces):
-            step, inner = divmod(index, pieces)
-            block = (2 * (place[1] ^ step) + part) * pieces + (inner ^ place[2])
+        for index in range(len(steps) * pieces):
+            turn, inner = divmod(index, pieces)
+            block = (place[1] ^ steps[turn]) * pieces + (inner ^ place[2])
             copies.append(
                 pltpu.make_async_copy(
                     ref.at[pl.ds(index * piece, piece)],
@@ -353,8 +354,7 @@
         if stride == 1:
             other_centre = added[1]
         stride *= steps
-    eighth = query_count // 8
-    quarter = 2 * eighth
+    quarter = query_count // 4
     keep, delta, *send = call(
         partial(combine_kernel, deltas=len(added), scale=scale),
         "combine",
@@ -407,15 +407,15 @@
     key_came = swap_shares(key_send)
 
     came = {step: flip(send[step - 1], 2 * step) for step in (3, 1, 2)}
-    totals = call(
+    (total,) = call(
         reduce_kernel,
         "reduce",
         (keep, came[3], came[1], came[2], value_send, key_send),
         [IN_VMEM] * 4 + [IN_HBM] * 2,
-        [pltpu.VMEM((eighth, width), bf16 if bits == 4 else f32)] * 2,
+        [pltpu.VMEM((quarter, width), bf16 if bits == 4 else f32)],
         work // 8,
     )
-    piece = eighth >> (bits - 4)
+    piece = quarter >> (bits - 4)
     inner = 0
     for bit in range(3, bits - 1):
         inner = 2 * inner + bit_of(bit)
@@ -430,41 +430,54 @@
     )
     pieces_place = jnp.stack([core, square, inner]).astype(jnp.int32)
 
-    def gathered(total, after):
-        whole = joined(total)
-        others = {step: flip(whole, 2 * step) for step in (3, 1, 2)}
-        return call(
-            gather_kernel,
-            "gather",
-            (whole, others[3], others[1], others[2], *after),
-            [IN_VMEM] * 4 + [IN_HBM] * len(after),
-            [pltpu.VMEM((4 * eighth, width), bf16)],
-            work // 16,
-        )[0]
-
     near = partial(pltpu.with_memory_space_constraint, memory_space=pltpu.VMEM)
     far = partial(pltpu.with_memory_space_constraint, memory_space=pltpu.HBM)
 
     def placed(name, sources, before, aliases):
         copied = len(sources)
         return call(
-            partial(place_kernel, sources=[source[1:] for source in sources], piece=piece),
+            partial(
+                place_kernel,
+                sources=[source[1:] for source in sources],
+                quarter=quarter,
+                piece=piece,
+            ),
             name,
             (pieces_place, *[near(source[0]) for source in sources], far(before)),
             [IN_SMEM] + [IN_VMEM] * copied + [IN_HBM],
             [pltpu.HBM((query_count, wide), bf16)],
             work // 2,
-            [pltpu.SemaphoreType.DMA((copied * 4 * eighth // piece,))],
+            [pltpu.SemaphoreType.DMA((4 * quarter // piece,))],
             [IN_HBM],
             {1 + copied: 0} if aliases else {},
         )[0]
 
-    mine = [gathered(totals[0], ())]
-    begun = placed("first_rows", [(mine[0], 0, 0)], key_grad, False)
-    mine.append(gathered(totals[1], (far(begun),)))
-    theirs = [flip(array, 1) for array in mine]
-    begun = placed("own_rows", [(mine[1], 0, 1), (theirs[0], 1, 0)], begun, True)
-    return placed("other_rows", [(theirs[1], 1, 1)], begun, True), key_grad, value_grad
+    part = joined(total)
+    steps = (3, 1, 2)
+    others = [flip(part, 2 * step) for step in steps]
+    begun = placed("first_rows", [(part, 0, (0,))], key_grad, False)
+    (same_part,) = call(
+        after_kernel,
+        "after",
+        (part, far(begun)),
+        [IN_HBM] * 2,
+        [pltpu.VMEM((quarter, width), bf16)],
+        work // 1000,
+        out_specs=[IN_HBM],
+        aliases={0: 0},
+    )
+    part_came = flip(same_part, 1)
+    (mine,) = call(
+        gather_kernel,
+        "gather",
+        (*others, same_part),
+        [IN_VMEM] * 3 + [IN_HBM],
+        [pltpu.VMEM((3 * quarter, width), bf16)],
+        work // 16,
+    )
+    theirs = flip(mine, 1)
+    begun = placed("own_rows", [(mine, 0, steps), (part_came, 1, (0,))], begun, True)
+    return placed("other_rows", [(theirs, 1, steps)], begun, True), key_grad, value_grad
 
 
 def solution(mesh):

time: 56.1 us -> 59.1 us (1.053)
  waiting for transfers between devices: 14.3 us -> 21.3 us
  starting transfers between devices: 22.2 us -> 18 us
    ppermute x20 -> x16, waiting for transfers between devices: 14.3 us -> 21.2 us  [flip(): lax.ppermute(array, 'val', [(i, i ^ mask) for i in range(value_devices)])]
    ppermute x20 -> x16, starting transfers between devices: 20.1 us -> 16 us  [flip(): lax.ppermute(array, 'val', [(i, i ^ mask) for i in range(value_devices)])]
    pallas_call x16 -> x15, Pallas kernels: 18.3 us -> 18.7 us  [call(): pl.pallas_call(kernel, in_specs=in_specs, out_specs=[IN_VMEM] * len(outpu...]
  transfers between devices with their start and end apart: 22 -> 18, of which waited for: 9 -> 8; matrix products, arithmetic and copies ran while one was open for 0% -> 0% of each run, Pallas kernels for 21% -> 19%
where the time goes in v12:
time: 59.1 us; the launch traced here: 58.8 us
  waiting for transfers between devices  21.3 us (36%)
  Pallas kernels  18.7 us (32%)
  starting transfers between devices  18 us (30%)
  between operations  0.8 us (1%)
    ppermute x16, waiting for transfers between devices, flip(): lax.ppermute(array, 'val', [(i, i ^ mask) for i in range(value_devices)])  21.2 us
    pallas_call x15, Pallas kernels, call(): pl.pallas_call(kernel, in_specs=in_specs, out_specs=[IN_VMEM] * len(outpu...  18.7 us
    ppermute x16, starting transfers between devices, flip(): lax.ppermute(array, 'val', [(i, i ^ mask) for i in range(value_devices)])  16 us
    ppermute x2, starting transfers between devices, swap_shares(): lax.ppermute(send[step - 1], 'qry', [(i, (i + step) % parts) for i in ran...  2.03 us
  transfers between devices with their start and end apart: 18, of which 8 were waited for; matrix products, arithmetic and copies ran while one was open for 0% of the time, Pallas kernels for 19%

profile of v12, /device:TPU:0, one launch (start us, length us, event | category | flops | bytes accessed | tf_op | source)
XLA Modules:
  0.0 58.8 jit_solution(16333386114020764477)
XLA Ops:
  0.7 0.1 pad_add_fusion.1.place
  0.7 0.0 copy-start
  0.7 4.5 %forward_pass.1 = (f32[4,1536]{1,0:T(4,128)S(1)}, f32[2,512,1536]{2,1,0:T(8,128)S(1)}, f32[2,512,1536]{2,1,0:T(8,128)S(1)}, bf16[1536,512]{1,0:T(8,128)(2,1)S(1)...) custom-call(s32[4]{0:T(128)S(1)} %pad_add_fusion.1.place, s32[2,1,6]{2,1,0:T(1,128)} %compat_hbm.1, ...), custom_call_target="tpu_custom_call" | custom-call | flops 1610612736 | bytes 1610612 | tf_op jit(solution)/shard_map/forward_pass/pallas_call | solution.py:239
  5.3 0.1 collective-permute-start
  5.4 3.0 %collective-permute-start.1 = (f32[4,1536]{1,0:T(4,128)S(1)}, f32[4,1536]{1,0:T(4,128)S(1)}, u32[]{:S(2)}, u32[]{:S(2)}) collective-permute-start(f32[4,1536]{1,0:T(4,128)S(1)} %get-tuple-element.22.delta_ref.refs_0_.centre_ref), channel_id=1, source_target_pairs={{0,4},{2,6},{4,0},{6,2},{8,12},{10,14},{12,8},{14,10},{16,20},{18,... | collective-permute-start | bytes 73736 | tf_op jit(solution)/shard_map/ppermute | solution.py:267
  8.4 0.1 collective-permute-start.2
  8.5 0.0 copy-done
  8.5 2.0 %other_head.1.refs_4_ = f32[2,1536,256]{2,1,0:T(8,128)S(1)} custom-call(s32[4]{0:T(128)S(1)} %pad_add_fusion.1.place, f32[4,1536]{1,0:T(4,128)S(1)} %get-tuple-element.22.delta_ref.refs_0_.centre_ref, f32[2,512,1536]{2,1,0:T(8,128)S(1)} %get-tuple-element.23.probs_ref, f32[2,512,1536]{2,1,0:T(8,128)S(1)} %get-tuple-element.24.dprobs_ref, ...), custom_call_target="tpu_custom_call" | custom-call | flops 805306368 | bytes 805306 | tf_op jit(solution)/shard_map/other_head/pallas_call | solution.py:239
  10.5 0.0 collective-permute-done.refs_1_.came_ref
  10.5 0.0 collective-permute-done.1.refs_2_
  10.5 1.2 %collective-permute-done.2.refs_3_ = f32[4,1536]{1,0:T(4,128)S(1)} collective-permute-done((f32[4,1536]{1,0:T(4,128)S(1)}, f32[4,1536]{1,0:T(4,128)S(1)}, u32[]{:S(2)}, u32[]{:S(2)}) %collective-permute-start.2) | collective-permute-done | bytes 24608 | tf_op jit(solution)/shard_map/ppermute | solution.py:267
  11.7 0.2 collective-permute-start.3
  11.9 0.9 %collective-permute-start.4 = (f32[2,1536]{1,0:T(2,128)S(1)}, f32[2,1536]{1,0:T(2,128)S(1)}, u32[]{:S(2)}, u32[]{:S(2)}) collective-permute-start(f32[2,1536]{1,0:T(2,128)S(1)} %get-tuple-element.27.rest_0_), channel_id=1, source_target_pairs={{0,8},{2,10},{4,12},{6,14},{8,0},{10,2},{12,4},{14,6},{16,24},{18,... | collective-permute-start | bytes 36872 | tf_op jit(solution)/shard_map/ppermute | solution.py:267
  12.8 2.5 %collective-permute-start.5 = (f32[2,1536]{1,0:T(2,128)S(1)}, f32[2,1536]{1,0:T(2,128)S(1)}, u32[]{:S(2)}, u32[]{:S(2)}) collective-permute-start(f32[2,1536]{1,0:T(2,128)S(1)} %get-tuple-element.27.rest_0_), channel_id=1, source_target_pairs={{0,16},{2,18},{4,20},{6,22},{8,24},{10,26},{12,28},{14,30},{16,0},... | collective-permute-start | bytes 36872 | tf_op jit(solution)/shard_map/ppermute | solution.py:267
  15.2 1.0 %collective-permute-start.6 = (f32[2,1536]{1,0:T(2,128)S(1)}, f32[2,1536]{1,0:T(2,128)S(1)}, u32[]{:S(2)}, u32[]{:S(2)}) collective-permute-start(f32[2,1536]{1,0:T(2,128)S(1)} %get-tuple-element.27.rest_0_), channel_id=1, source_target_pairs={{0,24},{2,26},{4,28},{6,30},{8,16},{10,18},{12,20},{14,22},{16,8},... | collective-permute-start | bytes 36872 | tf_op jit(solution)/shard_map/ppermute | solution.py:267
  16.3 2.0 %own_head.1.own_ref = f32[2,1536,256]{2,1,0:T(8,128)S(1)} custom-call(s32[4]{0:T(128)S(1)} %pad_add_fusion.1.place, f32[4,1536]{1,0:T(4,128)S(1)} %get-tuple-element.22.delta_ref.refs_0_.centre_ref, f32[2,512,1536]{2,1,0:T(8,128)S(1)} %get-tuple-element.23.probs_ref, f32[2,512,1536]{2,1,0:T(8,128)S(1)} %get-tuple-element.24.dprobs_ref, ...), custom_call_target="tpu_custom_call" | custom-call | flops 805306368 | bytes 805306 | tf_op jit(solution)/shard_map/own_head/pallas_call | solution.py:239
  18.3 0.0 collective-permute-done.4.rest_1_
  18.3 0.0 collective-permute-done.5.rest_2_
  18.3 2.5 %collective-permute-done.6.rest_3_ = f32[2,1536]{1,0:T(2,128)S(1)} collective-permute-done((f32[2,1536]{1,0:T(2,128)S(1)}, f32[2,1536]{1,0:T(2,128)S(1)}, u32[]{:S(2)}, u32[]{:S(2)}) %collective-permute-start.6) | collective-permute-done | bytes 12320 | tf_op jit(solution)/shard_map/ppermute | solution.py:267
  20.7 0.0 collective-permute-done.3.received_ref
  20.7 1.2 %combine.1 = (f32[384,256]{1,0:T(8,128)S(1)}, f32[2,1536]{1,0:T(2,128)S(1)}, bf16[384,256]{1,0:T(8,128)(2,1)S(1)}, bf16[384,256]{1,0:T(8,128)(2,1)S(1)}, bf16[384,256]{1,0:T(8,128)(2,1)S(1)}) custom-call(s32[4]{0:T(128)S(1)} %pad_add_fusion.1.place, f32[2,1536,256]{2,1,0:T(8,128)S(1)} %own_head.1.own_ref, ...), custom_call_target="tpu_custom_call" | custom-call | flops 100663296 | bytes 100663 | tf_op jit(solution)/shard_map/combine/pallas_call | solution.py:239
  21.9 0.1 collective-permute-start.7
  22.0 0.7 %collective-permute-start.8 = (bf16[384,256]{1,0:T(8,128)(2,1)S(1)}, bf16[384,256]{1,0:T(8,128)(2,1)S(1)}, u32[]{:S(2)}, u32[]{:S(2)}) collective-permute-start(bf16[384,256]{1,0:T(8,128)(2,1)S(1)} %get-tuple-element.30), channel_id=1, source_target_pairs={{0,4},{2,6},{4,0},{6,2},{8,12},{10,14},{12,8},{14,10},{16,20},{18,... | collective-permute-start | bytes 589832 | tf_op jit(solution)/shard_map/ppermute | solution.py:267
  22.7 2.8 %collective-permute-start.9 = (bf16[384,256]{1,0:T(8,128)(2,1)S(1)}, bf16[384,256]{1,0:T(8,128)(2,1)S(1)}, u32[]{:S(2)}, u32[]{:S(2)}) collective-permute-start(bf16[384,256]{1,0:T(8,128)(2,1)S(1)} %get-tuple-element.31), channel_id=1, source_target_pairs={{0,8},{2,10},{4,12},{6,14},{8,0},{10,2},{12,4},{14,6},{16,24},{18,... | collective-permute-start | bytes 589832 | tf_op jit(solution)/shard_map/ppermute | solution.py:267
  25.5 2.2 %key_terms.1 = (f32[256,512]{1,0:T(8,128)S(1)}, bf16[1,256,512]{2,1,0:T(8,128)(2,1)S(1)}) custom-call(s32[4]{0:T(128)S(1)} %pad_add_fusion.1.place, f32[2,1536]{1,0:T(2,128)S(1)} %get-tuple-element.33.after_ref.delta_ref, f32[2,512,1536]{2,1,0:T(8,128)S(1)} %get-tuple-element.23.probs_ref, f32[2,512,1536]{2,1,0:T(8,128)S(1)} %get-tuple-element.24.dprobs_ref, ...), custom_call_target="tpu_custom_call" | custom-call | flops 805306368 | bytes 805306 | tf_op jit(solution)/shard_map/key_terms/pallas_call | solution.py:239
  27.7 1.5 %value_terms.1 = (f32[256,512]{1,0:T(8,128)S(1)}, bf16[1,256,512]{2,1,0:T(8,128)(2,1)S(1)}) custom-call(s32[4]{0:T(128)S(1)} %pad_add_fusion.1.place, f32[2,512,1536]{2,1,0:T(8,128)S(1)} %get-tuple-element.23.probs_ref, bf16[1536,512]{1,0:T(8,128)(2,1)S(1)} %get-tuple-element.32.g_ref, f32[2,1536]{1,0:T(2,128)S(1)} %get-tuple-element.33.after_ref.delta_ref), custom_call_target="tpu_custom_call" | custom-call | flops 805306368 | bytes 805306 | tf_op jit(solution)/shard_map/value_terms/pallas_call | solution.py:239
  29.3 1.3 %collective-permute-done.7.first_ref = bf16[384,256]{1,0:T(8,128)(2,1)S(1)} collective-permute-done((bf16[384,256]{1,0:T(8,128)(2,1)S(1)}, bf16[384,256]{1,0:T(8,128)(2,1)S(1)}, u32[]{:S(2)}, u32[]{:S(2)}) %collective-permute-start.7) | collective-permute-done | bytes 196640 | tf_op jit(solution)/shard_map/ppermute | solution.py:267
  30.6 1.2 %collective-permute-done.8.second_ref = bf16[384,256]{1,0:T(8,128)(2,1)S(1)} collective-permute-done((bf16[384,256]{1,0:T(8,128)(2,1)S(1)}, bf16[384,256]{1,0:T(8,128)(2,1)S(1)}, u32[]{:S(2)}, u32[]{:S(2)}) %collective-permute-start.8) | collective-permute-done | bytes 196640 | tf_op jit(solution)/shard_map/ppermute | solution.py:267
  31.8 0.0 collective-permute-done.9.third_ref
  31.8 0.1 reduce.1.total_ref
  31.9 0.5 collective-permute-start.10
  32.4 1.6 %collective-permute-start.14 = (bf16[256,512]{1,0:T(8,128)(2,1)S(1)}, bf16[256,512]{1,0:T(8,128)(2,1)S(1)}, u32[]{:S(2)}, u32[]{:S(2)}) collective-permute-start(bf16[256,512]{1,0:T(8,128)(2,1)S(1)} %bitcast.9), channel_id=1, source_target_pairs={{0,1},{1,0},{2,3},{3,2},{4,5},{5,4},{6,7},{7,6},{8,9},{9,8},{10,11... | collective-permute-start | bytes 786440 | tf_op jit(solution)/shard_map/ppermute | solution.py:271
  34.1 0.4 collective-permute-start.15
  34.5 7.9 %collective-permute-done.10.came_ref = bf16[384,256]{1,0:T(8,128)(2,1)S(1)} collective-permute-done((bf16[384,256]{1,0:T(8,128)(2,1)S(1)}, bf16[384,256]{1,0:T(8,128)(2,1)S(1)}, u32[]{:S(2)}, u32[]{:S(2)}) %collective-permute-start.10) | collective-permute-done | bytes 196640 | tf_op jit(solution)/shard_map/ppermute | solution.py:267
  42.4 0.1 collective-permute-start.11
  42.5 1.0 %collective-permute-start.12 = (bf16[384,256]{1,0:T(8,128)(2,1)S(1)}, bf16[384,256]{1,0:T(8,128)(2,1)S(1)}, u32[]{:S(2)}, u32[]{:S(2)}) collective-permute-start(bf16[384,256]{1,0:T(8,128)(2,1)S(1)} %join.1.rest_0_.refs_0_), channel_id=1, source_target_pairs={{0,4},{2,6},{4,0},{6,2},{8,12},{10,14},{12,8},{14,10},{16,20},{18,... | collective-permute-start | bytes 589832 | tf_op jit(solution)/shard_map/ppermute | solution.py:267
  43.6 2.4 %collective-permute-start.13 = (bf16[384,256]{1,0:T(8,128)(2,1)S(1)}, bf16[384,256]{1,0:T(8,128)(2,1)S(1)}, u32[]{:S(2)}, u32[]{:S(2)}) collective-permute-start(bf16[384,256]{1,0:T(8,128)(2,1)S(1)} %join.1.rest_0_.refs_0_), channel_id=1, source_target_pairs={{0,8},{2,10},{4,12},{6,14},{8,0},{10,2},{12,4},{14,6},{16,24},{18,... | collective-permute-start | bytes 589832 | tf_op jit(solution)/shard_map/ppermute | solution.py:267
  46.0 0.1 pad_add_fusion.place
  46.0 0.0 collective-permute-done.14
  46.0 0.0 collective-permute-done.15
  46.0 0.9 %pool_sum.1 = (bf16[256,512]{1,0:T(8,128)(2,1)}, bf16[256,512]{1,0:T(8,128)(2,1)}) custom-call(f32[256,512]{1,0:T(8,128)S(1)} %get-tuple-element.37.key_ref, f32[256,512]{1,0:T(8,128)S(1)} %get-tuple-element.38.value_ref, bf16[1,256,512]{2,1,0:T(8,128)(2,1)S(1)} %bitcast.11, bf16[1,256,512]{2,1,0:T(8,128)(2,1)S(1)} %bitcast.12), custom_call_target="tpu_custom_call" | custom-call | flops 50331648 | bytes 50331 | tf_op jit(solution)/shard_map/pool_sum/pallas_call | solution.py:239
  46.9 1.3 %first_rows.1.refs_1_.rest_2_ = bf16[1536,512]{1,0:T(8,128)(2,1)} custom-call(s32[3]{0:T(128)S(1)} %pad_add_fusion.place, bf16[384,256]{1,0:T(8,128)(2,1)S(1)} %join.1.rest_0_.refs_0_, bf16[256,512]{1,0:T(8,128)(2,1)} %get-tuple-element.20.rest_1_), custom_call_target="tpu_custom_call" | custom-call | flops 201326592 | bytes 201326 | tf_op jit(solution)/shard_map/first_rows/pallas_call | solution.py:239
  48.2 3.0 %collective-permute-done.11.refs_0_ = bf16[384,256]{1,0:T(8,128)(2,1)S(1)} collective-permute-done((bf16[384,256]{1,0:T(8,128)(2,1)S(1)}, bf16[384,256]{1,0:T(8,128)(2,1)S(1)}, u32[]{:S(2)}, u32[]{:S(2)}) %collective-permute-start.11) | collective-permute-done | bytes 196640 | tf_op jit(solution)/shard_map/ppermute | solution.py:267
  51.2 2.4 %collective-permute-done.12.refs_1_ = bf16[384,256]{1,0:T(8,128)(2,1)S(1)} collective-permute-done((bf16[384,256]{1,0:T(8,128)(2,1)S(1)}, bf16[384,256]{1,0:T(8,128)(2,1)S(1)}, u32[]{:S(2)}, u32[]{:S(2)}) %collective-permute-start.12) | collective-permute-done | bytes 196640 | tf_op jit(solution)/shard_map/ppermute | solution.py:267
  53.6 0.0 collective-permute-done.13.refs_2_
  53.6 0.1 collective-permute-start.16
  53.7 0.5 collective-permute-start.17
  54.2 1.8 %collective-permute-done.17.rest_1_ = bf16[384,256]{1,0:T(8,128)(2,1)S(1)} collective-permute-done((bf16[384,256]{1,0:T(8,128)(2,1)S(1)}, bf16[384,256]{1,0:T(8,128)(2,1)S(1)}, u32[]{:S(2)}, u32[]{:S(2)}) %collective-permute-start.17) | collective-permute-done | bytes 196640 | tf_op jit(solution)/shard_map/ppermute | solution.py:267
  56.0 1.5 %own_rows.1.rest_1_ = bf16[1536,512]{1,0:T(8,128)(2,1)} custom-call(s32[3]{0:T(128)S(1)} %pad_add_fusion.place, bf16[1152,256]{1,0:T(8,128)(2,1)S(1)} %gather.1.rest_0_, bf16[384,256]{1,0:T(8,128)(2,1)S(1)} %collective-permute-done.17.rest_1_, bf16[1536,512]{1,0:T(8,128)(2,1)} %first_rows.1.refs_1_.rest_2_), custom_call_target="tpu_custom_call", output_to_operand_aliasing={{}: (3, {})} | custom-call | flops 201326592 | bytes 201326 | tf_op jit(solution)/shard_map/own_rows/pallas_call | solution.py:239
  57.4 0.0 collective-permute-done.16.rest_0_
  57.5 1.4 %other_rows.1 = bf16[1536,512]{1,0:T(8,128)(2,1)} custom-call(s32[3]{0:T(128)S(1)} %pad_add_fusion.place, bf16[1152,256]{1,0:T(8,128)(2,1)S(1)} %collective-permute-done.16.rest_0_, bf16[1536,512]{1,0:T(8,128)(2,1)} %own_rows.1.rest_1_), custom_call_target="tpu_custom_call", output_to_operand_aliasing={{}: (2, {})} | custom-call | flops 201326592 | bytes 201326 | tf_op jit(solution)/shard_map/other_rows/pallas_call | solution.py:239
  (4 shorter events, 0.1 us)
Async XLA Ops:
  0.7 7.7 %copy-start = (s32[1536,2]{0,1:T(2,128)S(1)}, s32[1536,2]{0,1:T(2,128)}, u32[]{:S(2)}) copy-start(s32[1536,2]{0,1:T(2,128)} %param.13) | copy-start | bytes 36868
  5.3 5.2 %collective-permute-start = (f32[4,1536]{1,0:T(4,128)S(1)}, f32[4,1536]{1,0:T(4,128)S(1)}, u32[]{:S(2)}, u32[]{:S(2)}) collective-permute-start(f32[4,1536]{1,0:T(4,128)S(1)} %get-tuple-element.22.delta_ref.refs_0_.centre_ref), channel_id=1, source_target_pairs={{0,2},{2,0},{4,6},{6,4},{8,10},{10,8},{12,14},{14,12},{16,18},{18,... | collective-permute-start | bytes 73736 | tf_op jit(solution)/shard_map/ppermute | solution.py:267
  5.4 5.1 %collective-permute-start.1 = (f32[4,1536]{1,0:T(4,128)S(1)}, f32[4,1536]{1,0:T(4,128)S(1)}, u32[]{:S(2)}, u32[]{:S(2)}) collective-permute-start(f32[4,1536]{1,0:T(4,128)S(1)} %get-tuple-element.22.delta_ref.refs_0_.centre_ref), channel_id=1, source_target_pairs={{0,4},{2,6},{4,0},{6,2},{8,12},{10,14},{12,8},{14,10},{16,20},{18,... | collective-permute-start | bytes 73736 | tf_op jit(solution)/shard_map/ppermute | solution.py:267
  8.4 3.3 %collective-permute-start.2 = (f32[4,1536]{1,0:T(4,128)S(1)}, f32[4,1536]{1,0:T(4,128)S(1)}, u32[]{:S(2)}, u32[]{:S(2)}) collective-permute-start(f32[4,1536]{1,0:T(4,128)S(1)} %get-tuple-element.22.delta_ref.refs_0_.centre_ref), channel_id=1, source_target_pairs={{0,6},{2,4},{4,2},{6,0},{8,14},{10,12},{12,10},{14,8},{16,22},{18,... | collective-permute-start | bytes 73736 | tf_op jit(solution)/shard_map/ppermute | solution.py:267
  11.7 9.1 %collective-permute-start.3 = (f32[2,1536,256]{2,1,0:T(8,128)S(1)}, f32[2,1536,256]{2,1,0:T(8,128)S(1)}, u32[]{:S(2)}, u32[]{:S(2)}) collective-permute-start(f32[2,1536,256]{2,1,0:T(8,128)S(1)} %get-tuple-element.26), channel_id=1, source_target_pairs={{0,2},{2,0},{4,6},{6,4},{8,10},{10,8},{12,14},{14,12},{16,18},{18,... | collective-permute-start | bytes 9437192 | tf_op jit(solution)/shard_map/ppermute | solution.py:267
  11.9 6.4 %collective-permute-start.4 = (f32[2,1536]{1,0:T(2,128)S(1)}, f32[2,1536]{1,0:T(2,128)S(1)}, u32[]{:S(2)}, u32[]{:S(2)}) collective-permute-start(f32[2,1536]{1,0:T(2,128)S(1)} %get-tuple-element.27.rest_0_), channel_id=1, source_target_pairs={{0,8},{2,10},{4,12},{6,14},{8,0},{10,2},{12,4},{14,6},{16,24},{18,... | collective-permute-start | bytes 36872 | tf_op jit(solution)/shard_map/ppermute | solution.py:267
  12.8 5.5 %collective-permute-start.5 = (f32[2,1536]{1,0:T(2,128)S(1)}, f32[2,1536]{1,0:T(2,128)S(1)}, u32[]{:S(2)}, u32[]{:S(2)}) collective-permute-start(f32[2,1536]{1,0:T(2,128)S(1)} %get-tuple-element.27.rest_0_), channel_id=1, source_target_pairs={{0,16},{2,18},{4,20},{6,22},{8,24},{10,26},{12,28},{14,30},{16,0},... | collective-permute-start | bytes 36872 | tf_op jit(solution)/shard_map/ppermute | solution.py:267
  15.2 5.5 %collective-permute-start.6 = (f32[2,1536]{1,0:T(2,128)S(1)}, f32[2,1536]{1,0:T(2,128)S(1)}, u32[]{:S(2)}, u32[]{:S(2)}) collective-permute-start(f32[2,1536]{1,0:T(2,128)S(1)} %get-tuple-element.27.rest_0_), channel_id=1, source_target_pairs={{0,24},{2,26},{4,28},{6,30},{8,16},{10,18},{12,20},{14,22},{16,8},... | collective-permute-start | bytes 36872 | tf_op jit(solution)/shard_map/ppermute | solution.py:267
  21.9 8.7 %collective-permute-start.7 = (bf16[384,256]{1,0:T(8,128)(2,1)S(1)}, bf16[384,256]{1,0:T(8,128)(2,1)S(1)}, u32[]{:S(2)}, u32[]{:S(2)}) collective-permute-start(bf16[384,256]{1,0:T(8,128)(2,1)S(1)} %get-tuple-element.29), channel_id=1, source_target_pairs={{0,12},{2,14},{4,8},{6,10},{8,4},{10,6},{12,0},{14,2},{16,28},{18,... | collective-permute-start | bytes 589832 | tf_op jit(solution)/shard_map/ppermute | solution.py:267
  22.0 9.8 %collective-permute-start.8 = (bf16[384,256]{1,0:T(8,128)(2,1)S(1)}, bf16[384,256]{1,0:T(8,128)(2,1)S(1)}, u32[]{:S(2)}, u32[]{:S(2)}) collective-permute-start(bf16[384,256]{1,0:T(8,128)(2,1)S(1)} %get-tuple-element.30), channel_id=1, source_target_pairs={{0,4},{2,6},{4,0},{6,2},{8,12},{10,14},{12,8},{14,10},{16,20},{18,... | collective-permute-start | bytes 589832 | tf_op jit(solution)/shard_map/ppermute | solution.py:267
  22.7 9.1 %collective-permute-start.9 = (bf16[384,256]{1,0:T(8,128)(2,1)S(1)}, bf16[384,256]{1,0:T(8,128)(2,1)S(1)}, u32[]{:S(2)}, u32[]{:S(2)}) collective-permute-start(bf16[384,256]{1,0:T(8,128)(2,1)S(1)} %get-tuple-element.31), channel_id=1, source_target_pairs={{0,8},{2,10},{4,12},{6,14},{8,0},{10,2},{12,4},{14,6},{16,24},{18,... | collective-permute-start | bytes 589832 | tf_op jit(solution)/shard_map/ppermute | solution.py:267
  31.9 10.4 %collective-permute-start.10 = (bf16[384,256]{1,0:T(8,128)(2,1)S(1)}, bf16[384,256]{1,0:T(8,128)(2,1)S(1)}, u32[]{:S(2)}, u32[]{:S(2)}) collective-permute-start(bf16[384,256]{1,0:T(8,128)(2,1)S(1)} %reduce.1.total_ref), channel_id=1, source_target_pairs={{0,16},{2,18},{4,20},{6,22},{8,24},{10,26},{12,28},{14,30},{16,0},... | collective-permute-start | bytes 589832 | tf_op jit(solution)/shard_map/ppermute | solution.py:267
  32.4 13.6 %collective-permute-start.14 = (bf16[256,512]{1,0:T(8,128)(2,1)S(1)}, bf16[256,512]{1,0:T(8,128)(2,1)S(1)}, u32[]{:S(2)}, u32[]{:S(2)}) collective-permute-start(bf16[256,512]{1,0:T(8,128)(2,1)S(1)} %bitcast.9), channel_id=1, source_target_pairs={{0,1},{1,0},{2,3},{3,2},{4,5},{5,4},{6,7},{7,6},{8,9},{9,8},{10,11... | collective-permute-start | bytes 786440 | tf_op jit(solution)/shard_map/ppermute | solution.py:271
  34.1 12.0 %collective-permute-start.15 = (bf16[256,512]{1,0:T(8,128)(2,1)S(1)}, bf16[256,512]{1,0:T(8,128)(2,1)S(1)}, u32[]{:S(2)}, u32[]{:S(2)}) collective-permute-start(bf16[256,512]{1,0:T(8,128)(2,1)S(1)} %bitcast.10), channel_id=1, source_target_pairs={{0,1},{1,0},{2,3},{3,2},{4,5},{5,4},{6,7},{7,6},{8,9},{9,8},{10,11... | collective-permute-start | bytes 786440 | tf_op jit(solution)/shard_map/ppermute | solution.py:271
  42.4 8.8 %collective-permute-start.11 = (bf16[384,256]{1,0:T(8,128)(2,1)S(1)}, bf16[384,256]{1,0:T(8,128)(2,1)S(1)}, u32[]{:S(2)}, u32[]{:S(2)}) collective-permute-start(bf16[384,256]{1,0:T(8,128)(2,1)S(1)} %join.1.rest_0_.refs_0_), channel_id=1, source_target_pairs={{0,12},{2,14},{4,8},{6,10},{8,4},{10,6},{12,0},{14,2},{16,28},{18,... | collective-permute-start | bytes 589832 | tf_op jit(solution)/shard_map/ppermute | solution.py:267
  42.5 11.1 %collective-permute-start.12 = (bf16[384,256]{1,0:T(8,128)(2,1)S(1)}, bf16[384,256]{1,0:T(8,128)(2,1)S(1)}, u32[]{:S(2)}, u32[]{:S(2)}) collective-permute-start(bf16[384,256]{1,0:T(8,128)(2,1)S(1)} %join.1.rest_0_.refs_0_), channel_id=1, source_target_pairs={{0,4},{2,6},{4,0},{6,2},{8,12},{10,14},{12,8},{14,10},{16,20},{18,... | collective-permute-start | bytes 589832 | tf_op jit(solution)/shard_map/ppermute | solution.py:267
  43.6 10.0 %collective-permute-start.13 = (bf16[384,256]{1,0:T(8,128)(2,1)S(1)}, bf16[384,256]{1,0:T(8,128)(2,1)S(1)}, u32[]{:S(2)}, u32[]{:S(2)}) collective-permute-start(bf16[384,256]{1,0:T(8,128)(2,1)S(1)} %join.1.rest_0_.refs_0_), channel_id=1, source_target_pairs={{0,8},{2,10},{4,12},{6,14},{8,0},{10,2},{12,4},{14,6},{16,24},{18,... | collective-permute-start | bytes 589832 | tf_op jit(solution)/shard_map/ppermute | solution.py:267
  53.6 3.8 %collective-permute-start.16 = (bf16[1152,256]{1,0:T(8,128)(2,1)S(1)}, bf16[1152,256]{1,0:T(8,128)(2,1)S(1)}, u32[]{:S(2)}, u32[]{:S(2)}) collective-permute-start(bf16[1152,256]{1,0:T(8,128)(2,1)S(1)} %gather.1.rest_0_), channel_id=1, source_target_pairs={{0,2},{2,0},{4,6},{6,4},{8,10},{10,8},{12,14},{14,12},{16,18},{18,... | collective-permute-start | bytes 1769480 | tf_op jit(solution)/shard_map/ppermute | solution.py:267
  53.7 2.3 %collective-permute-start.17 = (bf16[384,256]{1,0:T(8,128)(2,1)S(1)}, bf16[384,256]{1,0:T(8,128)(2,1)S(1)}, u32[]{:S(2)}, u32[]{:S(2)}) collective-permute-start(bf16[384,256]{1,0:T(8,128)(2,1)S(1)} %after.1.refs_3_), channel_id=1, source_target_pairs={{0,2},{2,0},{4,6},{6,4},{8,10},{10,8},{12,14},{14,12},{16,18},{18,... | collective-permute-start | bytes 589832 | tf_op jit(solution)/shard_map/ppermute | solution.py:267
